TPU v7x, 32 devices: a whole 2x2x4 slice. The times are simulated.
32 devices in a mesh: dp: 4 (over x, core), dap: 8 (over z, y).
Axes of the slice: x: 2, y: 2, z: 4, core: 2. Of those that a mesh axis runs over, the one named last changes fastest.
Arguments:
- pair_repr: bfloat16 [4, 32, 32, 128], P('dp', 'dap'), may hold values from -16 to 16
- pair_mask: int32 [4, 32, 32], P('dp', 'dap'), may hold values from 0 to 1, as said below
- cotangent: bfloat16 [4, 32, 32, 128], P('dp', 'dap'), may hold values from -6 to 6
- proj_weight: bfloat16 [2, 128, 640], replicated, may hold values from -0.5 to 0.5
- proj_bias: float32 [2, 640], replicated, may hold values from -3 to 3
- norm_gain: float32 [2, 256], replicated, may hold values from 0.1 to 1.9
- norm_shift: float32 [2, 256], replicated, may hold values from -3 to 3
- out_weight: bfloat16 [2, 128, 128], replicated, may hold values from -0.5 to 0.5
- out_bias: float32 [2, 128], replicated, may hold values from -3 to 3
Outputs:
- pair_grad: bfloat16 [4, 32, 32, 128], P('dp', 'dap')
- proj_weight_grad: float32 [2, 128, 640], replicated
- out_weight_grad: float32 [2, 128, 128], replicated
Inputs may be any that keep to these rules, and one draw needn't show every extreme that they name: pair_mask[c, i, j] is 1 exactly when residues i and j both lie below crop c's length, which is at least 16 and below 32.
All inputs are finite; a program needn't handle non-finite values.
Results may differ from a plain program's by a relative error of at most 0.015.
Values may be sent and summed in bfloat16 or wider, within the bound.
No kernel may reach another device: no remote copies, remote signals or barrier semaphores. Data moves between devices by JAX's collectives and lax.ppermute only.
A program may use at most 64 MiB of HBM per device.

v0:
```python
import jax
import jax.numpy as jnp
from jax import lax
from jax.sharding import PartitionSpec as P

NORM_EPSILON = 1e-05


def layer_norm(values, gain_vec, shift_vec, norm_axis):
    mean_value = jnp.mean(values, axis=norm_axis, keepdims=True)
    centred = values - mean_value
    variance = jnp.mean(centred * centred, axis=norm_axis, keepdims=True)
    return centred * lax.rsqrt(variance + NORM_EPSILON) * gain_vec + shift_vec


def norm_pullback(values, gain_vec, shift_vec, norm_axis, upstream):
    _, pull_back = jax.vjp(
        lambda inner_value: layer_norm(inner_value, gain_vec, shift_vec, norm_axis), values
    )
    return pull_back(upstream)[0]


def edge_pair(edge_pre, cell_mask):
    left_edge = jax.nn.sigmoid(edge_pre[1]) * edge_pre[0] * cell_mask
    right_edge = jax.nn.sigmoid(edge_pre[3]) * edge_pre[2] * cell_mask
    return jnp.stack([left_edge, right_edge]).astype(jnp.bfloat16)


def edge_pullback(edge_pre, cell_mask, grad_pair):
    sig_left = jax.nn.sigmoid(edge_pre[1])
    sig_right = jax.nn.sigmoid(edge_pre[3])
    grad_left = grad_pair[0].astype(jnp.float32) * cell_mask
    grad_right = grad_pair[1].astype(jnp.float32) * cell_mask
    return jnp.stack(
        [
            grad_left * sig_left,
            grad_left * edge_pre[0] * sig_left * (1.0 - sig_left),
            grad_right * sig_right,
            grad_right * edge_pre[2] * sig_right * (1.0 - sig_right),
        ]
    ).astype(jnp.bfloat16)


def triangle(pair_edges, outgoing):
    if outgoing:
        einsum_form = "cik,cjk->cij"
    else:
        einsum_form = "cki,ckj->cij"
    return jnp.einsum(
        einsum_form, pair_edges[0], pair_edges[1], preferred_element_type=jnp.float32
    ).astype(jnp.bfloat16)


def triangle_pullback(pair_edges, grad_product, outgoing):
    left_edge = pair_edges[0]
    right_edge = pair_edges[1]
    if outgoing:
        grad_left = jnp.einsum(
            "cij,cjk->cik", grad_product, right_edge, preferred_element_type=jnp.float32
        )
        grad_right = jnp.einsum(
            "cij,cik->cjk", grad_product, left_edge, preferred_element_type=jnp.float32
        )
    else:
        grad_left = jnp.einsum(
            "ckj,cij->cki", right_edge, grad_product, preferred_element_type=jnp.float32
        )
        grad_right = jnp.einsum(
            "cki,cij->ckj", left_edge, grad_product, preferred_element_type=jnp.float32
        )
    return jnp.stack([grad_left, grad_right]).astype(jnp.bfloat16)


def update_weights(proj_weight, proj_bias, norm_gain, norm_shift, update, channels, hidden):
    w_edge = proj_weight[update, :, : 4 * hidden].reshape(channels, 4, hidden)
    w_gate = proj_weight[update, :, 4 * hidden :]
    bias_edge = proj_bias[update, : 4 * hidden].reshape(4, hidden, 1, 1)
    bias_gate = proj_bias[update, 4 * hidden :]
    gain_in = norm_gain[update, :channels]
    shift_in = norm_shift[update, :channels]
    gain_out = norm_gain[update, channels:][:, None, None]
    shift_out = norm_shift[update, channels:][:, None, None]
    return (w_edge, w_gate, bias_edge, bias_gate, gain_in, shift_in, gain_out, shift_out)


def shards(
    pair_repr,
    pair_mask,
    cotangent,
    proj_weight,
    proj_bias,
    norm_gain,
    norm_shift,
    out_weight,
    out_bias,
):
    channels = pair_repr.shape[3]
    hidden = out_weight.shape[1]
    pair_state = pair_repr[0]
    cell_mask = pair_mask[0].astype(jnp.float32)
    records = []
    for update in range(2):
        w_edge, w_gate, bias_edge, bias_gate, gain_in, shift_in, gain_out, shift_out = (
            update_weights(proj_weight, proj_bias, norm_gain, norm_shift, update, channels, hidden)
        )
        state_f = pair_state.astype(jnp.float32)
        normed = layer_norm(state_f, gain_in, shift_in, -1).astype(jnp.bfloat16)
        edge_pre = (
            jnp.einsum("rnc,cgh->ghrn", normed, w_edge, preferred_element_type=jnp.float32)
            + bias_edge
        )
        gate_pre = (
            jnp.einsum("rnc,cd->rnd", normed, w_gate, preferred_element_type=jnp.float32)
            + bias_gate
        )
        pair_edges = edge_pair(edge_pre, cell_mask)
        spread = lax.all_to_all(pair_edges, "dap", split_axis=1, concat_axis=2, tiled=True)
        product = lax.all_to_all(
            triangle(spread, update == 0), "dap", split_axis=1, concat_axis=0, tiled=True
        )
        mixed_norm = layer_norm(product.astype(jnp.float32), gain_out, shift_out, 0).astype(
            jnp.bfloat16
        )
        branch = (
            jnp.einsum(
                "hrn,hd->rnd", mixed_norm, out_weight[update], preferred_element_type=jnp.float32
            )
            + out_bias[update]
        )
        records.append(
            (state_f, normed, edge_pre, gate_pre, pair_edges, spread, product, mixed_norm, branch)
        )
        pair_state = (state_f + jax.nn.sigmoid(gate_pre) * branch).astype(jnp.bfloat16)
    upstream = cotangent[0].astype(jnp.float32)
    proj_grads = []
    out_grads = []
    for update in (1, 0):
        state_f, normed, edge_pre, gate_pre, pair_edges, spread, product, mixed_norm, branch = (
            records[update]
        )
        w_edge, w_gate, bias_edge, bias_gate, gain_in, shift_in, gain_out, shift_out = (
            update_weights(proj_weight, proj_bias, norm_gain, norm_shift, update, channels, hidden)
        )
        gate_value = jax.nn.sigmoid(gate_pre)
        grad_branch = (upstream * gate_value).astype(jnp.bfloat16)
        grad_gate = (upstream * branch * gate_value * (1.0 - gate_value)).astype(jnp.bfloat16)
        out_grad = jnp.einsum(
            "hrn,rnd->hd", mixed_norm, grad_branch, preferred_element_type=jnp.float32
        )
        grad_mixed = jnp.einsum(
            "rnd,hd->hrn", grad_branch, out_weight[update], preferred_element_type=jnp.float32
        )
        grad_product = norm_pullback(
            product.astype(jnp.float32), gain_out, shift_out, 0, grad_mixed
        ).astype(jnp.bfloat16)
        column_edges, column_stack = (
            lax.all_to_all(pair_edges, "dap", split_axis=1, concat_axis=2, tiled=True),
            lax.all_to_all(grad_product[None], "dap", split_axis=1, concat_axis=2, tiled=True),
        )
        column_grad = column_stack[0]
        grad_pair = lax.all_to_all(
            triangle_pullback(column_edges, column_grad, update == 0),
            "dap",
            split_axis=2,
            concat_axis=1,
            tiled=True,
        )
        grad_edge = edge_pullback(edge_pre, cell_mask, grad_pair)
        edge_grad = jnp.einsum(
            "rnc,ghrn->cgh", normed, grad_edge, preferred_element_type=jnp.float32
        ).reshape(channels, 4 * hidden)
        gate_grad = jnp.einsum("rnc,rnd->cd", normed, grad_gate, preferred_element_type=jnp.float32)
        grad_normed = jnp.einsum(
            "ghrn,cgh->rnc", grad_edge, w_edge, preferred_element_type=jnp.float32
        )
        grad_normed = grad_normed + jnp.einsum(
            "rnd,cd->rnc", grad_gate, w_gate, preferred_element_type=jnp.float32
        )
        upstream = upstream + norm_pullback(state_f, gain_in, shift_in, -1, grad_normed)
        proj_part = jnp.concatenate([edge_grad, gate_grad], axis=1)
        proj_grads.append(proj_part)
        out_grads.append(out_grad)
    proj_total = jnp.stack(proj_grads[::-1])
    out_total = jnp.stack(out_grads[::-1])
    proj_total, out_total = lax.psum((proj_total, out_total), ("dp", "dap"))
    return (upstream.astype(jnp.bfloat16)[None], proj_total, out_total)


def solution(mesh):
    placed = (
        P("dp", "dap", None, None),
        P("dp", "dap", None),
        P("dp", "dap", None, None),
        P(),
        P(),
        P(),
        P(),
        P(),
        P(),
    )
    return jax.shard_map(
        shards,
        mesh=mesh,
        in_specs=placed,
        out_specs=(P("dp", "dap", None, None), P(), P()),
        check_vma=False,
    )
```

profile of v0, /device:TPU:0, one launch (start us, length us, event | category | flops | bytes accessed | tf_op | source)
XLA Modules:
  0.0 254.7 jit_solution(5220680960774518940)
XLA Ops:
  7.2 0.8 convert_reduce_fusion
  8.0 1.0 fusion.118
  9.2 0.5 copy-done.4
  10.0 0.7 copy-done.7
  10.7 0.7 copy-done.5
  11.4 0.2 fusion.1
  11.9 0.9 reshape.282
  12.8 7.3 %all-to-all-start = ((bf16[8,2,2048]{2,1,0:T(2,128)(2,1)}), bf16[8,2,2048]{2,1,0:T(2,128)(2,1)S(1)}, u32[]{:S(2)}, u32[]{:S(2)}) async-start(bf16[8,2,2048]{2,1,0:T(2,128)(2,1)} %reshape.282), calls=%async_computation | async-start | bytes 131072 | tf_op jit(solution)/shard_map/all_to_all | solution.py:117
  20.1 6.9 %all-to-all-done = bf16[8,2,2048]{2,1,0:T(2,128)(2,1)S(1)} async-done(((bf16[8,2,2048]{2,1,0:T(2,128)(2,1)}), bf16[8,2,2048]{2,1,0:T(2,128)(2,1)S(1)}, u32[]{:S(2)}, u32[]{:S(2)}) %all-to-all-start) | async-done | bytes 65568 | tf_op jit(solution)/shard_map/all_to_all | solution.py:117
  27.0 0.2 reshape.283
  27.5 0.2 convolution_convert_fusion.5
  27.7 0.8 reshape.284
  28.5 3.5 %all-to-all-start.1 = ((bf16[8,2,1024]{2,1,0:T(2,128)(2,1)}), bf16[8,2,1024]{2,1,0:T(2,128)(2,1)S(1)}, u32[]{:S(2)}, u32[]{:S(2)}) async-start(bf16[8,2,1024]{2,1,0:T(2,128)(2,1)} %reshape.284), calls=%async_computation.1 | async-start | bytes 65536 | tf_op jit(solution)/shard_map/all_to_all | solution.py:118
  32.3 6.3 %all-to-all-done.1 = bf16[8,2,1024]{2,1,0:T(2,128)(2,1)S(1)} async-done(((bf16[8,2,1024]{2,1,0:T(2,128)(2,1)}), bf16[8,2,1024]{2,1,0:T(2,128)(2,1)S(1)}, u32[]{:S(2)}, u32[]{:S(2)}) %all-to-all-start.1) | async-done | bytes 32800 | tf_op jit(solution)/shard_map/all_to_all | solution.py:118
  39.0 0.7 copy-done.2
  39.9 1.1 convert_reduce_fusion.1
  41.2 0.2 fusion
  41.7 0.9 reshape.286
  42.7 3.4 %all-to-all-start.2 = ((bf16[8,2,2048]{2,1,0:T(2,128)(2,1)}), bf16[8,2,2048]{2,1,0:T(2,128)(2,1)S(1)}, u32[]{:S(2)}, u32[]{:S(2)}) async-start(bf16[8,2,2048]{2,1,0:T(2,128)(2,1)} %reshape.286), calls=%async_computation.2 | async-start | bytes 131072 | tf_op jit(solution)/shard_map/all_to_all | solution.py:157
  46.2 6.7 %all-to-all-done.2 = bf16[8,2,2048]{2,1,0:T(2,128)(2,1)S(1)} async-done(((bf16[8,2,2048]{2,1,0:T(2,128)(2,1)}), bf16[8,2,2048]{2,1,0:T(2,128)(2,1)S(1)}, u32[]{:S(2)}, u32[]{:S(2)}) %all-to-all-start.2) | async-done | bytes 65568 | tf_op jit(solution)/shard_map/all_to_all | solution.py:157
  52.9 0.2 reshape.287
  53.3 0.2 convolution_convert_fusion.4
  53.5 0.8 reshape.288
  54.3 3.3 %all-to-all-start.3 = ((bf16[8,2,1024]{2,1,0:T(2,128)(2,1)}), bf16[8,2,1024]{2,1,0:T(2,128)(2,1)S(1)}, u32[]{:S(2)}, u32[]{:S(2)}) async-start(bf16[8,2,1024]{2,1,0:T(2,128)(2,1)} %reshape.288), calls=%async_computation.3 | async-start | bytes 65536 | tf_op jit(solution)/shard_map/all_to_all | solution.py:118
  57.7 1.0 fusion.14
  58.8 5.5 %all-to-all-done.3 = bf16[8,2,1024]{2,1,0:T(2,128)(2,1)S(1)} async-done(((bf16[8,2,1024]{2,1,0:T(2,128)(2,1)}), bf16[8,2,1024]{2,1,0:T(2,128)(2,1)S(1)}, u32[]{:S(2)}, u32[]{:S(2)}) %all-to-all-start.3) | async-done | bytes 32800 | tf_op jit(solution)/shard_map/all_to_all | solution.py:118
  64.7 0.6 copy-done.1
  65.4 0.2 multiply_reduce_fusion.3
  65.6 0.2 fusion.102
  66.1 0.8 reshape.290
  66.9 3.3 %all-to-all-start.4 = ((bf16[8,2,1024]{2,1,0:T(2,128)(2,1)}), bf16[8,2,1024]{2,1,0:T(2,128)(2,1)S(1)}, u32[]{:S(2)}, u32[]{:S(2)}) async-start(bf16[8,2,1024]{2,1,0:T(2,128)(2,1)} %reshape.290), calls=%async_computation.4 | async-start | bytes 65536 | tf_op jit(solution)/shard_map/all_to_all | solution.py:158
  70.4 0.2 fusion.21
  70.6 0.3 convolution_bitcast_fusion.2
  70.8 6.0 %all-to-all-done.4 = bf16[8,2,1024]{2,1,0:T(2,128)(2,1)S(1)} async-done(((bf16[8,2,1024]{2,1,0:T(2,128)(2,1)}), bf16[8,2,1024]{2,1,0:T(2,128)(2,1)S(1)}, u32[]{:S(2)}, u32[]{:S(2)}) %all-to-all-start.4) | async-done | bytes 32800 | tf_op jit(solution)/shard_map/all_to_all | solution.py:158
  77.3 0.2 fusion.2
  77.7 0.9 reshape.292
  78.6 3.4 %all-to-all-start.5 = ((bf16[8,2,2048]{2,1,0:T(2,128)(2,1)}), bf16[8,2,2048]{2,1,0:T(2,128)(2,1)S(1)}, u32[]{:S(2)}, u32[]{:S(2)}) async-start(bf16[8,2,2048]{2,1,0:T(2,128)(2,1)} %reshape.292), calls=%async_computation.5 | async-start | bytes 131072 | tf_op jit(solution)/shard_map/all_to_all | solution.py:161
  82.0 0.3 convolution_bitcast_fusion.4
  82.2 6.6 %all-to-all-done.5 = bf16[8,2,2048]{2,1,0:T(2,128)(2,1)S(1)} async-done(((bf16[8,2,2048]{2,1,0:T(2,128)(2,1)}), bf16[8,2,2048]{2,1,0:T(2,128)(2,1)S(1)}, u32[]{:S(2)}, u32[]{:S(2)}) %all-to-all-start.5) | async-done | bytes 65568 | tf_op jit(solution)/shard_map/all_to_all | solution.py:161
  88.8 0.2 reshape.293
  89.6 0.3 convolution_bitcast_fusion
  89.9 1.0 fusion.40
  91.0 0.2 fusion.95
  91.3 0.2 multiply_reduce_fusion.2
  91.6 0.2 fusion.103
  92.1 0.8 reshape.294
  92.9 3.3 %all-to-all-start.6 = ((bf16[8,2,1024]{2,1,0:T(2,128)(2,1)}), bf16[8,2,1024]{2,1,0:T(2,128)(2,1)S(1)}, u32[]{:S(2)}, u32[]{:S(2)}) async-start(bf16[8,2,1024]{2,1,0:T(2,128)(2,1)} %reshape.294), calls=%async_computation.6 | async-start | bytes 65536 | tf_op jit(solution)/shard_map/all_to_all | solution.py:158
  96.2 0.3 convolution_bitcast_fusion.3
  96.6 0.3 convolution_bitcast_fusion.5
  96.8 6.0 %all-to-all-done.6 = bf16[8,2,1024]{2,1,0:T(2,128)(2,1)S(1)} async-done(((bf16[8,2,1024]{2,1,0:T(2,128)(2,1)}), bf16[8,2,1024]{2,1,0:T(2,128)(2,1)S(1)}, u32[]{:S(2)}, u32[]{:S(2)}) %all-to-all-start.6) | async-done | bytes 32800 | tf_op jit(solution)/shard_map/all_to_all | solution.py:158
  103.1 0.2 fusion.5
  103.7 0.9 reshape.296
  104.6 3.4 %all-to-all-start.7 = ((bf16[8,2,2048]{2,1,0:T(2,128)(2,1)}), bf16[8,2,2048]{2,1,0:T(2,128)(2,1)S(1)}, u32[]{:S(2)}, u32[]{:S(2)}) async-start(bf16[8,2,2048]{2,1,0:T(2,128)(2,1)} %reshape.296), calls=%async_computation.7 | async-start | bytes 131072 | tf_op jit(solution)/shard_map/all_to_all | solution.py:161
  108.0 0.7 pad_maximum_fusion.5
  108.7 6.1 %all-to-all-done.7 = bf16[8,2,2048]{2,1,0:T(2,128)(2,1)S(1)} async-done(((bf16[8,2,2048]{2,1,0:T(2,128)(2,1)}), bf16[8,2,2048]{2,1,0:T(2,128)(2,1)S(1)}, u32[]{:S(2)}, u32[]{:S(2)}) %all-to-all-start.7) | async-done | bytes 65568 | tf_op jit(solution)/shard_map/all_to_all | solution.py:161
  114.8 0.2 reshape.297
  115.6 0.3 convolution_bitcast_fusion.1
  115.9 1.0 fusion.42
  117.0 0.2 fusion.96
  117.2 0.9 pad_maximum_fusion
  118.1 0.8 fusion.66
  118.9 126.2 %all-reduce.3.cloned.1.call-done = (f32[2,128,640]{2,1,0:T(8,128)}, f32[2,128,128]{2,1,0:T(8,128)}) async-done(((f32[2,128,640]{2,1,0:T(8,128)}, f32[2,128,128]{2,1,0:T(8,128)}), (f32[2,128,640]{2,1,0:T(8,128)}, f32[2,128,128]{2,1,0:T(8,128)})) %all-reduce.3.cloned.1.call-update) | async-done | bytes 786448 | tf_op jit(solution)/shard_map/psum | solution.py:185
  245.1 2.0 copy.167
  247.2 0.7 copy.168
  (110 shorter events, 6.5 us)
Async XLA Ops:
  9.0 0.7 copy-start.4
  9.0 0.8 copy-start
  10.0 0.7 copy-start.7
  10.6 0.7 copy-start.5
  10.7 0.7 copy-start.6
  12.8 14.2 %all-to-all-start = ((bf16[8,2,2048]{2,1,0:T(2,128)(2,1)}), bf16[8,2,2048]{2,1,0:T(2,128)(2,1)S(1)}, u32[]{:S(2)}, u32[]{:S(2)}) async-start(bf16[8,2,2048]{2,1,0:T(2,128)(2,1)} %reshape.282), calls=%async_computation | async-start | bytes 131072 | tf_op jit(solution)/shard_map/all_to_all | solution.py:117
  28.5 3.5 %copy-start.8 = (f32[2,128]{1,0:T(2,128)S(1)}, f32[2,128]{1,0:T(2,128)}, u32[]{:S(2)}) copy-start(f32[2,128]{1,0:T(2,128)} %param.17) | copy-start | bytes 3076
  28.5 10.1 %all-to-all-start.1 = ((bf16[8,2,1024]{2,1,0:T(2,128)(2,1)}), bf16[8,2,1024]{2,1,0:T(2,128)(2,1)S(1)}, u32[]{:S(2)}, u32[]{:S(2)}) async-start(bf16[8,2,1024]{2,1,0:T(2,128)(2,1)} %reshape.284), calls=%async_computation.1 | async-start | bytes 65536 | tf_op jit(solution)/shard_map/all_to_all | solution.py:118
  38.9 0.8 copy-start.2
  42.7 10.2 %all-to-all-start.2 = ((bf16[8,2,2048]{2,1,0:T(2,128)(2,1)}), bf16[8,2,2048]{2,1,0:T(2,128)(2,1)S(1)}, u32[]{:S(2)}, u32[]{:S(2)}) async-start(bf16[8,2,2048]{2,1,0:T(2,128)(2,1)} %reshape.286), calls=%async_computation.2 | async-start | bytes 131072 | tf_op jit(solution)/shard_map/all_to_all | solution.py:157
  54.3 10.0 %all-to-all-start.3 = ((bf16[8,2,1024]{2,1,0:T(2,128)(2,1)}), bf16[8,2,1024]{2,1,0:T(2,128)(2,1)S(1)}, u32[]{:S(2)}, u32[]{:S(2)}) async-start(bf16[8,2,1024]{2,1,0:T(2,128)(2,1)} %reshape.288), calls=%async_computation.3 | async-start | bytes 65536 | tf_op jit(solution)/shard_map/all_to_all | solution.py:118
  64.6 0.8 copy-start.1
  66.9 10.0 %all-to-all-start.4 = ((bf16[8,2,1024]{2,1,0:T(2,128)(2,1)}), bf16[8,2,1024]{2,1,0:T(2,128)(2,1)S(1)}, u32[]{:S(2)}, u32[]{:S(2)}) async-start(bf16[8,2,1024]{2,1,0:T(2,128)(2,1)} %reshape.290), calls=%async_computation.4 | async-start | bytes 65536 | tf_op jit(solution)/shard_map/all_to_all | solution.py:158
  78.6 10.2 %all-to-all-start.5 = ((bf16[8,2,2048]{2,1,0:T(2,128)(2,1)}), bf16[8,2,2048]{2,1,0:T(2,128)(2,1)S(1)}, u32[]{:S(2)}, u32[]{:S(2)}) async-start(bf16[8,2,2048]{2,1,0:T(2,128)(2,1)} %reshape.292), calls=%async_computation.5 | async-start | bytes 131072 | tf_op jit(solution)/shard_map/all_to_all | solution.py:161
  92.9 10.0 %all-to-all-start.6 = ((bf16[8,2,1024]{2,1,0:T(2,128)(2,1)}), bf16[8,2,1024]{2,1,0:T(2,128)(2,1)S(1)}, u32[]{:S(2)}, u32[]{:S(2)}) async-start(bf16[8,2,1024]{2,1,0:T(2,128)(2,1)} %reshape.294), calls=%async_computation.6 | async-start | bytes 65536 | tf_op jit(solution)/shard_map/all_to_all | solution.py:158
  104.6 10.2 %all-to-all-start.7 = ((bf16[8,2,2048]{2,1,0:T(2,128)(2,1)}), bf16[8,2,2048]{2,1,0:T(2,128)(2,1)S(1)}, u32[]{:S(2)}, u32[]{:S(2)}) async-start(bf16[8,2,2048]{2,1,0:T(2,128)(2,1)} %reshape.296), calls=%async_computation.7 | async-start | bytes 131072 | tf_op jit(solution)/shard_map/all_to_all | solution.py:161
  108.0 137.2 %all-reduce.3.cloned.1.call-start = ((), (), s32[]{:S(2)}) async-start(), calls=%async_computation.8 | async-start | bytes 1572864 | tf_op jit(solution)/shard_map/psum | solution.py:185
  245.1 2.0 copy-start.3
Sparse Core Ops, SparseCore 0:
  118.2 126.8 all-reduce.2
where the time goes:
time: 256 us; the launch traced here: 255 us
  waiting for transfers between devices  176 us (69%)
  starting transfers between devices  30.9 us (12%)
  local copies, waits for them, and re-layouts  18 us (7%)
  between operations  14.8 us (6%)
  matrix products  8.59 us (3%)
  other arithmetic  5.99 us (2%)
    psum x1, waiting for transfers between devices, shards(): proj_total, out_total = lax.psum((proj_total, out_total), ('dp', 'dap'))  126 us
    unnamed x38, local copies, waits for them, and re-layouts  14.3 us
    all_to_all x2, waiting for transfers between devices, shards(): lax.all_to_all(pair_edges, 'dap', split_axis=1, concat_axis=2, tiled=True)  13.6 us
    all_to_all x2, waiting for transfers between devices, shards(): lax.all_to_all(triangle_pullback(column_edges, column_grad, update == 0),...  12.7 us
    all_to_all x2, waiting for transfers between devices, shards(): lax.all_to_all(grad_product[None], 'dap', split_axis=1, concat_axis=2, ti...  12 us
    all_to_all x2, waiting for transfers between devices, shards(): lax.all_to_all(triangle(spread, update == 0), 'dap', split_axis=1, concat...  11.8 us
    all_to_all x2, starting transfers between devices, shards(): lax.all_to_all(pair_edges, 'dap', split_axis=1, concat_axis=2, tiled=True)  10.6 us
    all_to_all x2, starting transfers between devices, shards(): lax.all_to_all(triangle(spread, update == 0), 'dap', split_axis=1, concat...  6.81 us
  transfers between devices with their start and end apart: 9, of which 9 were waited for; matrix products, arithmetic and copies ran while one was open for 2% of the time, Pallas kernels for 0%

commit v1 on v0

--- a/solution.py
+++ b/solution.py
@@ -1,9 +1,434 @@
+import functools
+
 import jax
 import jax.numpy as jnp
 from jax import lax
+from jax.experimental import pallas as pl
+from jax.experimental.pallas import tpu as pltpu
 from jax.sharding import PartitionSpec as P
 
 NORM_EPSILON = 1e-05
+VMEM_BYTES = 48 * 1024 * 1024
+CROP_BUDGET = 32 * 1024 * 1024
+BLOCK_ROWS = 8
+F32 = jnp.float32
+BF16 = jnp.bfloat16
+
+
+def sigmoid(x):
+    return 0.5 * jnp.tanh(0.5 * x) + 0.5
+
+
+def dot(a, b, dims=((1,), (0,))):
+    return lax.dot_general(a, b, (dims, ((), ())), preferred_element_type=F32)
+
+
+def norm_parts(x):
+    centred = x - jnp.mean(x, axis=-1, keepdims=True)
+    rstd = lax.rsqrt(jnp.mean(centred * centred, axis=-1, keepdims=True) + NORM_EPSILON)
+    return centred * rstd, rstd
+
+
+def norm_vjp(x_hat, rstd, grad):
+    mean_grad = jnp.mean(grad, axis=-1, keepdims=True)
+    mean_prod = jnp.mean(grad * x_hat, axis=-1, keepdims=True)
+    return rstd * (grad - mean_grad - x_hat * mean_prod)
+
+
+def pair_mask_block(length, first_row, rows, n, lanes):
+    shape = (rows, n, lanes)
+    i = lax.broadcasted_iota(jnp.int32, shape, 0) + first_row
+    j = lax.broadcasted_iota(jnp.int32, shape, 1)
+    inside = jnp.where((i < length) & (j < length), 1.0, 0.0)
+    return inside.reshape(rows * n, lanes)
+
+
+def project(x, mask, u, w, b, gain, shift):
+    c = x.shape[1]
+    x_hat, rstd = norm_parts(x)
+    normed = (x_hat * gain[u : u + 1, :c] + shift[u : u + 1, :c]).astype(BF16)
+    pre = dot(normed, w[u]) + b[u : u + 1, :]
+    h = (pre.shape[1] - c) // 4
+    s_left = sigmoid(pre[:, h : 2 * h]) * mask
+    s_right = sigmoid(pre[:, 3 * h : 4 * h]) * mask
+    left = s_left * pre[:, :h]
+    right = s_right * pre[:, 2 * h : 3 * h]
+    gate = sigmoid(pre[:, 4 * h :])
+    return x_hat, rstd, normed, s_left, s_right, left, right, gate
+
+
+def mix(product, u, c, gain, shift, w_out, b_out):
+    p_hat, p_rstd = norm_parts(product.astype(F32))
+    mixed = (p_hat * gain[u : u + 1, c:] + shift[u : u + 1, c:]).astype(BF16)
+    branch = dot(mixed, w_out[u]) + b_out[u : u + 1, :]
+    return p_hat, p_rstd, mixed, branch
+
+
+def unmix(up, gate, branch, p_hat, p_rstd, u, c, gain, w_out):
+    d_branch = up * gate
+    d_gate = (d_branch * branch * (1.0 - gate)).astype(BF16)
+    d_branch = d_branch.astype(BF16)
+    d_mixed = dot(d_branch, w_out[u], ((1,), (1,))) * gain[u : u + 1, c:]
+    return d_branch, d_gate, norm_vjp(p_hat, p_rstd, d_mixed)
+
+
+def contract(n, first, row_of, x, y):
+    lanes = y.shape[1]
+
+    def step(e, totals):
+        block = y[pl.ds(pl.multiple_of(e * n, n), n), :]
+        return tuple(
+            totals[a] + x[pl.ds(row_of(first + a, e), 1), :] * block for a in range(BLOCK_ROWS)
+        )
+
+    zero = jnp.zeros((n, lanes), F32)
+    totals = lax.fori_loop(0, n, step, (zero,) * BLOCK_ROWS, unroll=4)
+    return totals
+
+
+def edge_grads(d_left, d_right, s_left, s_right, left, right):
+    return (
+        (d_left * s_left).astype(BF16),
+        (d_left * left * (1.0 - s_left)).astype(BF16),
+        (d_right * s_right).astype(BF16),
+        (d_right * right * (1.0 - s_right)).astype(BF16),
+    )
+
+
+def crop_length(state_ref, cells):
+    return jnp.max(state_ref[:, cells:, :].astype(F32)).astype(jnp.int32)
+
+
+def forward_first(
+    n, state_ref, w, b, gain, shift, w_out, b_out, next_ref, product_ref, left_s, right_s, gate_s
+):
+    parts, cells, c = state_ref.shape
+    rows = n // parts
+    cells = rows * n
+    length = crop_length(state_ref, cells)
+
+    @pl.loop(0, parts)
+    def _(t):
+        x = state_ref[t, :cells, :].astype(F32)
+        mask = pair_mask_block(length, t * rows, rows, n, c)
+        _, _, _, _, _, left, right, gate = project(x, mask, 0, w, b, gain, shift)
+        here = pl.ds(pl.multiple_of(t * cells, cells), cells)
+        left_s[here, :] = left
+        gate_s[here, :] = gate
+        for r in range(rows):
+            right_s[pl.ds(t * rows + r, n, stride=n), :] = right[r * n : (r + 1) * n]
+
+    @pl.loop(0, n // BLOCK_ROWS)
+    def _(t):
+        totals = contract(n, t * BLOCK_ROWS, lambda i, k: i * n + k, left_s, right_s)
+        here = pl.ds(pl.multiple_of(t * BLOCK_ROWS * n, BLOCK_ROWS * n), BLOCK_ROWS * n)
+        product = jnp.concatenate(totals, axis=0).astype(BF16)
+        product_ref[here, :] = product
+        _, _, _, branch = mix(product, 0, c, gain, shift, w_out, b_out)
+        per = BLOCK_ROWS // rows
+        x = jnp.concatenate([state_ref[t * per + q, :cells, :] for q in range(per)], axis=0)
+        next_ref[here, :] = (x.astype(F32) + gate_s[here, :] * branch).astype(BF16)
+
+
+def weight_grads(index_ref, normed_s, d_pre_s, mixed_s, d_branch_s, grad_s, slice_ref):
+    part = slice_ref.shape[0]
+    width = d_pre_s.shape[1]
+    grad_s[:, :width] = dot(normed_s[...], d_pre_s[...], ((0,), (0,)))
+    grad_s[:, width:] = dot(mixed_s[...], d_branch_s[...], ((0,), (0,)))
+    own = pl.ds(pl.multiple_of(index_ref[0] * part, part), part)
+    slice_ref[...] = grad_s[own, :].astype(BF16)
+
+
+def update_second(
+    n,
+    index_ref,
+    state_ref,
+    next_ref,
+    cot_ref,
+    w,
+    b,
+    gain,
+    shift,
+    w_out,
+    b_out,
+    up_ref,
+    slice_ref,
+    left_s,
+    right_s,
+    s_left_s,
+    s_right_s,
+    gate_s,
+    hat_s,
+    rstd_s,
+    d_product_s,
+    d_product_t_s,
+    normed_s,
+    mixed_s,
+    d_branch_s,
+    d_pre_s,
+    grad_s,
+):
+    parts, _, c = state_ref.shape
+    rows = n // parts
+    cells = rows * n
+    h = left_s.shape[1]
+    length = crop_length(state_ref, cells)
+
+    @pl.loop(0, parts)
+    def _(t):
+        here = pl.ds(pl.multiple_of(t * cells, cells), cells)
+        x = next_ref[here, :].astype(F32)
+        mask = pair_mask_block(length, t * rows, rows, n, c)
+        x_hat, rstd, normed, s_left, s_right, left, right, gate = project(
+            x, mask, 1, w, b, gain, shift
+        )
+        left_s[here, :] = left
+        right_s[here, :] = right
+        s_left_s[here, :] = s_left
+        s_right_s[here, :] = s_right
+        gate_s[here, :] = gate
+        hat_s[here, :] = x_hat
+        rstd_s[here, :] = jnp.broadcast_to(rstd, x_hat.shape)
+        normed_s[here, :] = normed
+
+    per = BLOCK_ROWS // rows
+
+    @pl.loop(0, n // BLOCK_ROWS)
+    def _(t):
+        totals = contract(n, t * BLOCK_ROWS, lambda i, k: k * n + i, left_s, right_s)
+        here = pl.ds(pl.multiple_of(t * BLOCK_ROWS * n, BLOCK_ROWS * n), BLOCK_ROWS * n)
+        product = jnp.concatenate(totals, axis=0).astype(BF16)
+        p_hat, p_rstd, mixed, branch = mix(product, 1, c, gain, shift, w_out, b_out)
+        up = jnp.concatenate([cot_ref[t * per + q] for q in range(per)], axis=0).astype(F32)
+        d_branch, d_gate, d_product = unmix(
+            up, gate_s[here, :], branch, p_hat, p_rstd, 1, c, gain, w_out
+        )
+        mixed_s[here, :] = mixed
+        d_branch_s[here, :] = d_branch
+        d_pre_s[here, 4 * h :] = d_gate
+        d_product_s[here, :] = d_product
+        for r in range(BLOCK_ROWS):
+            d_product_t_s[pl.ds(t * BLOCK_ROWS + r, n, stride=n), :] = d_product[
+                r * n : (r + 1) * n
+            ]
+
+    @pl.loop(0, n // BLOCK_ROWS)
+    def _(t):
+        first = t * BLOCK_ROWS
+        here = pl.ds(pl.multiple_of(first * n, BLOCK_ROWS * n), BLOCK_ROWS * n)
+        d_left = jnp.concatenate(
+            contract(n, first, lambda k, j: k * n + j, right_s, d_product_t_s), axis=0
+        )
+        d_right = jnp.concatenate(
+            contract(n, first, lambda k, i: k * n + i, left_s, d_product_s), axis=0
+        )
+        grads = edge_grads(
+            d_left, d_right, s_left_s[here, :], s_right_s[here, :], left_s[here, :], right_s[here, :]
+        )
+        for g in range(4):
+            d_pre_s[here, g * h : (g + 1) * h] = grads[g]
+        d_normed = dot(d_pre_s[here, :], w[1], ((1,), (1,))) * gain[1:2, :c]
+        up = jnp.concatenate([cot_ref[t * per + q] for q in range(per)], axis=0).astype(F32)
+        up_ref[here, :] = up + norm_vjp(hat_s[here, :], rstd_s[here, :], d_normed)
+
+    weight_grads(index_ref, normed_s, d_pre_s, mixed_s, d_branch_s, grad_s, slice_ref)
+
+
+def backward_first(
+    n,
+    index_ref,
+    state_ref,
+    product_ref,
+    up_ref,
+    w,
+    b,
+    gain,
+    shift,
+    w_out,
+    b_out,
+    out_ref,
+    slice_ref,
+    left_s,
+    right_s,
+    s_left_s,
+    s_right_s,
+    hat_s,
+    rstd_s,
+    d_product_s,
+    normed_s,
+    mixed_s,
+    d_branch_s,
+    d_pre_s,
+    grad_s,
+):
+    parts, _, c = state_ref.shape
+    rows = n // parts
+    cells = rows * n
+    h = left_s.shape[1]
+    length = crop_length(state_ref, cells)
+
+    @pl.loop(0, parts)
+    def _(t):
+        here = pl.ds(pl.multiple_of(t * cells, cells), cells)
+        x = state_ref[t, :cells, :].astype(F32)
+        mask = pair_mask_block(length, t * rows, rows, n, c)
+        x_hat, rstd, normed, s_left, s_right, left, right, gate = project(
+            x, mask, 0, w, b, gain, shift
+        )
+        left_s[here, :] = left
+        right_s[here, :] = right
+        s_left_s[here, :] = s_left
+        s_right_s[here, :] = s_right
+        hat_s[here, :] = x_hat
+        rstd_s[here, :] = jnp.broadcast_to(rstd, x_hat.shape)
+        normed_s[here, :] = normed
+        p_hat, p_rstd, mixed, branch = mix(
+            product_ref[here, :], 0, c, gain, shift, w_out, b_out
+        )
+        d_branch, d_gate, d_product = unmix(
+            up_ref[here, :], gate, branch, p_hat, p_rstd, 0, c, gain, w_out
+        )
+        mixed_s[here, :] = mixed
+        d_branch_s[here, :] = d_branch
+        d_pre_s[here, 4 * h :] = d_gate
+        d_product_s[here, :] = d_product
+
+    @pl.loop(0, n // BLOCK_ROWS)
+    def _(t):
+        first = t * BLOCK_ROWS
+        here = pl.ds(pl.multiple_of(first * n, BLOCK_ROWS * n), BLOCK_ROWS * n)
+        d_left = jnp.concatenate(
+            contract(n, first, lambda i, j: i * n + j, d_product_s, right_s), axis=0
+        )
+        d_right = jnp.concatenate(
+            contract(n, first, lambda j, i: i * n + j, d_product_s, left_s), axis=0
+        )
+        grads = edge_grads(
+            d_left, d_right, s_left_s[here, :], s_right_s[here, :], left_s[here, :], right_s[here, :]
+        )
+        for g in range(4):
+            d_pre_s[here, g * h : (g + 1) * h] = grads[g]
+
+    own = pl.ds(pl.multiple_of(index_ref[0] * cells, cells), cells)
+    d_normed = dot(d_pre_s[own, :], w[0], ((1,), (1,))) * gain[0:1, :c]
+    out_ref[...] = (
+        up_ref[own, :] + norm_vjp(hat_s[own, :], rstd_s[own, :], d_normed)
+    ).astype(BF16)
+    weight_grads(index_ref, normed_s, d_pre_s, mixed_s, d_branch_s, grad_s, slice_ref)
+
+
+def gather_rows(value, axis, size):
+    spread = jnp.broadcast_to(value[None], (size,) + value.shape)
+    return lax.all_to_all(spread, axis, split_axis=0, concat_axis=0, tiled=True)
+
+
+def gather_doubling(value, axis, size):
+    me = lax.axis_index(axis)
+    held = value[None]
+    step = 1
+    while step < size:
+        other = lax.ppermute(held, axis, [(d, d ^ step) for d in range(size)])
+        low = (me & step) == 0
+        held = jnp.concatenate(
+            [jnp.where(low, held, other), jnp.where(low, other, held)], axis=0
+        )
+        step *= 2
+    return held
+
+
+def sum_exchange(value, axis, size):
+    total = value.astype(F32)
+    for shift in range(1, size):
+        total = total + lax.ppermute(
+            value, axis, [(d, (d + shift) % size) for d in range(size)]
+        ).astype(F32)
+    return total
+
+
+def crop_shards(
+    groups,
+    parts,
+    pair_repr,
+    pair_mask,
+    cotangent,
+    proj_weight,
+    proj_bias,
+    norm_gain,
+    norm_shift,
+    out_weight,
+    out_bias,
+):
+    _, rows, n, c = pair_repr.shape
+    h = out_weight.shape[1]
+    width = proj_weight.shape[2]
+    cells, pairs = rows * n, n * n
+    part = c // parts
+    plane = pltpu.VMEM((pairs, h), F32)
+    narrow = pltpu.VMEM((pairs, h), BF16)
+    wide = pltpu.VMEM((pairs, width), BF16)
+    grads = pltpu.VMEM((c, width + c), F32)
+    vmem = pl.BlockSpec(memory_space=pltpu.VMEM)
+    smem = pl.BlockSpec(memory_space=pltpu.SMEM)
+    params = pltpu.CompilerParams(vmem_limit_bytes=VMEM_BYTES)
+    weights = (proj_weight, proj_bias, norm_gain, norm_shift, out_weight, out_bias)
+
+    index = lax.axis_index("dap").astype(jnp.int32)[None]
+    length = jnp.max(jnp.sum(pair_mask[0], axis=1)).astype(BF16)
+    sent = jnp.concatenate(
+        [pair_repr.reshape(cells, c), jnp.full((16, c), length, BF16)], axis=0
+    )
+    state = gather_rows(sent, "dap", parts)
+    cot = lax.all_gather(cotangent.reshape(cells, c), "dap")
+
+    state_1, product_0 = pl.pallas_call(
+        functools.partial(forward_first, n),
+        out_shape=(
+            jax.ShapeDtypeStruct((pairs, c), BF16),
+            jax.ShapeDtypeStruct((pairs, h), BF16),
+        ),
+        in_specs=[vmem] * 7,
+        out_specs=(vmem, vmem),
+        scratch_shapes=[plane] * 3,
+        compiler_params=params,
+        name="forward_first",
+    )(state, *weights)
+
+    up_1, slice_1 = pl.pallas_call(
+        functools.partial(update_second, n),
+        out_shape=(
+            jax.ShapeDtypeStruct((pairs, c), F32),
+            jax.ShapeDtypeStruct((part, width + c), BF16),
+        ),
+        in_specs=[smem] + [vmem] * 9,
+        out_specs=(vmem, vmem),
+        scratch_shapes=[plane] * 9 + [narrow] * 3 + [wide, grads],
+        compiler_params=params,
+        name="update_second",
+    )(index, state, state_1, cot, *weights)
+    total_1 = sum_exchange(slice_1, "dp", groups).astype(BF16)
+    whole_1 = gather_doubling(total_1, "dap", parts)
+
+    pair_grad, slice_0 = pl.pallas_call(
+        functools.partial(backward_first, n),
+        out_shape=(
+            jax.ShapeDtypeStruct((cells, c), BF16),
+            jax.ShapeDtypeStruct((part, width + c), BF16),
+        ),
+        in_specs=[smem] + [vmem] * 9,
+        out_specs=(vmem, vmem),
+        scratch_shapes=[plane] * 7 + [narrow] * 3 + [wide, grads],
+        compiler_params=params,
+        name="backward_first",
+    )(index, state, product_0, up_1, *weights)
+    total_0 = jnp.sum(gather_rows(slice_0, "dp", groups).astype(F32), axis=0).astype(BF16)
+    whole_0 = gather_rows(total_0, "dap", parts)
+
+    whole = jnp.stack([whole_0, whole_1]).reshape(2, c, width + c).astype(F32)
+    return (
+        pair_grad.reshape(pair_repr.shape),
+        whole[:, :, :width],
+        whole[:, :, width:],
+    )
 
 
 def layer_norm(values, gain_vec, shift_vec, norm_axis):
@@ -153,11 +578,10 @@
         grad_product = norm_pullback(
             product.astype(jnp.float32), gain_out, shift_out, 0, grad_mixed
         ).astype(jnp.bfloat16)
-        column_edges, column_stack = (
-            lax.all_to_all(pair_edges, "dap", split_axis=1, concat_axis=2, tiled=True),
-            lax.all_to_all(grad_product[None], "dap", split_axis=1, concat_axis=2, tiled=True),
-        )
-        column_grad = column_stack[0]
+        column_edges = spread
+        column_grad = lax.all_to_all(
+            grad_product[None], "dap", split_axis=1, concat_axis=2, tiled=True
+        )[0]
         grad_pair = lax.all_to_all(
             triangle_pullback(column_edges, column_grad, update == 0),
             "dap",
@@ -198,10 +622,23 @@
         P(),
         P(),
     )
-    return jax.shard_map(
-        shards,
-        mesh=mesh,
-        in_specs=placed,
-        out_specs=(P("dp", "dap", None, None), P(), P()),
-        check_vma=False,
-    )
+    groups, parts = mesh.shape["dp"], mesh.shape["dap"]
+
+    def program(*args):
+        n, c = args[0].shape[2:]
+        rows = n // parts
+        fits = 20 * n * n * c * 4 <= CROP_BUDGET
+        even = args[7].shape[1] == c and parts & (parts - 1) == 0 and BLOCK_ROWS % rows == 0 and n % 16 == 0
+        body = functools.partial(crop_shards, groups, parts) if fits and even else shards
+        return spread_over(body)(*args)
+
+    def spread_over(body):
+        return jax.shard_map(
+            body,
+            mesh=mesh,
+            in_specs=placed,
+            out_specs=(P("dp", "dap", None, None), P(), P()),
+            check_vma=False,
+        )
+
+    return program

time: 256 us -> 107 us (0.42)
  waiting for transfers between devices: 176 us -> 21.4 us
  blocking collectives: 0 us -> 33.9 us
  Pallas kernels: 0 us -> 25.7 us
  local copies, waits for them, and re-layouts: 18 us -> 3.77 us
  between operations: 14.8 us -> 1.49 us
  starting transfers between devices: 30.9 us -> 18.1 us
  matrix products: 8.59 us -> 0 us
  other arithmetic: 5.99 us -> 2.28 us
    psum x1 -> x0, waiting for transfers between devices: 126 us -> none  [shards(): proj_total, out_total = lax.psum((proj_total, out_total), ('dp', 'dap'))]
    all_to_all x8 -> x3, waiting for transfers between devices: 50.1 us -> 12 us  [gather_rows(): return lax.all_to_all(spread, axis, split_axis=0, concat_axis=0, tiled=True)]
    all_gather x0 -> x1, blocking collectives: none -> 33.9 us  [crop_shards(): cot = lax.all_gather(cotangent.reshape(cells, c), 'dap')]
    pallas_call x0 -> x3, Pallas kernels: none -> 25.7 us  [the longest x1 11.1 us: crop_shards(): pl.pallas_call(functools.partial(update_second, n), out_shape=(jax.ShapeD...]
    all_to_all x8 -> x3, starting transfers between devices: 30.8 us -> 14.9 us  [gather_rows(): return lax.all_to_all(spread, axis, split_axis=0, concat_axis=0, tiled=True)]
    unnamed x38 -> x14, local copies, waits for them, and re-layouts: 14.3 us -> 0.04 us
    ppermute x0 -> x6, waiting for transfers between devices: none -> 9.4 us  [the longest x3 7.88 us: gather_doubling(): other = lax.ppermute(held, axis, [(d, d ^ step) for d in range(size)])]
    dot_general x24 -> x0, matrix products: 8.59 us -> none  [the longest x2 2.08 us: shards(): jnp.einsum('rnc,cd->rnd', normed, w_gate, preferred_element_type=jnp.floa...]
  transfers between devices with their start and end apart: 9 -> 9, of which waited for: 9 -> 7; matrix products, arithmetic and copies ran while one was open for 2% -> 1% of each run, Pallas kernels for 0% -> 8%
where the time goes in v1:
time: 107 us
  blocking collectives  33.9 us (32%)
  Pallas kernels  25.7 us (24%)
  waiting for transfers between devices  21.4 us (20%)
  starting transfers between devices  18.1 us (17%)
  local copies, waits for them, and re-layouts  3.77 us (4%)
  other arithmetic  2.28 us (2%)
  between operations  1.49 us (1%)
    all_gather x1, blocking collectives, crop_shards(): cot = lax.all_gather(cotangent.reshape(cells, c), 'dap')  33.9 us
    all_to_all x3, starting transfers between devices, gather_rows(): return lax.all_to_all(spread, axis, split_axis=0, concat_axis=0, tiled=True)  14.9 us
    all_to_all x3, waiting for transfers between devices, gather_rows(): return lax.all_to_all(spread, axis, split_axis=0, concat_axis=0, tiled=True)  12 us
    pallas_call x1, Pallas kernels, crop_shards(): pl.pallas_call(functools.partial(update_second, n), out_shape=(jax.ShapeD...  11.1 us
    pallas_call x1, Pallas kernels, crop_shards(): pl.pallas_call(functools.partial(backward_first, n), out_shape=(jax.Shape...  8.64 us
    ppermute x3, waiting for transfers between devices, gather_doubling(): other = lax.ppermute(held, axis, [(d, d ^ step) for d in range(size)])  7.88 us
    pallas_call x1, Pallas kernels, crop_shards(): pl.pallas_call(functools.partial(forward_first, n), out_shape=(jax.ShapeD...  5.93 us
    ppermute x3, starting transfers between devices, sum_exchange(): lax.ppermute(value, axis, [(d, (d + shift) % size) for d in range(size)])  3 us
  transfers between devices with their start and end apart: 9, of which 7 were waited for; matrix products, arithmetic and copies ran while one was open for 1% of the time, Pallas kernels for 8%

profile of v1, /device:TPU:0, one launch (start us, length us, event | category | flops | bytes accessed | tf_op | source)
XLA Modules:
  0.0 106.6 jit_solution(8382958624332725003)
XLA Ops:
  0.6 0.8 reduce_sum.21
  1.4 0.6 reduce_max.9
  2.7 0.8 concatenate.13
  3.5 0.8 broadcast_in_dim.11
  4.2 0.0 copy-start.6
  4.2 0.0 copy-start
  4.2 7.4 %all-to-all-start = ((bf16[8,144,128]{2,1,0:T(8,128)(2,1)}), bf16[8,144,128]{2,1,0:T(8,128)(2,1)S(1)}, u32[]{:S(2)}, u32[]{:S(2)}) async-start(bf16[8,144,128]{2,1,0:T(8,128)(2,1)} %broadcast_in_dim.11), calls=%async_computation | async-start | bytes 589824 | tf_op jit(solution)/shard_map/all_to_all | solution.py:322
  11.7 0.0 copy-done.6
  11.7 0.0 copy-start.1
  11.7 0.0 copy-start.2
  11.7 0.0 copy-start.3
  11.7 0.0 copy-start.4
  11.7 0.0 copy-start.5
  11.7 33.9 %all_gather.3.cot_ref = bf16[8,128,128]{2,1,0:T(8,128)(2,1)S(1)} all-gather(bf16[1,128,128]{2,1,0:T(8,128)(2,1)S(1)} %bitcast.12), channel_id=1, replica_groups=mesh['dp'=4,'dap'=8] {'dap'}, dimensions={0}, use_global_device_ids=true | all-gather | bytes 294912 | tf_op jit(solution)/shard_map/all_gather | solution.py:381
  45.6 0.0 all-to-all-done.state_ref
  45.6 0.0 copy-done
  45.6 0.0 copy-done.1
  45.6 0.0 copy-done.2
  45.6 0.0 copy-done.3
  45.6 0.0 copy-done.4
  45.7 0.0 copy-done.5
  45.7 5.9 %forward_first.1 = (bf16[1024,128]{1,0:T(8,128)(2,1)S(1)}, bf16[1024,128]{1,0:T(8,128)(2,1)S(1)}) custom-call(bf16[8,144,128]{2,1,0:T(8,128)(2,1)S(1)} %all-to-all-done.state_ref, bf16[2,128,640]{2,1,0:T(8,128)(2,1)S(1)} %copy-done, f32[2,640]{1,0:T(2,128)S(1)} %copy-done.2, f32[2,256]{1,0:T(2,128)S(1)} %copy-done.3, f32[2,256]{1,0:T(2,128)S(1)} %copy-done.4, ...), custom_call_target="tpu_custom_call" | custom-call | tf_op jit(solution)/shard_map/forward_first/pallas_call | solution.py:383
  51.6 11.1 %update_second.1 = (f32[1024,128]{1,0:T(8,128)S(1)}, bf16[16,768]{1,0:T(8,128)(2,1)S(1)}) custom-call(s32[1]{0:T(128)} %bitcast.index_ref, bf16[8,144,128]{2,1,0:T(8,128)(2,1)S(1)} %all-to-all-done.state_ref, bf16[1024,128]{1,0:T(8,128)(2,1)S(1)} %get-tuple-element.10.next_ref, bf16[8,128,128]{2,1,0:T(8,128)(2,1)S(1)} %all_gather.3.cot_ref, ...), custom_call_target="tpu_custom_call" | custom-call | tf_op jit(solution)/shard_map/update_second/pallas_call | solution.py:396
  62.7 0.1 collective-permute-start
  62.8 1.6 %collective-permute-start.1 = (bf16[16,768]{1,0:T(8,128)(2,1)S(1)}, bf16[16,768]{1,0:T(8,128)(2,1)S(1)}, u32[]{:S(2)}, u32[]{:S(2)}) collective-permute-start(bf16[16,768]{1,0:T(8,128)(2,1)S(1)} %get-tuple-element.14), channel_id=1, source_target_pairs={{0,16},{8,24},{16,0},{24,8},{1,17},{9,25},{17,1},{25,9},{2,18},{10... | collective-permute-start | bytes 73736 | tf_op jit(solution)/shard_map/ppermute | solution.py:342
  64.3 1.4 %collective-permute-start.2 = (bf16[16,768]{1,0:T(8,128)(2,1)S(1)}, bf16[16,768]{1,0:T(8,128)(2,1)S(1)}, u32[]{:S(2)}, u32[]{:S(2)}) collective-permute-start(bf16[16,768]{1,0:T(8,128)(2,1)S(1)} %get-tuple-element.14), channel_id=1, source_target_pairs={{0,24},{8,0},{16,8},{24,16},{1,25},{9,1},{17,9},{25,17},{2,26},{10... | collective-permute-start | bytes 73736 | tf_op jit(solution)/shard_map/ppermute | solution.py:342
  65.7 0.3 collective-permute-done
  66.0 0.7 collective-permute-done.1
  66.7 0.6 collective-permute-done.2
  67.3 0.1 collective-permute-start.3
  67.3 3.8 %collective-permute-done.3 = bf16[1,16,768]{2,1,0:T(8,128)(2,1)S(1)} collective-permute-done((bf16[1,16,768]{2,1,0:T(8,128)(2,1)S(1)}, bf16[1,16,768]{2,1,0:T(8,128)(2,1)S(1)}, u32[]{:S(2)}, u32[]{:S(2)}) %collective-permute-start.3) | collective-permute-done | bytes 24608 | tf_op jit(solution)/shard_map/ppermute | solution.py:330
  71.2 0.1 collective-permute-start.4
  71.3 4.1 %collective-permute-done.4 = bf16[2,16,768]{2,1,0:T(8,128)(2,1)S(1)} collective-permute-done((bf16[2,16,768]{2,1,0:T(8,128)(2,1)S(1)}, bf16[2,16,768]{2,1,0:T(8,128)(2,1)S(1)}, u32[]{:S(2)}, u32[]{:S(2)}) %collective-permute-start.4) | collective-permute-done | bytes 49184 | tf_op jit(solution)/shard_map/ppermute | solution.py:330
  75.4 0.1 collective-permute-start.5
  75.4 8.6 %backward_first.1 = (bf16[128,128]{1,0:T(8,128)(2,1)}, bf16[16,768]{1,0:T(8,128)(2,1)S(1)}) custom-call(s32[1]{0:T(128)} %bitcast.index_ref, bf16[8,144,128]{2,1,0:T(8,128)(2,1)S(1)} %all-to-all-done.state_ref, bf16[1024,128]{1,0:T(8,128)(2,1)S(1)} %get-tuple-element.9.product_ref, f32[1024,128]{1,0:T(8,128)S(1)} %get-tuple-element.11.up_ref, ...), custom_call_target="tpu_custom_call" | custom-call | tf_op jit(solution)/shard_map/backward_first/pallas_call | solution.py:411
  84.1 0.6 broadcast_in_dim.12
  84.7 3.3 %all-to-all-start.1 = ((bf16[4,16,768]{2,1,0:T(8,128)(2,1)}), bf16[4,16,768]{2,1,0:T(8,128)(2,1)S(1)}, u32[]{:S(2)}, u32[]{:S(2)}) async-start(bf16[4,16,768]{2,1,0:T(8,128)(2,1)} %broadcast_in_dim.12), calls=%async_computation.1 | async-start | bytes 196608 | tf_op jit(solution)/shard_map/all_to_all | solution.py:322
  88.1 4.3 %all-to-all-done.1 = bf16[4,16,768]{2,1,0:T(8,128)(2,1)S(1)} async-done(((bf16[4,16,768]{2,1,0:T(8,128)(2,1)}), bf16[4,16,768]{2,1,0:T(8,128)(2,1)S(1)}, u32[]{:S(2)}, u32[]{:S(2)}) %all-to-all-start.1) | async-done | bytes 98336 | tf_op jit(solution)/shard_map/all_to_all | solution.py:322
  92.3 0.7 broadcast_in_dim.13
  93.0 4.2 %all-to-all-start.2 = ((bf16[8,16,768]{2,1,0:T(8,128)(2,1)}), bf16[8,16,768]{2,1,0:T(8,128)(2,1)S(1)}, u32[]{:S(2)}, u32[]{:S(2)}) async-start(bf16[8,16,768]{2,1,0:T(8,128)(2,1)} %broadcast_in_dim.13), calls=%async_computation.2 | async-start | bytes 393216 | tf_op jit(solution)/shard_map/all_to_all | solution.py:322
  97.2 0.0 collective-permute-done.5
  97.3 7.7 %all-to-all-done.2 = bf16[8,16,768]{2,1,0:T(8,128)(2,1)S(1)} async-done(((bf16[8,16,768]{2,1,0:T(8,128)(2,1)}), bf16[8,16,768]{2,1,0:T(8,128)(2,1)S(1)}, u32[]{:S(2)}, u32[]{:S(2)}) %all-to-all-start.2) | async-done | bytes 196640 | tf_op jit(solution)/shard_map/all_to_all | solution.py:322
  105.0 0.7 maximum_convert_fusion.1
  105.7 0.1 maximum_convert_fusion
  105.7 0.9 slice.8
  (8 shorter events, 0.1 us)
Async XLA Ops:
  4.2 7.4 %copy-start.6 = (bf16[1,4,32,128]{3,2,1,0:T(8,128)(2,1)S(1)}, bf16[1,4,32,128]{3,2,1,0:T(8,128)(2,1)}, u32[]{:S(2)}) copy-start(bf16[1,4,32,128]{3,2,1,0:T(8,128)(2,1)} %param.11) | copy-start | bytes 98308
  4.2 41.4 %copy-start = (bf16[2,128,640]{2,1,0:T(8,128)(2,1)S(1)}, bf16[2,128,640]{2,1,0:T(8,128)(2,1)}, u32[]{:S(2)}) copy-start(bf16[2,128,640]{2,1,0:T(8,128)(2,1)} %w.5) | copy-start | bytes 983044
  4.2 41.4 %all-to-all-start = ((bf16[8,144,128]{2,1,0:T(8,128)(2,1)}), bf16[8,144,128]{2,1,0:T(8,128)(2,1)S(1)}, u32[]{:S(2)}, u32[]{:S(2)}) async-start(bf16[8,144,128]{2,1,0:T(8,128)(2,1)} %broadcast_in_dim.11), calls=%async_computation | async-start | bytes 589824 | tf_op jit(solution)/shard_map/all_to_all | solution.py:322
  11.7 34.0 %copy-start.1 = (bf16[2,128,128]{2,1,0:T(8,128)(2,1)S(1)}, bf16[2,128,128]{2,1,0:T(8,128)(2,1)}, u32[]{:S(2)}) copy-start(bf16[2,128,128]{2,1,0:T(8,128)(2,1)} %w_out.5) | copy-start | bytes 196612
  11.7 34.0 %copy-start.2 = (f32[2,640]{1,0:T(2,128)S(1)}, f32[2,640]{1,0:T(2,128)}, u32[]{:S(2)}) copy-start(f32[2,640]{1,0:T(2,128)} %b.5) | copy-start | bytes 15364
  11.7 33.9 %copy-start.3 = (f32[2,256]{1,0:T(2,128)S(1)}, f32[2,256]{1,0:T(2,128)}, u32[]{:S(2)}) copy-start(f32[2,256]{1,0:T(2,128)} %gain.5) | copy-start | bytes 6148
  11.7 33.9 %copy-start.4 = (f32[2,256]{1,0:T(2,128)S(1)}, f32[2,256]{1,0:T(2,128)}, u32[]{:S(2)}) copy-start(f32[2,256]{1,0:T(2,128)} %shift.5) | copy-start | bytes 6148
  11.7 33.9 %copy-start.5 = (f32[2,128]{1,0:T(2,128)S(1)}, f32[2,128]{1,0:T(2,128)}, u32[]{:S(2)}) copy-start(f32[2,128]{1,0:T(2,128)} %b_out.5) | copy-start | bytes 3076
  62.7 3.3 %collective-permute-start = (bf16[16,768]{1,0:T(8,128)(2,1)S(1)}, bf16[16,768]{1,0:T(8,128)(2,1)S(1)}, u32[]{:S(2)}, u32[]{:S(2)}) collective-permute-start(bf16[16,768]{1,0:T(8,128)(2,1)S(1)} %get-tuple-element.14), channel_id=1, source_target_pairs={{0,8},{8,16},{16,24},{24,0},{1,9},{9,17},{17,25},{25,1},{2,10},{10... | collective-permute-start | bytes 73736 | tf_op jit(solution)/shard_map/ppermute | solution.py:342
  62.8 3.9 %collective-permute-start.1 = (bf16[16,768]{1,0:T(8,128)(2,1)S(1)}, bf16[16,768]{1,0:T(8,128)(2,1)S(1)}, u32[]{:S(2)}, u32[]{:S(2)}) collective-permute-start(bf16[16,768]{1,0:T(8,128)(2,1)S(1)} %get-tuple-element.14), channel_id=1, source_target_pairs={{0,16},{8,24},{16,0},{24,8},{1,17},{9,25},{17,1},{25,9},{2,18},{10... | collective-permute-start | bytes 73736 | tf_op jit(solution)/shard_map/ppermute | solution.py:342
  64.3 2.9 %collective-permute-start.2 = (bf16[16,768]{1,0:T(8,128)(2,1)S(1)}, bf16[16,768]{1,0:T(8,128)(2,1)S(1)}, u32[]{:S(2)}, u32[]{:S(2)}) collective-permute-start(bf16[16,768]{1,0:T(8,128)(2,1)S(1)} %get-tuple-element.14), channel_id=1, source_target_pairs={{0,24},{8,0},{16,8},{24,16},{1,25},{9,1},{17,9},{25,17},{2,26},{10... | collective-permute-start | bytes 73736 | tf_op jit(solution)/shard_map/ppermute | solution.py:342
  67.3 3.9 %collective-permute-start.3 = (bf16[1,16,768]{2,1,0:T(8,128)(2,1)S(1)}, bf16[1,16,768]{2,1,0:T(8,128)(2,1)S(1)}, u32[]{:S(2)}, u32[]{:S(2)}) collective-permute-start(bf16[1,16,768]{2,1,0:T(8,128)(2,1)S(1)} %fusion), channel_id=1, source_target_pairs={{0,1},{1,0},{2,3},{3,2},{4,5},{5,4},{6,7},{7,6},{8,9},{9,8},{10,11... | collective-permute-start | bytes 73736 | tf_op jit(solution)/shard_map/ppermute | solution.py:330
  71.2 4.2 %collective-permute-start.4 = (bf16[2,16,768]{2,1,0:T(8,128)(2,1)S(1)}, bf16[2,16,768]{2,1,0:T(8,128)(2,1)S(1)}, u32[]{:S(2)}, u32[]{:S(2)}) collective-permute-start(bf16[2,16,768]{2,1,0:T(8,128)(2,1)S(1)} %pad_maximum_fusion.2), channel_id=1, source_target_pairs={{0,2},{1,3},{2,0},{3,1},{4,6},{5,7},{6,4},{7,5},{8,10},{9,11},{10,... | collective-permute-start | bytes 147464 | tf_op jit(solution)/shard_map/ppermute | solution.py:330
  75.4 21.8 %collective-permute-start.5 = (bf16[4,16,768]{2,1,0:T(8,128)(2,1)S(1)}, bf16[4,16,768]{2,1,0:T(8,128)(2,1)S(1)}, u32[]{:S(2)}, u32[]{:S(2)}) collective-permute-start(bf16[4,16,768]{2,1,0:T(8,128)(2,1)S(1)} %pad_maximum_fusion.1), channel_id=1, source_target_pairs={{0,4},{1,5},{2,6},{3,7},{4,0},{5,1},{6,2},{7,3},{8,12},{9,13},{10,... | collective-permute-start | bytes 294920 | tf_op jit(solution)/shard_map/ppermute | solution.py:330
  84.7 7.6 %all-to-all-start.1 = ((bf16[4,16,768]{2,1,0:T(8,128)(2,1)}), bf16[4,16,768]{2,1,0:T(8,128)(2,1)S(1)}, u32[]{:S(2)}, u32[]{:S(2)}) async-start(bf16[4,16,768]{2,1,0:T(8,128)(2,1)} %broadcast_in_dim.12), calls=%async_computation.1 | async-start | bytes 196608 | tf_op jit(solution)/shard_map/all_to_all | solution.py:322
  93.0 12.0 %all-to-all-start.2 = ((bf16[8,16,768]{2,1,0:T(8,128)(2,1)}), bf16[8,16,768]{2,1,0:T(8,128)(2,1)S(1)}, u32[]{:S(2)}, u32[]{:S(2)}) async-start(bf16[8,16,768]{2,1,0:T(8,128)(2,1)} %broadcast_in_dim.13), calls=%async_computation.2 | async-start | bytes 393216 | tf_op jit(solution)/shard_map/all_to_all | solution.py:322

commit v2 on v1

--- a/solution.py
+++ b/solution.py
@@ -74,16 +74,18 @@
 
 def contract(n, first, row_of, x, y):
     lanes = y.shape[1]
+    tiles = (n // 8, 8, lanes)
 
     def step(e, totals):
-        block = y[pl.ds(pl.multiple_of(e * n, n), n), :]
+        block = y[pl.ds(pl.multiple_of(e * n, n), n), :].reshape(tiles)
         return tuple(
-            totals[a] + x[pl.ds(row_of(first + a, e), 1), :] * block for a in range(BLOCK_ROWS)
-        )
-
-    zero = jnp.zeros((n, lanes), F32)
+            totals[a] + x[pl.ds(row_of(first + a, e), 8, stride=0), :][None] * block
+            for a in range(BLOCK_ROWS)
+        )
+
+    zero = jnp.zeros(tiles, F32)
     totals = lax.fori_loop(0, n, step, (zero,) * BLOCK_ROWS, unroll=4)
-    return totals
+    return jnp.stack(totals).reshape(BLOCK_ROWS * n, lanes)
 
 
 def edge_grads(d_left, d_right, s_left, s_right, left, right):
@@ -99,6 +101,10 @@
     return jnp.max(state_ref[:, cells:, :].astype(F32)).astype(jnp.int32)
 
 
+def joined(ref, first, count, cells):
+    return jnp.concatenate([ref[first + q, :cells, :] for q in range(count)], axis=0)
+
+
 def forward_first(
     n, state_ref, w, b, gain, shift, w_out, b_out, next_ref, product_ref, left_s, right_s, gate_s
 ):
@@ -107,41 +113,39 @@
     cells = rows * n
     length = crop_length(state_ref, cells)
 
-    @pl.loop(0, parts)
+    per = BLOCK_ROWS // rows
+
+    @pl.loop(0, n // BLOCK_ROWS)
     def _(t):
-        x = state_ref[t, :cells, :].astype(F32)
-        mask = pair_mask_block(length, t * rows, rows, n, c)
+        first = t * BLOCK_ROWS
+        here = pl.ds(pl.multiple_of(first * n, BLOCK_ROWS * n), BLOCK_ROWS * n)
+        x = joined(state_ref, t * per, per, cells).astype(F32)
+        mask = pair_mask_block(length, first, BLOCK_ROWS, n, c)
         _, _, _, _, _, left, right, gate = project(x, mask, 0, w, b, gain, shift)
-        here = pl.ds(pl.multiple_of(t * cells, cells), cells)
         left_s[here, :] = left
         gate_s[here, :] = gate
-        for r in range(rows):
-            right_s[pl.ds(t * rows + r, n, stride=n), :] = right[r * n : (r + 1) * n]
+        for r in range(BLOCK_ROWS):
+            right_s[pl.ds(first + r, n, stride=n), :] = right[r * n : (r + 1) * n]
 
     @pl.loop(0, n // BLOCK_ROWS)
     def _(t):
         totals = contract(n, t * BLOCK_ROWS, lambda i, k: i * n + k, left_s, right_s)
         here = pl.ds(pl.multiple_of(t * BLOCK_ROWS * n, BLOCK_ROWS * n), BLOCK_ROWS * n)
-        product = jnp.concatenate(totals, axis=0).astype(BF16)
+        product = totals.astype(BF16)
         product_ref[here, :] = product
         _, _, _, branch = mix(product, 0, c, gain, shift, w_out, b_out)
-        per = BLOCK_ROWS // rows
-        x = jnp.concatenate([state_ref[t * per + q, :cells, :] for q in range(per)], axis=0)
+        x = joined(state_ref, t * per, per, cells)
         next_ref[here, :] = (x.astype(F32) + gate_s[here, :] * branch).astype(BF16)
 
 
-def weight_grads(index_ref, normed_s, d_pre_s, mixed_s, d_branch_s, grad_s, slice_ref):
-    part = slice_ref.shape[0]
+def weight_grads(normed_s, d_pre_s, mixed_s, d_branch_s, grads_ref):
     width = d_pre_s.shape[1]
-    grad_s[:, :width] = dot(normed_s[...], d_pre_s[...], ((0,), (0,)))
-    grad_s[:, width:] = dot(mixed_s[...], d_branch_s[...], ((0,), (0,)))
-    own = pl.ds(pl.multiple_of(index_ref[0] * part, part), part)
-    slice_ref[...] = grad_s[own, :].astype(BF16)
+    grads_ref[:, :width] = dot(normed_s[...], d_pre_s[...], ((0,), (0,))).astype(BF16)
+    grads_ref[:, width:] = dot(mixed_s[...], d_branch_s[...], ((0,), (0,))).astype(BF16)
 
 
 def update_second(
     n,
-    index_ref,
     state_ref,
     next_ref,
     cot_ref,
@@ -152,7 +156,7 @@
     w_out,
     b_out,
     up_ref,
-    slice_ref,
+    grads_ref,
     left_s,
     right_s,
     s_left_s,
@@ -166,7 +170,6 @@
     mixed_s,
     d_branch_s,
     d_pre_s,
-    grad_s,
 ):
     parts, _, c = state_ref.shape
     rows = n // parts
@@ -174,11 +177,13 @@
     h = left_s.shape[1]
     length = crop_length(state_ref, cells)
 
-    @pl.loop(0, parts)
+    per = BLOCK_ROWS // rows
+
+    @pl.loop(0, n // BLOCK_ROWS)
     def _(t):
-        here = pl.ds(pl.multiple_of(t * cells, cells), cells)
+        here = pl.ds(pl.multiple_of(t * BLOCK_ROWS * n, BLOCK_ROWS * n), BLOCK_ROWS * n)
         x = next_ref[here, :].astype(F32)
-        mask = pair_mask_block(length, t * rows, rows, n, c)
+        mask = pair_mask_block(length, t * BLOCK_ROWS, BLOCK_ROWS, n, c)
         x_hat, rstd, normed, s_left, s_right, left, right, gate = project(
             x, mask, 1, w, b, gain, shift
         )
@@ -191,15 +196,13 @@
         rstd_s[here, :] = jnp.broadcast_to(rstd, x_hat.shape)
         normed_s[here, :] = normed
 
-    per = BLOCK_ROWS // rows
-
     @pl.loop(0, n // BLOCK_ROWS)
     def _(t):
         totals = contract(n, t * BLOCK_ROWS, lambda i, k: k * n + i, left_s, right_s)
         here = pl.ds(pl.multiple_of(t * BLOCK_ROWS * n, BLOCK_ROWS * n), BLOCK_ROWS * n)
-        product = jnp.concatenate(totals, axis=0).astype(BF16)
+        product = totals.astype(BF16)
         p_hat, p_rstd, mixed, branch = mix(product, 1, c, gain, shift, w_out, b_out)
-        up = jnp.concatenate([cot_ref[t * per + q] for q in range(per)], axis=0).astype(F32)
+        up = joined(cot_ref, t * per, per, cells).astype(F32)
         d_branch, d_gate, d_product = unmix(
             up, gate_s[here, :], branch, p_hat, p_rstd, 1, c, gain, w_out
         )
@@ -216,22 +219,18 @@
     def _(t):
         first = t * BLOCK_ROWS
         here = pl.ds(pl.multiple_of(first * n, BLOCK_ROWS * n), BLOCK_ROWS * n)
-        d_left = jnp.concatenate(
-            contract(n, first, lambda k, j: k * n + j, right_s, d_product_t_s), axis=0
-        )
-        d_right = jnp.concatenate(
-            contract(n, first, lambda k, i: k * n + i, left_s, d_product_s), axis=0
-        )
+        d_left = contract(n, first, lambda k, j: k * n + j, right_s, d_product_t_s)
+        d_right = contract(n, first, lambda k, i: k * n + i, left_s, d_product_s)
         grads = edge_grads(
             d_left, d_right, s_left_s[here, :], s_right_s[here, :], left_s[here, :], right_s[here, :]
         )
         for g in range(4):
             d_pre_s[here, g * h : (g + 1) * h] = grads[g]
         d_normed = dot(d_pre_s[here, :], w[1], ((1,), (1,))) * gain[1:2, :c]
-        up = jnp.concatenate([cot_ref[t * per + q] for q in range(per)], axis=0).astype(F32)
+        up = joined(cot_ref, t * per, per, cells).astype(F32)
         up_ref[here, :] = up + norm_vjp(hat_s[here, :], rstd_s[here, :], d_normed)
 
-    weight_grads(index_ref, normed_s, d_pre_s, mixed_s, d_branch_s, grad_s, slice_ref)
+    weight_grads(normed_s, d_pre_s, mixed_s, d_branch_s, grads_ref)
 
 
 def backward_first(
@@ -247,7 +246,7 @@
     w_out,
     b_out,
     out_ref,
-    slice_ref,
+    grads_ref,
     left_s,
     right_s,
     s_left_s,
@@ -259,7 +258,6 @@
     mixed_s,
     d_branch_s,
     d_pre_s,
-    grad_s,
 ):
     parts, _, c = state_ref.shape
     rows = n // parts
@@ -267,11 +265,13 @@
     h = left_s.shape[1]
     length = crop_length(state_ref, cells)
 
-    @pl.loop(0, parts)
+    per = BLOCK_ROWS // rows
+
+    @pl.loop(0, n // BLOCK_ROWS)
     def _(t):
-        here = pl.ds(pl.multiple_of(t * cells, cells), cells)
-        x = state_ref[t, :cells, :].astype(F32)
-        mask = pair_mask_block(length, t * rows, rows, n, c)
+        here = pl.ds(pl.multiple_of(t * BLOCK_ROWS * n, BLOCK_ROWS * n), BLOCK_ROWS * n)
+        x = joined(state_ref, t * per, per, cells).astype(F32)
+        mask = pair_mask_block(length, t * BLOCK_ROWS, BLOCK_ROWS, n, c)
         x_hat, rstd, normed, s_left, s_right, left, right, gate = project(
             x, mask, 0, w, b, gain, shift
         )
@@ -297,12 +297,8 @@
     def _(t):
         first = t * BLOCK_ROWS
         here = pl.ds(pl.multiple_of(first * n, BLOCK_ROWS * n), BLOCK_ROWS * n)
-        d_left = jnp.concatenate(
-            contract(n, first, lambda i, j: i * n + j, d_product_s, right_s), axis=0
-        )
-        d_right = jnp.concatenate(
-            contract(n, first, lambda j, i: i * n + j, d_product_s, left_s), axis=0
-        )
+        d_left = contract(n, first, lambda i, j: i * n + j, d_product_s, right_s)
+        d_right = contract(n, first, lambda j, i: i * n + j, d_product_s, left_s)
         grads = edge_grads(
             d_left, d_right, s_left_s[here, :], s_right_s[here, :], left_s[here, :], right_s[here, :]
         )
@@ -314,7 +310,7 @@
     out_ref[...] = (
         up_ref[own, :] + norm_vjp(hat_s[own, :], rstd_s[own, :], d_normed)
     ).astype(BF16)
-    weight_grads(index_ref, normed_s, d_pre_s, mixed_s, d_branch_s, grad_s, slice_ref)
+    weight_grads(normed_s, d_pre_s, mixed_s, d_branch_s, grads_ref)
 
 
 def gather_rows(value, axis, size):
@@ -322,27 +318,32 @@
     return lax.all_to_all(spread, axis, split_axis=0, concat_axis=0, tiled=True)
 
 
-def gather_doubling(value, axis, size):
-    me = lax.axis_index(axis)
-    held = value[None]
-    step = 1
+def pair_rounds(value, axis, size):
+    step, other = 1, None
     while step < size:
-        other = lax.ppermute(held, axis, [(d, d ^ step) for d in range(size)])
-        low = (me & step) == 0
-        held = jnp.concatenate(
-            [jnp.where(low, held, other), jnp.where(low, other, held)], axis=0
-        )
+        if other is not None:
+            value = (value.astype(F32) + other.astype(F32)).astype(BF16)
+        other = lax.ppermute(value, axis, [(d, d ^ step) for d in range(size)])
         step *= 2
-    return held
-
-
-def sum_exchange(value, axis, size):
-    total = value.astype(F32)
-    for shift in range(1, size):
-        total = total + lax.ppermute(
-            value, axis, [(d, (d + shift) % size) for d in range(size)]
-        ).astype(F32)
-    return total
+    return value, other
+
+
+def prepare(state_ref, mask_ref, sent_ref):
+    parts, _, c = sent_ref.shape
+    cells = state_ref.shape[0]
+    length = jnp.max(jnp.sum(mask_ref[...].astype(F32), axis=1, keepdims=True))
+    below = jnp.full((sent_ref.shape[1] - cells, c), length, F32).astype(BF16)
+    for part in range(parts):
+        sent_ref[part, :cells, :] = state_ref[...]
+        sent_ref[part, cells:, :] = below
+
+
+def add_grads(own_0, other_0, own_1, other_1, proj_ref, out_ref):
+    width = proj_ref.shape[2]
+    for u, (own, other) in enumerate(((own_0, other_0), (own_1, other_1))):
+        total = own[...].astype(F32) + other[...].astype(F32)
+        proj_ref[u] = total[:, :width]
+        out_ref[u] = total[:, width:]
 
 
 def crop_shards(
@@ -362,23 +363,26 @@
     h = out_weight.shape[1]
     width = proj_weight.shape[2]
     cells, pairs = rows * n, n * n
-    part = c // parts
-    plane = pltpu.VMEM((pairs, h), F32)
+    plane = pltpu.VMEM((pairs + 8, h), F32)
     narrow = pltpu.VMEM((pairs, h), BF16)
     wide = pltpu.VMEM((pairs, width), BF16)
-    grads = pltpu.VMEM((c, width + c), F32)
+    grads = jax.ShapeDtypeStruct((c, width + c), BF16)
     vmem = pl.BlockSpec(memory_space=pltpu.VMEM)
     smem = pl.BlockSpec(memory_space=pltpu.SMEM)
     params = pltpu.CompilerParams(vmem_limit_bytes=VMEM_BYTES)
     weights = (proj_weight, proj_bias, norm_gain, norm_shift, out_weight, out_bias)
 
     index = lax.axis_index("dap").astype(jnp.int32)[None]
-    length = jnp.max(jnp.sum(pair_mask[0], axis=1)).astype(BF16)
-    sent = jnp.concatenate(
-        [pair_repr.reshape(cells, c), jnp.full((16, c), length, BF16)], axis=0
-    )
-    state = gather_rows(sent, "dap", parts)
-    cot = lax.all_gather(cotangent.reshape(cells, c), "dap")
+    sent = pl.pallas_call(
+        prepare,
+        out_shape=jax.ShapeDtypeStruct((parts, cells + 16, c), BF16),
+        in_specs=[vmem] * 2,
+        out_specs=vmem,
+        compiler_params=params,
+        name="prepare",
+    )(pair_repr.reshape(cells, c), pair_mask[0])
+    state = lax.all_to_all(sent, "dap", split_axis=0, concat_axis=0, tiled=True)
+    cot = gather_rows(cotangent.reshape(cells, c), "dap", parts)
 
     state_1, product_0 = pl.pallas_call(
         functools.partial(forward_first, n),
@@ -393,42 +397,46 @@
         name="forward_first",
     )(state, *weights)
 
-    up_1, slice_1 = pl.pallas_call(
+    up_1, grads_1 = pl.pallas_call(
         functools.partial(update_second, n),
         out_shape=(
             jax.ShapeDtypeStruct((pairs, c), F32),
-            jax.ShapeDtypeStruct((part, width + c), BF16),
+            grads,
+        ),
+        in_specs=[vmem] * 9,
+        out_specs=(vmem, vmem),
+        scratch_shapes=[plane] * 9 + [narrow] * 3 + [wide],
+        compiler_params=params,
+        name="update_second",
+    )(state, state_1, cot, *weights)
+    ends_1 = pair_rounds(grads_1, "dp", groups)
+
+    pair_grad, grads_0 = pl.pallas_call(
+        functools.partial(backward_first, n),
+        out_shape=(
+            jax.ShapeDtypeStruct((cells, c), BF16),
+            grads,
         ),
         in_specs=[smem] + [vmem] * 9,
         out_specs=(vmem, vmem),
-        scratch_shapes=[plane] * 9 + [narrow] * 3 + [wide, grads],
-        compiler_params=params,
-        name="update_second",
-    )(index, state, state_1, cot, *weights)
-    total_1 = sum_exchange(slice_1, "dp", groups).astype(BF16)
-    whole_1 = gather_doubling(total_1, "dap", parts)
-
-    pair_grad, slice_0 = pl.pallas_call(
-        functools.partial(backward_first, n),
-        out_shape=(
-            jax.ShapeDtypeStruct((cells, c), BF16),
-            jax.ShapeDtypeStruct((part, width + c), BF16),
-        ),
-        in_specs=[smem] + [vmem] * 9,
-        out_specs=(vmem, vmem),
-        scratch_shapes=[plane] * 7 + [narrow] * 3 + [wide, grads],
+        scratch_shapes=[plane] * 7 + [narrow] * 3 + [wide],
         compiler_params=params,
         name="backward_first",
     )(index, state, product_0, up_1, *weights)
-    total_0 = jnp.sum(gather_rows(slice_0, "dp", groups).astype(F32), axis=0).astype(BF16)
-    whole_0 = gather_rows(total_0, "dap", parts)
-
-    whole = jnp.stack([whole_0, whole_1]).reshape(2, c, width + c).astype(F32)
-    return (
-        pair_grad.reshape(pair_repr.shape),
-        whole[:, :, :width],
-        whole[:, :, width:],
-    )
+    ends_0 = pair_rounds(grads_0, "dp", groups)
+
+    proj_total, out_total = pl.pallas_call(
+        add_grads,
+        out_shape=(
+            jax.ShapeDtypeStruct((2, c, width), F32),
+            jax.ShapeDtypeStruct((2, h, c), F32),
+        ),
+        in_specs=[vmem] * 4,
+        out_specs=(vmem, vmem),
+        compiler_params=params,
+        name="add_grads",
+    )(*ends_0, *ends_1)
+    return pair_grad.reshape(pair_repr.shape), proj_total, out_total
 
 
 def layer_norm(values, gain_vec, shift_vec, norm_axis):
@@ -628,7 +636,7 @@
         n, c = args[0].shape[2:]
         rows = n // parts
         fits = 20 * n * n * c * 4 <= CROP_BUDGET
-        even = args[7].shape[1] == c and parts & (parts - 1) == 0 and BLOCK_ROWS % rows == 0 and n % 16 == 0
+        even = args[7].shape[1] == c and groups > 1 and groups & (groups - 1) == 0 and BLOCK_ROWS % rows == 0 and n % 16 == 0
         body = functools.partial(crop_shards, groups, parts) if fits and even else shards
         return spread_over(body)(*args)
 

time: 107 us -> 63.3 us (0.59)
  blocking collectives: 33.9 us -> 17.4 us
  starting transfers between devices: 18.1 us -> 6.22 us
  waiting for transfers between devices: 21.4 us -> 12.8 us
  Pallas kernels: 25.7 us -> 22.7 us
  other arithmetic: 2.28 us -> 0.1 us
    all_gather x1 -> x0, blocking collectives: 33.9 us -> none  [crop_shards(): cot = lax.all_gather(cotangent.reshape(cells, c), 'dap')]
    all_to_all x0 -> x1, blocking collectives: none -> 17.4 us  [crop_shards(): state = lax.all_to_all(sent, 'dap', split_axis=0, concat_axis=0, tiled=True)]
    all_to_all x3 -> x1, starting transfers between devices: 14.9 us -> 3.56 us  [gather_rows(): return lax.all_to_all(spread, axis, split_axis=0, concat_axis=0, tiled=True)]
    all_to_all x3 -> x1, waiting for transfers between devices: 12 us -> 2.9 us  [gather_rows(): return lax.all_to_all(spread, axis, split_axis=0, concat_axis=0, tiled=True)]
    unnamed x14 -> x18, local copies, waits for them, and re-layouts: 0.04 us -> 2.09 us
    pallas_call x1, Pallas kernels: 8.64 us -> 6.91 us  [crop_shards(): pl.pallas_call(functools.partial(backward_first, n), out_shape=(jax.Shape...]
    broadcast_in_dim x3 -> x1, local copies, waits for them, and re-layouts: 2.09 us -> 0.74 us  [gather_rows(): spread = jnp.broadcast_to(value[None], (size,) + value.shape)]
    pallas_call x1, Pallas kernels: 5.93 us -> 4.74 us  [crop_shards(): pl.pallas_call(functools.partial(forward_first, n), out_shape=(jax.ShapeD...]
  transfers between devices with their start and end apart: 9 -> 5, of which waited for: 7 -> 4; matrix products, arithmetic and copies ran while one was open for 1% -> 0% of each run, Pallas kernels for 8% -> 8%
where the time goes in v2:
time: 63.3 us; the launch traced here: 62.9 us
  Pallas kernels  22.7 us (36%)
  blocking collectives  17.4 us (27%)
  waiting for transfers between devices  12.8 us (20%)
  starting transfers between devices  6.22 us (10%)
  local copies, waits for them, and re-layouts  2.83 us (4%)
  between operations  0.76 us (1%)
    all_to_all x1, blocking collectives, crop_shards(): state = lax.all_to_all(sent, 'dap', split_axis=0, concat_axis=0, tiled=True)  17.4 us
    pallas_call x1, Pallas kernels, crop_shards(): pl.pallas_call(functools.partial(update_second, n), out_shape=(jax.ShapeD...  9.98 us
    ppermute x4, waiting for transfers between devices, pair_rounds(): other = lax.ppermute(value, axis, [(d, d ^ step) for d in range(size)])  9.94 us
    pallas_call x1, Pallas kernels, crop_shards(): pl.pallas_call(functools.partial(backward_first, n), out_shape=(jax.Shape...  6.91 us
    pallas_call x1, Pallas kernels, crop_shards(): pl.pallas_call(functools.partial(forward_first, n), out_shape=(jax.ShapeD...  4.74 us
    all_to_all x1, starting transfers between devices, gather_rows(): return lax.all_to_all(spread, axis, split_axis=0, concat_axis=0, tiled=True)  3.56 us
    all_to_all x1, waiting for transfers between devices, gather_rows(): return lax.all_to_all(spread, axis, split_axis=0, concat_axis=0, tiled=True)  2.9 us
    ppermute x4, starting transfers between devices, pair_rounds(): other = lax.ppermute(value, axis, [(d, d ^ step) for d in range(size)])  2.67 us
  transfers between devices with their start and end apart: 5, of which 4 were waited for; matrix products, arithmetic and copies ran while one was open for 0% of the time, Pallas kernels for 8%

profile of v2, /device:TPU:0, one launch (start us, length us, event | category | flops | bytes accessed | tf_op | source)
XLA Modules:
  0.0 62.9 jit_solution(6471596388608612018)
XLA Ops:
  0.6 0.0 copy-start.7
  0.6 0.7 %copy-done.7 = s32[1,4,32]{2,1,0:T(4,128)S(1)} copy-done((s32[1,4,32]{2,1,0:T(4,128)S(1)}, s32[1,4,32]{2,1,0:T(4,128)}, u32[]{:S(2)}) %copy-start.7) | copy-done | bytes 536
  1.3 0.0 copy-start.3
  1.3 0.8 %copy-done.3 = bf16[1,4,32,128]{3,2,1,0:T(8,128)(2,1)S(1)} copy-done((bf16[1,4,32,128]{3,2,1,0:T(8,128)(2,1)S(1)}, bf16[1,4,32,128]{3,2,1,0:T(8,128)(2,1)}, u32[]{:S(2)}) %copy-start.3) | copy-done | bytes 32792
  2.1 0.1 prepare.1
  2.2 0.0 copy-start.8
  2.2 17.4 %all_to_all.10.state_ref = bf16[8,144,128]{2,1,0:T(8,128)(2,1)S(1)} all-to-all(bf16[8,144,128]{2,1,0:T(8,128)(2,1)S(1)} %prepare.1), channel_id=1, replica_groups=mesh['dp'=4,'dap'=8] {'dap'}, dimensions={0} | all-to-all | bytes 589824 | tf_op jit(solution)/shard_map/all_to_all | solution.py:384
  19.6 0.0 copy-done.8
  19.6 0.7 %broadcast_in_dim.12 = bf16[8,128,128]{2,1,0:T(8,128)(2,1)} broadcast(bf16[128,128]{1,0:T(8,128)(2,1)S(1)} %bitcast.7), dimensions={1,2} | broadcast | bytes 294912 | tf_op jit(solution)/shard_map/broadcast_in_dim | solution.py:317
  20.4 0.0 copy-start
  20.4 0.0 copy-start.1
  20.4 0.0 copy-start.4
  20.4 0.0 copy-start.5
  20.4 0.0 copy-start.6
  20.4 3.6 %all-to-all-start.1 = ((bf16[8,128,128]{2,1,0:T(8,128)(2,1)}), bf16[8,128,128]{2,1,0:T(8,128)(2,1)S(1)}, u32[]{:S(2)}, u32[]{:S(2)}) async-start(bf16[8,128,128]{2,1,0:T(8,128)(2,1)} %broadcast_in_dim.12), calls=%async_computation.1 | async-start | bytes 524288 | tf_op jit(solution)/shard_map/all_to_all | solution.py:318
  24.0 0.0 copy-start.2
  24.0 0.0 copy-done
  24.0 0.0 copy-done.1
  24.0 0.0 copy-done.4
  24.0 0.0 copy-done.5
  24.0 0.0 copy-done.6
  24.0 0.6 copy-done.2
  24.7 4.7 %forward_first.1 = (bf16[1024,128]{1,0:T(8,128)(2,1)S(1)}, bf16[1024,128]{1,0:T(8,128)(2,1)S(1)}) custom-call(bf16[8,144,128]{2,1,0:T(8,128)(2,1)S(1)} %all_to_all.10.state_ref, bf16[2,128,640]{2,1,0:T(8,128)(2,1)S(1)} %copy-done, f32[2,640]{1,0:T(2,128)S(1)} %copy-done.2, f32[2,256]{1,0:T(2,128)S(1)} %copy-done.4, f32[2,256]{1,0:T(2,128)S(1)} %copy-done.5, ...), custom_call_target="tpu_custom_call" | custom-call | tf_op jit(solution)/shard_map/forward_first/pallas_call | solution.py:387
  29.4 2.9 %all-to-all-done.1.cot_ref = bf16[8,128,128]{2,1,0:T(8,128)(2,1)S(1)} async-done(((bf16[8,128,128]{2,1,0:T(8,128)(2,1)}), bf16[8,128,128]{2,1,0:T(8,128)(2,1)S(1)}, u32[]{:S(2)}, u32[]{:S(2)}) %all-to-all-start.1) | async-done | bytes 262176 | tf_op jit(solution)/shard_map/all_to_all | solution.py:318
  32.3 10.0 %update_second.1 = (f32[1024,128]{1,0:T(8,128)S(1)}, bf16[128,768]{1,0:T(8,128)(2,1)S(1)}) custom-call(bf16[8,144,128]{2,1,0:T(8,128)(2,1)S(1)} %all_to_all.10.state_ref, bf16[1024,128]{1,0:T(8,128)(2,1)S(1)} %get-tuple-element.12.next_ref, bf16[8,128,128]{2,1,0:T(8,128)(2,1)S(1)} %all-to-all-done.1.cot_ref, bf16[2,128,640]{2,1,0:T(8,128)(2,1)S(1)} %copy-done, ...), custom_call_target="tpu_custom_call" | custom-call | tf_op jit(solution)/shard_map/update_second/pallas_call | solution.py:400
  42.3 6.9 %backward_first.1 = (bf16[128,128]{1,0:T(8,128)(2,1)}, bf16[128,768]{1,0:T(8,128)(2,1)S(1)}) custom-call(s32[1]{0:T(128)} %bitcast.index_ref, bf16[8,144,128]{2,1,0:T(8,128)(2,1)S(1)} %all_to_all.10.state_ref, bf16[1024,128]{1,0:T(8,128)(2,1)S(1)} %get-tuple-element.11.product_ref, f32[1024,128]{1,0:T(8,128)S(1)} %get-tuple-element.13.up_ref, ...), custom_call_target="tpu_custom_call" | custom-call | tf_op jit(solution)/shard_map/backward_first/pallas_call | solution.py:414
  49.2 0.0 collective-permute-start
  49.2 0.5 collective-permute-start.2
  49.7 0.9 %collective-permute-done = bf16[128,768]{1,0:T(8,128)(2,1)S(1)} collective-permute-done((bf16[128,768]{1,0:T(8,128)(2,1)S(1)}, bf16[128,768]{1,0:T(8,128)(2,1)S(1)}, u32[]{:S(2)}, u32[]{:S(2)}) %collective-permute-start) | collective-permute-done | bytes 196640 | tf_op jit(solution)/shard_map/ppermute | solution.py:326
  50.7 1.6 %collective-permute-start.1 = (bf16[128,768]{1,0:T(8,128)(2,1)S(1)}, bf16[128,768]{1,0:T(8,128)(2,1)S(1)}, u32[]{:S(2)}, u32[]{:S(2)}) collective-permute-start(bf16[128,768]{1,0:T(8,128)(2,1)S(1)} %add_convert_fusion.1.own_0), channel_id=1, source_target_pairs={{0,16},{8,24},{16,0},{24,8},{1,17},{9,25},{17,1},{25,9},{2,18},{10... | collective-permute-start | bytes 589832 | tf_op jit(solution)/shard_map/ppermute | solution.py:326
  52.2 0.0 collective-permute-done.2
  52.3 0.6 collective-permute-start.3
  52.9 5.6 %collective-permute-done.1.other_0 = bf16[128,768]{1,0:T(8,128)(2,1)S(1)} collective-permute-done((bf16[128,768]{1,0:T(8,128)(2,1)S(1)}, bf16[128,768]{1,0:T(8,128)(2,1)S(1)}, u32[]{:S(2)}, u32[]{:S(2)}) %collective-permute-start.1) | collective-permute-done | bytes 196640 | tf_op jit(solution)/shard_map/ppermute | solution.py:326
  58.5 3.4 %collective-permute-done.3.other_1 = bf16[128,768]{1,0:T(8,128)(2,1)S(1)} collective-permute-done((bf16[128,768]{1,0:T(8,128)(2,1)S(1)}, bf16[128,768]{1,0:T(8,128)(2,1)S(1)}, u32[]{:S(2)}, u32[]{:S(2)}) %collective-permute-start.3) | collective-permute-done | bytes 196640 | tf_op jit(solution)/shard_map/ppermute | solution.py:326
  61.9 0.9 %add_grads.1 = (f32[2,128,640]{2,1,0:T(8,128)}, f32[2,128,128]{2,1,0:T(8,128)}) custom-call(bf16[128,768]{1,0:T(8,128)(2,1)S(1)} %add_convert_fusion.1.own_0, bf16[128,768]{1,0:T(8,128)(2,1)S(1)} %collective-permute-done.1.other_0, bf16[128,768]{1,0:T(8,128)(2,1)S(1)} %add_convert_fusion.own_1, bf16[128,768]{1,0:T(8,128)(2,1)S(1)} %collective-permute-done.3.other_1), custom_call_target="tpu_custom_call" | custom-call | tf_op jit(solution)/shard_map/add_grads/pallas_call | solution.py:428
  (2 shorter events, 0.1 us)
Async XLA Ops:
  0.6 0.7 %copy-start.7 = (s32[1,4,32]{2,1,0:T(4,128)S(1)}, s32[1,4,32]{2,1,0:T(4,128)}, u32[]{:S(2)}) copy-start(s32[1,4,32]{2,1,0:T(4,128)} %param.10) | copy-start | bytes 1540
  1.3 0.8 %copy-start.3 = (bf16[1,4,32,128]{3,2,1,0:T(8,128)(2,1)S(1)}, bf16[1,4,32,128]{3,2,1,0:T(8,128)(2,1)}, u32[]{:S(2)}) copy-start(bf16[1,4,32,128]{3,2,1,0:T(8,128)(2,1)} %param.9) | copy-start | bytes 98308
  2.2 17.4 %copy-start.8 = (bf16[1,4,32,128]{3,2,1,0:T(8,128)(2,1)S(1)}, bf16[1,4,32,128]{3,2,1,0:T(8,128)(2,1)}, u32[]{:S(2)}) copy-start(bf16[1,4,32,128]{3,2,1,0:T(8,128)(2,1)} %param.11) | copy-start | bytes 98308
  20.4 3.6 %copy-start = (bf16[2,128,640]{2,1,0:T(8,128)(2,1)S(1)}, bf16[2,128,640]{2,1,0:T(8,128)(2,1)}, u32[]{:S(2)}) copy-start(bf16[2,128,640]{2,1,0:T(8,128)(2,1)} %w.5) | copy-start | bytes 983044
  20.4 3.6 %copy-start.1 = (bf16[2,128,128]{2,1,0:T(8,128)(2,1)S(1)}, bf16[2,128,128]{2,1,0:T(8,128)(2,1)}, u32[]{:S(2)}) copy-start(bf16[2,128,128]{2,1,0:T(8,128)(2,1)} %w_out.5) | copy-start | bytes 196612
  20.4 3.6 %copy-start.4 = (f32[2,256]{1,0:T(2,128)S(1)}, f32[2,256]{1,0:T(2,128)}, u32[]{:S(2)}) copy-start(f32[2,256]{1,0:T(2,128)} %gain.5) | copy-start | bytes 6148
  20.4 3.6 %copy-start.5 = (f32[2,256]{1,0:T(2,128)S(1)}, f32[2,256]{1,0:T(2,128)}, u32[]{:S(2)}) copy-start(f32[2,256]{1,0:T(2,128)} %shift.5) | copy-start | bytes 6148
  20.4 3.6 %copy-start.6 = (f32[2,128]{1,0:T(2,128)S(1)}, f32[2,128]{1,0:T(2,128)}, u32[]{:S(2)}) copy-start(f32[2,128]{1,0:T(2,128)} %b_out.5) | copy-start | bytes 3076
  20.4 11.9 %all-to-all-start.1 = ((bf16[8,128,128]{2,1,0:T(8,128)(2,1)}), bf16[8,128,128]{2,1,0:T(8,128)(2,1)S(1)}, u32[]{:S(2)}, u32[]{:S(2)}) async-start(bf16[8,128,128]{2,1,0:T(8,128)(2,1)} %broadcast_in_dim.12), calls=%async_computation.1 | async-start | bytes 524288 | tf_op jit(solution)/shard_map/all_to_all | solution.py:318
  24.0 0.7 %copy-start.2 = (f32[2,640]{1,0:T(2,128)S(1)}, f32[2,640]{1,0:T(2,128)}, u32[]{:S(2)}) copy-start(f32[2,640]{1,0:T(2,128)} %b.5) | copy-start | bytes 15364
  49.2 1.4 %collective-permute-start = (bf16[128,768]{1,0:T(8,128)(2,1)S(1)}, bf16[128,768]{1,0:T(8,128)(2,1)S(1)}, u32[]{:S(2)}, u32[]{:S(2)}) collective-permute-start(bf16[128,768]{1,0:T(8,128)(2,1)S(1)} %get-tuple-element.15), channel_id=1, source_target_pairs={{0,8},{8,0},{16,24},{24,16},{1,9},{9,1},{17,25},{25,17},{2,10},{10... | collective-permute-start | bytes 589832 | tf_op jit(solution)/shard_map/ppermute | solution.py:326
  49.2 3.1 %collective-permute-start.2 = (bf16[128,768]{1,0:T(8,128)(2,1)S(1)}, bf16[128,768]{1,0:T(8,128)(2,1)S(1)}, u32[]{:S(2)}, u32[]{:S(2)}) collective-permute-start(bf16[128,768]{1,0:T(8,128)(2,1)S(1)} %get-tuple-element.16), channel_id=1, source_target_pairs={{0,8},{8,0},{16,24},{24,16},{1,9},{9,1},{17,25},{25,17},{2,10},{10... | collective-permute-start | bytes 589832 | tf_op jit(solution)/shard_map/ppermute | solution.py:326
  50.7 7.8 %collective-permute-start.1 = (bf16[128,768]{1,0:T(8,128)(2,1)S(1)}, bf16[128,768]{1,0:T(8,128)(2,1)S(1)}, u32[]{:S(2)}, u32[]{:S(2)}) collective-permute-start(bf16[128,768]{1,0:T(8,128)(2,1)S(1)} %add_convert_fusion.1.own_0), channel_id=1, source_target_pairs={{0,16},{8,24},{16,0},{24,8},{1,17},{9,25},{17,1},{25,9},{2,18},{10... | collective-permute-start | bytes 589832 | tf_op jit(solution)/shard_map/ppermute | solution.py:326
  52.3 9.6 %collective-permute-start.3 = (bf16[128,768]{1,0:T(8,128)(2,1)S(1)}, bf16[128,768]{1,0:T(8,128)(2,1)S(1)}, u32[]{:S(2)}, u32[]{:S(2)}) collective-permute-start(bf16[128,768]{1,0:T(8,128)(2,1)S(1)} %add_convert_fusion.own_1), channel_id=1, source_target_pairs={{0,16},{8,24},{16,0},{24,8},{1,17},{9,25},{17,1},{25,9},{2,18},{10... | collective-permute-start | bytes 589832 | tf_op jit(solution)/shard_map/ppermute | solution.py:326

commit v3 on v0

--- a/solution.py
+++ b/solution.py
@@ -1,9 +1,390 @@
+import functools
+
 import jax
 import jax.numpy as jnp
 from jax import lax
+from jax.experimental import pallas as pl
+from jax.experimental.pallas import tpu as pltpu
 from jax.sharding import PartitionSpec as P
 
 NORM_EPSILON = 1e-05
+VMEM_BYTES = 24 * 1024 * 1024
+PREPARE_BYTES = 63 * 1024 * 1024
+CROP_BUDGET = 32 * 1024 * 1024
+BLOCK_ROWS = 8
+KEPT = 12
+F32 = jnp.float32
+BF16 = jnp.bfloat16
+
+
+def sigmoid(x):
+    return 0.5 * jnp.tanh(0.5 * x) + 0.5
+
+
+def dot(a, b, dims=((1,), (0,))):
+    return lax.dot_general(a, b, (dims, ((), ())), preferred_element_type=F32)
+
+
+def norm_parts(x):
+    centred = x - jnp.mean(x, axis=-1, keepdims=True)
+    rstd = lax.rsqrt(jnp.mean(centred * centred, axis=-1, keepdims=True) + NORM_EPSILON)
+    return centred * rstd, rstd
+
+
+def norm_vjp(x_hat, rstd, grad):
+    mean_grad = jnp.mean(grad, axis=-1, keepdims=True)
+    mean_prod = jnp.mean(grad * x_hat, axis=-1, keepdims=True)
+    return rstd * (grad - mean_grad - x_hat * mean_prod)
+
+
+def pair_mask_block(length, first_row, rows, n, lanes):
+    shape = (rows, n, lanes)
+    i = lax.broadcasted_iota(jnp.int32, shape, 0) + first_row
+    j = lax.broadcasted_iota(jnp.int32, shape, 1)
+    inside = jnp.where((i < length) & (j < length), 1.0, 0.0)
+    return inside.reshape(rows * n, lanes)
+
+
+def project(x, mask, u, w, b, gain, shift):
+    c = x.shape[1]
+    x_hat, rstd = norm_parts(x)
+    normed = (x_hat * gain[u : u + 1, :c] + shift[u : u + 1, :c]).astype(BF16)
+    pre = dot(normed, w[u]) + b[u : u + 1, :]
+    h = (pre.shape[1] - c) // 4
+    s_left = sigmoid(pre[:, h : 2 * h]) * mask
+    s_right = sigmoid(pre[:, 3 * h : 4 * h]) * mask
+    left = s_left * pre[:, :h]
+    right = s_right * pre[:, 2 * h : 3 * h]
+    gate = sigmoid(pre[:, 4 * h :])
+    return x_hat, rstd, normed, s_left, s_right, left, right, gate
+
+
+def mix(product, u, c, gain, shift, w_out, b_out):
+    p_hat, p_rstd = norm_parts(product.astype(F32))
+    mixed = (p_hat * gain[u : u + 1, c:] + shift[u : u + 1, c:]).astype(BF16)
+    branch = dot(mixed, w_out[u]) + b_out[u : u + 1, :]
+    return p_hat, p_rstd, mixed, branch
+
+
+def unmix(up, gate, branch, p_hat, p_rstd, u, c, gain, w_out):
+    d_branch = up * gate
+    d_gate = (d_branch * branch * (1.0 - gate)).astype(BF16)
+    d_branch = d_branch.astype(BF16)
+    d_mixed = dot(d_branch, w_out[u], ((1,), (1,))) * gain[u : u + 1, c:]
+    return d_branch, d_gate, norm_vjp(p_hat, p_rstd, d_mixed)
+
+
+def contract(n, first, row_of, x, y):
+    lanes = y.shape[1]
+    tiles = (n // 8, 8, lanes)
+
+    def step(e, totals):
+        block = y[pl.ds(pl.multiple_of(e * n, n), n), :].reshape(tiles)
+        return tuple(
+            totals[a] + x[pl.ds(row_of(first + a, e), 8, stride=0), :][None] * block
+            for a in range(BLOCK_ROWS)
+        )
+
+    zero = jnp.zeros(tiles, F32)
+    totals = lax.fori_loop(0, n, step, (zero,) * BLOCK_ROWS, unroll=4)
+    return jnp.stack(totals).reshape(BLOCK_ROWS * n, lanes)
+
+
+def edge_grads(d_left, d_right, s_left, s_right, left, right):
+    return (
+        (d_left * s_left).astype(BF16),
+        (d_left * left * (1.0 - s_left)).astype(BF16),
+        (d_right * s_right).astype(BF16),
+        (d_right * right * (1.0 - s_right)).astype(BF16),
+    )
+
+
+def crop_length(state_ref, cells):
+    return jnp.max(state_ref[:, cells:, :].astype(F32)).astype(jnp.int32)
+
+
+def joined(ref, first, count, cells):
+    return jnp.concatenate([ref[first + q, :cells, :] for q in range(count)], axis=0)
+
+
+def forward(n, state_ref, w, b, gain, shift, w_out, b_out, *refs):
+    kept, (right_t_s, next_s) = (refs[:KEPT], refs[KEPT : 2 * KEPT]), refs[2 * KEPT :]
+    parts, _, c = state_ref.shape
+    rows = n // parts
+    cells = rows * n
+    length = crop_length(state_ref, cells)
+    per = BLOCK_ROWS // rows
+    blocks = n // BLOCK_ROWS
+
+    for u in range(2):
+        (left_s, right_s, s_left_s, s_right_s, gate_s, hat_s, rstd_s) = kept[u][:7]
+        (p_hat_s, p_rstd_s, branch_s, normed_s, mixed_s) = kept[u][7:]
+
+        @pl.loop(0, blocks)
+        def _(t):
+            first = t * BLOCK_ROWS
+            here = pl.ds(pl.multiple_of(first * n, BLOCK_ROWS * n), BLOCK_ROWS * n)
+            x = joined(state_ref, t * per, per, cells) if u == 0 else next_s[here, :]
+            mask = pair_mask_block(length, first, BLOCK_ROWS, n, c)
+            x_hat, rstd, normed, s_left, s_right, left, right, gate = project(
+                x.astype(F32), mask, u, w, b, gain, shift
+            )
+            left_s[here, :] = left
+            right_s[here, :] = right
+            s_left_s[here, :] = s_left
+            s_right_s[here, :] = s_right
+            gate_s[here, :] = gate
+            hat_s[here, :] = x_hat
+            rstd_s[here, :] = jnp.broadcast_to(rstd, x_hat.shape)
+            normed_s[here, :] = normed
+            if u == 0:
+                for r in range(BLOCK_ROWS):
+                    right_t_s[pl.ds(first + r, n, stride=n), :] = right[r * n : (r + 1) * n]
+
+        @pl.loop(0, blocks)
+        def _(t):
+            first = t * BLOCK_ROWS
+            here = pl.ds(pl.multiple_of(first * n, BLOCK_ROWS * n), BLOCK_ROWS * n)
+            if u == 0:
+                product = contract(n, first, lambda i, k: i * n + k, left_s, right_t_s)
+            else:
+                product = contract(n, first, lambda i, k: k * n + i, left_s, right_s)
+            p_hat, p_rstd, mixed, branch = mix(
+                product.astype(BF16), u, c, gain, shift, w_out, b_out
+            )
+            p_hat_s[here, :] = p_hat
+            p_rstd_s[here, :] = jnp.broadcast_to(p_rstd, p_hat.shape)
+            mixed_s[here, :] = mixed
+            branch_s[here, :] = branch
+            if u == 0:
+                x = joined(state_ref, t * per, per, cells).astype(F32)
+                next_s[here, :] = (x + gate_s[here, :] * branch).astype(BF16)
+
+
+def weight_grads(normed_s, d_pre_s, mixed_s, d_branch_s, grads_ref):
+    width = d_pre_s.shape[1]
+    grads_ref[:, :width] = dot(normed_s[...], d_pre_s[...], ((0,), (0,))).astype(BF16)
+    grads_ref[:, width:] = dot(mixed_s[...], d_branch_s[...], ((0,), (0,))).astype(BF16)
+
+
+def backward(n, u, *refs):
+    if u == 0:
+        index_ref, refs = refs[0], refs[1:]
+    up_in_ref, w, gain, w_out = refs[:4]
+    (left_s, right_s, s_left_s, s_right_s, gate_s, hat_s, rstd_s) = refs[4:11]
+    (p_hat_s, p_rstd_s, branch_s, normed_s, mixed_s) = refs[11 : 4 + KEPT]
+    up_ref, grads_ref, d_product_s, d_branch_s, d_pre_s = refs[4 + KEPT : 9 + KEPT]
+    c, h = w.shape[1], left_s.shape[1]
+    blocks = n // BLOCK_ROWS
+
+    def upstream(t, here):
+        if u == 0:
+            return up_in_ref[here, :]
+        rows = n // up_in_ref.shape[0]
+        per = BLOCK_ROWS // rows
+        return joined(up_in_ref, t * per, per, rows * n).astype(F32)
+
+    def input_pullback(here, up):
+        d_normed = dot(d_pre_s[here, :], w[u], ((1,), (1,))) * gain[u : u + 1, :c]
+        return up + norm_vjp(hat_s[here, :], rstd_s[here, :], d_normed)
+
+    @pl.loop(0, blocks)
+    def _(t):
+        first = t * BLOCK_ROWS
+        here = pl.ds(pl.multiple_of(first * n, BLOCK_ROWS * n), BLOCK_ROWS * n)
+        d_branch, d_gate, d_product = unmix(
+            upstream(t, here),
+            gate_s[here, :],
+            branch_s[here, :],
+            p_hat_s[here, :],
+            p_rstd_s[here, :],
+            u,
+            c,
+            gain,
+            w_out,
+        )
+        d_branch_s[here, :] = d_branch
+        d_pre_s[here, 4 * h :] = d_gate
+        d_product_s[here, :] = d_product
+        if u == 1:
+            d_product_t_s = refs[9 + KEPT]
+            for r in range(BLOCK_ROWS):
+                d_product_t_s[pl.ds(first + r, n, stride=n), :] = d_product[r * n : (r + 1) * n]
+
+    @pl.loop(0, blocks)
+    def _(t):
+        first = t * BLOCK_ROWS
+        here = pl.ds(pl.multiple_of(first * n, BLOCK_ROWS * n), BLOCK_ROWS * n)
+        if u == 1:
+            d_left = contract(n, first, lambda k, j: k * n + j, right_s, refs[9 + KEPT])
+            d_right = contract(n, first, lambda k, i: k * n + i, left_s, d_product_s)
+        else:
+            d_left = contract(n, first, lambda i, j: i * n + j, d_product_s, right_s)
+            d_right = contract(n, first, lambda j, i: i * n + j, d_product_s, left_s)
+        grads = edge_grads(
+            d_left, d_right, s_left_s[here, :], s_right_s[here, :], left_s[here, :], right_s[here, :]
+        )
+        for g in range(4):
+            d_pre_s[here, g * h : (g + 1) * h] = grads[g]
+        if u == 1:
+            up_ref[here, :] = input_pullback(here, upstream(t, here))
+
+    if u == 0:
+        cells = up_ref.shape[0]
+        own = pl.ds(pl.multiple_of(index_ref[0] * cells, cells), cells)
+        up_ref[...] = input_pullback(own, up_in_ref[own, :]).astype(BF16)
+    weight_grads(normed_s, d_pre_s, mixed_s, d_branch_s, grads_ref)
+
+
+def exchange(value, axis, size, step):
+    return lax.ppermute(value, axis, [(d, d ^ step) for d in range(size)])
+
+
+def add_narrow(a, b):
+    return (a.astype(F32) + b.astype(F32)).astype(BF16)
+
+
+def prepare(state_ref, mask_ref, cot_ref, sent_ref, sent_cot_ref, state_s, mask_s, cot_s, sems):
+    parts, _, c = sent_ref.shape
+    cells = state_s.shape[0]
+    copies = [
+        pltpu.make_async_copy(*pair, sems.at[k])
+        for k, pair in enumerate(((mask_ref, mask_s), (state_ref, state_s), (cot_ref, cot_s)))
+    ]
+    for copy in copies:
+        copy.start()
+    copies[0].wait()
+    length = jnp.max(jnp.sum(mask_s[...].astype(F32), axis=1, keepdims=True))
+    below = jnp.full((sent_ref.shape[1] - cells, c), length, F32).astype(BF16)
+    for copy in copies[1:]:
+        copy.wait()
+    for part in range(parts):
+        sent_ref[part, :cells, :] = state_s[...]
+        sent_ref[part, cells:, :] = below
+        sent_cot_ref[part] = cot_s[...]
+
+
+def add_grads(own_0, other_0, own_1, other_1, proj_ref, out_ref):
+    width = proj_ref.shape[2]
+    for u, (own, other) in enumerate(((own_0, other_0), (own_1, other_1))):
+        total = own[...].astype(F32) + other[...].astype(F32)
+        proj_ref[u] = total[:, :width]
+        out_ref[u] = total[:, width:]
+
+
+def crop_shards(
+    groups,
+    parts,
+    pair_repr,
+    pair_mask,
+    cotangent,
+    proj_weight,
+    proj_bias,
+    norm_gain,
+    norm_shift,
+    out_weight,
+    out_bias,
+):
+    _, rows, n, c = pair_repr.shape
+    h = out_weight.shape[1]
+    width = proj_weight.shape[2]
+    cells, pairs = rows * n, n * n
+    plane = jax.ShapeDtypeStruct((pairs + 8, h), F32)
+    narrow = jax.ShapeDtypeStruct((pairs, h), BF16)
+    grads = jax.ShapeDtypeStruct((c, width + c), BF16)
+    kept = (plane,) * 10 + (narrow,) * 2
+    vmem = pl.BlockSpec(memory_space=pltpu.VMEM)
+    smem = pl.BlockSpec(memory_space=pltpu.SMEM)
+    main = pl.BlockSpec(memory_space=pltpu.HBM)
+    params = pltpu.CompilerParams(vmem_limit_bytes=VMEM_BYTES)
+
+    def scratch(array):
+        return pltpu.VMEM(array.shape, array.dtype)
+
+    def cost(planes):
+        flops = 4 * pairs * width * c
+        return pl.CostEstimate(
+            flops=flops, bytes_accessed=planes * pairs * c * 4, transcendentals=0
+        )
+
+    index = lax.axis_index("dap").astype(jnp.int32)[None]
+    sent, sent_cot = pl.pallas_call(
+        prepare,
+        out_shape=(
+            jax.ShapeDtypeStruct((parts, cells + 16, c), BF16),
+            jax.ShapeDtypeStruct((parts, cells, c), BF16),
+        ),
+        in_specs=[main] * 3,
+        out_specs=(vmem, vmem),
+        scratch_shapes=[
+            pltpu.VMEM((cells, c), BF16),
+            pltpu.VMEM((rows, n), jnp.int32),
+            pltpu.VMEM((cells, c), BF16),
+            pltpu.SemaphoreType.DMA((3,)),
+        ],
+        compiler_params=pltpu.CompilerParams(vmem_limit_bytes=PREPARE_BYTES),
+        name="prepare",
+    )(pair_repr.reshape(cells, c), pair_mask[0], cotangent.reshape(cells, c))
+    state = lax.all_to_all(sent, "dap", split_axis=0, concat_axis=0, tiled=True)
+    cot = lax.all_to_all(sent_cot, "dap", split_axis=0, concat_axis=0, tiled=True)
+
+    held = pl.pallas_call(
+        functools.partial(forward, n),
+        out_shape=kept * 2,
+        in_specs=[vmem] * 7,
+        out_specs=(vmem,) * (2 * KEPT),
+        scratch_shapes=[scratch(plane), scratch(narrow)],
+        compiler_params=params,
+        cost_estimate=cost(64),
+        name="forward",
+    )(state, proj_weight, proj_bias, norm_gain, norm_shift, out_weight, out_bias)
+
+    up_1, grads_1 = pl.pallas_call(
+        functools.partial(backward, n, 1),
+        out_shape=(jax.ShapeDtypeStruct((pairs, c), F32), grads),
+        in_specs=[vmem] * (4 + KEPT),
+        out_specs=(vmem, vmem),
+        scratch_shapes=[scratch(plane), scratch(narrow), pltpu.VMEM((pairs, width), BF16)]
+        + [scratch(plane)],
+        compiler_params=params,
+        cost_estimate=cost(48),
+        name="backward_second",
+    )(cot, proj_weight, norm_gain, out_weight, *held[KEPT:])
+    far = groups // 2
+    others_1 = exchange(grads_1, "dp", groups, far)
+
+    pair_grad, grads_0 = pl.pallas_call(
+        functools.partial(backward, n, 0),
+        out_shape=(jax.ShapeDtypeStruct((cells, c), BF16), grads),
+        in_specs=[smem] + [vmem] * (4 + KEPT),
+        out_specs=(vmem, vmem),
+        scratch_shapes=[scratch(plane), scratch(narrow), pltpu.VMEM((pairs, width), BF16)],
+        compiler_params=params,
+        cost_estimate=cost(48),
+        name="backward_first",
+    )(index, up_1, proj_weight, norm_gain, out_weight, *held[:KEPT])
+
+    step = 1
+    while step < far:
+        near_1 = add_narrow(grads_1, others_1)
+        others_1 = exchange(near_1, "dp", groups, step)
+        others_0 = exchange(grads_0, "dp", groups, step)
+        grads_1, grads_0 = near_1, add_narrow(grads_0, others_0)
+        step *= 2
+    others_0 = exchange(grads_0, "dp", groups, far)
+
+    proj_total, out_total = pl.pallas_call(
+        add_grads,
+        out_shape=(
+            jax.ShapeDtypeStruct((2, c, width), F32),
+            jax.ShapeDtypeStruct((2, h, c), F32),
+        ),
+        in_specs=[vmem] * 4,
+        out_specs=(vmem, vmem),
+        compiler_params=params,
+        name="add_grads",
+    )(grads_0, others_0, grads_1, others_1)
+    return pair_grad.reshape(pair_repr.shape), proj_total, out_total
 
 
 def layer_norm(values, gain_vec, shift_vec, norm_axis):
@@ -153,11 +534,10 @@
         grad_product = norm_pullback(
             product.astype(jnp.float32), gain_out, shift_out, 0, grad_mixed
         ).astype(jnp.bfloat16)
-        column_edges, column_stack = (
-            lax.all_to_all(pair_edges, "dap", split_axis=1, concat_axis=2, tiled=True),
-            lax.all_to_all(grad_product[None], "dap", split_axis=1, concat_axis=2, tiled=True),
-        )
-        column_grad = column_stack[0]
+        column_edges = spread
+        column_grad = lax.all_to_all(
+            grad_product[None], "dap", split_axis=1, concat_axis=2, tiled=True
+        )[0]
         grad_pair = lax.all_to_all(
             triangle_pullback(column_edges, column_grad, update == 0),
             "dap",
@@ -198,10 +578,23 @@
         P(),
         P(),
     )
-    return jax.shard_map(
-        shards,
-        mesh=mesh,
-        in_specs=placed,
-        out_specs=(P("dp", "dap", None, None), P(), P()),
-        check_vma=False,
-    )
+    groups, parts = mesh.shape["dp"], mesh.shape["dap"]
+
+    def program(*args):
+        n, c = args[0].shape[2:]
+        rows = n // parts
+        fits = 20 * n * n * c * 4 <= CROP_BUDGET
+        even = args[7].shape[1] == c and groups > 1 and groups & (groups - 1) == 0 and BLOCK_ROWS % rows == 0 and n % 16 == 0
+        body = functools.partial(crop_shards, groups, parts) if fits and even else shards
+        return spread_over(body)(*args)
+
+    def spread_over(body):
+        return jax.shard_map(
+            body,
+            mesh=mesh,
+            in_specs=placed,
+            out_specs=(P("dp", "dap", None, None), P(), P()),
+            check_vma=False,
+        )
+
+    return program

time: 256 us -> 94.7 us (0.37)
  waiting for transfers between devices: 176 us -> 6.3 us
  starting transfers between devices: 30.9 us -> 6.22 us
  Pallas kernels: 0 us -> 23.5 us
  local copies, waits for them, and re-layouts: 18 us -> 37.8 us
  blocking collectives: 0 us -> 17.6 us
  between operations: 14.8 us -> 0.79 us
  matrix products: 8.59 us -> 0 us
  other arithmetic: 5.99 us -> 1.04 us
    psum x1 -> x0, waiting for transfers between devices: 126 us -> none  [shards(): proj_total, out_total = lax.psum((proj_total, out_total), ('dp', 'dap'))]
    all_to_all x8 -> x1, waiting for transfers between devices: 50.1 us -> 0.01 us  [crop_shards(): lax.all_to_all(sent_cot, 'dap', split_axis=0, concat_axis=0, tiled=True)]
    all_to_all x8 -> x1, starting transfers between devices: 30.8 us -> 3.55 us  [crop_shards(): lax.all_to_all(sent_cot, 'dap', split_axis=0, concat_axis=0, tiled=True)]
    unnamed x38 -> x96, local copies, waits for them, and re-layouts: 14.3 us -> 37.8 us
    pallas_call x0 -> x5, Pallas kernels: none -> 23.5 us  [the longest x1 9.15 us: crop_shards(): pl.pallas_call(functools.partial(forward, n), out_shape=kept * 2, in_spec...]
    all_to_all x0 -> x1, blocking collectives: none -> 17.6 us  [crop_shards(): state = lax.all_to_all(sent, 'dap', split_axis=0, concat_axis=0, tiled=True)]
    dot_general x24 -> x0, matrix products: 8.59 us -> none  [the longest x2 2.08 us: shards(): jnp.einsum('rnc,cd->rnd', normed, w_gate, preferred_element_type=jnp.floa...]
    ppermute x0 -> x4, waiting for transfers between devices: none -> 6.3 us  [exchange(): return lax.ppermute(value, axis, [(d, d ^ step) for d in range(size)])]
  transfers between devices with their start and end apart: 9 -> 5, of which waited for: 9 -> 2; matrix products, arithmetic and copies ran while one was open for 2% -> 1% of each run, Pallas kernels for 0% -> 15%
where the time goes in v3:
time: 94.7 us; the launch traced here: 93.3 us
  local copies, waits for them, and re-layouts  37.8 us (40%)
  Pallas kernels  23.5 us (25%)
  blocking collectives  17.6 us (19%)
  waiting for transfers between devices  6.3 us (7%)
  starting transfers between devices  6.22 us (7%)
  other arithmetic  1.04 us (1%)
    unnamed x96, local copies, waits for them, and re-layouts  37.8 us
    all_to_all x1, blocking collectives, crop_shards(): state = lax.all_to_all(sent, 'dap', split_axis=0, concat_axis=0, tiled=True)  17.6 us
    pallas_call x1, Pallas kernels, crop_shards(): pl.pallas_call(functools.partial(forward, n), out_shape=kept * 2, in_spec...  9.15 us
    pallas_call x1, Pallas kernels, crop_shards(): pl.pallas_call(functools.partial(backward, n, 1), out_shape=(jax.ShapeDty...  6.37 us
    ppermute x4, waiting for transfers between devices, exchange(): return lax.ppermute(value, axis, [(d, d ^ step) for d in range(size)])  6.3 us
    pallas_call x1, Pallas kernels, crop_shards(): pl.pallas_call(functools.partial(backward, n, 0), out_shape=(jax.ShapeDty...  5.3 us
    all_to_all x1, starting transfers between devices, crop_shards(): lax.all_to_all(sent_cot, 'dap', split_axis=0, concat_axis=0, tiled=True)  3.55 us
    ppermute x4, starting transfers between devices, exchange(): return lax.ppermute(value, axis, [(d, d ^ step) for d in range(size)])  2.67 us
  transfers between devices with their start and end apart: 5, of which 2 were waited for; matrix products, arithmetic and copies ran while one was open for 1% of the time, Pallas kernels for 15%

profile of v3, /device:TPU:0, one launch (start us, length us, event | category | flops | bytes accessed | tf_op | source)
XLA Modules:
  0.0 93.3 jit_solution(8942455124920095855)
XLA Ops:
  0.6 1.7 %prepare.1 = (bf16[8,144,128]{2,1,0:T(8,128)(2,1)}, bf16[8,128,128]{2,1,0:T(8,128)(2,1)}) custom-call(bf16[128,128]{1,0:T(8,128)(2,1)} %bitcast.5, s32[4,32]{1,0:T(4,128)} %bitcast.7, bf16[128,128]{1,0:T(8,128)(2,1)} %bitcast.6), custom_call_target="tpu_custom_call" | custom-call | tf_op jit(solution)/shard_map/prepare/pallas_call | solution.py:311
  2.3 17.6 %all_to_all.10.state_ref = bf16[8,144,128]{2,1,0:T(8,128)(2,1)S(1)} all-to-all(bf16[8,144,128]{2,1,0:T(8,128)(2,1)} %get-tuple-element.36), channel_id=1, replica_groups=mesh['dp'=4,'dap'=8] {'dap'}, dimensions={0} | all-to-all | bytes 589824 | tf_op jit(solution)/shard_map/all_to_all | solution.py:328
  20.0 0.0 copy-start.47
  20.0 3.6 %all-to-all-start = ((bf16[8,128,128]{2,1,0:T(8,128)(2,1)}), bf16[8,128,128]{2,1,0:T(8,128)(2,1)S(1)}, u32[]{:S(2)}, u32[]{:S(2)}) async-start(bf16[8,128,128]{2,1,0:T(8,128)(2,1)} %get-tuple-element.35), calls=%async_computation | async-start | bytes 524288 | tf_op jit(solution)/shard_map/all_to_all | solution.py:329
  23.6 0.0 copy-done
  23.6 0.0 copy-done.44
  23.6 0.0 copy-start.33
  23.6 0.8 copy-done.33
  24.4 9.1 %forward.1 = (f32[1032,128]{1,0:T(8,128)S(1)}, f32[1032,128]{1,0:T(8,128)S(1)}, f32[1032,128]{1,0:T(8,128)S(1)}, f32[1032,128]{1,0:T(8,128)S(1)}, f32[1032,128]{...) custom-call(bf16[8,144,128]{2,1,0:T(8,128)(2,1)S(1)} %all_to_all.10., ...), custom_call_target="tpu_custom_call" | custom-call | flops 335544320 | bytes 33554432 | tf_op jit(solution)/shard_map/forward/pallas_call | solution.py:331
  33.6 0.8 copy-done.1
  34.4 0.8 copy-done.3
  35.2 0.8 copy-done.5
  36.0 0.8 copy-done.7
  36.8 0.8 copy-done.9
  37.6 0.8 copy-done.11
  38.4 0.8 copy-done.13
  39.2 0.8 copy-done.15
  40.0 0.8 copy-done.17
  40.8 0.8 copy-done.19
  41.6 0.8 copy-done.21
  42.4 0.8 copy-done.23
  43.2 0.8 copy-done.25
  44.0 0.8 copy-done.27
  44.8 0.8 copy-done.29
  45.7 0.7 copy-done.36
  46.4 0.7 copy-done.38
  47.1 0.7 copy-done.40
  47.8 0.7 copy-done.42
  48.5 0.0 all-to-all-done.refs_0_
  48.5 1.0 %copy-done.12 = f32[1032,128]{1,0:T(8,128)S(1)} copy-done((f32[1032,128]{1,0:T(8,128)S(1)}, f32[1032,128]{1,0:T(8,128)}, u32[]{:S(2)}) %copy-start.12) | copy-done | bytes 528408
  49.5 1.0 %copy-done.14 = f32[1032,128]{1,0:T(8,128)S(1)} copy-done((f32[1032,128]{1,0:T(8,128)S(1)}, f32[1032,128]{1,0:T(8,128)}, u32[]{:S(2)}) %copy-start.14) | copy-done | bytes 528408
  50.6 1.0 %copy-done.16 = f32[1032,128]{1,0:T(8,128)S(1)} copy-done((f32[1032,128]{1,0:T(8,128)S(1)}, f32[1032,128]{1,0:T(8,128)}, u32[]{:S(2)}) %copy-start.16) | copy-done | bytes 528408
  51.6 1.0 %copy-done.18 = f32[1032,128]{1,0:T(8,128)S(1)} copy-done((f32[1032,128]{1,0:T(8,128)S(1)}, f32[1032,128]{1,0:T(8,128)}, u32[]{:S(2)}) %copy-start.18) | copy-done | bytes 528408
  52.7 1.0 %copy-done.20 = f32[1032,128]{1,0:T(8,128)S(1)} copy-done((f32[1032,128]{1,0:T(8,128)S(1)}, f32[1032,128]{1,0:T(8,128)}, u32[]{:S(2)}) %copy-start.20) | copy-done | bytes 528408
  53.7 1.0 %copy-done.22 = f32[1032,128]{1,0:T(8,128)S(1)} copy-done((f32[1032,128]{1,0:T(8,128)S(1)}, f32[1032,128]{1,0:T(8,128)}, u32[]{:S(2)}) %copy-start.22) | copy-done | bytes 528408
  54.8 1.0 %copy-done.24 = f32[1032,128]{1,0:T(8,128)S(1)} copy-done((f32[1032,128]{1,0:T(8,128)S(1)}, f32[1032,128]{1,0:T(8,128)}, u32[]{:S(2)}) %copy-start.24) | copy-done | bytes 528408
  55.8 1.0 %copy-done.26 = f32[1032,128]{1,0:T(8,128)S(1)} copy-done((f32[1032,128]{1,0:T(8,128)S(1)}, f32[1032,128]{1,0:T(8,128)}, u32[]{:S(2)}) %copy-start.26) | copy-done | bytes 528408
  56.9 1.0 %copy-done.28 = f32[1032,128]{1,0:T(8,128)S(1)} copy-done((f32[1032,128]{1,0:T(8,128)S(1)}, f32[1032,128]{1,0:T(8,128)}, u32[]{:S(2)}) %copy-start.28) | copy-done | bytes 528408
  57.9 1.0 %copy-done.30 = f32[1032,128]{1,0:T(8,128)S(1)} copy-done((f32[1032,128]{1,0:T(8,128)S(1)}, f32[1032,128]{1,0:T(8,128)}, u32[]{:S(2)}) %copy-start.30) | copy-done | bytes 528408
  58.9 0.8 copy-done.34
  59.8 0.9 %copy-done.41 = bf16[1024,128]{1,0:T(8,128)(2,1)S(1)} copy-done((bf16[1024,128]{1,0:T(8,128)(2,1)S(1)}, bf16[1024,128]{1,0:T(8,128)(2,1)}, u32[]{:S(2)}) %copy-start.41) | copy-done | bytes 262168
  60.7 0.9 %copy-done.43 = bf16[1024,128]{1,0:T(8,128)(2,1)S(1)} copy-done((bf16[1024,128]{1,0:T(8,128)(2,1)S(1)}, bf16[1024,128]{1,0:T(8,128)(2,1)}, u32[]{:S(2)}) %copy-start.43) | copy-done | bytes 262168
  61.7 6.4 %backward_second.1 = (f32[1024,128]{1,0:T(8,128)S(1)}, bf16[128,768]{1,0:T(8,128)(2,1)S(1)}) custom-call(bf16[8,128,128]{2,1,0:T(8,128)(2,1)S(1)} %all-to-all-done.refs_0_, bf16[2,128,640]{2,1,0:T(8,128)(2,1)S(1)} %copy-done, f32[2,256]{1,0:T(2,128)S(1)} %copy-done.44, bf16[2,128,128]{2,1,0:T(8,128)(2,1)S(1)} %copy-done.34, f32[1032,128]{1,0:T(8,128)S(1)} %copy-done.12, ...), custom_call_target="tpu_custom_call" | custom-call | flops 335544320 | bytes 25165824 | tf_op jit(solution)/shard_map/backward_second/pallas_call | solution.py:342
  68.1 0.0 copy-start.31
  68.1 0.8 copy-done.31
  68.9 1.5 %collective-permute-start.2 = (bf16[128,768]{1,0:T(8,128)(2,1)S(1)}, bf16[128,768]{1,0:T(8,128)(2,1)}, u32[]{:S(2)}, u32[]{:S(2)}) collective-permute-start(bf16[128,768]{1,0:T(8,128)(2,1)S(1)} %get-tuple-element.64), channel_id=1, source_target_pairs={{0,16},{8,24},{16,0},{24,8},{1,17},{9,25},{17,1},{25,9},{2,18},{10... | collective-permute-start | bytes 589832 | tf_op jit(solution)/shard_map/ppermute | solution.py:240
  70.3 1.0 %copy-done.2 = f32[1032,128]{1,0:T(8,128)S(1)} copy-done((f32[1032,128]{1,0:T(8,128)S(1)}, f32[1032,128]{1,0:T(8,128)}, u32[]{:S(2)}) %copy-start.2) | copy-done | bytes 528408
  71.4 1.0 %copy-done.4 = f32[1032,128]{1,0:T(8,128)S(1)} copy-done((f32[1032,128]{1,0:T(8,128)S(1)}, f32[1032,128]{1,0:T(8,128)}, u32[]{:S(2)}) %copy-start.4) | copy-done | bytes 528408
  72.4 1.0 %copy-done.6 = f32[1032,128]{1,0:T(8,128)S(1)} copy-done((f32[1032,128]{1,0:T(8,128)S(1)}, f32[1032,128]{1,0:T(8,128)}, u32[]{:S(2)}) %copy-start.6) | copy-done | bytes 528408
  73.5 1.0 %copy-done.8 = f32[1032,128]{1,0:T(8,128)S(1)} copy-done((f32[1032,128]{1,0:T(8,128)S(1)}, f32[1032,128]{1,0:T(8,128)}, u32[]{:S(2)}) %copy-start.8) | copy-done | bytes 528408
  74.5 1.0 %copy-done.10 = f32[1032,128]{1,0:T(8,128)S(1)} copy-done((f32[1032,128]{1,0:T(8,128)S(1)}, f32[1032,128]{1,0:T(8,128)}, u32[]{:S(2)}) %copy-start.10) | copy-done | bytes 528408
  75.6 1.0 %copy-done.32 = f32[1024,128]{1,0:T(8,128)S(1)} copy-done((f32[1024,128]{1,0:T(8,128)S(1)}, f32[1024,128]{1,0:T(8,128)}, u32[]{:S(2)}) %copy-start.32) | copy-done | bytes 524312
  76.6 0.9 %copy-done.37 = bf16[1024,128]{1,0:T(8,128)(2,1)S(1)} copy-done((bf16[1024,128]{1,0:T(8,128)(2,1)S(1)}, bf16[1024,128]{1,0:T(8,128)(2,1)}, u32[]{:S(2)}) %copy-start.37) | copy-done | bytes 262168
  77.6 0.9 %copy-done.39 = bf16[1024,128]{1,0:T(8,128)(2,1)S(1)} copy-done((bf16[1024,128]{1,0:T(8,128)(2,1)S(1)}, bf16[1024,128]{1,0:T(8,128)(2,1)}, u32[]{:S(2)}) %copy-start.39) | copy-done | bytes 262168
  78.5 5.3 %backward_first.1 = (bf16[128,128]{1,0:T(8,128)(2,1)}, bf16[128,768]{1,0:T(8,128)(2,1)S(1)}) custom-call(s32[1]{0:T(128)} %bitcast.refs_0_, f32[1024,128]{1,0:T(8,128)S(1)} %copy-done.32, bf16[2,128,640]{2,1,0:T(8,128)(2,1)S(1)} %copy-done, f32[2,256]{1,0:T(2,128)S(1)} %copy-done.44, bf16[2,128,128]{2,1,0:T(8,128)(2,1)S(1)} %copy-done.35, ...), custom_call_target="tpu_custom_call" | custom-call | flops 335544320 | bytes 25165824 | tf_op jit(solution)/shard_map/backward_first/pallas_call | solution.py:356
  83.8 0.0 collective-permute-start
  83.8 0.0 collective-permute-done.2
  83.8 1.0 %add_convert_fusion.own_1 = bf16[128,768]{1,0:T(8,128)(2,1)S(1)} fusion(bf16[128,768]{1,0:T(8,128)(2,1)} %collective-permute-done.2, bf16[128,768]{1,0:T(8,128)(2,1)S(1)} %get-tuple-element.64), kind=kLoop, calls=%fused_computation | loop fusion | flops 393216 | bytes 589824 | tf_op jit(solution)/shard_map/convert_element_type | solution.py:244
  84.8 0.6 collective-permute-start.3
  85.4 0.0 collective-permute-done
  85.4 0.6 collective-permute-start.1
  86.0 0.4 collective-permute-done.3.other_1
  86.5 5.9 %collective-permute-done.1.other_0 = bf16[128,768]{1,0:T(8,128)(2,1)S(1)} collective-permute-done((bf16[128,768]{1,0:T(8,128)(2,1)S(1)}, bf16[128,768]{1,0:T(8,128)(2,1)S(1)}, u32[]{:S(2)}, u32[]{:S(2)}) %collective-permute-start.1) | collective-permute-done | bytes 196640 | tf_op jit(solution)/shard_map/ppermute | solution.py:240
  92.3 0.9 %add_grads.1 = (f32[2,128,640]{2,1,0:T(8,128)}, f32[2,128,128]{2,1,0:T(8,128)}) custom-call(bf16[128,768]{1,0:T(8,128)(2,1)S(1)} %add_convert_fusion.1.own_0, bf16[128,768]{1,0:T(8,128)(2,1)S(1)} %collective-permute-done.1.other_0, bf16[128,768]{1,0:T(8,128)(2,1)S(1)} %add_convert_fusion.own_1, bf16[128,768]{1,0:T(8,128)(2,1)S(1)} %collective-permute-done.3.other_1), custom_call_target="tpu_custom_call" | custom-call | tf_op jit(solution)/shard_map/add_grads/pallas_call | solution.py:376
  (50 shorter events, 0.1 us)
Async XLA Ops:
  20.0 3.6 %copy-start = (bf16[2,128,640]{2,1,0:T(8,128)(2,1)S(1)}, bf16[2,128,640]{2,1,0:T(8,128)(2,1)}, u32[]{:S(2)}) copy-start(bf16[2,128,640]{2,1,0:T(8,128)(2,1)} %refs_2_.3) | copy-start | bytes 983044
  20.0 3.6 %copy-start.44 = (f32[2,256]{1,0:T(2,128)S(1)}, f32[2,256]{1,0:T(2,128)}, u32[]{:S(2)}) copy-start(f32[2,256]{1,0:T(2,128)} %refs_3_.3) | copy-start | bytes 6148
  20.0 3.6 %copy-start.45 = (f32[2,640]{1,0:T(2,128)S(1)}, f32[2,640]{1,0:T(2,128)}, u32[]{:S(2)}) copy-start(f32[2,640]{1,0:T(2,128)} %b.1) | copy-start | bytes 15364
  20.0 3.6 %copy-start.46 = (f32[2,256]{1,0:T(2,128)S(1)}, f32[2,256]{1,0:T(2,128)}, u32[]{:S(2)}) copy-start(f32[2,256]{1,0:T(2,128)} %shift.1) | copy-start | bytes 6148
  20.0 3.6 %copy-start.47 = (f32[2,128]{1,0:T(2,128)S(1)}, f32[2,128]{1,0:T(2,128)}, u32[]{:S(2)}) copy-start(f32[2,128]{1,0:T(2,128)} %b_out.1) | copy-start | bytes 3076
  20.0 28.5 %all-to-all-start = ((bf16[8,128,128]{2,1,0:T(8,128)(2,1)}), bf16[8,128,128]{2,1,0:T(8,128)(2,1)S(1)}, u32[]{:S(2)}, u32[]{:S(2)}) async-start(bf16[8,128,128]{2,1,0:T(8,128)(2,1)} %get-tuple-element.35), calls=%async_computation | async-start | bytes 524288 | tf_op jit(solution)/shard_map/all_to_all | solution.py:329
  23.6 0.8 copy-start.33
  33.6 0.8 copy-start.1
  34.4 0.8 copy-start.3
  35.2 0.8 copy-start.5
  36.0 0.8 copy-start.7
  36.8 0.8 copy-start.9
  37.6 0.8 copy-start.11
  38.4 0.8 copy-start.13
  39.2 0.8 copy-start.15
  40.0 0.8 copy-start.17
  40.8 0.8 copy-start.19
  41.6 0.8 copy-start.21
  42.4 0.8 copy-start.23
  43.2 0.8 copy-start.25
  44.0 0.8 copy-start.27
  44.8 0.8 copy-start.29
  45.7 0.7 copy-start.36
  46.4 0.7 copy-start.38
  47.1 0.7 copy-start.40
  47.8 0.7 copy-start.42
  48.5 1.0 %copy-start.12 = (f32[1032,128]{1,0:T(8,128)S(1)}, f32[1032,128]{1,0:T(8,128)}, u32[]{:S(2)}) copy-start(f32[1032,128]{1,0:T(8,128)} %copy-done.11) | copy-start | bytes 1585156
  49.5 1.0 %copy-start.14 = (f32[1032,128]{1,0:T(8,128)S(1)}, f32[1032,128]{1,0:T(8,128)}, u32[]{:S(2)}) copy-start(f32[1032,128]{1,0:T(8,128)} %copy-done.13) | copy-start | bytes 1585156
  50.6 1.0 %copy-start.16 = (f32[1032,128]{1,0:T(8,128)S(1)}, f32[1032,128]{1,0:T(8,128)}, u32[]{:S(2)}) copy-start(f32[1032,128]{1,0:T(8,128)} %copy-done.15) | copy-start | bytes 1585156
  51.6 1.0 %copy-start.18 = (f32[1032,128]{1,0:T(8,128)S(1)}, f32[1032,128]{1,0:T(8,128)}, u32[]{:S(2)}) copy-start(f32[1032,128]{1,0:T(8,128)} %copy-done.17) | copy-start | bytes 1585156
  52.7 1.0 %copy-start.20 = (f32[1032,128]{1,0:T(8,128)S(1)}, f32[1032,128]{1,0:T(8,128)}, u32[]{:S(2)}) copy-start(f32[1032,128]{1,0:T(8,128)} %copy-done.19) | copy-start | bytes 1585156
  53.7 1.0 %copy-start.22 = (f32[1032,128]{1,0:T(8,128)S(1)}, f32[1032,128]{1,0:T(8,128)}, u32[]{:S(2)}) copy-start(f32[1032,128]{1,0:T(8,128)} %copy-done.21) | copy-start | bytes 1585156
  54.8 1.0 %copy-start.24 = (f32[1032,128]{1,0:T(8,128)S(1)}, f32[1032,128]{1,0:T(8,128)}, u32[]{:S(2)}) copy-start(f32[1032,128]{1,0:T(8,128)} %copy-done.23) | copy-start | bytes 1585156
  55.8 1.0 %copy-start.26 = (f32[1032,128]{1,0:T(8,128)S(1)}, f32[1032,128]{1,0:T(8,128)}, u32[]{:S(2)}) copy-start(f32[1032,128]{1,0:T(8,128)} %copy-done.25) | copy-start | bytes 1585156
  56.8 1.0 %copy-start.28 = (f32[1032,128]{1,0:T(8,128)S(1)}, f32[1032,128]{1,0:T(8,128)}, u32[]{:S(2)}) copy-start(f32[1032,128]{1,0:T(8,128)} %copy-done.27) | copy-start | bytes 1585156
  57.9 1.0 %copy-start.30 = (f32[1032,128]{1,0:T(8,128)S(1)}, f32[1032,128]{1,0:T(8,128)}, u32[]{:S(2)}) copy-start(f32[1032,128]{1,0:T(8,128)} %copy-done.29) | copy-start | bytes 1585156
  58.9 0.8 copy-start.34
  59.8 0.9 %copy-start.41 = (bf16[1024,128]{1,0:T(8,128)(2,1)S(1)}, bf16[1024,128]{1,0:T(8,128)(2,1)}, u32[]{:S(2)}) copy-start(bf16[1024,128]{1,0:T(8,128)(2,1)} %copy-done.40) | copy-start | bytes 786436
  60.7 0.9 %copy-start.43 = (bf16[1024,128]{1,0:T(8,128)(2,1)S(1)}, bf16[1024,128]{1,0:T(8,128)(2,1)}, u32[]{:S(2)}) copy-start(bf16[1024,128]{1,0:T(8,128)(2,1)} %copy-done.42) | copy-start | bytes 786436
  61.7 8.7 %copy-start.35 = (bf16[2,128,128]{2,1,0:T(8,128)(2,1)S(1)}, bf16[2,128,128]{2,1,0:T(8,128)(2,1)}, u32[]{:S(2)}) copy-start(bf16[2,128,128]{2,1,0:T(8,128)(2,1)} %refs_4_.1) | copy-start | bytes 196612
  68.1 0.8 copy-start.31
  68.9 15.0 %collective-permute-start.2 = (bf16[128,768]{1,0:T(8,128)(2,1)S(1)}, bf16[128,768]{1,0:T(8,128)(2,1)}, u32[]{:S(2)}, u32[]{:S(2)}) collective-permute-start(bf16[128,768]{1,0:T(8,128)(2,1)S(1)} %get-tuple-element.64), channel_id=1, source_target_pairs={{0,16},{8,24},{16,0},{24,8},{1,17},{9,25},{17,1},{25,9},{2,18},{10... | collective-permute-start | bytes 589832 | tf_op jit(solution)/shard_map/ppermute | solution.py:240
  70.3 1.0 %copy-start.2 = (f32[1032,128]{1,0:T(8,128)S(1)}, f32[1032,128]{1,0:T(8,128)}, u32[]{:S(2)}) copy-start(f32[1032,128]{1,0:T(8,128)} %copy-done.1) | copy-start | bytes 1585156
  71.4 1.0 %copy-start.4 = (f32[1032,128]{1,0:T(8,128)S(1)}, f32[1032,128]{1,0:T(8,128)}, u32[]{:S(2)}) copy-start(f32[1032,128]{1,0:T(8,128)} %copy-done.3) | copy-start | bytes 1585156
  72.4 1.0 %copy-start.6 = (f32[1032,128]{1,0:T(8,128)S(1)}, f32[1032,128]{1,0:T(8,128)}, u32[]{:S(2)}) copy-start(f32[1032,128]{1,0:T(8,128)} %copy-done.5) | copy-start | bytes 1585156
  73.5 1.0 %copy-start.8 = (f32[1032,128]{1,0:T(8,128)S(1)}, f32[1032,128]{1,0:T(8,128)}, u32[]{:S(2)}) copy-start(f32[1032,128]{1,0:T(8,128)} %copy-done.7) | copy-start | bytes 1585156
  74.5 1.0 %copy-start.10 = (f32[1032,128]{1,0:T(8,128)S(1)}, f32[1032,128]{1,0:T(8,128)}, u32[]{:S(2)}) copy-start(f32[1032,128]{1,0:T(8,128)} %copy-done.9) | copy-start | bytes 1585156
  75.6 1.0 %copy-start.32 = (f32[1024,128]{1,0:T(8,128)S(1)}, f32[1024,128]{1,0:T(8,128)}, u32[]{:S(2)}) copy-start(f32[1024,128]{1,0:T(8,128)} %copy-done.31) | copy-start | bytes 1572868
  76.6 0.9 %copy-start.37 = (bf16[1024,128]{1,0:T(8,128)(2,1)S(1)}, bf16[1024,128]{1,0:T(8,128)(2,1)}, u32[]{:S(2)}) copy-start(bf16[1024,128]{1,0:T(8,128)(2,1)} %copy-done.36) | copy-start | bytes 786436
  77.6 0.9 %copy-start.39 = (bf16[1024,128]{1,0:T(8,128)(2,1)S(1)}, bf16[1024,128]{1,0:T(8,128)(2,1)}, u32[]{:S(2)}) copy-start(bf16[1024,128]{1,0:T(8,128)(2,1)} %copy-done.38) | copy-start | bytes 786436
  83.8 1.6 %collective-permute-start = (bf16[128,768]{1,0:T(8,128)(2,1)S(1)}, bf16[128,768]{1,0:T(8,128)(2,1)S(1)}, u32[]{:S(2)}, u32[]{:S(2)}) collective-permute-start(bf16[128,768]{1,0:T(8,128)(2,1)S(1)} %get-tuple-element.63), channel_id=1, source_target_pairs={{0,8},{8,0},{16,24},{24,16},{1,9},{9,1},{17,25},{25,17},{2,10},{10... | collective-permute-start | bytes 589832 | tf_op jit(solution)/shard_map/ppermute | solution.py:240
  84.8 1.6 %collective-permute-start.3 = (bf16[128,768]{1,0:T(8,128)(2,1)S(1)}, bf16[128,768]{1,0:T(8,128)(2,1)S(1)}, u32[]{:S(2)}, u32[]{:S(2)}) collective-permute-start(bf16[128,768]{1,0:T(8,128)(2,1)S(1)} %add_convert_fusion.own_1), channel_id=1, source_target_pairs={{0,8},{8,0},{16,24},{24,16},{1,9},{9,1},{17,25},{25,17},{2,10},{10... | collective-permute-start | bytes 589832 | tf_op jit(solution)/shard_map/ppermute | solution.py:240
  85.4 6.9 %collective-permute-start.1 = (bf16[128,768]{1,0:T(8,128)(2,1)S(1)}, bf16[128,768]{1,0:T(8,128)(2,1)S(1)}, u32[]{:S(2)}, u32[]{:S(2)}) collective-permute-start(bf16[128,768]{1,0:T(8,128)(2,1)S(1)} %add_convert_fusion.1.own_0), channel_id=1, source_target_pairs={{0,16},{8,24},{16,0},{24,8},{1,17},{9,25},{17,1},{25,9},{2,18},{10... | collective-permute-start | bytes 589832 | tf_op jit(solution)/shard_map/ppermute | solution.py:240

commit v4 on v3

--- a/solution.py
+++ b/solution.py
@@ -100,11 +100,12 @@
 
 
 def crop_length(state_ref, cells):
-    return jnp.max(state_ref[:, cells:, :].astype(F32)).astype(jnp.int32)
-
-
-def joined(ref, first, count, cells):
-    return jnp.concatenate([ref[first + q, :cells, :] for q in range(count)], axis=0)
+    return jnp.max(state_ref[:, 2 * cells :, :].astype(F32)).astype(jnp.int32)
+
+
+def joined(ref, first, count, cells, place):
+    span = slice(place * cells, (place + 1) * cells)
+    return jnp.concatenate([ref[first + q, span, :] for q in range(count)], axis=0)
 
 
 def forward(n, state_ref, w, b, gain, shift, w_out, b_out, *refs):
@@ -124,7 +125,7 @@
         def _(t):
             first = t * BLOCK_ROWS
             here = pl.ds(pl.multiple_of(first * n, BLOCK_ROWS * n), BLOCK_ROWS * n)
-            x = joined(state_ref, t * per, per, cells) if u == 0 else next_s[here, :]
+            x = joined(state_ref, t * per, per, cells, 0) if u == 0 else next_s[here, :]
             mask = pair_mask_block(length, first, BLOCK_ROWS, n, c)
             x_hat, rstd, normed, s_left, s_right, left, right, gate = project(
                 x.astype(F32), mask, u, w, b, gain, shift
@@ -157,7 +158,7 @@
             mixed_s[here, :] = mixed
             branch_s[here, :] = branch
             if u == 0:
-                x = joined(state_ref, t * per, per, cells).astype(F32)
+                x = joined(state_ref, t * per, per, cells, 0).astype(F32)
                 next_s[here, :] = (x + gate_s[here, :] * branch).astype(BF16)
 
 
@@ -182,7 +183,7 @@
             return up_in_ref[here, :]
         rows = n // up_in_ref.shape[0]
         per = BLOCK_ROWS // rows
-        return joined(up_in_ref, t * per, per, rows * n).astype(F32)
+        return joined(up_in_ref, t * per, per, rows * n, 1).astype(F32)
 
     def input_pullback(here, up):
         d_normed = dot(d_pre_s[here, :], w[u], ((1,), (1,))) * gain[u : u + 1, :c]
@@ -244,7 +245,7 @@
     return (a.astype(F32) + b.astype(F32)).astype(BF16)
 
 
-def prepare(state_ref, mask_ref, cot_ref, sent_ref, sent_cot_ref, state_s, mask_s, cot_s, sems):
+def prepare(state_ref, mask_ref, cot_ref, sent_ref, state_s, mask_s, cot_s, sems):
     parts, _, c = sent_ref.shape
     cells = state_s.shape[0]
     copies = [
@@ -255,13 +256,13 @@
         copy.start()
     copies[0].wait()
     length = jnp.max(jnp.sum(mask_s[...].astype(F32), axis=1, keepdims=True))
-    below = jnp.full((sent_ref.shape[1] - cells, c), length, F32).astype(BF16)
+    below = jnp.full((sent_ref.shape[1] - 2 * cells, c), length, F32).astype(BF16)
     for copy in copies[1:]:
         copy.wait()
     for part in range(parts):
         sent_ref[part, :cells, :] = state_s[...]
-        sent_ref[part, cells:, :] = below
-        sent_cot_ref[part] = cot_s[...]
+        sent_ref[part, cells : 2 * cells, :] = cot_s[...]
+        sent_ref[part, 2 * cells :, :] = below
 
 
 def add_grads(own_0, other_0, own_1, other_1, proj_ref, out_ref):
@@ -308,14 +309,11 @@
         )
 
     index = lax.axis_index("dap").astype(jnp.int32)[None]
-    sent, sent_cot = pl.pallas_call(
+    sent = pl.pallas_call(
         prepare,
-        out_shape=(
-            jax.ShapeDtypeStruct((parts, cells + 16, c), BF16),
-            jax.ShapeDtypeStruct((parts, cells, c), BF16),
-        ),
+        out_shape=jax.ShapeDtypeStruct((parts, 2 * cells + 16, c), BF16),
         in_specs=[main] * 3,
-        out_specs=(vmem, vmem),
+        out_specs=vmem,
         scratch_shapes=[
             pltpu.VMEM((cells, c), BF16),
             pltpu.VMEM((rows, n), jnp.int32),
@@ -326,7 +324,6 @@
         name="prepare",
     )(pair_repr.reshape(cells, c), pair_mask[0], cotangent.reshape(cells, c))
     state = lax.all_to_all(sent, "dap", split_axis=0, concat_axis=0, tiled=True)
-    cot = lax.all_to_all(sent_cot, "dap", split_axis=0, concat_axis=0, tiled=True)
 
     held = pl.pallas_call(
         functools.partial(forward, n),
@@ -349,7 +346,7 @@
         compiler_params=params,
         cost_estimate=cost(48),
         name="backward_second",
-    )(cot, proj_weight, norm_gain, out_weight, *held[KEPT:])
+    )(state, proj_weight, norm_gain, out_weight, *held[KEPT:])
     far = groups // 2
     others_1 = exchange(grads_1, "dp", groups, far)
 

time: 94.7 us -> 70.3 us (0.74)
  local copies, waits for them, and re-layouts: 37.8 us -> 11.2 us
  blocking collectives: 17.6 us -> 23.4 us
  starting transfers between devices: 6.22 us -> 2.67 us
    unnamed x96 -> x42, local copies, waits for them, and re-layouts: 37.8 us -> 11.2 us
    all_to_all x1, blocking collectives: 17.6 us -> 23.4 us  [crop_shards(): state = lax.all_to_all(sent, 'dap', split_axis=0, concat_axis=0, tiled=True)]
    all_to_all x1 -> x0, starting transfers between devices: 3.55 us -> none  [crop_shards(): lax.all_to_all(sent_cot, 'dap', split_axis=0, concat_axis=0, tiled=True)]
  transfers between devices with their start and end apart: 5 -> 4, of which waited for: 2 -> 2; matrix products, arithmetic and copies ran while one was open for 1% -> 2% of each run, Pallas kernels for 15% -> 8%
where the time goes in v4:
time: 70.3 us; the launch traced here: 69.7 us
  Pallas kernels  24.2 us (34%)
  blocking collectives  23.4 us (33%)
  local copies, waits for them, and re-layouts  11.2 us (16%)
  waiting for transfers between devices  6.3 us (9%)
  starting transfers between devices  2.67 us (4%)
  other arithmetic  1.13 us (2%)
  between operations  0.76 us (1%)
    all_to_all x1, blocking collectives, crop_shards(): state = lax.all_to_all(sent, 'dap', split_axis=0, concat_axis=0, tiled=True)  23.4 us
    unnamed x42, local copies, waits for them, and re-layouts  11.2 us
    pallas_call x1, Pallas kernels, crop_shards(): pl.pallas_call(functools.partial(forward, n), out_shape=kept * 2, in_spec...  9.17 us
    pallas_call x1, Pallas kernels, crop_shards(): pl.pallas_call(functools.partial(backward, n, 1), out_shape=(jax.ShapeDty...  7.06 us
    ppermute x4, waiting for transfers between devices, exchange(): return lax.ppermute(value, axis, [(d, d ^ step) for d in range(size)])  6.3 us
    pallas_call x1, Pallas kernels, crop_shards(): pl.pallas_call(functools.partial(backward, n, 0), out_shape=(jax.ShapeDty...  5.28 us
    ppermute x4, starting transfers between devices, exchange(): return lax.ppermute(value, axis, [(d, d ^ step) for d in range(size)])  2.67 us
    pallas_call x1, Pallas kernels, crop_shards(): pl.pallas_call(prepare, out_shape=jax.ShapeDtypeStruct((parts, 2 * cells...  1.7 us
  transfers between devices with their start and end apart: 4, of which 2 were waited for; matrix products, arithmetic and copies ran while one was open for 2% of the time, Pallas kernels for 8%

profile of v4, /device:TPU:0, one launch (start us, length us, event | category | flops | bytes accessed | tf_op | source)
XLA Modules:
  0.0 69.7 jit_solution(14697915247721295270)
XLA Ops:
  0.6 1.7 %prepare.1 = bf16[8,272,128]{2,1,0:T(8,128)(2,1)} custom-call(bf16[128,128]{1,0:T(8,128)(2,1)} %bitcast.5, s32[4,32]{1,0:T(4,128)} %bitcast.7, bf16[128,128]{1,0:T(8,128)(2,1)} %bitcast.6), custom_call_target="tpu_custom_call" | custom-call | tf_op jit(solution)/shard_map/prepare/pallas_call | solution.py:312
  2.3 0.0 copy-start
  2.4 0.0 copy-start.11
  2.4 0.0 copy-start.17
  2.4 0.0 copy-start.18
  2.4 0.0 copy-start.19
  2.4 0.0 copy-start.20
  2.4 23.4 %all_to_all.5.state_ref.refs_0_ = bf16[8,272,128]{2,1,0:T(8,128)(2,1)S(1)} all-to-all(bf16[8,272,128]{2,1,0:T(8,128)(2,1)} %prepare.1), channel_id=1, replica_groups=mesh['dp'=4,'dap'=8] {'dap'}, dimensions={0} | all-to-all | bytes 1114112 | tf_op jit(solution)/shard_map/all_to_all | solution.py:326
  25.8 0.0 copy-done
  25.8 0.0 copy-done.11
  25.8 0.0 copy-done.17
  25.8 0.0 copy-done.18
  25.9 0.0 copy-done.19
  25.9 0.0 copy-done.20
  25.9 9.2 %forward.1 = (f32[1032,128]{1,0:T(8,128)S(1)}, f32[1032,128]{1,0:T(8,128)S(1)}, f32[1032,128]{1,0:T(8,128)S(1)}, f32[1032,128]{1,0:T(8,128)S(1)}, f32[1032,128]{...) custom-call(bf16[8,272,128]{2,1,0:T(8,128)(2,1)S(1)} %all_to_all.5.s, ...), custom_call_target="tpu_custom_call" | custom-call | flops 335544320 | bytes 33554432 | tf_op jit(solution)/shard_map/forward/pallas_call | solution.py:328
  35.0 0.0 copy-start.3
  35.1 0.8 %copy-done.3 = f32[1032,128]{1,0:T(8,128)} copy-done((f32[1032,128]{1,0:T(8,128)}, f32[1032,128]{1,0:T(8,128)S(1)}, u32[]{:S(2)}) %copy-start.3) | copy-done | bytes 528408
  35.9 0.0 copy-start.5
  35.9 0.8 %copy-done.5 = f32[1032,128]{1,0:T(8,128)} copy-done((f32[1032,128]{1,0:T(8,128)}, f32[1032,128]{1,0:T(8,128)S(1)}, u32[]{:S(2)}) %copy-start.5) | copy-done | bytes 528408
  36.7 0.0 copy-start.7
  36.7 0.8 %copy-done.7 = f32[1032,128]{1,0:T(8,128)} copy-done((f32[1032,128]{1,0:T(8,128)}, f32[1032,128]{1,0:T(8,128)S(1)}, u32[]{:S(2)}) %copy-start.7) | copy-done | bytes 528408
  37.5 0.0 copy-start.1
  37.5 0.0 copy-start.13
  37.5 0.0 copy-start.15
  37.5 7.1 %backward_second.1 = (f32[1024,128]{1,0:T(8,128)S(1)}, bf16[128,768]{1,0:T(8,128)(2,1)}) custom-call(bf16[8,272,128]{2,1,0:T(8,128)(2,1)S(1)} %all_to_all.5.state_ref.refs_0_, bf16[2,128,640]{2,1,0:T(8,128)(2,1)S(1)} %copy-done, f32[2,256]{1,0:T(2,128)S(1)} %copy-done.17, bf16[2,128,128]{2,1,0:T(8,128)(2,1)S(1)} %copy-done.11, ...), custom_call_target="tpu_custom_call" | custom-call | flops 335544320 | bytes 25165824 | tf_op jit(solution)/shard_map/backward_second/pallas_call | solution.py:339
  44.6 0.0 copy-done.1
  44.6 0.0 copy-done.13
  44.6 0.0 copy-done.15
  44.6 0.0 copy-start.9
  44.6 0.8 %copy-done.9 = f32[1024,128]{1,0:T(8,128)} copy-done((f32[1024,128]{1,0:T(8,128)}, f32[1024,128]{1,0:T(8,128)S(1)}, u32[]{:S(2)}) %copy-start.9) | copy-done | bytes 524312
  45.4 1.5 %collective-permute-start.2 = (bf16[128,768]{1,0:T(8,128)(2,1)}, bf16[128,768]{1,0:T(8,128)(2,1)}, u32[]{:S(2)}, u32[]{:S(2)}) collective-permute-start(bf16[128,768]{1,0:T(8,128)(2,1)} %get-tuple-element.60), channel_id=1, source_target_pairs={{0,16},{8,24},{16,0},{24,8},{1,17},{9,25},{17,1},{25,9},{2,18},{10... | collective-permute-start | bytes 589832 | tf_op jit(solution)/shard_map/ppermute | solution.py:241
  46.9 0.0 copy-start.2
  46.9 1.0 %copy-done.2 = f32[1032,128]{1,0:T(8,128)S(1)} copy-done((f32[1032,128]{1,0:T(8,128)S(1)}, f32[1032,128]{1,0:T(8,128)}, u32[]{:S(2)}) %copy-start.2) | copy-done | bytes 528408
  47.9 0.0 copy-start.4
  47.9 1.0 %copy-done.4 = f32[1032,128]{1,0:T(8,128)S(1)} copy-done((f32[1032,128]{1,0:T(8,128)S(1)}, f32[1032,128]{1,0:T(8,128)}, u32[]{:S(2)}) %copy-start.4) | copy-done | bytes 528408
  49.0 0.0 copy-start.6
  49.0 1.0 %copy-done.6 = f32[1032,128]{1,0:T(8,128)S(1)} copy-done((f32[1032,128]{1,0:T(8,128)S(1)}, f32[1032,128]{1,0:T(8,128)}, u32[]{:S(2)}) %copy-start.6) | copy-done | bytes 528408
  50.0 0.0 copy-start.8
  50.0 1.0 %copy-done.8 = f32[1032,128]{1,0:T(8,128)S(1)} copy-done((f32[1032,128]{1,0:T(8,128)S(1)}, f32[1032,128]{1,0:T(8,128)}, u32[]{:S(2)}) %copy-start.8) | copy-done | bytes 528408
  51.0 0.0 copy-start.10
  51.0 1.0 %copy-done.10 = f32[1024,128]{1,0:T(8,128)S(1)} copy-done((f32[1024,128]{1,0:T(8,128)S(1)}, f32[1024,128]{1,0:T(8,128)}, u32[]{:S(2)}) %copy-start.10) | copy-done | bytes 524312
  52.1 0.0 copy-start.12
  52.1 0.8 %copy-done.12 = bf16[2,128,128]{2,1,0:T(8,128)(2,1)S(1)} copy-done((bf16[2,128,128]{2,1,0:T(8,128)(2,1)S(1)}, bf16[2,128,128]{2,1,0:T(8,128)(2,1)}, u32[]{:S(2)}) %copy-start.12) | copy-done | bytes 65560
  52.9 0.0 copy-start.14
  52.9 0.9 %copy-done.14 = bf16[1024,128]{1,0:T(8,128)(2,1)S(1)} copy-done((bf16[1024,128]{1,0:T(8,128)(2,1)S(1)}, bf16[1024,128]{1,0:T(8,128)(2,1)}, u32[]{:S(2)}) %copy-start.14) | copy-done | bytes 262168
  53.9 0.0 copy-start.16
  53.9 0.9 %copy-done.16 = bf16[1024,128]{1,0:T(8,128)(2,1)S(1)} copy-done((bf16[1024,128]{1,0:T(8,128)(2,1)S(1)}, bf16[1024,128]{1,0:T(8,128)(2,1)}, u32[]{:S(2)}) %copy-start.16) | copy-done | bytes 262168
  54.8 5.3 %backward_first.1 = (bf16[128,128]{1,0:T(8,128)(2,1)}, bf16[128,768]{1,0:T(8,128)(2,1)S(1)}) custom-call(s32[1]{0:T(128)} %bitcast.refs_0_, f32[1024,128]{1,0:T(8,128)S(1)} %copy-done.10, bf16[2,128,640]{2,1,0:T(8,128)(2,1)S(1)} %copy-done, f32[2,256]{1,0:T(2,128)S(1)} %copy-done.17, bf16[2,128,128]{2,1,0:T(8,128)(2,1)S(1)} %copy-done.12, ...), custom_call_target="tpu_custom_call" | custom-call | flops 335544320 | bytes 25165824 | tf_op jit(solution)/shard_map/backward_first/pallas_call | solution.py:353
  60.1 0.0 collective-permute-start
  60.1 0.0 collective-permute-done.2
  60.1 1.1 %add_convert_fusion.own_1 = bf16[128,768]{1,0:T(8,128)(2,1)S(1)} fusion(bf16[128,768]{1,0:T(8,128)(2,1)} %collective-permute-done.2, bf16[128,768]{1,0:T(8,128)(2,1)} %get-tuple-element.60), kind=kLoop, calls=%fused_computation | loop fusion | flops 393216 | bytes 589824 | tf_op jit(solution)/shard_map/convert_element_type | solution.py:245
  61.2 0.6 collective-permute-start.3
  61.8 0.0 collective-permute-done
  61.8 0.1 add_convert_fusion.1.own_0
  61.8 0.6 collective-permute-start.1
  62.4 0.4 collective-permute-done.3.other_1
  62.8 5.9 %collective-permute-done.1.other_0 = bf16[128,768]{1,0:T(8,128)(2,1)S(1)} collective-permute-done((bf16[128,768]{1,0:T(8,128)(2,1)S(1)}, bf16[128,768]{1,0:T(8,128)(2,1)S(1)}, u32[]{:S(2)}, u32[]{:S(2)}) %collective-permute-start.1) | collective-permute-done | bytes 196640 | tf_op jit(solution)/shard_map/ppermute | solution.py:241
  68.7 0.9 %add_grads.1 = (f32[2,128,640]{2,1,0:T(8,128)}, f32[2,128,128]{2,1,0:T(8,128)}) custom-call(bf16[128,768]{1,0:T(8,128)(2,1)S(1)} %add_convert_fusion.1.own_0, bf16[128,768]{1,0:T(8,128)(2,1)S(1)} %collective-permute-done.1.other_0, bf16[128,768]{1,0:T(8,128)(2,1)S(1)} %add_convert_fusion.own_1, bf16[128,768]{1,0:T(8,128)(2,1)S(1)} %collective-permute-done.3.other_1), custom_call_target="tpu_custom_call" | custom-call | tf_op jit(solution)/shard_map/add_grads/pallas_call | solution.py:373
Async XLA Ops:
  2.3 23.5 %copy-start = (bf16[2,128,640]{2,1,0:T(8,128)(2,1)S(1)}, bf16[2,128,640]{2,1,0:T(8,128)(2,1)}, u32[]{:S(2)}) copy-start(bf16[2,128,640]{2,1,0:T(8,128)(2,1)} %refs_2_.3) | copy-start | bytes 983044
  2.4 23.5 %copy-start.11 = (bf16[2,128,128]{2,1,0:T(8,128)(2,1)S(1)}, bf16[2,128,128]{2,1,0:T(8,128)(2,1)}, u32[]{:S(2)}) copy-start(bf16[2,128,128]{2,1,0:T(8,128)(2,1)} %refs_4_.1) | copy-start | bytes 196612
  2.4 23.5 %copy-start.17 = (f32[2,256]{1,0:T(2,128)S(1)}, f32[2,256]{1,0:T(2,128)}, u32[]{:S(2)}) copy-start(f32[2,256]{1,0:T(2,128)} %refs_3_.3) | copy-start | bytes 6148
  2.4 23.5 %copy-start.18 = (f32[2,640]{1,0:T(2,128)S(1)}, f32[2,640]{1,0:T(2,128)}, u32[]{:S(2)}) copy-start(f32[2,640]{1,0:T(2,128)} %b.1) | copy-start | bytes 15364
  2.4 23.5 %copy-start.19 = (f32[2,256]{1,0:T(2,128)S(1)}, f32[2,256]{1,0:T(2,128)}, u32[]{:S(2)}) copy-start(f32[2,256]{1,0:T(2,128)} %shift.1) | copy-start | bytes 6148
  2.4 23.5 %copy-start.20 = (f32[2,128]{1,0:T(2,128)S(1)}, f32[2,128]{1,0:T(2,128)}, u32[]{:S(2)}) copy-start(f32[2,128]{1,0:T(2,128)} %b_out.1) | copy-start | bytes 3076
  35.0 0.8 %copy-start.3 = (f32[1032,128]{1,0:T(8,128)}, f32[1032,128]{1,0:T(8,128)S(1)}, u32[]{:S(2)}) copy-start(f32[1032,128]{1,0:T(8,128)S(1)} %get-tuple-element.53.refs_12_) | copy-start | bytes 1585156
  35.9 0.8 %copy-start.5 = (f32[1032,128]{1,0:T(8,128)}, f32[1032,128]{1,0:T(8,128)S(1)}, u32[]{:S(2)}) copy-start(f32[1032,128]{1,0:T(8,128)S(1)} %get-tuple-element.54.refs_13_) | copy-start | bytes 1585156
  36.7 0.8 %copy-start.7 = (f32[1032,128]{1,0:T(8,128)}, f32[1032,128]{1,0:T(8,128)S(1)}, u32[]{:S(2)}) copy-start(f32[1032,128]{1,0:T(8,128)S(1)} %get-tuple-element.55.refs_14_) | copy-start | bytes 1585156
  37.5 7.1 %copy-start.1 = (f32[1032,128]{1,0:T(8,128)}, f32[1032,128]{1,0:T(8,128)S(1)}, u32[]{:S(2)}) copy-start(f32[1032,128]{1,0:T(8,128)S(1)} %get-tuple-element.52.refs_11_) | copy-start | bytes 1585156
  37.5 7.1 %copy-start.13 = (bf16[1024,128]{1,0:T(8,128)(2,1)}, bf16[1024,128]{1,0:T(8,128)(2,1)S(1)}, u32[]{:S(2)}) copy-start(bf16[1024,128]{1,0:T(8,128)(2,1)S(1)} %get-tuple-element.56.refs_15_) | copy-start | bytes 786436
  37.5 7.1 %copy-start.15 = (bf16[1024,128]{1,0:T(8,128)(2,1)}, bf16[1024,128]{1,0:T(8,128)(2,1)S(1)}, u32[]{:S(2)}) copy-start(bf16[1024,128]{1,0:T(8,128)(2,1)S(1)} %get-tuple-element.57.refs_16_) | copy-start | bytes 786436
  44.6 0.8 %copy-start.9 = (f32[1024,128]{1,0:T(8,128)}, f32[1024,128]{1,0:T(8,128)S(1)}, u32[]{:S(2)}) copy-start(f32[1024,128]{1,0:T(8,128)S(1)} %get-tuple-element.45.refs_1_) | copy-start | bytes 1572868
  45.4 14.7 %collective-permute-start.2 = (bf16[128,768]{1,0:T(8,128)(2,1)}, bf16[128,768]{1,0:T(8,128)(2,1)}, u32[]{:S(2)}, u32[]{:S(2)}) collective-permute-start(bf16[128,768]{1,0:T(8,128)(2,1)} %get-tuple-element.60), channel_id=1, source_target_pairs={{0,16},{8,24},{16,0},{24,8},{1,17},{9,25},{17,1},{25,9},{2,18},{10... | collective-permute-start | bytes 589832 | tf_op jit(solution)/shard_map/ppermute | solution.py:241
  46.9 1.0 %copy-start.2 = (f32[1032,128]{1,0:T(8,128)S(1)}, f32[1032,128]{1,0:T(8,128)}, u32[]{:S(2)}) copy-start(f32[1032,128]{1,0:T(8,128)} %copy-done.1) | copy-start | bytes 1585156
  47.9 1.0 %copy-start.4 = (f32[1032,128]{1,0:T(8,128)S(1)}, f32[1032,128]{1,0:T(8,128)}, u32[]{:S(2)}) copy-start(f32[1032,128]{1,0:T(8,128)} %copy-done.3) | copy-start | bytes 1585156
  49.0 1.0 %copy-start.6 = (f32[1032,128]{1,0:T(8,128)S(1)}, f32[1032,128]{1,0:T(8,128)}, u32[]{:S(2)}) copy-start(f32[1032,128]{1,0:T(8,128)} %copy-done.5) | copy-start | bytes 1585156
  50.0 1.0 %copy-start.8 = (f32[1032,128]{1,0:T(8,128)S(1)}, f32[1032,128]{1,0:T(8,128)}, u32[]{:S(2)}) copy-start(f32[1032,128]{1,0:T(8,128)} %copy-done.7) | copy-start | bytes 1585156
  51.0 1.0 %copy-start.10 = (f32[1024,128]{1,0:T(8,128)S(1)}, f32[1024,128]{1,0:T(8,128)}, u32[]{:S(2)}) copy-start(f32[1024,128]{1,0:T(8,128)} %copy-done.9) | copy-start | bytes 1572868
  52.1 0.8 %copy-start.12 = (bf16[2,128,128]{2,1,0:T(8,128)(2,1)S(1)}, bf16[2,128,128]{2,1,0:T(8,128)(2,1)}, u32[]{:S(2)}) copy-start(bf16[2,128,128]{2,1,0:T(8,128)(2,1)} %refs_4_.1) | copy-start | bytes 196612
  52.9 0.9 %copy-start.14 = (bf16[1024,128]{1,0:T(8,128)(2,1)S(1)}, bf16[1024,128]{1,0:T(8,128)(2,1)}, u32[]{:S(2)}) copy-start(bf16[1024,128]{1,0:T(8,128)(2,1)} %copy-done.13) | copy-start | bytes 786436
  53.9 0.9 %copy-start.16 = (bf16[1024,128]{1,0:T(8,128)(2,1)S(1)}, bf16[1024,128]{1,0:T(8,128)(2,1)}, u32[]{:S(2)}) copy-start(bf16[1024,128]{1,0:T(8,128)(2,1)} %copy-done.15) | copy-start | bytes 786436
  60.1 1.7 %collective-permute-start = (bf16[128,768]{1,0:T(8,128)(2,1)S(1)}, bf16[128,768]{1,0:T(8,128)(2,1)S(1)}, u32[]{:S(2)}, u32[]{:S(2)}) collective-permute-start(bf16[128,768]{1,0:T(8,128)(2,1)S(1)} %get-tuple-element.59), channel_id=1, source_target_pairs={{0,8},{8,0},{16,24},{24,16},{1,9},{9,1},{17,25},{25,17},{2,10},{10... | collective-permute-start | bytes 589832 | tf_op jit(solution)/shard_map/ppermute | solution.py:241
  61.2 1.6 %collective-permute-start.3 = (bf16[128,768]{1,0:T(8,128)(2,1)S(1)}, bf16[128,768]{1,0:T(8,128)(2,1)S(1)}, u32[]{:S(2)}, u32[]{:S(2)}) collective-permute-start(bf16[128,768]{1,0:T(8,128)(2,1)S(1)} %add_convert_fusion.own_1), channel_id=1, source_target_pairs={{0,8},{8,0},{16,24},{24,16},{1,9},{9,1},{17,25},{25,17},{2,10},{10... | collective-permute-start | bytes 589832 | tf_op jit(solution)/shard_map/ppermute | solution.py:241
  61.8 6.9 %collective-permute-start.1 = (bf16[128,768]{1,0:T(8,128)(2,1)S(1)}, bf16[128,768]{1,0:T(8,128)(2,1)S(1)}, u32[]{:S(2)}, u32[]{:S(2)}) collective-permute-start(bf16[128,768]{1,0:T(8,128)(2,1)S(1)} %add_convert_fusion.1.own_0), channel_id=1, source_target_pairs={{0,16},{8,24},{16,0},{24,8},{1,17},{9,25},{17,1},{25,9},{2,18},{10... | collective-permute-start | bytes 589832 | tf_op jit(solution)/shard_map/ppermute | solution.py:241

commit v5 on v4

--- a/solution.py
+++ b/solution.py
@@ -8,7 +8,7 @@
 from jax.sharding import PartitionSpec as P
 
 NORM_EPSILON = 1e-05
-VMEM_BYTES = 24 * 1024 * 1024
+VMEM_BYTES = 16 * 1024 * 1024
 PREPARE_BYTES = 63 * 1024 * 1024
 CROP_BUDGET = 32 * 1024 * 1024
 BLOCK_ROWS = 8
@@ -245,7 +245,8 @@
     return (a.astype(F32) + b.astype(F32)).astype(BF16)
 
 
-def prepare(state_ref, mask_ref, cot_ref, sent_ref, state_s, mask_s, cot_s, sems):
+def prepare(index_ref, state_ref, mask_ref, cot_ref, sent_ref, own_ref, state_s, mask_s, cot_s, sems):
+    own_ref[0] = index_ref[0]
     parts, _, c = sent_ref.shape
     cells = state_s.shape[0]
     copies = [
@@ -309,11 +310,14 @@
         )
 
     index = lax.axis_index("dap").astype(jnp.int32)[None]
-    sent = pl.pallas_call(
+    sent, own = pl.pallas_call(
         prepare,
-        out_shape=jax.ShapeDtypeStruct((parts, 2 * cells + 16, c), BF16),
-        in_specs=[main] * 3,
-        out_specs=vmem,
+        out_shape=(
+            jax.ShapeDtypeStruct((parts, 2 * cells + 16, c), BF16),
+            jax.ShapeDtypeStruct((1,), jnp.int32),
+        ),
+        in_specs=[smem] + [main] * 3,
+        out_specs=(vmem, smem),
         scratch_shapes=[
             pltpu.VMEM((cells, c), BF16),
             pltpu.VMEM((rows, n), jnp.int32),
@@ -322,7 +326,7 @@
         ],
         compiler_params=pltpu.CompilerParams(vmem_limit_bytes=PREPARE_BYTES),
         name="prepare",
-    )(pair_repr.reshape(cells, c), pair_mask[0], cotangent.reshape(cells, c))
+    )(index, pair_repr.reshape(cells, c), pair_mask[0], cotangent.reshape(cells, c))
     state = lax.all_to_all(sent, "dap", split_axis=0, concat_axis=0, tiled=True)
 
     held = pl.pallas_call(
@@ -359,7 +363,7 @@
         compiler_params=params,
         cost_estimate=cost(48),
         name="backward_first",
-    )(index, up_1, proj_weight, norm_gain, out_weight, *held[:KEPT])
+    )(own, up_1, proj_weight, norm_gain, out_weight, *held[:KEPT])
 
     step = 1
     while step < far:

time: 70.3 us -> 60.2 us (0.86)
  local copies, waits for them, and re-layouts: 11.2 us -> 0.04 us
  waiting for transfers between devices: 6.3 us -> 8.36 us
  other arithmetic: 1.13 us -> 0.1 us
    unnamed x42 -> x12, local copies, waits for them, and re-layouts: 11.2 us -> 0.04 us
    ppermute x4, waiting for transfers between devices: 6.3 us -> 8.36 us  [exchange(): return lax.ppermute(value, axis, [(d, d ^ step) for d in range(size)])]
    convert_element_type x2, other arithmetic: 1.13 us -> 0.1 us  [add_narrow(): return (a.astype(F32) + b.astype(F32)).astype(BF16)]
  transfers between devices with their start and end apart: 4 -> 4, of which waited for: 2 -> 2; matrix products, arithmetic and copies ran while one was open for 2% -> 0% of each run, Pallas kernels for 8% -> 0%
where the time goes in v5:
time: 60.2 us; the launch traced here: 59.9 us
  Pallas kernels  24.2 us (40%)
  blocking collectives  23.4 us (39%)
  waiting for transfers between devices  8.36 us (14%)
  starting transfers between devices  3.06 us (5%)
  between operations  0.75 us (1%)
    all_to_all x1, blocking collectives, crop_shards(): state = lax.all_to_all(sent, 'dap', split_axis=0, concat_axis=0, tiled=True)  23.4 us
    pallas_call x1, Pallas kernels, crop_shards(): pl.pallas_call(functools.partial(forward, n), out_shape=kept * 2, in_spec...  9.17 us
    ppermute x4, waiting for transfers between devices, exchange(): return lax.ppermute(value, axis, [(d, d ^ step) for d in range(size)])  8.36 us
    pallas_call x1, Pallas kernels, crop_shards(): pl.pallas_call(functools.partial(backward, n, 1), out_shape=(jax.ShapeDty...  6.38 us
    pallas_call x1, Pallas kernels, crop_shards(): pl.pallas_call(functools.partial(backward, n, 0), out_shape=(jax.ShapeDty...  5.95 us
    ppermute x4, starting transfers between devices, exchange(): return lax.ppermute(value, axis, [(d, d ^ step) for d in range(size)])  3.06 us
    pallas_call x1, Pallas kernels, crop_shards(): pl.pallas_call(prepare, out_shape=(jax.ShapeDtypeStruct((parts, 2 * cells...  1.71 us
  transfers between devices with their start and end apart: 4, of which 2 were waited for; matrix products, arithmetic and copies ran while one was open for 0% of the time, Pallas kernels for 0%

profile of v5, /device:TPU:0, one launch (start us, length us, event | category | flops | bytes accessed | tf_op | source)
XLA Modules:
  0.0 59.9 jit_solution(7880946705517806829)
XLA Ops:
  0.6 1.7 %prepare.1 = (bf16[8,272,128]{2,1,0:T(8,128)(2,1)}, s32[1]{0:T(128)}) custom-call(s32[1]{0:T(128)} %bitcast.index_ref, bf16[128,128]{1,0:T(8,128)(2,1)} %bitcast.5, s32[4,32]{1,0:T(4,128)} %bitcast.7, bf16[128,128]{1,0:T(8,128)(2,1)} %bitcast.6), custom_call_target="tpu_custom_call" | custom-call | tf_op jit(solution)/shard_map/prepare/pallas_call | solution.py:313
  2.4 0.0 copy-start
  2.4 0.0 copy-start.1
  2.4 0.0 copy-start.2
  2.4 0.0 copy-start.3
  2.4 0.0 copy-start.4
  2.4 0.0 copy-start.5
  2.4 23.4 %all_to_all.5.state_ref.refs_0_ = bf16[8,272,128]{2,1,0:T(8,128)(2,1)S(1)} all-to-all(bf16[8,272,128]{2,1,0:T(8,128)(2,1)} %get-tuple-element.36), channel_id=1, replica_groups=mesh['dp'=4,'dap'=8] {'dap'}, dimensions={0} | all-to-all | bytes 1114112 | tf_op jit(solution)/shard_map/all_to_all | solution.py:330
  25.8 0.0 copy-done
  25.8 0.0 copy-done.1
  25.9 0.0 copy-done.2
  25.9 0.0 copy-done.3
  25.9 0.0 copy-done.4
  25.9 0.0 copy-done.5
  25.9 9.2 %forward.1 = (f32[1032,128]{1,0:T(8,128)S(1)}, f32[1032,128]{1,0:T(8,128)S(1)}, f32[1032,128]{1,0:T(8,128)S(1)}, f32[1032,128]{1,0:T(8,128)S(1)}, f32[1032,128]{...) custom-call(bf16[8,272,128]{2,1,0:T(8,128)(2,1)S(1)} %all_to_all.5.s, ...), custom_call_target="tpu_custom_call" | custom-call | flops 335544320 | bytes 33554432 | tf_op jit(solution)/shard_map/forward/pallas_call | solution.py:332
  35.1 6.4 %backward_second.1 = (f32[1024,128]{1,0:T(8,128)S(1)}, bf16[128,768]{1,0:T(8,128)(2,1)S(1)}) custom-call(bf16[8,272,128]{2,1,0:T(8,128)(2,1)S(1)} %all_to_all.5.state_ref.refs_0_, bf16[2,128,640]{2,1,0:T(8,128)(2,1)S(1)} %copy-done, f32[2,256]{1,0:T(2,128)S(1)} %copy-done.2, bf16[2,128,128]{2,1,0:T(8,128)(2,1)S(1)} %copy-done.1, ...), custom_call_target="tpu_custom_call" | custom-call | flops 335544320 | bytes 25165824 | tf_op jit(solution)/shard_map/backward_second/pallas_call | solution.py:343
  41.4 6.0 %backward_first.1 = (bf16[128,128]{1,0:T(8,128)(2,1)}, bf16[128,768]{1,0:T(8,128)(2,1)S(1)}) custom-call(s32[1]{0:T(128)} %get-tuple-element.35.refs_0_, f32[1024,128]{1,0:T(8,128)S(1)} %get-tuple-element.49.refs_1_, bf16[2,128,640]{2,1,0:T(8,128)(2,1)S(1)} %copy-done, f32[2,256]{1,0:T(2,128)S(1)} %copy-done.2, bf16[2,128,128]{2,1,0:T(8,128)(2,1)S(1)} %copy-done.1, ...), custom_call_target="tpu_custom_call" | custom-call | flops 335544320 | bytes 25165824 | tf_op jit(solution)/shard_map/backward_first/pallas_call | solution.py:357
  47.4 0.0 collective-permute-start
  47.4 1.5 %collective-permute-start.2 = (bf16[128,768]{1,0:T(8,128)(2,1)S(1)}, bf16[128,768]{1,0:T(8,128)(2,1)S(1)}, u32[]{:S(2)}, u32[]{:S(2)}) collective-permute-start(bf16[128,768]{1,0:T(8,128)(2,1)S(1)} %get-tuple-element.64), channel_id=1, source_target_pairs={{0,16},{8,24},{16,0},{24,8},{1,17},{9,25},{17,1},{25,9},{2,18},{10... | collective-permute-start | bytes 589832 | tf_op jit(solution)/shard_map/ppermute | solution.py:241
  48.9 0.0 collective-permute-done
  48.9 1.5 %collective-permute-start.1 = (bf16[128,768]{1,0:T(8,128)(2,1)S(1)}, bf16[128,768]{1,0:T(8,128)(2,1)S(1)}, u32[]{:S(2)}, u32[]{:S(2)}) collective-permute-start(bf16[128,768]{1,0:T(8,128)(2,1)S(1)} %add_convert_fusion.1.own_0), channel_id=1, source_target_pairs={{0,16},{8,24},{16,0},{24,8},{1,17},{9,25},{17,1},{25,9},{2,18},{10... | collective-permute-start | bytes 589832 | tf_op jit(solution)/shard_map/ppermute | solution.py:241
  50.4 4.7 %collective-permute-done.2 = bf16[128,768]{1,0:T(8,128)(2,1)S(1)} collective-permute-done((bf16[128,768]{1,0:T(8,128)(2,1)S(1)}, bf16[128,768]{1,0:T(8,128)(2,1)S(1)}, u32[]{:S(2)}, u32[]{:S(2)}) %collective-permute-start.2) | collective-permute-done | bytes 196640 | tf_op jit(solution)/shard_map/ppermute | solution.py:241
  55.2 0.1 collective-permute-start.3
  55.2 3.7 %collective-permute-done.1.other_0 = bf16[128,768]{1,0:T(8,128)(2,1)S(1)} collective-permute-done((bf16[128,768]{1,0:T(8,128)(2,1)S(1)}, bf16[128,768]{1,0:T(8,128)(2,1)S(1)}, u32[]{:S(2)}, u32[]{:S(2)}) %collective-permute-start.1) | collective-permute-done | bytes 196640 | tf_op jit(solution)/shard_map/ppermute | solution.py:241
  58.9 0.0 collective-permute-done.3.other_1
  58.9 0.9 %add_grads.1 = (f32[2,128,640]{2,1,0:T(8,128)}, f32[2,128,128]{2,1,0:T(8,128)}) custom-call(bf16[128,768]{1,0:T(8,128)(2,1)S(1)} %add_convert_fusion.1.own_0, bf16[128,768]{1,0:T(8,128)(2,1)S(1)} %collective-permute-done.1.other_0, bf16[128,768]{1,0:T(8,128)(2,1)S(1)} %add_convert_fusion.own_1, bf16[128,768]{1,0:T(8,128)(2,1)S(1)} %collective-permute-done.3.other_1), custom_call_target="tpu_custom_call" | custom-call | tf_op jit(solution)/shard_map/add_grads/pallas_call | solution.py:377
  (2 shorter events, 0.1 us)
Async XLA Ops:
  2.4 23.5 %copy-start = (bf16[2,128,640]{2,1,0:T(8,128)(2,1)S(1)}, bf16[2,128,640]{2,1,0:T(8,128)(2,1)}, u32[]{:S(2)}) copy-start(bf16[2,128,640]{2,1,0:T(8,128)(2,1)} %refs_2_.3) | copy-start | bytes 983044
  2.4 23.5 %copy-start.1 = (bf16[2,128,128]{2,1,0:T(8,128)(2,1)S(1)}, bf16[2,128,128]{2,1,0:T(8,128)(2,1)}, u32[]{:S(2)}) copy-start(bf16[2,128,128]{2,1,0:T(8,128)(2,1)} %refs_4_.1) | copy-start | bytes 196612
  2.4 23.5 %copy-start.2 = (f32[2,256]{1,0:T(2,128)S(1)}, f32[2,256]{1,0:T(2,128)}, u32[]{:S(2)}) copy-start(f32[2,256]{1,0:T(2,128)} %refs_3_.3) | copy-start | bytes 6148
  2.4 23.5 %copy-start.3 = (f32[2,640]{1,0:T(2,128)S(1)}, f32[2,640]{1,0:T(2,128)}, u32[]{:S(2)}) copy-start(f32[2,640]{1,0:T(2,128)} %b.1) | copy-start | bytes 15364
  2.4 23.5 %copy-start.4 = (f32[2,256]{1,0:T(2,128)S(1)}, f32[2,256]{1,0:T(2,128)}, u32[]{:S(2)}) copy-start(f32[2,256]{1,0:T(2,128)} %shift.1) | copy-start | bytes 6148
  2.4 23.5 %copy-start.5 = (f32[2,128]{1,0:T(2,128)S(1)}, f32[2,128]{1,0:T(2,128)}, u32[]{:S(2)}) copy-start(f32[2,128]{1,0:T(2,128)} %b_out.1) | copy-start | bytes 3076
  47.4 1.5 %collective-permute-start = (bf16[128,768]{1,0:T(8,128)(2,1)S(1)}, bf16[128,768]{1,0:T(8,128)(2,1)S(1)}, u32[]{:S(2)}, u32[]{:S(2)}) collective-permute-start(bf16[128,768]{1,0:T(8,128)(2,1)S(1)} %get-tuple-element.63), channel_id=1, source_target_pairs={{0,8},{8,0},{16,24},{24,16},{1,9},{9,1},{17,25},{25,17},{2,10},{10... | collective-permute-start | bytes 589832 | tf_op jit(solution)/shard_map/ppermute | solution.py:241
  47.4 7.7 %collective-permute-start.2 = (bf16[128,768]{1,0:T(8,128)(2,1)S(1)}, bf16[128,768]{1,0:T(8,128)(2,1)S(1)}, u32[]{:S(2)}, u32[]{:S(2)}) collective-permute-start(bf16[128,768]{1,0:T(8,128)(2,1)S(1)} %get-tuple-element.64), channel_id=1, source_target_pairs={{0,16},{8,24},{16,0},{24,8},{1,17},{9,25},{17,1},{25,9},{2,18},{10... | collective-permute-start | bytes 589832 | tf_op jit(solution)/shard_map/ppermute | solution.py:241
  48.9 10.0 %collective-permute-start.1 = (bf16[128,768]{1,0:T(8,128)(2,1)S(1)}, bf16[128,768]{1,0:T(8,128)(2,1)S(1)}, u32[]{:S(2)}, u32[]{:S(2)}) collective-permute-start(bf16[128,768]{1,0:T(8,128)(2,1)S(1)} %add_convert_fusion.1.own_0), channel_id=1, source_target_pairs={{0,16},{8,24},{16,0},{24,8},{1,17},{9,25},{17,1},{25,9},{2,18},{10... | collective-permute-start | bytes 589832 | tf_op jit(solution)/shard_map/ppermute | solution.py:241
  55.2 3.8 %collective-permute-start.3 = (bf16[128,768]{1,0:T(8,128)(2,1)S(1)}, bf16[128,768]{1,0:T(8,128)(2,1)S(1)}, u32[]{:S(2)}, u32[]{:S(2)}) collective-permute-start(bf16[128,768]{1,0:T(8,128)(2,1)S(1)} %add_convert_fusion.own_1), channel_id=1, source_target_pairs={{0,8},{8,0},{16,24},{24,16},{1,9},{9,1},{17,25},{25,17},{2,10},{10... | collective-permute-start | bytes 589832 | tf_op jit(solution)/shard_map/ppermute | solution.py:241

commit v6 on v5

--- a/solution.py
+++ b/solution.py
@@ -86,7 +86,7 @@
         )
 
     zero = jnp.zeros(tiles, F32)
-    totals = lax.fori_loop(0, n, step, (zero,) * BLOCK_ROWS, unroll=4)
+    totals = lax.fori_loop(0, n, step, (zero,) * BLOCK_ROWS, unroll=True)
     return jnp.stack(totals).reshape(BLOCK_ROWS * n, lanes)
 
 
@@ -266,9 +266,9 @@
         sent_ref[part, 2 * cells :, :] = below
 
 
-def add_grads(own_0, other_0, own_1, other_1, proj_ref, out_ref):
+def add_grads(own_0, other_0, own_both, other_both, proj_ref, out_ref):
     width = proj_ref.shape[2]
-    for u, (own, other) in enumerate(((own_0, other_0), (own_1, other_1))):
+    for u, (own, other) in enumerate(((own_0, other_0), (own_both.at[1], other_both.at[1]))):
         total = own[...].astype(F32) + other[...].astype(F32)
         proj_ref[u] = total[:, :width]
         out_ref[u] = total[:, width:]
@@ -365,13 +365,14 @@
         name="backward_first",
     )(own, up_1, proj_weight, norm_gain, out_weight, *held[:KEPT])
 
+    both = jnp.stack([grads_0, add_narrow(grads_1, others_1)])
+    others = jnp.zeros_like(both)
     step = 1
     while step < far:
-        near_1 = add_narrow(grads_1, others_1)
-        others_1 = exchange(near_1, "dp", groups, step)
-        others_0 = exchange(grads_0, "dp", groups, step)
-        grads_1, grads_0 = near_1, add_narrow(grads_0, others_0)
+        both = add_narrow(both, others) if step > 1 else both
+        others = exchange(both, "dp", groups, step)
         step *= 2
+    grads_0 = add_narrow(both[0], others[0])
     others_0 = exchange(grads_0, "dp", groups, far)
 
     proj_total, out_total = pl.pallas_call(
@@ -384,7 +385,7 @@
         out_specs=(vmem, vmem),
         compiler_params=params,
         name="add_grads",
-    )(grads_0, others_0, grads_1, others_1)
+    )(grads_0, others_0, both, others)
     return pair_grad.reshape(pair_repr.shape), proj_total, out_total
 
 

time: 60.2 us -> 59.6 us (0.990)
  starting transfers between devices: 3.06 us -> 2.23 us
    pallas_call x1, Pallas kernels: 5.95 us -> 7.31 us  [crop_shards(): pl.pallas_call(functools.partial(backward, n, 0), out_shape=(jax.ShapeDty...]
    ppermute x4 -> x3, starting transfers between devices: 3.06 us -> 2.23 us  [exchange(): return lax.ppermute(value, axis, [(d, d ^ step) for d in range(size)])]
    ppermute x4 -> x3, waiting for transfers between devices: 8.36 us -> 8.12 us  [exchange(): return lax.ppermute(value, axis, [(d, d ^ step) for d in range(size)])]
  transfers between devices with their start and end apart: 4 -> 3, of which waited for: 2 -> 2; matrix products, arithmetic and copies ran while one was open for 0% -> 0% of each run, Pallas kernels for 0% -> 12%
where the time goes in v6:
time: 59.6 us; the launch traced here: 59.4 us
  Pallas kernels  24.7 us (41%)
  blocking collectives  23.4 us (39%)
  waiting for transfers between devices  8.12 us (14%)
  starting transfers between devices  2.23 us (4%)
  between operations  0.75 us (1%)
    all_to_all x1, blocking collectives, crop_shards(): state = lax.all_to_all(sent, 'dap', split_axis=0, concat_axis=0, tiled=True)  23.4 us
    pallas_call x1, Pallas kernels, crop_shards(): pl.pallas_call(functools.partial(forward, n), out_shape=kept * 2, in_spec...  8.79 us
    ppermute x3, waiting for transfers between devices, exchange(): return lax.ppermute(value, axis, [(d, d ^ step) for d in range(size)])  8.12 us
    pallas_call x1, Pallas kernels, crop_shards(): pl.pallas_call(functools.partial(backward, n, 0), out_shape=(jax.ShapeDty...  7.31 us
    pallas_call x1, Pallas kernels, crop_shards(): pl.pallas_call(functools.partial(backward, n, 1), out_shape=(jax.ShapeDty...  5.91 us
    ppermute x3, starting transfers between devices, exchange(): return lax.ppermute(value, axis, [(d, d ^ step) for d in range(size)])  2.23 us
    pallas_call x1, Pallas kernels, crop_shards(): pl.pallas_call(prepare, out_shape=(jax.ShapeDtypeStruct((parts, 2 * cells...  1.71 us
  transfers between devices with their start and end apart: 3, of which 2 were waited for; matrix products, arithmetic and copies ran while one was open for 0% of the time, Pallas kernels for 12%

profile of v6, /device:TPU:0, one launch (start us, length us, event | category | flops | bytes accessed | tf_op | source)
XLA Modules:
  0.0 59.4 jit_solution(1700577338432196109)
XLA Ops:
  0.6 1.7 %prepare.1 = (bf16[8,272,128]{2,1,0:T(8,128)(2,1)}, s32[1]{0:T(128)}) custom-call(s32[1]{0:T(128)} %bitcast.index_ref, bf16[128,128]{1,0:T(8,128)(2,1)} %bitcast.14, s32[4,32]{1,0:T(4,128)} %bitcast.16, bf16[128,128]{1,0:T(8,128)(2,1)} %bitcast.15), custom_call_target="tpu_custom_call" | custom-call | tf_op jit(solution)/shard_map/prepare/pallas_call | solution.py:313
  2.4 0.0 copy-start
  2.4 0.0 copy-start.1
  2.4 0.0 copy-start.2
  2.4 0.0 copy-start.3
  2.4 0.0 copy-start.4
  2.4 0.0 copy-start.5
  2.4 23.4 %all_to_all.5.state_ref.refs_0_ = bf16[8,272,128]{2,1,0:T(8,128)(2,1)S(1)} all-to-all(bf16[8,272,128]{2,1,0:T(8,128)(2,1)} %get-tuple-element.36), channel_id=1, replica_groups=mesh['dp'=4,'dap'=8] {'dap'}, dimensions={0} | all-to-all | bytes 1114112 | tf_op jit(solution)/shard_map/all_to_all | solution.py:330
  25.8 0.0 copy-done
  25.8 0.0 copy-done.1
  25.9 0.0 copy-done.2
  25.9 0.0 copy-done.3
  25.9 0.0 copy-done.4
  25.9 0.0 copy-done.5
  25.9 8.8 %forward.1 = (f32[1032,128]{1,0:T(8,128)S(1)}, f32[1032,128]{1,0:T(8,128)S(1)}, f32[1032,128]{1,0:T(8,128)S(1)}, f32[1032,128]{1,0:T(8,128)S(1)}, f32[1032,128]{...) custom-call(bf16[8,272,128]{2,1,0:T(8,128)(2,1)S(1)} %all_to_all.5.s, ...), custom_call_target="tpu_custom_call" | custom-call | flops 335544320 | bytes 33554432 | tf_op jit(solution)/shard_map/forward/pallas_call | solution.py:332
  34.7 5.9 %backward_second.1 = (f32[1024,128]{1,0:T(8,128)S(1)}, bf16[128,768]{1,0:T(8,128)(2,1)S(1)}) custom-call(bf16[8,272,128]{2,1,0:T(8,128)(2,1)S(1)} %all_to_all.5.state_ref.refs_0_, bf16[2,128,640]{2,1,0:T(8,128)(2,1)S(1)} %copy-done, f32[2,256]{1,0:T(2,128)S(1)} %copy-done.2, bf16[2,128,128]{2,1,0:T(8,128)(2,1)S(1)} %copy-done.1, ...), custom_call_target="tpu_custom_call" | custom-call | flops 335544320 | bytes 25165824 | tf_op jit(solution)/shard_map/backward_second/pallas_call | solution.py:343
  40.6 1.6 %collective-permute-start = (bf16[128,768]{1,0:T(8,128)(2,1)S(1)}, bf16[128,768]{1,0:T(8,128)(2,1)S(1)}, u32[]{:S(2)}, u32[]{:S(2)}) collective-permute-start(bf16[128,768]{1,0:T(8,128)(2,1)S(1)} %get-tuple-element.64), channel_id=1, source_target_pairs={{0,16},{8,24},{16,0},{24,8},{1,17},{9,25},{17,1},{25,9},{2,18},{10... | collective-permute-start | bytes 589832 | tf_op jit(solution)/shard_map/ppermute | solution.py:241
  42.1 7.3 %backward_first.1 = (bf16[128,128]{1,0:T(8,128)(2,1)}, bf16[128,768]{1,0:T(8,128)(2,1)S(1)}) custom-call(s32[1]{0:T(128)} %get-tuple-element.35.refs_0_, f32[1024,128]{1,0:T(8,128)S(1)} %get-tuple-element.49.refs_1_, bf16[2,128,640]{2,1,0:T(8,128)(2,1)S(1)} %copy-done, f32[2,256]{1,0:T(2,128)S(1)} %copy-done.2, bf16[2,128,128]{2,1,0:T(8,128)(2,1)S(1)} %copy-done.1, ...), custom_call_target="tpu_custom_call" | custom-call | flops 335544320 | bytes 25165824 | tf_op jit(solution)/shard_map/backward_first/pallas_call | solution.py:357
  49.4 0.0 collective-permute-done
  49.6 0.1 collective-permute-start.1
  49.6 1.7 %collective-permute-done.1.other_both = bf16[2,128,768]{2,1,0:T(8,128)(2,1)S(1)} collective-permute-done((bf16[2,128,768]{2,1,0:T(8,128)(2,1)S(1)}, bf16[2,128,768]{2,1,0:T(8,128)(2,1)S(1)}, u32[]{:S(2)}, u32[]{:S(2)}) %collective-permute-start.1) | collective-permute-done | bytes 393248 | tf_op jit(solution)/shard_map/ppermute | solution.py:241
  51.3 0.1 fusion.own_0
  51.4 0.6 %collective-permute-start.2 = (bf16[128,768]{1,0:T(8,128)(2,1)S(1)}, bf16[128,768]{1,0:T(8,128)(2,1)S(1)}, u32[]{:S(2)}, u32[]{:S(2)}) collective-permute-start(bf16[128,768]{1,0:T(8,128)(2,1)S(1)} %fusion.own_0), channel_id=1, source_target_pairs={{0,16},{8,24},{16,0},{24,8},{1,17},{9,25},{17,1},{25,9},{2,18},{10... | collective-permute-start | bytes 589832 | tf_op jit(solution)/shard_map/ppermute | solution.py:241
  52.0 6.4 %collective-permute-done.2.other_0 = bf16[128,768]{1,0:T(8,128)(2,1)S(1)} collective-permute-done((bf16[128,768]{1,0:T(8,128)(2,1)S(1)}, bf16[128,768]{1,0:T(8,128)(2,1)S(1)}, u32[]{:S(2)}, u32[]{:S(2)}) %collective-permute-start.2) | collective-permute-done | bytes 196640 | tf_op jit(solution)/shard_map/ppermute | solution.py:241
  58.4 0.9 %add_grads.1 = (f32[2,128,640]{2,1,0:T(8,128)}, f32[2,128,128]{2,1,0:T(8,128)}) custom-call(bf16[128,768]{1,0:T(8,128)(2,1)S(1)} %fusion.own_0, bf16[128,768]{1,0:T(8,128)(2,1)S(1)} %collective-permute-done.2.other_0, bf16[2,128,768]{2,1,0:T(8,128)(2,1)S(1)} %pad_maximum_fusion.own_both, bf16[2,128,768]{2,1,0:T(8,128)(2,1)S(1)} %collective-permute-done.1.other_both), custom_call_target="tpu_custom_call" | custom-call | tf_op jit(solution)/shard_map/add_grads/pallas_call | solution.py:378
  (2 shorter events, 0.1 us)
Async XLA Ops:
  2.4 23.5 %copy-start = (bf16[2,128,640]{2,1,0:T(8,128)(2,1)S(1)}, bf16[2,128,640]{2,1,0:T(8,128)(2,1)}, u32[]{:S(2)}) copy-start(bf16[2,128,640]{2,1,0:T(8,128)(2,1)} %refs_2_.3) | copy-start | bytes 983044
  2.4 23.5 %copy-start.1 = (bf16[2,128,128]{2,1,0:T(8,128)(2,1)S(1)}, bf16[2,128,128]{2,1,0:T(8,128)(2,1)}, u32[]{:S(2)}) copy-start(bf16[2,128,128]{2,1,0:T(8,128)(2,1)} %refs_4_.1) | copy-start | bytes 196612
  2.4 23.5 %copy-start.2 = (f32[2,256]{1,0:T(2,128)S(1)}, f32[2,256]{1,0:T(2,128)}, u32[]{:S(2)}) copy-start(f32[2,256]{1,0:T(2,128)} %refs_3_.3) | copy-start | bytes 6148
  2.4 23.5 %copy-start.3 = (f32[2,640]{1,0:T(2,128)S(1)}, f32[2,640]{1,0:T(2,128)}, u32[]{:S(2)}) copy-start(f32[2,640]{1,0:T(2,128)} %b.1) | copy-start | bytes 15364
  2.4 23.5 %copy-start.4 = (f32[2,256]{1,0:T(2,128)S(1)}, f32[2,256]{1,0:T(2,128)}, u32[]{:S(2)}) copy-start(f32[2,256]{1,0:T(2,128)} %shift.1) | copy-start | bytes 6148
  2.4 23.5 %copy-start.5 = (f32[2,128]{1,0:T(2,128)S(1)}, f32[2,128]{1,0:T(2,128)}, u32[]{:S(2)}) copy-start(f32[2,128]{1,0:T(2,128)} %b_out.1) | copy-start | bytes 3076
  40.6 8.9 %collective-permute-start = (bf16[128,768]{1,0:T(8,128)(2,1)S(1)}, bf16[128,768]{1,0:T(8,128)(2,1)S(1)}, u32[]{:S(2)}, u32[]{:S(2)}) collective-permute-start(bf16[128,768]{1,0:T(8,128)(2,1)S(1)} %get-tuple-element.64), channel_id=1, source_target_pairs={{0,16},{8,24},{16,0},{24,8},{1,17},{9,25},{17,1},{25,9},{2,18},{10... | collective-permute-start | bytes 589832 | tf_op jit(solution)/shard_map/ppermute | solution.py:241
  49.6 1.8 %collective-permute-start.1 = (bf16[2,128,768]{2,1,0:T(8,128)(2,1)S(1)}, bf16[2,128,768]{2,1,0:T(8,128)(2,1)S(1)}, u32[]{:S(2)}, u32[]{:S(2)}) collective-permute-start(bf16[2,128,768]{2,1,0:T(8,128)(2,1)S(1)} %pad_maximum_fusion.own_both), channel_id=1, source_target_pairs={{0,8},{8,0},{16,24},{24,16},{1,9},{9,1},{17,25},{25,17},{2,10},{10... | collective-permute-start | bytes 1179656 | tf_op jit(solution)/shard_map/ppermute | solution.py:241
  51.4 7.0 %collective-permute-start.2 = (bf16[128,768]{1,0:T(8,128)(2,1)S(1)}, bf16[128,768]{1,0:T(8,128)(2,1)S(1)}, u32[]{:S(2)}, u32[]{:S(2)}) collective-permute-start(bf16[128,768]{1,0:T(8,128)(2,1)S(1)} %fusion.own_0), channel_id=1, source_target_pairs={{0,16},{8,24},{16,0},{24,8},{1,17},{9,25},{17,1},{25,9},{2,18},{10... | collective-permute-start | bytes 589832 | tf_op jit(solution)/shard_map/ppermute | solution.py:241

commit v7 on v6

--- a/solution.py
+++ b/solution.py
@@ -12,7 +12,7 @@
 PREPARE_BYTES = 63 * 1024 * 1024
 CROP_BUDGET = 32 * 1024 * 1024
 BLOCK_ROWS = 8
-KEPT = 12
+KEPT = 10
 F32 = jnp.float32
 BF16 = jnp.bfloat16
 
@@ -118,8 +118,8 @@
     blocks = n // BLOCK_ROWS
 
     for u in range(2):
-        (left_s, right_s, s_left_s, s_right_s, gate_s, hat_s, rstd_s) = kept[u][:7]
-        (p_hat_s, p_rstd_s, branch_s, normed_s, mixed_s) = kept[u][7:]
+        (edges_s, slopes_s, gate_s, hat_s, rstd_s) = kept[u][:5]
+        (p_hat_s, p_rstd_s, branch_s, normed_s, mixed_s) = kept[u][5:]
 
         @pl.loop(0, blocks)
         def _(t):
@@ -130,10 +130,10 @@
             x_hat, rstd, normed, s_left, s_right, left, right, gate = project(
                 x.astype(F32), mask, u, w, b, gain, shift
             )
-            left_s[here, :] = left
-            right_s[here, :] = right
-            s_left_s[here, :] = s_left
-            s_right_s[here, :] = s_right
+            edges_s[0, here, :] = left
+            edges_s[1, here, :] = right
+            slopes_s[0, here, :] = s_left
+            slopes_s[1, here, :] = s_right
             gate_s[here, :] = gate
             hat_s[here, :] = x_hat
             rstd_s[here, :] = jnp.broadcast_to(rstd, x_hat.shape)
@@ -147,9 +147,9 @@
             first = t * BLOCK_ROWS
             here = pl.ds(pl.multiple_of(first * n, BLOCK_ROWS * n), BLOCK_ROWS * n)
             if u == 0:
-                product = contract(n, first, lambda i, k: i * n + k, left_s, right_t_s)
+                product = contract(n, first, lambda i, k: i * n + k, edges_s.at[0], right_t_s)
             else:
-                product = contract(n, first, lambda i, k: k * n + i, left_s, right_s)
+                product = contract(n, first, lambda i, k: k * n + i, edges_s.at[0], edges_s.at[1])
             p_hat, p_rstd, mixed, branch = mix(
                 product.astype(BF16), u, c, gain, shift, w_out, b_out
             )
@@ -172,10 +172,10 @@
     if u == 0:
         index_ref, refs = refs[0], refs[1:]
     up_in_ref, w, gain, w_out = refs[:4]
-    (left_s, right_s, s_left_s, s_right_s, gate_s, hat_s, rstd_s) = refs[4:11]
-    (p_hat_s, p_rstd_s, branch_s, normed_s, mixed_s) = refs[11 : 4 + KEPT]
-    up_ref, grads_ref, d_product_s, d_branch_s, d_pre_s = refs[4 + KEPT : 9 + KEPT]
-    c, h = w.shape[1], left_s.shape[1]
+    (edges_s, slopes_s, gate_s, hat_s, rstd_s) = refs[4:9]
+    (p_hat_s, p_rstd_s, branch_s, normed_s, mixed_s) = refs[9 : 4 + KEPT]
+    up_ref, grads_ref, d_product_s, d_edges_s, d_branch_s, d_pre_s = refs[4 + KEPT :]
+    c, h = w.shape[1], edges_s.shape[2]
     blocks = n // BLOCK_ROWS
 
     def upstream(t, here):
@@ -206,24 +206,33 @@
         )
         d_branch_s[here, :] = d_branch
         d_pre_s[here, 4 * h :] = d_gate
-        d_product_s[here, :] = d_product
         if u == 1:
-            d_product_t_s = refs[9 + KEPT]
             for r in range(BLOCK_ROWS):
-                d_product_t_s[pl.ds(first + r, n, stride=n), :] = d_product[r * n : (r + 1) * n]
+                d_product_s[0, pl.ds(first + r, n, stride=n), :] = d_product[r * n : (r + 1) * n]
+            d_product_s[1, here, :] = d_product
+        else:
+            d_product_s[0, here, :] = d_product
+            for r in range(BLOCK_ROWS):
+                d_product_s[1, pl.ds(first + r, n, stride=n), :] = d_product[r * n : (r + 1) * n]
+
+    @pl.loop(0, 2 * blocks)
+    def _(step):
+        side, first = step // blocks, step % blocks * BLOCK_ROWS
+        here = pl.ds(pl.multiple_of(first * n, BLOCK_ROWS * n), BLOCK_ROWS * n)
+        edges, d_product = edges_s.at[1 - side], d_product_s.at[side]
+        x, y = (edges, d_product) if u == 1 else (d_product, edges)
+        d_edges_s[side, here, :] = contract(n, first, lambda a, e: a * n + e, x, y)
 
     @pl.loop(0, blocks)
     def _(t):
-        first = t * BLOCK_ROWS
-        here = pl.ds(pl.multiple_of(first * n, BLOCK_ROWS * n), BLOCK_ROWS * n)
-        if u == 1:
-            d_left = contract(n, first, lambda k, j: k * n + j, right_s, refs[9 + KEPT])
-            d_right = contract(n, first, lambda k, i: k * n + i, left_s, d_product_s)
-        else:
-            d_left = contract(n, first, lambda i, j: i * n + j, d_product_s, right_s)
-            d_right = contract(n, first, lambda j, i: i * n + j, d_product_s, left_s)
+        here = pl.ds(pl.multiple_of(t * BLOCK_ROWS * n, BLOCK_ROWS * n), BLOCK_ROWS * n)
         grads = edge_grads(
-            d_left, d_right, s_left_s[here, :], s_right_s[here, :], left_s[here, :], right_s[here, :]
+            d_edges_s[0, here, :],
+            d_edges_s[1, here, :],
+            slopes_s[0, here, :],
+            slopes_s[1, here, :],
+            edges_s[0, here, :],
+            edges_s[1, here, :],
         )
         for g in range(4):
             d_pre_s[here, g * h : (g + 1) * h] = grads[g]
@@ -294,7 +303,8 @@
     plane = jax.ShapeDtypeStruct((pairs + 8, h), F32)
     narrow = jax.ShapeDtypeStruct((pairs, h), BF16)
     grads = jax.ShapeDtypeStruct((c, width + c), BF16)
-    kept = (plane,) * 10 + (narrow,) * 2
+    double = jax.ShapeDtypeStruct((2, pairs + 8, h), F32)
+    kept = (double,) * 2 + (plane,) * 6 + (narrow,) * 2
     vmem = pl.BlockSpec(memory_space=pltpu.VMEM)
     smem = pl.BlockSpec(memory_space=pltpu.SMEM)
     main = pl.BlockSpec(memory_space=pltpu.HBM)
@@ -340,13 +350,14 @@
         name="forward",
     )(state, proj_weight, proj_bias, norm_gain, norm_shift, out_weight, out_bias)
 
+    work = [scratch(double), scratch(double), scratch(narrow)]
+    work.append(pltpu.VMEM((pairs, width), BF16))
     up_1, grads_1 = pl.pallas_call(
         functools.partial(backward, n, 1),
         out_shape=(jax.ShapeDtypeStruct((pairs, c), F32), grads),
         in_specs=[vmem] * (4 + KEPT),
         out_specs=(vmem, vmem),
-        scratch_shapes=[scratch(plane), scratch(narrow), pltpu.VMEM((pairs, width), BF16)]
-        + [scratch(plane)],
+        scratch_shapes=work,
         compiler_params=params,
         cost_estimate=cost(48),
         name="backward_second",
@@ -359,7 +370,7 @@
         out_shape=(jax.ShapeDtypeStruct((cells, c), BF16), grads),
         in_specs=[smem] + [vmem] * (4 + KEPT),
         out_specs=(vmem, vmem),
-        scratch_shapes=[scratch(plane), scratch(narrow), pltpu.VMEM((pairs, width), BF16)],
+        scratch_shapes=work,
         compiler_params=params,
         cost_estimate=cost(48),
         name="backward_first",

time: 59.6 us -> 59.1 us (level)
    pallas_call x1, Pallas kernels: 7.31 us -> 6.55 us  [crop_shards(): pl.pallas_call(functools.partial(backward, n, 0), out_shape=(jax.ShapeDty...]
  transfers between devices with their start and end apart: 3 -> 3, of which waited for: 2 -> 2; matrix products, arithmetic and copies ran while one was open for 0% -> 0% of each run, Pallas kernels for 12% -> 11%
where the time goes in v7:
time: 59.1 us; the launch traced here: 58.8 us
  Pallas kernels  24.3 us (41%)
  blocking collectives  23.3 us (39%)
  waiting for transfers between devices  8.13 us (14%)
  starting transfers between devices  2.22 us (4%)
  between operations  0.75 us (1%)
    all_to_all x1, blocking collectives, crop_shards(): state = lax.all_to_all(sent, 'dap', split_axis=0, concat_axis=0, tiled=True)  23.3 us
    pallas_call x1, Pallas kernels, crop_shards(): pl.pallas_call(functools.partial(forward, n), out_shape=kept * 2, in_spec...  8.81 us
    ppermute x3, waiting for transfers between devices, exchange(): return lax.ppermute(value, axis, [(d, d ^ step) for d in range(size)])  8.13 us
    pallas_call x1, Pallas kernels, crop_shards(): pl.pallas_call(functools.partial(backward, n, 0), out_shape=(jax.ShapeDty...  6.55 us
    pallas_call x1, Pallas kernels, crop_shards(): pl.pallas_call(functools.partial(backward, n, 1), out_shape=(jax.ShapeDty...  6.24 us
    ppermute x3, starting transfers between devices, exchange(): return lax.ppermute(value, axis, [(d, d ^ step) for d in range(size)])  2.22 us
    pallas_call x1, Pallas kernels, crop_shards(): pl.pallas_call(prepare, out_shape=(jax.ShapeDtypeStruct((parts, 2 * cells...  1.76 us
  transfers between devices with their start and end apart: 3, of which 2 were waited for; matrix products, arithmetic and copies ran while one was open for 0% of the time, Pallas kernels for 11%

profile of v7, /device:TPU:0, one launch (start us, length us, event | category | flops | bytes accessed | tf_op | source)
XLA Modules:
  0.0 58.8 jit_solution(7305370719467198808)
XLA Ops:
  0.6 0.0 copy-start.1
  0.6 0.0 copy-start.2
  0.7 0.0 copy-start
  0.7 0.0 copy-start.5
  0.7 0.0 copy-start.4
  0.7 0.0 copy-start.3
  0.7 1.8 %prepare.1 = (bf16[8,272,128]{2,1,0:T(8,128)(2,1)}, s32[1]{0:T(128)}) custom-call(s32[1]{0:T(128)} %bitcast.index_ref, bf16[128,128]{1,0:T(8,128)(2,1)} %bitcast.14, s32[4,32]{1,0:T(4,128)} %bitcast.16, bf16[128,128]{1,0:T(8,128)(2,1)} %bitcast.15), custom_call_target="tpu_custom_call" | custom-call | tf_op jit(solution)/shard_map/prepare/pallas_call | solution.py:323
  2.5 23.3 %all_to_all.5.state_ref.refs_0_ = bf16[8,272,128]{2,1,0:T(8,128)(2,1)S(1)} all-to-all(bf16[8,272,128]{2,1,0:T(8,128)(2,1)} %get-tuple-element.32), channel_id=1, replica_groups=mesh['dp'=4,'dap'=8] {'dap'}, dimensions={0} | all-to-all | bytes 1114112 | tf_op jit(solution)/shard_map/all_to_all | solution.py:340
  25.8 0.0 copy-done.1
  25.8 0.0 copy-done.2
  25.8 0.0 copy-done
  25.8 0.0 copy-done.5
  25.8 0.0 copy-done.4
  25.8 0.0 copy-done.3
  25.8 8.8 %forward.1 = (f32[2,1032,128]{2,1,0:T(8,128)S(1)}, f32[2,1032,128]{2,1,0:T(8,128)S(1)}, f32[1032,128]{1,0:T(8,128)S(1)}, f32[1032,128]{1,0:T(8,128)S(1)}, f32[10...) custom-call(bf16[8,272,128]{2,1,0:T(8,128)(2,1)S(1)} %all_to_all.5.s, ...), custom_call_target="tpu_custom_call" | custom-call | flops 335544320 | bytes 33554432 | tf_op jit(solution)/shard_map/forward/pallas_call | solution.py:342
  34.6 6.2 %backward_second.1 = (f32[1024,128]{1,0:T(8,128)S(1)}, bf16[128,768]{1,0:T(8,128)(2,1)S(1)}) custom-call(bf16[8,272,128]{2,1,0:T(8,128)(2,1)S(1)} %all_to_all.5.state_ref.refs_0_, bf16[2,128,640]{2,1,0:T(8,128)(2,1)S(1)} %copy-done, f32[2,256]{1,0:T(2,128)S(1)} %copy-done.2, bf16[2,128,128]{2,1,0:T(8,128)(2,1)S(1)} %copy-done.1, ...), custom_call_target="tpu_custom_call" | custom-call | flops 335544320 | bytes 25165824 | tf_op jit(solution)/shard_map/backward_second/pallas_call | solution.py:355
  40.8 1.6 %collective-permute-start = (bf16[128,768]{1,0:T(8,128)(2,1)S(1)}, bf16[128,768]{1,0:T(8,128)(2,1)S(1)}, u32[]{:S(2)}, u32[]{:S(2)}) collective-permute-start(bf16[128,768]{1,0:T(8,128)(2,1)S(1)} %get-tuple-element.56), channel_id=1, source_target_pairs={{0,16},{8,24},{16,0},{24,8},{1,17},{9,25},{17,1},{25,9},{2,18},{10... | collective-permute-start | bytes 589832 | tf_op jit(solution)/shard_map/ppermute | solution.py:250
  42.4 6.5 %backward_first.1 = (bf16[128,128]{1,0:T(8,128)(2,1)}, bf16[128,768]{1,0:T(8,128)(2,1)S(1)}) custom-call(s32[1]{0:T(128)} %get-tuple-element.31.refs_0_, f32[1024,128]{1,0:T(8,128)S(1)} %get-tuple-element.43.refs_1_, bf16[2,128,640]{2,1,0:T(8,128)(2,1)S(1)} %copy-done, f32[2,256]{1,0:T(2,128)S(1)} %copy-done.2, bf16[2,128,128]{2,1,0:T(8,128)(2,1)S(1)} %copy-done.1, ...), custom_call_target="tpu_custom_call" | custom-call | flops 335544320 | bytes 25165824 | tf_op jit(solution)/shard_map/backward_first/pallas_call | solution.py:368
  49.0 0.0 collective-permute-done
  49.1 0.1 collective-permute-start.1
  49.1 1.7 %collective-permute-done.1.other_both = bf16[2,128,768]{2,1,0:T(8,128)(2,1)S(1)} collective-permute-done((bf16[2,128,768]{2,1,0:T(8,128)(2,1)S(1)}, bf16[2,128,768]{2,1,0:T(8,128)(2,1)S(1)}, u32[]{:S(2)}, u32[]{:S(2)}) %collective-permute-start.1) | collective-permute-done | bytes 393248 | tf_op jit(solution)/shard_map/ppermute | solution.py:250
  50.9 0.6 %collective-permute-start.2 = (bf16[128,768]{1,0:T(8,128)(2,1)S(1)}, bf16[128,768]{1,0:T(8,128)(2,1)S(1)}, u32[]{:S(2)}, u32[]{:S(2)}) collective-permute-start(bf16[128,768]{1,0:T(8,128)(2,1)S(1)} %fusion.own_0), channel_id=1, source_target_pairs={{0,16},{8,24},{16,0},{24,8},{1,17},{9,25},{17,1},{25,9},{2,18},{10... | collective-permute-start | bytes 589832 | tf_op jit(solution)/shard_map/ppermute | solution.py:250
  51.5 6.4 %collective-permute-done.2.other_0 = bf16[128,768]{1,0:T(8,128)(2,1)S(1)} collective-permute-done((bf16[128,768]{1,0:T(8,128)(2,1)S(1)}, bf16[128,768]{1,0:T(8,128)(2,1)S(1)}, u32[]{:S(2)}, u32[]{:S(2)}) %collective-permute-start.2) | collective-permute-done | bytes 196640 | tf_op jit(solution)/shard_map/ppermute | solution.py:250
  57.9 0.9 %add_grads.1 = (f32[2,128,640]{2,1,0:T(8,128)}, f32[2,128,128]{2,1,0:T(8,128)}) custom-call(bf16[128,768]{1,0:T(8,128)(2,1)S(1)} %fusion.own_0, bf16[128,768]{1,0:T(8,128)(2,1)S(1)} %collective-permute-done.2.other_0, bf16[2,128,768]{2,1,0:T(8,128)(2,1)S(1)} %pad_maximum_fusion.own_both, bf16[2,128,768]{2,1,0:T(8,128)(2,1)S(1)} %collective-permute-done.1.other_both), custom_call_target="tpu_custom_call" | custom-call | tf_op jit(solution)/shard_map/add_grads/pallas_call | solution.py:389
  (3 shorter events, 0.1 us)
Async XLA Ops:
  0.6 25.1 %copy-start.1 = (bf16[2,128,128]{2,1,0:T(8,128)(2,1)S(1)}, bf16[2,128,128]{2,1,0:T(8,128)(2,1)}, u32[]{:S(2)}) copy-start(bf16[2,128,128]{2,1,0:T(8,128)(2,1)} %refs_4_.1) | copy-start | bytes 196612
  0.6 25.1 %copy-start.2 = (f32[2,256]{1,0:T(2,128)S(1)}, f32[2,256]{1,0:T(2,128)}, u32[]{:S(2)}) copy-start(f32[2,256]{1,0:T(2,128)} %refs_3_.3) | copy-start | bytes 6148
  0.7 25.1 %copy-start = (bf16[2,128,640]{2,1,0:T(8,128)(2,1)S(1)}, bf16[2,128,640]{2,1,0:T(8,128)(2,1)}, u32[]{:S(2)}) copy-start(bf16[2,128,640]{2,1,0:T(8,128)(2,1)} %refs_2_.3) | copy-start | bytes 983044
  0.7 25.1 %copy-start.5 = (f32[2,128]{1,0:T(2,128)S(1)}, f32[2,128]{1,0:T(2,128)}, u32[]{:S(2)}) copy-start(f32[2,128]{1,0:T(2,128)} %b_out.1) | copy-start | bytes 3076
  0.7 25.1 %copy-start.4 = (f32[2,256]{1,0:T(2,128)S(1)}, f32[2,256]{1,0:T(2,128)}, u32[]{:S(2)}) copy-start(f32[2,256]{1,0:T(2,128)} %shift.1) | copy-start | bytes 6148
  0.7 25.1 %copy-start.3 = (f32[2,640]{1,0:T(2,128)S(1)}, f32[2,640]{1,0:T(2,128)}, u32[]{:S(2)}) copy-start(f32[2,640]{1,0:T(2,128)} %b.1) | copy-start | bytes 15364
  40.8 8.1 %collective-permute-start = (bf16[128,768]{1,0:T(8,128)(2,1)S(1)}, bf16[128,768]{1,0:T(8,128)(2,1)S(1)}, u32[]{:S(2)}, u32[]{:S(2)}) collective-permute-start(bf16[128,768]{1,0:T(8,128)(2,1)S(1)} %get-tuple-element.56), channel_id=1, source_target_pairs={{0,16},{8,24},{16,0},{24,8},{1,17},{9,25},{17,1},{25,9},{2,18},{10... | collective-permute-start | bytes 589832 | tf_op jit(solution)/shard_map/ppermute | solution.py:250
  49.1 1.8 %collective-permute-start.1 = (bf16[2,128,768]{2,1,0:T(8,128)(2,1)S(1)}, bf16[2,128,768]{2,1,0:T(8,128)(2,1)S(1)}, u32[]{:S(2)}, u32[]{:S(2)}) collective-permute-start(bf16[2,128,768]{2,1,0:T(8,128)(2,1)S(1)} %pad_maximum_fusion.own_both), channel_id=1, source_target_pairs={{0,8},{8,0},{16,24},{24,16},{1,9},{9,1},{17,25},{25,17},{2,10},{10... | collective-permute-start | bytes 1179656 | tf_op jit(solution)/shard_map/ppermute | solution.py:250
  50.9 7.0 %collective-permute-start.2 = (bf16[128,768]{1,0:T(8,128)(2,1)S(1)}, bf16[128,768]{1,0:T(8,128)(2,1)S(1)}, u32[]{:S(2)}, u32[]{:S(2)}) collective-permute-start(bf16[128,768]{1,0:T(8,128)(2,1)S(1)} %fusion.own_0), channel_id=1, source_target_pairs={{0,16},{8,24},{16,0},{24,8},{1,17},{9,25},{17,1},{25,9},{2,18},{10... | collective-permute-start | bytes 589832 | tf_op jit(solution)/shard_map/ppermute | solution.py:250

commit v8 on v7

--- a/solution.py
+++ b/solution.py
@@ -25,16 +25,19 @@
     return lax.dot_general(a, b, (dims, ((), ())), preferred_element_type=F32)
 
 
+def lane_mean(x):
+    c = x.shape[1]
+    return dot(x.astype(BF16), jnp.full((c, c), 1.0 / c, BF16))
+
+
 def norm_parts(x):
-    centred = x - jnp.mean(x, axis=-1, keepdims=True)
-    rstd = lax.rsqrt(jnp.mean(centred * centred, axis=-1, keepdims=True) + NORM_EPSILON)
+    centred = x.astype(F32) - lane_mean(x)
+    rstd = lax.rsqrt(lane_mean(centred * centred) + NORM_EPSILON)
     return centred * rstd, rstd
 
 
 def norm_vjp(x_hat, rstd, grad):
-    mean_grad = jnp.mean(grad, axis=-1, keepdims=True)
-    mean_prod = jnp.mean(grad * x_hat, axis=-1, keepdims=True)
-    return rstd * (grad - mean_grad - x_hat * mean_prod)
+    return rstd * (grad - lane_mean(grad) - x_hat * lane_mean(grad * x_hat))
 
 
 def pair_mask_block(length, first_row, rows, n, lanes):
@@ -60,7 +63,7 @@
 
 
 def mix(product, u, c, gain, shift, w_out, b_out):
-    p_hat, p_rstd = norm_parts(product.astype(F32))
+    p_hat, p_rstd = norm_parts(product)
     mixed = (p_hat * gain[u : u + 1, c:] + shift[u : u + 1, c:]).astype(BF16)
     branch = dot(mixed, w_out[u]) + b_out[u : u + 1, :]
     return p_hat, p_rstd, mixed, branch
@@ -128,7 +131,7 @@
             x = joined(state_ref, t * per, per, cells, 0) if u == 0 else next_s[here, :]
             mask = pair_mask_block(length, first, BLOCK_ROWS, n, c)
             x_hat, rstd, normed, s_left, s_right, left, right, gate = project(
-                x.astype(F32), mask, u, w, b, gain, shift
+                x, mask, u, w, b, gain, shift
             )
             edges_s[0, here, :] = left
             edges_s[1, here, :] = right
@@ -136,7 +139,7 @@
             slopes_s[1, here, :] = s_right
             gate_s[here, :] = gate
             hat_s[here, :] = x_hat
-            rstd_s[here, :] = jnp.broadcast_to(rstd, x_hat.shape)
+            rstd_s[here, :] = rstd
             normed_s[here, :] = normed
             if u == 0:
                 for r in range(BLOCK_ROWS):
@@ -154,18 +157,12 @@
                 product.astype(BF16), u, c, gain, shift, w_out, b_out
             )
             p_hat_s[here, :] = p_hat
-            p_rstd_s[here, :] = jnp.broadcast_to(p_rstd, p_hat.shape)
+            p_rstd_s[here, :] = p_rstd
             mixed_s[here, :] = mixed
             branch_s[here, :] = branch
             if u == 0:
                 x = joined(state_ref, t * per, per, cells, 0).astype(F32)
                 next_s[here, :] = (x + gate_s[here, :] * branch).astype(BF16)
-
-
-def weight_grads(normed_s, d_pre_s, mixed_s, d_branch_s, grads_ref):
-    width = d_pre_s.shape[1]
-    grads_ref[:, :width] = dot(normed_s[...], d_pre_s[...], ((0,), (0,))).astype(BF16)
-    grads_ref[:, width:] = dot(mixed_s[...], d_branch_s[...], ((0,), (0,))).astype(BF16)
 
 
 def backward(n, u, *refs):
@@ -174,9 +171,12 @@
     up_in_ref, w, gain, w_out = refs[:4]
     (edges_s, slopes_s, gate_s, hat_s, rstd_s) = refs[4:9]
     (p_hat_s, p_rstd_s, branch_s, normed_s, mixed_s) = refs[9 : 4 + KEPT]
-    up_ref, grads_ref, d_product_s, d_edges_s, d_branch_s, d_pre_s = refs[4 + KEPT :]
+    up_ref, grads_ref, d_product_s, d_edges_s, d_pre_s, sums_s = refs[4 + KEPT :]
     c, h = w.shape[1], edges_s.shape[2]
     blocks = n // BLOCK_ROWS
+
+    width = 4 * h + c
+    sums_s[...] = jnp.zeros_like(sums_s)
 
     def upstream(t, here):
         if u == 0:
@@ -204,7 +204,7 @@
             gain,
             w_out,
         )
-        d_branch_s[here, :] = d_branch
+        sums_s[:, width:] += dot(mixed_s[here, :], d_branch, ((0,), (0,)))
         d_pre_s[here, 4 * h :] = d_gate
         if u == 1:
             for r in range(BLOCK_ROWS):
@@ -236,6 +236,7 @@
         )
         for g in range(4):
             d_pre_s[here, g * h : (g + 1) * h] = grads[g]
+        sums_s[:, :width] += dot(normed_s[here, :], d_pre_s[here, :], ((0,), (0,)))
         if u == 1:
             up_ref[here, :] = input_pullback(here, upstream(t, here))
 
@@ -243,7 +244,7 @@
         cells = up_ref.shape[0]
         own = pl.ds(pl.multiple_of(index_ref[0] * cells, cells), cells)
         up_ref[...] = input_pullback(own, up_in_ref[own, :]).astype(BF16)
-    weight_grads(normed_s, d_pre_s, mixed_s, d_branch_s, grads_ref)
+    grads_ref[...] = sums_s[...].astype(BF16)
 
 
 def exchange(value, axis, size, step):
@@ -350,8 +351,8 @@
         name="forward",
     )(state, proj_weight, proj_bias, norm_gain, norm_shift, out_weight, out_bias)
 
-    work = [scratch(double), scratch(double), scratch(narrow)]
-    work.append(pltpu.VMEM((pairs, width), BF16))
+    work = [scratch(double), scratch(double)]
+    work += [pltpu.VMEM((pairs, width), BF16), pltpu.VMEM(grads.shape, F32)]
     up_1, grads_1 = pl.pallas_call(
         functools.partial(backward, n, 1),
         out_shape=(jax.ShapeDtypeStruct((pairs, c), F32), grads),
@@ -597,7 +598,7 @@
         n, c = args[0].shape[2:]
         rows = n // parts
         fits = 20 * n * n * c * 4 <= CROP_BUDGET
-        even = args[7].shape[1] == c and groups > 1 and groups & (groups - 1) == 0 and BLOCK_ROWS % rows == 0 and n % 16 == 0
+        even = c & (c - 1) == 0 and args[7].shape[1] == c and groups > 1 and groups & (groups - 1) == 0 and BLOCK_ROWS % rows == 0 and n % 16 == 0
         body = functools.partial(crop_shards, groups, parts) if fits and even else shards
         return spread_over(body)(*args)
 

time: 59.1 us -> 62 us (1.049)
  Pallas kernels: 24.3 us -> 27.3 us
    pallas_call x1, Pallas kernels: 8.81 us -> 10.2 us  [crop_shards(): pl.pallas_call(functools.partial(forward, n), out_shape=kept * 2, in_spec...]
    pallas_call x1, Pallas kernels: 6.55 us -> 7.61 us  [crop_shards(): pl.pallas_call(functools.partial(backward, n, 0), out_shape=(jax.ShapeDty...]
  transfers between devices with their start and end apart: 3 -> 3, of which waited for: 2 -> 2; matrix products, arithmetic and copies ran while one was open for 0% -> 0% of each run, Pallas kernels for 11% -> 12%
where the time goes in v8:
time: 62 us; the launch traced here: 61.8 us
  Pallas kernels  27.3 us (44%)
  blocking collectives  23.3 us (38%)
  waiting for transfers between devices  8.12 us (13%)
  starting transfers between devices  2.23 us (4%)
  between operations  0.76 us (1%)
    all_to_all x1, blocking collectives, crop_shards(): state = lax.all_to_all(sent, 'dap', split_axis=0, concat_axis=0, tiled=True)  23.3 us
    pallas_call x1, Pallas kernels, crop_shards(): pl.pallas_call(functools.partial(forward, n), out_shape=kept * 2, in_spec...  10.2 us
    ppermute x3, waiting for transfers between devices, exchange(): return lax.ppermute(value, axis, [(d, d ^ step) for d in range(size)])  8.12 us
    pallas_call x1, Pallas kernels, crop_shards(): pl.pallas_call(functools.partial(backward, n, 0), out_shape=(jax.ShapeDty...  7.61 us
    pallas_call x1, Pallas kernels, crop_shards(): pl.pallas_call(functools.partial(backward, n, 1), out_shape=(jax.ShapeDty...  6.72 us
    ppermute x3, starting transfers between devices, exchange(): return lax.ppermute(value, axis, [(d, d ^ step) for d in range(size)])  2.23 us
    pallas_call x1, Pallas kernels, crop_shards(): pl.pallas_call(prepare, out_shape=(jax.ShapeDtypeStruct((parts, 2 * cells...  1.76 us
  transfers between devices with their start and end apart: 3, of which 2 were waited for; matrix products, arithmetic and copies ran while one was open for 0% of the time, Pallas kernels for 12%

profile of v8, /device:TPU:0, one launch (start us, length us, event | category | flops | bytes accessed | tf_op | source)
XLA Modules:
  0.0 61.8 jit_solution(12607437257661582870)
XLA Ops:
  0.6 0.0 copy-start.1
  0.6 0.0 copy-start.2
  0.7 0.0 copy-start
  0.7 0.0 copy-start.5
  0.7 0.0 copy-start.4
  0.7 0.0 copy-start.3
  0.7 1.8 %prepare.1 = (bf16[8,272,128]{2,1,0:T(8,128)(2,1)}, s32[1]{0:T(128)}) custom-call(s32[1]{0:T(128)} %bitcast.index_ref, bf16[128,128]{1,0:T(8,128)(2,1)} %bitcast.14, s32[4,32]{1,0:T(4,128)} %bitcast.16, bf16[128,128]{1,0:T(8,128)(2,1)} %bitcast.15), custom_call_target="tpu_custom_call" | custom-call | tf_op jit(solution)/shard_map/prepare/pallas_call | solution.py:324
  2.5 23.3 %all_to_all.5.state_ref.refs_0_ = bf16[8,272,128]{2,1,0:T(8,128)(2,1)S(1)} all-to-all(bf16[8,272,128]{2,1,0:T(8,128)(2,1)} %get-tuple-element.32), channel_id=1, replica_groups=mesh['dp'=4,'dap'=8] {'dap'}, dimensions={0} | all-to-all | bytes 1114112 | tf_op jit(solution)/shard_map/all_to_all | solution.py:341
  25.8 0.0 copy-done.1
  25.8 0.0 copy-done.2
  25.8 0.0 copy-done
  25.8 0.0 copy-done.5
  25.8 0.0 copy-done.4
  25.8 0.0 copy-done.3
  25.8 10.2 %forward.1 = (f32[2,1032,128]{2,1,0:T(8,128)S(1)}, f32[2,1032,128]{2,1,0:T(8,128)S(1)}, f32[1032,128]{1,0:T(8,128)S(1)}, f32[1032,128]{1,0:T(8,128)S(1)}, f32[10...) custom-call(bf16[8,272,128]{2,1,0:T(8,128)(2,1)S(1)} %all_to_all.5.s, ...), custom_call_target="tpu_custom_call" | custom-call | flops 335544320 | bytes 33554432 | tf_op jit(solution)/shard_map/forward/pallas_call | solution.py:343
  36.0 6.7 %backward_second.1 = (f32[1024,128]{1,0:T(8,128)S(1)}, bf16[128,768]{1,0:T(8,128)(2,1)S(1)}) custom-call(bf16[8,272,128]{2,1,0:T(8,128)(2,1)S(1)} %all_to_all.5.state_ref.refs_0_, bf16[2,128,640]{2,1,0:T(8,128)(2,1)S(1)} %copy-done, f32[2,256]{1,0:T(2,128)S(1)} %copy-done.2, bf16[2,128,128]{2,1,0:T(8,128)(2,1)S(1)} %copy-done.1, ...), custom_call_target="tpu_custom_call" | custom-call | flops 335544320 | bytes 25165824 | tf_op jit(solution)/shard_map/backward_second/pallas_call | solution.py:356
  42.7 1.6 %collective-permute-start = (bf16[128,768]{1,0:T(8,128)(2,1)S(1)}, bf16[128,768]{1,0:T(8,128)(2,1)S(1)}, u32[]{:S(2)}, u32[]{:S(2)}) collective-permute-start(bf16[128,768]{1,0:T(8,128)(2,1)S(1)} %get-tuple-element.56), channel_id=1, source_target_pairs={{0,16},{8,24},{16,0},{24,8},{1,17},{9,25},{17,1},{25,9},{2,18},{10... | collective-permute-start | bytes 589832 | tf_op jit(solution)/shard_map/ppermute | solution.py:251
  44.3 7.6 %backward_first.1 = (bf16[128,128]{1,0:T(8,128)(2,1)}, bf16[128,768]{1,0:T(8,128)(2,1)S(1)}) custom-call(s32[1]{0:T(128)} %get-tuple-element.31.refs_0_, f32[1024,128]{1,0:T(8,128)S(1)} %get-tuple-element.43.refs_1_, bf16[2,128,640]{2,1,0:T(8,128)(2,1)S(1)} %copy-done, f32[2,256]{1,0:T(2,128)S(1)} %copy-done.2, bf16[2,128,128]{2,1,0:T(8,128)(2,1)S(1)} %copy-done.1, ...), custom_call_target="tpu_custom_call" | custom-call | flops 335544320 | bytes 25165824 | tf_op jit(solution)/shard_map/backward_first/pallas_call | solution.py:369
  51.9 0.0 collective-permute-done
  52.0 0.1 collective-permute-start.1
  52.1 1.7 %collective-permute-done.1.other_both = bf16[2,128,768]{2,1,0:T(8,128)(2,1)S(1)} collective-permute-done((bf16[2,128,768]{2,1,0:T(8,128)(2,1)S(1)}, bf16[2,128,768]{2,1,0:T(8,128)(2,1)S(1)}, u32[]{:S(2)}, u32[]{:S(2)}) %collective-permute-start.1) | collective-permute-done | bytes 393248 | tf_op jit(solution)/shard_map/ppermute | solution.py:251
  53.9 0.6 collective-permute-start.2
  54.5 6.4 %collective-permute-done.2.other_0 = bf16[128,768]{1,0:T(8,128)(2,1)S(1)} collective-permute-done((bf16[128,768]{1,0:T(8,128)(2,1)S(1)}, bf16[128,768]{1,0:T(8,128)(2,1)S(1)}, u32[]{:S(2)}, u32[]{:S(2)}) %collective-permute-start.2) | collective-permute-done | bytes 196640 | tf_op jit(solution)/shard_map/ppermute | solution.py:251
  60.9 0.9 %add_grads.1 = (f32[2,128,640]{2,1,0:T(8,128)}, f32[2,128,128]{2,1,0:T(8,128)}) custom-call(bf16[128,768]{1,0:T(8,128)(2,1)S(1)} %fusion.own_0, bf16[128,768]{1,0:T(8,128)(2,1)S(1)} %collective-permute-done.2.other_0, bf16[2,128,768]{2,1,0:T(8,128)(2,1)S(1)} %pad_maximum_fusion.own_both, bf16[2,128,768]{2,1,0:T(8,128)(2,1)S(1)} %collective-permute-done.1.other_both), custom_call_target="tpu_custom_call" | custom-call | tf_op jit(solution)/shard_map/add_grads/pallas_call | solution.py:390
  (3 shorter events, 0.1 us)
Async XLA Ops:
  0.6 25.1 %copy-start.1 = (bf16[2,128,128]{2,1,0:T(8,128)(2,1)S(1)}, bf16[2,128,128]{2,1,0:T(8,128)(2,1)}, u32[]{:S(2)}) copy-start(bf16[2,128,128]{2,1,0:T(8,128)(2,1)} %refs_4_.1) | copy-start | bytes 196612
  0.6 25.1 %copy-start.2 = (f32[2,256]{1,0:T(2,128)S(1)}, f32[2,256]{1,0:T(2,128)}, u32[]{:S(2)}) copy-start(f32[2,256]{1,0:T(2,128)} %refs_3_.3) | copy-start | bytes 6148
  0.7 25.1 %copy-start = (bf16[2,128,640]{2,1,0:T(8,128)(2,1)S(1)}, bf16[2,128,640]{2,1,0:T(8,128)(2,1)}, u32[]{:S(2)}) copy-start(bf16[2,128,640]{2,1,0:T(8,128)(2,1)} %refs_2_.3) | copy-start | bytes 983044
  0.7 25.1 %copy-start.5 = (f32[2,128]{1,0:T(2,128)S(1)}, f32[2,128]{1,0:T(2,128)}, u32[]{:S(2)}) copy-start(f32[2,128]{1,0:T(2,128)} %b_out.1) | copy-start | bytes 3076
  0.7 25.1 %copy-start.4 = (f32[2,256]{1,0:T(2,128)S(1)}, f32[2,256]{1,0:T(2,128)}, u32[]{:S(2)}) copy-start(f32[2,256]{1,0:T(2,128)} %shift.1) | copy-start | bytes 6148
  0.7 25.1 %copy-start.3 = (f32[2,640]{1,0:T(2,128)S(1)}, f32[2,640]{1,0:T(2,128)}, u32[]{:S(2)}) copy-start(f32[2,640]{1,0:T(2,128)} %b.1) | copy-start | bytes 15364
  42.7 9.2 %collective-permute-start = (bf16[128,768]{1,0:T(8,128)(2,1)S(1)}, bf16[128,768]{1,0:T(8,128)(2,1)S(1)}, u32[]{:S(2)}, u32[]{:S(2)}) collective-permute-start(bf16[128,768]{1,0:T(8,128)(2,1)S(1)} %get-tuple-element.56), channel_id=1, source_target_pairs={{0,16},{8,24},{16,0},{24,8},{1,17},{9,25},{17,1},{25,9},{2,18},{10... | collective-permute-start | bytes 589832 | tf_op jit(solution)/shard_map/ppermute | solution.py:251
  52.0 1.8 %collective-permute-start.1 = (bf16[2,128,768]{2,1,0:T(8,128)(2,1)S(1)}, bf16[2,128,768]{2,1,0:T(8,128)(2,1)S(1)}, u32[]{:S(2)}, u32[]{:S(2)}) collective-permute-start(bf16[2,128,768]{2,1,0:T(8,128)(2,1)S(1)} %pad_maximum_fusion.own_both), channel_id=1, source_target_pairs={{0,8},{8,0},{16,24},{24,16},{1,9},{9,1},{17,25},{25,17},{2,10},{10... | collective-permute-start | bytes 1179656 | tf_op jit(solution)/shard_map/ppermute | solution.py:251
  53.9 7.0 %collective-permute-start.2 = (bf16[128,768]{1,0:T(8,128)(2,1)S(1)}, bf16[128,768]{1,0:T(8,128)(2,1)S(1)}, u32[]{:S(2)}, u32[]{:S(2)}) collective-permute-start(bf16[128,768]{1,0:T(8,128)(2,1)S(1)} %fusion.own_0), channel_id=1, source_target_pairs={{0,16},{8,24},{16,0},{24,8},{1,17},{9,25},{17,1},{25,9},{2,18},{10... | collective-permute-start | bytes 589832 | tf_op jit(solution)/shard_map/ppermute | solution.py:251

commit v9 on v8

--- a/solution.py
+++ b/solution.py
@@ -25,19 +25,17 @@
     return lax.dot_general(a, b, (dims, ((), ())), preferred_element_type=F32)
 
 
-def lane_mean(x):
-    c = x.shape[1]
-    return dot(x.astype(BF16), jnp.full((c, c), 1.0 / c, BF16))
-
-
 def norm_parts(x):
-    centred = x.astype(F32) - lane_mean(x)
-    rstd = lax.rsqrt(lane_mean(centred * centred) + NORM_EPSILON)
-    return centred * rstd, rstd
+    x = x.astype(F32)
+    centred = x - jnp.mean(x, axis=-1, keepdims=True)
+    rstd = lax.rsqrt(jnp.mean(centred * centred, axis=-1, keepdims=True) + NORM_EPSILON)
+    return centred * rstd, jnp.broadcast_to(rstd, x.shape)
 
 
 def norm_vjp(x_hat, rstd, grad):
-    return rstd * (grad - lane_mean(grad) - x_hat * lane_mean(grad * x_hat))
+    mean_grad = jnp.mean(grad, axis=-1, keepdims=True)
+    mean_prod = jnp.mean(grad * x_hat, axis=-1, keepdims=True)
+    return rstd * (grad - mean_grad - x_hat * mean_prod)
 
 
 def pair_mask_block(length, first_row, rows, n, lanes):
@@ -48,12 +46,11 @@
     return inside.reshape(rows * n, lanes)
 
 
-def project(x, mask, u, w, b, gain, shift):
-    c = x.shape[1]
+def project(x, mask, w, b, gain, shift):
     x_hat, rstd = norm_parts(x)
-    normed = (x_hat * gain[u : u + 1, :c] + shift[u : u + 1, :c]).astype(BF16)
-    pre = dot(normed, w[u]) + b[u : u + 1, :]
-    h = (pre.shape[1] - c) // 4
+    normed = (x_hat * gain + shift).astype(BF16)
+    pre = dot(normed, w) + b
+    h = (pre.shape[1] - x.shape[1]) // 4
     s_left = sigmoid(pre[:, h : 2 * h]) * mask
     s_right = sigmoid(pre[:, 3 * h : 4 * h]) * mask
     left = s_left * pre[:, :h]
@@ -62,34 +59,33 @@
     return x_hat, rstd, normed, s_left, s_right, left, right, gate
 
 
-def mix(product, u, c, gain, shift, w_out, b_out):
+def mix(product, gain, shift, w_out, b_out):
     p_hat, p_rstd = norm_parts(product)
-    mixed = (p_hat * gain[u : u + 1, c:] + shift[u : u + 1, c:]).astype(BF16)
-    branch = dot(mixed, w_out[u]) + b_out[u : u + 1, :]
-    return p_hat, p_rstd, mixed, branch
-
-
-def unmix(up, gate, branch, p_hat, p_rstd, u, c, gain, w_out):
+    mixed = (p_hat * gain + shift).astype(BF16)
+    return p_hat, p_rstd, mixed, dot(mixed, w_out) + b_out
+
+
+def unmix(up, gate, branch, p_hat, p_rstd, gain, w_out):
     d_branch = up * gate
     d_gate = (d_branch * branch * (1.0 - gate)).astype(BF16)
     d_branch = d_branch.astype(BF16)
-    d_mixed = dot(d_branch, w_out[u], ((1,), (1,))) * gain[u : u + 1, c:]
+    d_mixed = dot(d_branch, w_out, ((1,), (1,))) * gain
     return d_branch, d_gate, norm_vjp(p_hat, p_rstd, d_mixed)
 
 
-def contract(n, first, row_of, x, y):
+def contract(n, first, x, y, unroll=True):
     lanes = y.shape[1]
     tiles = (n // 8, 8, lanes)
 
     def step(e, totals):
         block = y[pl.ds(pl.multiple_of(e * n, n), n), :].reshape(tiles)
         return tuple(
-            totals[a] + x[pl.ds(row_of(first + a, e), 8, stride=0), :][None] * block
+            totals[a] + x[pl.ds((first + a) * n + e, 8, stride=0), :][None] * block
             for a in range(BLOCK_ROWS)
         )
 
     zero = jnp.zeros(tiles, F32)
-    totals = lax.fori_loop(0, n, step, (zero,) * BLOCK_ROWS, unroll=True)
+    totals = lax.fori_loop(0, n, step, (zero,) * BLOCK_ROWS, unroll=unroll)
     return jnp.stack(totals).reshape(BLOCK_ROWS * n, lanes)
 
 
@@ -111,121 +107,119 @@
     return jnp.concatenate([ref[first + q, span, :] for q in range(count)], axis=0)
 
 
+def block(t, rows, n):
+    return pl.ds(pl.multiple_of(t * rows * n, rows * n), rows * n)
+
+
 def forward(n, state_ref, w, b, gain, shift, w_out, b_out, *refs):
-    kept, (right_t_s, next_s) = (refs[:KEPT], refs[KEPT : 2 * KEPT]), refs[2 * KEPT :]
+    (edges_s, slopes_s, gate_s, hat_s, rstd_s) = refs[:5]
+    (p_hat_s, p_rstd_s, branch_s, normed_s, mixed_s) = refs[5:KEPT]
+    (next_s,) = refs[KEPT:]
     parts, _, c = state_ref.shape
     rows = n // parts
     cells = rows * n
     length = crop_length(state_ref, cells)
-    per = BLOCK_ROWS // rows
     blocks = n // BLOCK_ROWS
 
-    for u in range(2):
-        (edges_s, slopes_s, gate_s, hat_s, rstd_s) = kept[u][:5]
-        (p_hat_s, p_rstd_s, branch_s, normed_s, mixed_s) = kept[u][5:]
-
-        @pl.loop(0, blocks)
+    @pl.loop(0, parts)
+    def _(t):
+        next_s[block(t, rows, n), :] = state_ref[t, :cells, :]
+
+    @pl.loop(0, 2)
+    def _(u):
+        bias, gains, shifts, bias_out = (
+            jnp.where(u == 0, ref[0:1, :], ref[1:2, :]) for ref in (b, gain, shift, b_out)
+        )
+
+        @pl.loop(0, blocks, unroll=2)
         def _(t):
             first = t * BLOCK_ROWS
-            here = pl.ds(pl.multiple_of(first * n, BLOCK_ROWS * n), BLOCK_ROWS * n)
-            x = joined(state_ref, t * per, per, cells, 0) if u == 0 else next_s[here, :]
+            here = block(t, BLOCK_ROWS, n)
             mask = pair_mask_block(length, first, BLOCK_ROWS, n, c)
             x_hat, rstd, normed, s_left, s_right, left, right, gate = project(
-                x, mask, u, w, b, gain, shift
+                next_s[here, :], mask, w[u], bias, gains[:, :c], shifts[:, :c]
             )
-            edges_s[0, here, :] = left
-            edges_s[1, here, :] = right
-            slopes_s[0, here, :] = s_left
-            slopes_s[1, here, :] = s_right
-            gate_s[here, :] = gate
-            hat_s[here, :] = x_hat
-            rstd_s[here, :] = rstd
-            normed_s[here, :] = normed
-            if u == 0:
-                for r in range(BLOCK_ROWS):
-                    right_t_s[pl.ds(first + r, n, stride=n), :] = right[r * n : (r + 1) * n]
-
-        @pl.loop(0, blocks)
+            edges_s[u, 0, here, :] = left
+            edges_s[u, 1, here, :] = right
+            for r in range(BLOCK_ROWS):
+                swapped = pl.ds(first + r, n, stride=n)
+                edges_s[u, 2, swapped, :] = right[r * n : (r + 1) * n]
+                edges_s[u, 3, swapped, :] = left[r * n : (r + 1) * n]
+            slopes_s[u, 0, here, :] = s_left
+            slopes_s[u, 1, here, :] = s_right
+            gate_s[u, here, :] = gate
+            hat_s[u, here, :] = x_hat
+            rstd_s[u, here, :] = rstd
+            normed_s[u, here, :] = normed
+
+        @pl.loop(0, blocks, unroll=2)
         def _(t):
-            first = t * BLOCK_ROWS
-            here = pl.ds(pl.multiple_of(first * n, BLOCK_ROWS * n), BLOCK_ROWS * n)
-            if u == 0:
-                product = contract(n, first, lambda i, k: i * n + k, edges_s.at[0], right_t_s)
-            else:
-                product = contract(n, first, lambda i, k: k * n + i, edges_s.at[0], edges_s.at[1])
+            here = block(t, BLOCK_ROWS, n)
+            product = contract(n, t * BLOCK_ROWS, edges_s.at[u, 3 * u], edges_s.at[u, 2 - u])
             p_hat, p_rstd, mixed, branch = mix(
-                product.astype(BF16), u, c, gain, shift, w_out, b_out
+                product.astype(BF16), gains[:, c:], shifts[:, c:], w_out[u], bias_out
             )
-            p_hat_s[here, :] = p_hat
-            p_rstd_s[here, :] = p_rstd
-            mixed_s[here, :] = mixed
-            branch_s[here, :] = branch
-            if u == 0:
-                x = joined(state_ref, t * per, per, cells, 0).astype(F32)
-                next_s[here, :] = (x + gate_s[here, :] * branch).astype(BF16)
-
-
-def backward(n, u, *refs):
+            p_hat_s[u, here, :] = p_hat
+            p_rstd_s[u, here, :] = p_rstd
+            mixed_s[u, here, :] = mixed
+            branch_s[u, here, :] = branch
+            x = next_s[here, :].astype(F32)
+            next_s[here, :] = (x + gate_s[u, here, :] * branch).astype(BF16)
+
+
+def backward(n, u, unmix_rows, unroll, *refs):
     if u == 0:
         index_ref, refs = refs[0], refs[1:]
     up_in_ref, w, gain, w_out = refs[:4]
-    (edges_s, slopes_s, gate_s, hat_s, rstd_s) = refs[4:9]
-    (p_hat_s, p_rstd_s, branch_s, normed_s, mixed_s) = refs[9 : 4 + KEPT]
+    (edges_s, slopes_s, gate_s, hat_s, rstd_s) = (ref.at[u] for ref in refs[4:9])
+    (p_hat_s, p_rstd_s, branch_s, normed_s, mixed_s) = (ref.at[u] for ref in refs[9 : 4 + KEPT])
     up_ref, grads_ref, d_product_s, d_edges_s, d_pre_s, sums_s = refs[4 + KEPT :]
     c, h = w.shape[1], edges_s.shape[2]
-    blocks = n // BLOCK_ROWS
-
     width = 4 * h + c
     sums_s[...] = jnp.zeros_like(sums_s)
 
-    def upstream(t, here):
+    def upstream(t, rows):
         if u == 0:
-            return up_in_ref[here, :]
-        rows = n // up_in_ref.shape[0]
-        per = BLOCK_ROWS // rows
-        return joined(up_in_ref, t * per, per, rows * n, 1).astype(F32)
+            return up_in_ref[block(t, rows, n), :]
+        own = n // up_in_ref.shape[0]
+        per = rows // own
+        return joined(up_in_ref, t * per, per, own * n, 1).astype(F32)
 
     def input_pullback(here, up):
         d_normed = dot(d_pre_s[here, :], w[u], ((1,), (1,))) * gain[u : u + 1, :c]
         return up + norm_vjp(hat_s[here, :], rstd_s[here, :], d_normed)
 
-    @pl.loop(0, blocks)
+    @pl.loop(0, n // unmix_rows)
     def _(t):
-        first = t * BLOCK_ROWS
-        here = pl.ds(pl.multiple_of(first * n, BLOCK_ROWS * n), BLOCK_ROWS * n)
+        here = block(t, unmix_rows, n)
         d_branch, d_gate, d_product = unmix(
-            upstream(t, here),
+            upstream(t, unmix_rows),
             gate_s[here, :],
             branch_s[here, :],
             p_hat_s[here, :],
             p_rstd_s[here, :],
-            u,
-            c,
-            gain,
-            w_out,
+            gain[u : u + 1, c:],
+            w_out[u],
         )
         sums_s[:, width:] += dot(mixed_s[here, :], d_branch, ((0,), (0,)))
         d_pre_s[here, 4 * h :] = d_gate
-        if u == 1:
-            for r in range(BLOCK_ROWS):
-                d_product_s[0, pl.ds(first + r, n, stride=n), :] = d_product[r * n : (r + 1) * n]
-            d_product_s[1, here, :] = d_product
-        else:
-            d_product_s[0, here, :] = d_product
-            for r in range(BLOCK_ROWS):
-                d_product_s[1, pl.ds(first + r, n, stride=n), :] = d_product[r * n : (r + 1) * n]
+        d_product_s[u, here, :] = d_product
+        for r in range(unmix_rows):
+            swapped = pl.ds(t * unmix_rows + r, n, stride=n)
+            d_product_s[1 - u, swapped, :] = d_product[r * n : (r + 1) * n]
+
+    blocks = n // BLOCK_ROWS
 
     @pl.loop(0, 2 * blocks)
     def _(step):
-        side, first = step // blocks, step % blocks * BLOCK_ROWS
-        here = pl.ds(pl.multiple_of(first * n, BLOCK_ROWS * n), BLOCK_ROWS * n)
+        side, t = step // blocks, step % blocks
         edges, d_product = edges_s.at[1 - side], d_product_s.at[side]
         x, y = (edges, d_product) if u == 1 else (d_product, edges)
-        d_edges_s[side, here, :] = contract(n, first, lambda a, e: a * n + e, x, y)
+        d_edges_s[side, block(t, BLOCK_ROWS, n), :] = contract(n, t * BLOCK_ROWS, x, y, unroll)
 
     @pl.loop(0, blocks)
     def _(t):
-        here = pl.ds(pl.multiple_of(t * BLOCK_ROWS * n, BLOCK_ROWS * n), BLOCK_ROWS * n)
+        here = block(t, BLOCK_ROWS, n)
         grads = edge_grads(
             d_edges_s[0, here, :],
             d_edges_s[1, here, :],
@@ -238,7 +232,7 @@
             d_pre_s[here, g * h : (g + 1) * h] = grads[g]
         sums_s[:, :width] += dot(normed_s[here, :], d_pre_s[here, :], ((0,), (0,)))
         if u == 1:
-            up_ref[here, :] = input_pullback(here, upstream(t, here))
+            up_ref[here, :] = input_pullback(here, upstream(t, BLOCK_ROWS))
 
     if u == 0:
         cells = up_ref.shape[0]
@@ -301,18 +295,15 @@
     h = out_weight.shape[1]
     width = proj_weight.shape[2]
     cells, pairs = rows * n, n * n
-    plane = jax.ShapeDtypeStruct((pairs + 8, h), F32)
-    narrow = jax.ShapeDtypeStruct((pairs, h), BF16)
+    plane = (pairs + 8, h)
+    kept = [jax.ShapeDtypeStruct((2, 4) + plane, F32), jax.ShapeDtypeStruct((2, 2) + plane, F32)]
+    kept += [jax.ShapeDtypeStruct((2,) + plane, F32)] * 6
+    kept += [jax.ShapeDtypeStruct((2, pairs, h), BF16)] * 2
     grads = jax.ShapeDtypeStruct((c, width + c), BF16)
-    double = jax.ShapeDtypeStruct((2, pairs + 8, h), F32)
-    kept = (double,) * 2 + (plane,) * 6 + (narrow,) * 2
     vmem = pl.BlockSpec(memory_space=pltpu.VMEM)
     smem = pl.BlockSpec(memory_space=pltpu.SMEM)
     main = pl.BlockSpec(memory_space=pltpu.HBM)
     params = pltpu.CompilerParams(vmem_limit_bytes=VMEM_BYTES)
-
-    def scratch(array):
-        return pltpu.VMEM(array.shape, array.dtype)
 
     def cost(planes):
         flops = 4 * pairs * width * c
@@ -342,19 +333,19 @@
 
     held = pl.pallas_call(
         functools.partial(forward, n),
-        out_shape=kept * 2,
+        out_shape=kept,
         in_specs=[vmem] * 7,
-        out_specs=(vmem,) * (2 * KEPT),
-        scratch_shapes=[scratch(plane), scratch(narrow)],
+        out_specs=(vmem,) * KEPT,
+        scratch_shapes=[pltpu.VMEM((pairs, c), BF16)],
         compiler_params=params,
         cost_estimate=cost(64),
         name="forward",
     )(state, proj_weight, proj_bias, norm_gain, norm_shift, out_weight, out_bias)
 
-    work = [scratch(double), scratch(double)]
+    work = [pltpu.VMEM((2,) + plane, F32)] * 2
     work += [pltpu.VMEM((pairs, width), BF16), pltpu.VMEM(grads.shape, F32)]
     up_1, grads_1 = pl.pallas_call(
-        functools.partial(backward, n, 1),
+        functools.partial(backward, n, 1, BLOCK_ROWS, True),
         out_shape=(jax.ShapeDtypeStruct((pairs, c), F32), grads),
         in_specs=[vmem] * (4 + KEPT),
         out_specs=(vmem, vmem),
@@ -362,12 +353,12 @@
         compiler_params=params,
         cost_estimate=cost(48),
         name="backward_second",
-    )(state, proj_weight, norm_gain, out_weight, *held[KEPT:])
+    )(state, proj_weight, norm_gain, out_weight, *held)
     far = groups // 2
     others_1 = exchange(grads_1, "dp", groups, far)
 
     pair_grad, grads_0 = pl.pallas_call(
-        functools.partial(backward, n, 0),
+        functools.partial(backward, n, 0, BLOCK_ROWS // 2, 8),
         out_shape=(jax.ShapeDtypeStruct((cells, c), BF16), grads),
         in_specs=[smem] + [vmem] * (4 + KEPT),
         out_specs=(vmem, vmem),
@@ -375,7 +366,7 @@
         compiler_params=params,
         cost_estimate=cost(48),
         name="backward_first",
-    )(own, up_1, proj_weight, norm_gain, out_weight, *held[:KEPT])
+    )(own, up_1, proj_weight, norm_gain, out_weight, *held)
 
     both = jnp.stack([grads_0, add_narrow(grads_1, others_1)])
     others = jnp.zeros_like(both)
@@ -598,8 +589,9 @@
         n, c = args[0].shape[2:]
         rows = n // parts
         fits = 20 * n * n * c * 4 <= CROP_BUDGET
-        even = c & (c - 1) == 0 and args[7].shape[1] == c and groups > 1 and groups & (groups - 1) == 0 and BLOCK_ROWS % rows == 0 and n % 16 == 0
-        body = functools.partial(crop_shards, groups, parts) if fits and even else shards
+        paired = groups > 1 and groups & (groups - 1) == 0
+        even = args[7].shape[1] == c and BLOCK_ROWS // 2 % rows == 0 and n % 16 == 0
+        body = functools.partial(crop_shards, groups, parts) if fits and even and paired else shards
         return spread_over(body)(*args)
 
     def spread_over(body):

time: 62 us -> 60.1 us (0.969)
  Pallas kernels: 27.3 us -> 25.4 us
    pallas_call x3, Pallas kernels: 24.5 us -> 22.6 us  [the longest x1 8.51 us: crop_shards(): pl.pallas_call(functools.partial(forward, n), out_shape=kept, in_specs=[v...]
  transfers between devices with their start and end apart: 3 -> 3, of which waited for: 2 -> 2; matrix products, arithmetic and copies ran while one was open for 0% -> 0% of each run, Pallas kernels for 12% -> 13%
where the time goes in v9:
time: 60.1 us; the launch traced here: 59.9 us
  Pallas kernels  25.4 us (42%)
  blocking collectives  23.3 us (39%)
  waiting for transfers between devices  8.12 us (14%)
  starting transfers between devices  2.23 us (4%)
  between operations  0.76 us (1%)
    all_to_all x1, blocking collectives, crop_shards(): state = lax.all_to_all(sent, 'dap', split_axis=0, concat_axis=0, tiled=True)  23.3 us
    pallas_call x1, Pallas kernels, crop_shards(): pl.pallas_call(functools.partial(forward, n), out_shape=kept, in_specs=[v...  8.51 us
    ppermute x3, waiting for transfers between devices, exchange(): return lax.ppermute(value, axis, [(d, d ^ step) for d in range(size)])  8.12 us
    pallas_call x1, Pallas kernels, crop_shards(): pl.pallas_call(functools.partial(backward, n, 0, BLOCK_ROWS // 2, 8), out...  7.99 us
    pallas_call x1, Pallas kernels, crop_shards(): pl.pallas_call(functools.partial(backward, n, 1, BLOCK_ROWS, True), out_s...  6.15 us
    ppermute x3, starting transfers between devices, exchange(): return lax.ppermute(value, axis, [(d, d ^ step) for d in range(size)])  2.23 us
    pallas_call x1, Pallas kernels, crop_shards(): pl.pallas_call(prepare, out_shape=(jax.ShapeDtypeStruct((parts, 2 * cells...  1.76 us
  transfers between devices with their start and end apart: 3, of which 2 were waited for; matrix products, arithmetic and copies ran while one was open for 0% of the time, Pallas kernels for 13%

profile of v9, /device:TPU:0, one launch (start us, length us, event | category | flops | bytes accessed | tf_op | source)
XLA Modules:
  0.0 59.9 jit_solution(16144566047372811766)
XLA Ops:
  0.6 0.0 copy-start.1
  0.6 0.0 copy-start.2
  0.7 0.0 copy-start
  0.7 0.0 copy-start.5
  0.7 0.0 copy-start.4
  0.7 0.0 copy-start.3
  0.7 1.8 %prepare.1 = (bf16[8,272,128]{2,1,0:T(8,128)(2,1)}, s32[1]{0:T(128)}) custom-call(s32[1]{0:T(128)} %bitcast.index_ref, bf16[128,128]{1,0:T(8,128)(2,1)} %bitcast.14, s32[4,32]{1,0:T(4,128)} %bitcast.16, bf16[128,128]{1,0:T(8,128)(2,1)} %bitcast.15), custom_call_target="tpu_custom_call" | custom-call | tf_op jit(solution)/shard_map/prepare/pallas_call | solution.py:315
  2.5 23.3 %all_to_all.5.state_ref.refs_0_ = bf16[8,272,128]{2,1,0:T(8,128)(2,1)S(1)} all-to-all(bf16[8,272,128]{2,1,0:T(8,128)(2,1)} %get-tuple-element.22), channel_id=1, replica_groups=mesh['dp'=4,'dap'=8] {'dap'}, dimensions={0} | all-to-all | bytes 1114112 | tf_op jit(solution)/shard_map/all_to_all | solution.py:332
  25.8 0.0 copy-done.1
  25.8 0.0 copy-done.2
  25.8 0.0 copy-done
  25.8 0.0 copy-done.5
  25.8 0.0 copy-done.4
  25.8 0.0 copy-done.3
  25.8 8.5 %forward.1 = (f32[2,4,1032,128]{3,2,1,0:T(8,128)S(1)}, f32[2,2,1032,128]{3,2,1,0:T(8,128)S(1)}, f32[2,1032,128]{2,1,0:T(8,128)S(1)}, f32[2,1032,128]{2,1,0:T(8,1...) custom-call(bf16[8,272,128]{2,1,0:T(8,128)(2,1)S(1)} %all_to_all.5.s, ...), custom_call_target="tpu_custom_call" | custom-call | flops 335544320 | bytes 33554432 | tf_op jit(solution)/shard_map/forward/pallas_call | solution.py:334
  34.3 6.2 %backward_second.1 = (f32[1024,128]{1,0:T(8,128)S(1)}, bf16[128,768]{1,0:T(8,128)(2,1)S(1)}) custom-call(bf16[8,272,128]{2,1,0:T(8,128)(2,1)S(1)} %all_to_all.5.state_ref.refs_0_, bf16[2,128,640]{2,1,0:T(8,128)(2,1)S(1)} %copy-done, f32[2,256]{1,0:T(2,128)S(1)} %copy-done.2, bf16[2,128,128]{2,1,0:T(8,128)(2,1)S(1)} %copy-done.1, ...), custom_call_target="tpu_custom_call" | custom-call | flops 335544320 | bytes 25165824 | tf_op jit(solution)/shard_map/backward_second/pallas_call | solution.py:347
  40.5 1.6 %collective-permute-start = (bf16[128,768]{1,0:T(8,128)(2,1)S(1)}, bf16[128,768]{1,0:T(8,128)(2,1)S(1)}, u32[]{:S(2)}, u32[]{:S(2)}) collective-permute-start(bf16[128,768]{1,0:T(8,128)(2,1)S(1)} %get-tuple-element.36), channel_id=1, source_target_pairs={{0,16},{8,24},{16,0},{24,8},{1,17},{9,25},{17,1},{25,9},{2,18},{10... | collective-permute-start | bytes 589832 | tf_op jit(solution)/shard_map/ppermute | solution.py:245
  42.0 8.0 %backward_first.1 = (bf16[128,128]{1,0:T(8,128)(2,1)}, bf16[128,768]{1,0:T(8,128)(2,1)S(1)}) custom-call(s32[1]{0:T(128)} %get-tuple-element.21.refs_0_, f32[1024,128]{1,0:T(8,128)S(1)} %get-tuple-element.33.refs_1_, bf16[2,128,640]{2,1,0:T(8,128)(2,1)S(1)} %copy-done, f32[2,256]{1,0:T(2,128)S(1)} %copy-done.2, bf16[2,128,128]{2,1,0:T(8,128)(2,1)S(1)} %copy-done.1, ...), custom_call_target="tpu_custom_call" | custom-call | flops 335544320 | bytes 25165824 | tf_op jit(solution)/shard_map/backward_first/pallas_call | solution.py:360
  50.0 0.0 collective-permute-done
  50.1 0.1 collective-permute-start.1
  50.2 1.7 %collective-permute-done.1.other_both = bf16[2,128,768]{2,1,0:T(8,128)(2,1)S(1)} collective-permute-done((bf16[2,128,768]{2,1,0:T(8,128)(2,1)S(1)}, bf16[2,128,768]{2,1,0:T(8,128)(2,1)S(1)}, u32[]{:S(2)}, u32[]{:S(2)}) %collective-permute-start.1) | collective-permute-done | bytes 393248 | tf_op jit(solution)/shard_map/ppermute | solution.py:245
  51.9 0.1 fusion.own_0
  52.0 0.6 %collective-permute-start.2 = (bf16[128,768]{1,0:T(8,128)(2,1)S(1)}, bf16[128,768]{1,0:T(8,128)(2,1)S(1)}, u32[]{:S(2)}, u32[]{:S(2)}) collective-permute-start(bf16[128,768]{1,0:T(8,128)(2,1)S(1)} %fusion.own_0), channel_id=1, source_target_pairs={{0,16},{8,24},{16,0},{24,8},{1,17},{9,25},{17,1},{25,9},{2,18},{10... | collective-permute-start | bytes 589832 | tf_op jit(solution)/shard_map/ppermute | solution.py:245
  52.6 6.4 %collective-permute-done.2.other_0 = bf16[128,768]{1,0:T(8,128)(2,1)S(1)} collective-permute-done((bf16[128,768]{1,0:T(8,128)(2,1)S(1)}, bf16[128,768]{1,0:T(8,128)(2,1)S(1)}, u32[]{:S(2)}, u32[]{:S(2)}) %collective-permute-start.2) | collective-permute-done | bytes 196640 | tf_op jit(solution)/shard_map/ppermute | solution.py:245
  59.0 0.9 %add_grads.1 = (f32[2,128,640]{2,1,0:T(8,128)}, f32[2,128,128]{2,1,0:T(8,128)}) custom-call(bf16[128,768]{1,0:T(8,128)(2,1)S(1)} %fusion.own_0, bf16[128,768]{1,0:T(8,128)(2,1)S(1)} %collective-permute-done.2.other_0, bf16[2,128,768]{2,1,0:T(8,128)(2,1)S(1)} %pad_maximum_fusion.own_both, bf16[2,128,768]{2,1,0:T(8,128)(2,1)S(1)} %collective-permute-done.1.other_both), custom_call_target="tpu_custom_call" | custom-call | tf_op jit(solution)/shard_map/add_grads/pallas_call | solution.py:381
  (2 shorter events, 0.1 us)
Async XLA Ops:
  0.6 25.1 %copy-start.1 = (bf16[2,128,128]{2,1,0:T(8,128)(2,1)S(1)}, bf16[2,128,128]{2,1,0:T(8,128)(2,1)}, u32[]{:S(2)}) copy-start(bf16[2,128,128]{2,1,0:T(8,128)(2,1)} %refs_4_.1) | copy-start | bytes 196612
  0.6 25.1 %copy-start.2 = (f32[2,256]{1,0:T(2,128)S(1)}, f32[2,256]{1,0:T(2,128)}, u32[]{:S(2)}) copy-start(f32[2,256]{1,0:T(2,128)} %refs_3_.3) | copy-start | bytes 6148
  0.7 25.1 %copy-start = (bf16[2,128,640]{2,1,0:T(8,128)(2,1)S(1)}, bf16[2,128,640]{2,1,0:T(8,128)(2,1)}, u32[]{:S(2)}) copy-start(bf16[2,128,640]{2,1,0:T(8,128)(2,1)} %refs_2_.3) | copy-start | bytes 983044
  0.7 25.1 %copy-start.5 = (f32[2,128]{1,0:T(2,128)S(1)}, f32[2,128]{1,0:T(2,128)}, u32[]{:S(2)}) copy-start(f32[2,128]{1,0:T(2,128)} %b_out.1) | copy-start | bytes 3076
  0.7 25.1 %copy-start.4 = (f32[2,256]{1,0:T(2,128)S(1)}, f32[2,256]{1,0:T(2,128)}, u32[]{:S(2)}) copy-start(f32[2,256]{1,0:T(2,128)} %shift.1) | copy-start | bytes 6148
  0.7 25.1 %copy-start.3 = (f32[2,640]{1,0:T(2,128)S(1)}, f32[2,640]{1,0:T(2,128)}, u32[]{:S(2)}) copy-start(f32[2,640]{1,0:T(2,128)} %b.1) | copy-start | bytes 15364
  40.5 9.5 %collective-permute-start = (bf16[128,768]{1,0:T(8,128)(2,1)S(1)}, bf16[128,768]{1,0:T(8,128)(2,1)S(1)}, u32[]{:S(2)}, u32[]{:S(2)}) collective-permute-start(bf16[128,768]{1,0:T(8,128)(2,1)S(1)} %get-tuple-element.36), channel_id=1, source_target_pairs={{0,16},{8,24},{16,0},{24,8},{1,17},{9,25},{17,1},{25,9},{2,18},{10... | collective-permute-start | bytes 589832 | tf_op jit(solution)/shard_map/ppermute | solution.py:245
  50.1 1.8 %collective-permute-start.1 = (bf16[2,128,768]{2,1,0:T(8,128)(2,1)S(1)}, bf16[2,128,768]{2,1,0:T(8,128)(2,1)S(1)}, u32[]{:S(2)}, u32[]{:S(2)}) collective-permute-start(bf16[2,128,768]{2,1,0:T(8,128)(2,1)S(1)} %pad_maximum_fusion.own_both), channel_id=1, source_target_pairs={{0,8},{8,0},{16,24},{24,16},{1,9},{9,1},{17,25},{25,17},{2,10},{10... | collective-permute-start | bytes 1179656 | tf_op jit(solution)/shard_map/ppermute | solution.py:245
  52.0 7.0 %collective-permute-start.2 = (bf16[128,768]{1,0:T(8,128)(2,1)S(1)}, bf16[128,768]{1,0:T(8,128)(2,1)S(1)}, u32[]{:S(2)}, u32[]{:S(2)}) collective-permute-start(bf16[128,768]{1,0:T(8,128)(2,1)S(1)} %fusion.own_0), channel_id=1, source_target_pairs={{0,16},{8,24},{16,0},{24,8},{1,17},{9,25},{17,1},{25,9},{2,18},{10... | collective-permute-start | bytes 589832 | tf_op jit(solution)/shard_map/ppermute | solution.py:245

commit v10 on v9

--- a/solution.py
+++ b/solution.py
@@ -12,6 +12,7 @@
 PREPARE_BYTES = 63 * 1024 * 1024
 CROP_BUDGET = 32 * 1024 * 1024
 BLOCK_ROWS = 8
+STEP_ROWS = 16
 KEPT = 10
 F32 = jnp.float32
 BF16 = jnp.bfloat16
@@ -73,7 +74,7 @@
     return d_branch, d_gate, norm_vjp(p_hat, p_rstd, d_mixed)
 
 
-def contract(n, first, x, y, unroll=True):
+def contract(n, first, x, y):
     lanes = y.shape[1]
     tiles = (n // 8, 8, lanes)
 
@@ -85,7 +86,7 @@
         )
 
     zero = jnp.zeros(tiles, F32)
-    totals = lax.fori_loop(0, n, step, (zero,) * BLOCK_ROWS, unroll=unroll)
+    totals = lax.fori_loop(0, n, step, (zero,) * BLOCK_ROWS, unroll=True)
     return jnp.stack(totals).reshape(BLOCK_ROWS * n, lanes)
 
 
@@ -98,8 +99,18 @@
     )
 
 
+def tail_values(block, lanes_from, lanes_to):
+    lane = lax.broadcasted_iota(jnp.int32, block.shape, block.ndim - 1)
+    inside = (lane >= lanes_from) & (lane < lanes_to)
+    return jnp.max(jnp.where(inside, block.astype(F32), 0.0)).astype(jnp.int32)
+
+
 def crop_length(state_ref, cells):
-    return jnp.max(state_ref[:, 2 * cells :, :].astype(F32)).astype(jnp.int32)
+    return tail_values(state_ref[:, 2 * cells :, :], 0, 64)
+
+
+def own_place(state_ref, cells):
+    return tail_values(state_ref[0, 2 * cells :, :], 64, 128)
 
 
 def joined(ref, first, count, cells, place):
@@ -119,7 +130,7 @@
     rows = n // parts
     cells = rows * n
     length = crop_length(state_ref, cells)
-    blocks = n // BLOCK_ROWS
+    steps = n // STEP_ROWS
 
     @pl.loop(0, parts)
     def _(t):
@@ -131,17 +142,17 @@
             jnp.where(u == 0, ref[0:1, :], ref[1:2, :]) for ref in (b, gain, shift, b_out)
         )
 
-        @pl.loop(0, blocks, unroll=2)
+        @pl.loop(0, steps)
         def _(t):
-            first = t * BLOCK_ROWS
-            here = block(t, BLOCK_ROWS, n)
-            mask = pair_mask_block(length, first, BLOCK_ROWS, n, c)
+            first = t * STEP_ROWS
+            here = block(t, STEP_ROWS, n)
+            mask = pair_mask_block(length, first, STEP_ROWS, n, c)
             x_hat, rstd, normed, s_left, s_right, left, right, gate = project(
                 next_s[here, :], mask, w[u], bias, gains[:, :c], shifts[:, :c]
             )
             edges_s[u, 0, here, :] = left
             edges_s[u, 1, here, :] = right
-            for r in range(BLOCK_ROWS):
+            for r in range(STEP_ROWS):
                 swapped = pl.ds(first + r, n, stride=n)
                 edges_s[u, 2, swapped, :] = right[r * n : (r + 1) * n]
                 edges_s[u, 3, swapped, :] = left[r * n : (r + 1) * n]
@@ -152,12 +163,15 @@
             rstd_s[u, here, :] = rstd
             normed_s[u, here, :] = normed
 
-        @pl.loop(0, blocks, unroll=2)
+        @pl.loop(0, steps)
         def _(t):
-            here = block(t, BLOCK_ROWS, n)
-            product = contract(n, t * BLOCK_ROWS, edges_s.at[u, 3 * u], edges_s.at[u, 2 - u])
+            here = block(t, STEP_ROWS, n)
+            x, y = edges_s.at[u, 3 * u], edges_s.at[u, 2 - u]
+            product = [
+                contract(n, t * STEP_ROWS + r, x, y) for r in range(0, STEP_ROWS, BLOCK_ROWS)
+            ]
             p_hat, p_rstd, mixed, branch = mix(
-                product.astype(BF16), gains[:, c:], shifts[:, c:], w_out[u], bias_out
+                jnp.concatenate(product).astype(BF16), gains[:, c:], shifts[:, c:], w_out[u], bias_out
             )
             p_hat_s[u, here, :] = p_hat
             p_rstd_s[u, here, :] = p_rstd
@@ -167,13 +181,14 @@
             next_s[here, :] = (x + gate_s[u, here, :] * branch).astype(BF16)
 
 
-def backward(n, u, unmix_rows, unroll, *refs):
-    if u == 0:
-        index_ref, refs = refs[0], refs[1:]
+def backward(n, u, *refs):
     up_in_ref, w, gain, w_out = refs[:4]
     (edges_s, slopes_s, gate_s, hat_s, rstd_s) = (ref.at[u] for ref in refs[4:9])
     (p_hat_s, p_rstd_s, branch_s, normed_s, mixed_s) = (ref.at[u] for ref in refs[9 : 4 + KEPT])
-    up_ref, grads_ref, d_product_s, d_edges_s, d_pre_s, sums_s = refs[4 + KEPT :]
+    if u == 1:
+        up_ref, grads_ref, d_product_s, d_edges_s, sums_s, d_pre_s = refs[4 + KEPT :]
+    else:
+        d_pre_s, grads_ref, d_product_s, d_edges_s, sums_s = refs[4 + KEPT :]
     c, h = w.shape[1], edges_s.shape[2]
     width = 4 * h + c
     sums_s[...] = jnp.zeros_like(sums_s)
@@ -185,15 +200,11 @@
         per = rows // own
         return joined(up_in_ref, t * per, per, own * n, 1).astype(F32)
 
-    def input_pullback(here, up):
-        d_normed = dot(d_pre_s[here, :], w[u], ((1,), (1,))) * gain[u : u + 1, :c]
-        return up + norm_vjp(hat_s[here, :], rstd_s[here, :], d_normed)
-
-    @pl.loop(0, n // unmix_rows)
+    @pl.loop(0, n // STEP_ROWS)
     def _(t):
-        here = block(t, unmix_rows, n)
+        here = block(t, STEP_ROWS, n)
         d_branch, d_gate, d_product = unmix(
-            upstream(t, unmix_rows),
+            upstream(t, STEP_ROWS),
             gate_s[here, :],
             branch_s[here, :],
             p_hat_s[here, :],
@@ -204,8 +215,8 @@
         sums_s[:, width:] += dot(mixed_s[here, :], d_branch, ((0,), (0,)))
         d_pre_s[here, 4 * h :] = d_gate
         d_product_s[u, here, :] = d_product
-        for r in range(unmix_rows):
-            swapped = pl.ds(t * unmix_rows + r, n, stride=n)
+        for r in range(STEP_ROWS):
+            swapped = pl.ds(t * STEP_ROWS + r, n, stride=n)
             d_product_s[1 - u, swapped, :] = d_product[r * n : (r + 1) * n]
 
     blocks = n // BLOCK_ROWS
@@ -215,11 +226,11 @@
         side, t = step // blocks, step % blocks
         edges, d_product = edges_s.at[1 - side], d_product_s.at[side]
         x, y = (edges, d_product) if u == 1 else (d_product, edges)
-        d_edges_s[side, block(t, BLOCK_ROWS, n), :] = contract(n, t * BLOCK_ROWS, x, y, unroll)
-
-    @pl.loop(0, blocks)
+        d_edges_s[side, block(t, BLOCK_ROWS, n), :] = contract(n, t * BLOCK_ROWS, x, y)
+
+    @pl.loop(0, n // STEP_ROWS)
     def _(t):
-        here = block(t, BLOCK_ROWS, n)
+        here = block(t, STEP_ROWS, n)
         grads = edge_grads(
             d_edges_s[0, here, :],
             d_edges_s[1, here, :],
@@ -228,17 +239,26 @@
             edges_s[0, here, :],
             edges_s[1, here, :],
         )
-        for g in range(4):
-            d_pre_s[here, g * h : (g + 1) * h] = grads[g]
-        sums_s[:, :width] += dot(normed_s[here, :], d_pre_s[here, :], ((0,), (0,)))
+        d_pre = jnp.concatenate([*grads, d_pre_s[here, 4 * h :]], axis=1)
+        normed = normed_s[here, :]
         if u == 1:
-            up_ref[here, :] = input_pullback(here, upstream(t, BLOCK_ROWS))
-
-    if u == 0:
-        cells = up_ref.shape[0]
-        own = pl.ds(pl.multiple_of(index_ref[0] * cells, cells), cells)
-        up_ref[...] = input_pullback(own, up_in_ref[own, :]).astype(BF16)
+            d_normed = dot(d_pre, w[u], ((1,), (1,))) * gain[u : u + 1, :c]
+            pulled = norm_vjp(hat_s[here, :], rstd_s[here, :], d_normed)
+            up_ref[here, :] = upstream(t, STEP_ROWS) + pulled
+        else:
+            d_pre_s[here, : 4 * h] = d_pre[:, : 4 * h]
+        sums_s[:, :width] += dot(normed, d_pre, ((0,), (0,)))
+
     grads_ref[...] = sums_s[...].astype(BF16)
+
+
+def own_rows(state_ref, up_ref, d_pre_ref, w, gain, hat_ref, rstd_ref, out_ref):
+    cells, c = out_ref.shape
+    place = own_place(state_ref, cells)
+    own = pl.ds(pl.multiple_of(place * cells, cells), cells)
+    d_normed = dot(d_pre_ref[own, :], w[0], ((1,), (1,))) * gain[0:1, :c]
+    pulled = norm_vjp(hat_ref[0, own, :], rstd_ref[0, own, :], d_normed)
+    out_ref[...] = (up_ref[own, :] + pulled).astype(BF16)
 
 
 def exchange(value, axis, size, step):
@@ -249,8 +269,7 @@
     return (a.astype(F32) + b.astype(F32)).astype(BF16)
 
 
-def prepare(index_ref, state_ref, mask_ref, cot_ref, sent_ref, own_ref, state_s, mask_s, cot_s, sems):
-    own_ref[0] = index_ref[0]
+def prepare(state_ref, mask_ref, cot_ref, sent_ref, state_s, mask_s, cot_s, sems):
     parts, _, c = sent_ref.shape
     cells = state_s.shape[0]
     copies = [
@@ -261,13 +280,13 @@
         copy.start()
     copies[0].wait()
     length = jnp.max(jnp.sum(mask_s[...].astype(F32), axis=1, keepdims=True))
-    below = jnp.full((sent_ref.shape[1] - 2 * cells, c), length, F32).astype(BF16)
+    in_length = lax.broadcasted_iota(jnp.int32, (16, c), 1) < 64
     for copy in copies[1:]:
         copy.wait()
     for part in range(parts):
         sent_ref[part, :cells, :] = state_s[...]
         sent_ref[part, cells : 2 * cells, :] = cot_s[...]
-        sent_ref[part, 2 * cells :, :] = below
+        sent_ref[part, 2 * cells :, :] = jnp.where(in_length, length, float(part)).astype(BF16)
 
 
 def add_grads(own_0, other_0, own_both, other_both, proj_ref, out_ref):
@@ -301,7 +320,6 @@
     kept += [jax.ShapeDtypeStruct((2, pairs, h), BF16)] * 2
     grads = jax.ShapeDtypeStruct((c, width + c), BF16)
     vmem = pl.BlockSpec(memory_space=pltpu.VMEM)
-    smem = pl.BlockSpec(memory_space=pltpu.SMEM)
     main = pl.BlockSpec(memory_space=pltpu.HBM)
     params = pltpu.CompilerParams(vmem_limit_bytes=VMEM_BYTES)
 
@@ -311,15 +329,11 @@
             flops=flops, bytes_accessed=planes * pairs * c * 4, transcendentals=0
         )
 
-    index = lax.axis_index("dap").astype(jnp.int32)[None]
-    sent, own = pl.pallas_call(
+    sent = pl.pallas_call(
         prepare,
-        out_shape=(
-            jax.ShapeDtypeStruct((parts, 2 * cells + 16, c), BF16),
-            jax.ShapeDtypeStruct((1,), jnp.int32),
-        ),
-        in_specs=[smem] + [main] * 3,
-        out_specs=(vmem, smem),
+        out_shape=jax.ShapeDtypeStruct((parts, 2 * cells + 16, c), BF16),
+        in_specs=[main] * 3,
+        out_specs=vmem,
         scratch_shapes=[
             pltpu.VMEM((cells, c), BF16),
             pltpu.VMEM((rows, n), jnp.int32),
@@ -328,7 +342,7 @@
         ],
         compiler_params=pltpu.CompilerParams(vmem_limit_bytes=PREPARE_BYTES),
         name="prepare",
-    )(index, pair_repr.reshape(cells, c), pair_mask[0], cotangent.reshape(cells, c))
+    )(pair_repr.reshape(cells, c), pair_mask[0], cotangent.reshape(cells, c))
     state = lax.all_to_all(sent, "dap", split_axis=0, concat_axis=0, tiled=True)
 
     held = pl.pallas_call(
@@ -343,13 +357,14 @@
     )(state, proj_weight, proj_bias, norm_gain, norm_shift, out_weight, out_bias)
 
     work = [pltpu.VMEM((2,) + plane, F32)] * 2
-    work += [pltpu.VMEM((pairs, width), BF16), pltpu.VMEM(grads.shape, F32)]
+    work += [pltpu.VMEM(grads.shape, F32)]
+    d_pre = jax.ShapeDtypeStruct((pairs, width), BF16)
     up_1, grads_1 = pl.pallas_call(
-        functools.partial(backward, n, 1, BLOCK_ROWS, True),
+        functools.partial(backward, n, 1),
         out_shape=(jax.ShapeDtypeStruct((pairs, c), F32), grads),
         in_specs=[vmem] * (4 + KEPT),
         out_specs=(vmem, vmem),
-        scratch_shapes=work,
+        scratch_shapes=work + [pltpu.VMEM(d_pre.shape, BF16)],
         compiler_params=params,
         cost_estimate=cost(48),
         name="backward_second",
@@ -357,16 +372,26 @@
     far = groups // 2
     others_1 = exchange(grads_1, "dp", groups, far)
 
-    pair_grad, grads_0 = pl.pallas_call(
-        functools.partial(backward, n, 0, BLOCK_ROWS // 2, 8),
-        out_shape=(jax.ShapeDtypeStruct((cells, c), BF16), grads),
-        in_specs=[smem] + [vmem] * (4 + KEPT),
+    d_pre_0, grads_0 = pl.pallas_call(
+        functools.partial(backward, n, 0),
+        out_shape=(d_pre, grads),
+        in_specs=[vmem] * (4 + KEPT),
         out_specs=(vmem, vmem),
         scratch_shapes=work,
         compiler_params=params,
         cost_estimate=cost(48),
         name="backward_first",
-    )(own, up_1, proj_weight, norm_gain, out_weight, *held)
+    )(up_1, proj_weight, norm_gain, out_weight, *held)
+
+    pair_grad = pl.pallas_call(
+        own_rows,
+        out_shape=jax.ShapeDtypeStruct((cells, c), BF16),
+        in_specs=[vmem] * 7,
+        out_specs=vmem,
+        compiler_params=params,
+        cost_estimate=cost(8),
+        name="own_rows",
+    )(state, up_1, d_pre_0, proj_weight, norm_gain, held[3], held[4])
 
     both = jnp.stack([grads_0, add_narrow(grads_1, others_1)])
     others = jnp.zeros_like(both)
@@ -590,7 +615,7 @@
         rows = n // parts
         fits = 20 * n * n * c * 4 <= CROP_BUDGET
         paired = groups > 1 and groups & (groups - 1) == 0
-        even = args[7].shape[1] == c and BLOCK_ROWS // 2 % rows == 0 and n % 16 == 0
+        even = args[7].shape[1] == c == 128 and STEP_ROWS % rows == 0 and n % STEP_ROWS == 0
         body = functools.partial(crop_shards, groups, parts) if fits and even and paired else shards
         return spread_over(body)(*args)
 

time: 60.1 us -> 55.6 us (0.925)
  Pallas kernels: 25.4 us -> 21.8 us
  waiting for transfers between devices: 8.12 us -> 6.85 us
    pallas_call x3 -> x4, Pallas kernels: 15.9 us -> 12.7 us  [the longest x1 5.02 us: crop_shards(): pl.pallas_call(functools.partial(backward, n, 1), out_shape=(jax.ShapeDty...]
    ppermute x3, waiting for transfers between devices: 8.12 us -> 6.85 us  [exchange(): return lax.ppermute(value, axis, [(d, d ^ step) for d in range(size)])]
  transfers between devices with their start and end apart: 3 -> 3, of which waited for: 2 -> 2; matrix products, arithmetic and copies ran while one was open for 0% -> 0% of each run, Pallas kernels for 13% -> 11%
where the time goes in v10:
time: 55.6 us; the launch traced here: 55.4 us
  blocking collectives  23.3 us (42%)
  Pallas kernels  21.8 us (39%)
  waiting for transfers between devices  6.85 us (12%)
  starting transfers between devices  2.47 us (4%)
  between operations  0.78 us (1%)
    all_to_all x1, blocking collectives, crop_shards(): state = lax.all_to_all(sent, 'dap', split_axis=0, concat_axis=0, tiled=True)  23.3 us
    pallas_call x1, Pallas kernels, crop_shards(): pl.pallas_call(functools.partial(forward, n), out_shape=kept, in_specs=[v...  8.16 us
    ppermute x3, waiting for transfers between devices, exchange(): return lax.ppermute(value, axis, [(d, d ^ step) for d in range(size)])  6.85 us
    pallas_call x1, Pallas kernels, crop_shards(): pl.pallas_call(functools.partial(backward, n, 1), out_shape=(jax.ShapeDty...  5.02 us
    pallas_call x1, Pallas kernels, crop_shards(): pl.pallas_call(functools.partial(backward, n, 0), out_shape=(d_pre, grads...  4.87 us
    ppermute x3, starting transfers between devices, exchange(): return lax.ppermute(value, axis, [(d, d ^ step) for d in range(size)])  2.47 us
    pallas_call x1, Pallas kernels, crop_shards(): pl.pallas_call(prepare, out_shape=jax.ShapeDtypeStruct((parts, 2 * cells...  1.74 us
  transfers between devices with their start and end apart: 3, of which 2 were waited for; matrix products, arithmetic and copies ran while one was open for 0% of the time, Pallas kernels for 11%

profile of v10, /device:TPU:0, one launch (start us, length us, event | category | flops | bytes accessed | tf_op | source)
XLA Modules:
  0.0 55.4 jit_solution(10591431681588005228)
XLA Ops:
  0.6 0.0 copy-start.2
  0.6 0.0 copy-start
  0.7 0.0 copy-start.1
  0.7 0.0 copy-start.5
  0.7 0.0 copy-start.4
  0.7 0.0 copy-start.3
  0.7 1.7 %prepare.1 = bf16[8,272,128]{2,1,0:T(8,128)(2,1)} custom-call(bf16[128,128]{1,0:T(8,128)(2,1)} %bitcast.14, s32[4,32]{1,0:T(4,128)} %bitcast.16, bf16[128,128]{1,0:T(8,128)(2,1)} %bitcast.15), custom_call_target="tpu_custom_call" | custom-call | tf_op jit(solution)/shard_map/prepare/pallas_call | solution.py:332
  2.4 23.3 %all_to_all.5.state_ref.refs_0_ = bf16[8,272,128]{2,1,0:T(8,128)(2,1)S(1)} all-to-all(bf16[8,272,128]{2,1,0:T(8,128)(2,1)} %prepare.1), channel_id=1, replica_groups=mesh['dp'=4,'dap'=8] {'dap'}, dimensions={0} | all-to-all | bytes 1114112 | tf_op jit(solution)/shard_map/all_to_all | solution.py:346
  25.7 0.0 copy-done.2
  25.7 0.0 copy-done
  25.7 0.0 copy-done.1
  25.7 0.0 copy-done.5
  25.8 0.0 copy-done.4
  25.8 0.0 copy-done.3
  25.8 8.2 %forward.1 = (f32[2,4,1032,128]{3,2,1,0:T(8,128)S(1)}, f32[2,2,1032,128]{3,2,1,0:T(8,128)S(1)}, f32[2,1032,128]{2,1,0:T(8,128)S(1)}, f32[2,1032,128]{2,1,0:T(8,1...) custom-call(bf16[8,272,128]{2,1,0:T(8,128)(2,1)S(1)} %all_to_all.5.s, ...), custom_call_target="tpu_custom_call" | custom-call | flops 335544320 | bytes 33554432 | tf_op jit(solution)/shard_map/forward/pallas_call | solution.py:348
  33.9 5.0 %backward_second.1 = (f32[1024,128]{1,0:T(8,128)S(1)}, bf16[128,768]{1,0:T(8,128)(2,1)S(1)}) custom-call(bf16[8,272,128]{2,1,0:T(8,128)(2,1)S(1)} %all_to_all.5.state_ref.refs_0_, bf16[2,128,640]{2,1,0:T(8,128)(2,1)S(1)} %copy-done, f32[2,256]{1,0:T(2,128)S(1)} %copy-done.2, bf16[2,128,128]{2,1,0:T(8,128)(2,1)S(1)} %copy-done.1, ...), custom_call_target="tpu_custom_call" | custom-call | flops 335544320 | bytes 25165824 | tf_op jit(solution)/shard_map/backward_second/pallas_call | solution.py:362
  39.0 1.6 %collective-permute-start = (bf16[128,768]{1,0:T(8,128)(2,1)S(1)}, bf16[128,768]{1,0:T(8,128)(2,1)S(1)}, u32[]{:S(2)}, u32[]{:S(2)}) collective-permute-start(bf16[128,768]{1,0:T(8,128)(2,1)S(1)} %get-tuple-element.32), channel_id=1, source_target_pairs={{0,16},{8,24},{16,0},{24,8},{1,17},{9,25},{17,1},{25,9},{2,18},{10... | collective-permute-start | bytes 589832 | tf_op jit(solution)/shard_map/ppermute | solution.py:265
  40.5 4.9 %backward_first.1 = (bf16[1024,640]{1,0:T(8,128)(2,1)S(1)}, bf16[128,768]{1,0:T(8,128)(2,1)S(1)}) custom-call(f32[1024,128]{1,0:T(8,128)S(1)} %get-tuple-element.29.refs_0_.up_ref, bf16[2,128,640]{2,1,0:T(8,128)(2,1)S(1)} %copy-done, f32[2,256]{1,0:T(2,128)S(1)} %copy-done.2, bf16[2,128,128]{2,1,0:T(8,128)(2,1)S(1)} %copy-done.1, ...), custom_call_target="tpu_custom_call" | custom-call | flops 335544320 | bytes 25165824 | tf_op jit(solution)/shard_map/backward_first/pallas_call | solution.py:375
  45.4 0.0 collective-permute-done
  45.5 0.1 collective-permute-start.1
  45.6 1.7 %collective-permute-done.1.other_both = bf16[2,128,768]{2,1,0:T(8,128)(2,1)S(1)} collective-permute-done((bf16[2,128,768]{2,1,0:T(8,128)(2,1)S(1)}, bf16[2,128,768]{2,1,0:T(8,128)(2,1)S(1)}, u32[]{:S(2)}, u32[]{:S(2)}) %collective-permute-start.1) | collective-permute-done | bytes 393248 | tf_op jit(solution)/shard_map/ppermute | solution.py:265
  47.3 0.1 fusion.own_0
  47.4 0.8 %collective-permute-start.2 = (bf16[128,768]{1,0:T(8,128)(2,1)S(1)}, bf16[128,768]{1,0:T(8,128)(2,1)S(1)}, u32[]{:S(2)}, u32[]{:S(2)}) collective-permute-start(bf16[128,768]{1,0:T(8,128)(2,1)S(1)} %fusion.own_0), channel_id=1, source_target_pairs={{0,16},{8,24},{16,0},{24,8},{1,17},{9,25},{17,1},{25,9},{2,18},{10... | collective-permute-start | bytes 589832 | tf_op jit(solution)/shard_map/ppermute | solution.py:265
  48.2 1.0 %own_rows.1 = bf16[128,128]{1,0:T(8,128)(2,1)} custom-call(bf16[8,272,128]{2,1,0:T(8,128)(2,1)S(1)} %all_to_all.5.state_ref.refs_0_, f32[1024,128]{1,0:T(8,128)S(1)} %get-tuple-element.29.refs_0_.up_ref, bf16[1024,640]{1,0:T(8,128)(2,1)S(1)} %get-tuple-element.30.d_pre_ref, bf16[2,128,640]{2,1,0:T(8,128)(2,1)S(1)} %copy-done, f32[2,256]{1,0:T(2,128)S(1)} %copy-done.2, ...), custom_call_target="tpu_custom_call" | custom-call | flops 335544320 | bytes 4194304 | tf_op jit(solution)/shard_map/own_rows/pallas_call | solution.py:386
  49.2 5.1 %collective-permute-done.2.other_0 = bf16[128,768]{1,0:T(8,128)(2,1)S(1)} collective-permute-done((bf16[128,768]{1,0:T(8,128)(2,1)S(1)}, bf16[128,768]{1,0:T(8,128)(2,1)S(1)}, u32[]{:S(2)}, u32[]{:S(2)}) %collective-permute-start.2) | collective-permute-done | bytes 196640 | tf_op jit(solution)/shard_map/ppermute | solution.py:265
  54.4 1.0 %add_grads.1 = (f32[2,128,640]{2,1,0:T(8,128)}, f32[2,128,128]{2,1,0:T(8,128)}) custom-call(bf16[128,768]{1,0:T(8,128)(2,1)S(1)} %fusion.own_0, bf16[128,768]{1,0:T(8,128)(2,1)S(1)} %collective-permute-done.2.other_0, bf16[2,128,768]{2,1,0:T(8,128)(2,1)S(1)} %pad_maximum_fusion.own_both, bf16[2,128,768]{2,1,0:T(8,128)(2,1)S(1)} %collective-permute-done.1.other_both), custom_call_target="tpu_custom_call" | custom-call | tf_op jit(solution)/shard_map/add_grads/pallas_call | solution.py:406
  (2 shorter events, 0.1 us)
Async XLA Ops:
  0.6 25.1 %copy-start.2 = (f32[2,256]{1,0:T(2,128)S(1)}, f32[2,256]{1,0:T(2,128)}, u32[]{:S(2)}) copy-start(f32[2,256]{1,0:T(2,128)} %gain.3) | copy-start | bytes 6148
  0.6 25.1 %copy-start = (bf16[2,128,640]{2,1,0:T(8,128)(2,1)S(1)}, bf16[2,128,640]{2,1,0:T(8,128)(2,1)}, u32[]{:S(2)}) copy-start(bf16[2,128,640]{2,1,0:T(8,128)(2,1)} %w.3) | copy-start | bytes 983044
  0.7 25.1 %copy-start.1 = (bf16[2,128,128]{2,1,0:T(8,128)(2,1)S(1)}, bf16[2,128,128]{2,1,0:T(8,128)(2,1)}, u32[]{:S(2)}) copy-start(bf16[2,128,128]{2,1,0:T(8,128)(2,1)} %refs_3_.3) | copy-start | bytes 196612
  0.7 25.1 %copy-start.5 = (f32[2,128]{1,0:T(2,128)S(1)}, f32[2,128]{1,0:T(2,128)}, u32[]{:S(2)}) copy-start(f32[2,128]{1,0:T(2,128)} %b_out.1) | copy-start | bytes 3076
  0.7 25.1 %copy-start.4 = (f32[2,256]{1,0:T(2,128)S(1)}, f32[2,256]{1,0:T(2,128)}, u32[]{:S(2)}) copy-start(f32[2,256]{1,0:T(2,128)} %shift.1) | copy-start | bytes 6148
  0.7 25.1 %copy-start.3 = (f32[2,640]{1,0:T(2,128)S(1)}, f32[2,640]{1,0:T(2,128)}, u32[]{:S(2)}) copy-start(f32[2,640]{1,0:T(2,128)} %b.1) | copy-start | bytes 15364
  39.0 6.4 %collective-permute-start = (bf16[128,768]{1,0:T(8,128)(2,1)S(1)}, bf16[128,768]{1,0:T(8,128)(2,1)S(1)}, u32[]{:S(2)}, u32[]{:S(2)}) collective-permute-start(bf16[128,768]{1,0:T(8,128)(2,1)S(1)} %get-tuple-element.32), channel_id=1, source_target_pairs={{0,16},{8,24},{16,0},{24,8},{1,17},{9,25},{17,1},{25,9},{2,18},{10... | collective-permute-start | bytes 589832 | tf_op jit(solution)/shard_map/ppermute | solution.py:265
  45.5 1.8 %collective-permute-start.1 = (bf16[2,128,768]{2,1,0:T(8,128)(2,1)S(1)}, bf16[2,128,768]{2,1,0:T(8,128)(2,1)S(1)}, u32[]{:S(2)}, u32[]{:S(2)}) collective-permute-start(bf16[2,128,768]{2,1,0:T(8,128)(2,1)S(1)} %pad_maximum_fusion.own_both), channel_id=1, source_target_pairs={{0,8},{8,0},{16,24},{24,16},{1,9},{9,1},{17,25},{25,17},{2,10},{10... | collective-permute-start | bytes 1179656 | tf_op jit(solution)/shard_map/ppermute | solution.py:265
  47.4 7.0 %collective-permute-start.2 = (bf16[128,768]{1,0:T(8,128)(2,1)S(1)}, bf16[128,768]{1,0:T(8,128)(2,1)S(1)}, u32[]{:S(2)}, u32[]{:S(2)}) collective-permute-start(bf16[128,768]{1,0:T(8,128)(2,1)S(1)} %fusion.own_0), channel_id=1, source_target_pairs={{0,16},{8,24},{16,0},{24,8},{1,17},{9,25},{17,1},{25,9},{2,18},{10... | collective-permute-start | bytes 589832 | tf_op jit(solution)/shard_map/ppermute | solution.py:265

commit v11 on v10

--- a/solution.py
+++ b/solution.py
@@ -12,8 +12,9 @@
 PREPARE_BYTES = 63 * 1024 * 1024
 CROP_BUDGET = 32 * 1024 * 1024
 BLOCK_ROWS = 8
-STEP_ROWS = 16
+STEP_ROWS = 32
 KEPT = 10
+TAIL_ROWS = 16
 F32 = jnp.float32
 BF16 = jnp.bfloat16
 
@@ -105,42 +106,40 @@
     return jnp.max(jnp.where(inside, block.astype(F32), 0.0)).astype(jnp.int32)
 
 
-def crop_length(state_ref, cells):
-    return tail_values(state_ref[:, 2 * cells :, :], 0, 64)
-
-
-def own_place(state_ref, cells):
-    return tail_values(state_ref[0, 2 * cells :, :], 64, 128)
-
-
-def joined(ref, first, count, cells, place):
-    span = slice(place * cells, (place + 1) * cells)
-    return jnp.concatenate([ref[first + q, span, :] for q in range(count)], axis=0)
+def own_place(pair_ref):
+    return tail_values(pair_ref[0, -TAIL_ROWS:, :], 64, 128)
+
+
+def place_of(own, jump, side):
+    return own ^ (2 * jump) ^ side
 
 
 def block(t, rows, n):
     return pl.ds(pl.multiple_of(t * rows * n, rows * n), rows * n)
 
 
-def forward(n, state_ref, w, b, gain, shift, w_out, b_out, *refs):
+def forward(n, jumps, *refs):
+    pairs, refs = refs[: len(jumps)], refs[len(jumps) :]
+    (weights, vectors), refs = refs[:2], refs[2:]
     (edges_s, slopes_s, gate_s, hat_s, rstd_s) = refs[:5]
     (p_hat_s, p_rstd_s, branch_s, normed_s, mixed_s) = refs[5:KEPT]
     (next_s,) = refs[KEPT:]
-    parts, _, c = state_ref.shape
-    rows = n // parts
+    c = weights.shape[1]
+    width = weights.shape[2] - c
+    rows = n // (2 * len(jumps))
     cells = rows * n
-    length = crop_length(state_ref, cells)
+    tails = jnp.stack([pair[:, cells:, :] for pair in pairs])
+    length = tail_values(tails, 0, 64)
+    own = own_place(pairs[0])
+    for pair, jump in zip(pairs, jumps):
+        for side in range(2):
+            next_s[block(place_of(own, jump, side), rows, n), :] = pair[side, :cells, :]
     steps = n // STEP_ROWS
-
-    @pl.loop(0, parts)
-    def _(t):
-        next_s[block(t, rows, n), :] = state_ref[t, :cells, :]
 
     @pl.loop(0, 2)
     def _(u):
-        bias, gains, shifts, bias_out = (
-            jnp.where(u == 0, ref[0:1, :], ref[1:2, :]) for ref in (b, gain, shift, b_out)
-        )
+        row = jnp.where(u == 0, vectors[0:1, :], vectors[1:2, :])
+        bias, gains, shifts, bias_out = vector_parts(row, c, width)
 
         @pl.loop(0, steps)
         def _(t):
@@ -148,7 +147,7 @@
             here = block(t, STEP_ROWS, n)
             mask = pair_mask_block(length, first, STEP_ROWS, n, c)
             x_hat, rstd, normed, s_left, s_right, left, right, gate = project(
-                next_s[here, :], mask, w[u], bias, gains[:, :c], shifts[:, :c]
+                next_s[here, :], mask, weights[u, :, :width], bias, gains[:, :c], shifts[:, :c]
             )
             edges_s[u, 0, here, :] = left
             edges_s[u, 1, here, :] = right
@@ -171,7 +170,7 @@
                 contract(n, t * STEP_ROWS + r, x, y) for r in range(0, STEP_ROWS, BLOCK_ROWS)
             ]
             p_hat, p_rstd, mixed, branch = mix(
-                jnp.concatenate(product).astype(BF16), gains[:, c:], shifts[:, c:], w_out[u], bias_out
+                jnp.concatenate(product).astype(BF16), gains[:, c:], shifts[:, c:], weights[u, :, width:], bias_out
             )
             p_hat_s[u, here, :] = p_hat
             p_rstd_s[u, here, :] = p_rstd
@@ -181,36 +180,40 @@
             next_s[here, :] = (x + gate_s[u, here, :] * branch).astype(BF16)
 
 
-def backward(n, u, *refs):
-    up_in_ref, w, gain, w_out = refs[:4]
-    (edges_s, slopes_s, gate_s, hat_s, rstd_s) = (ref.at[u] for ref in refs[4:9])
-    (p_hat_s, p_rstd_s, branch_s, normed_s, mixed_s) = (ref.at[u] for ref in refs[9 : 4 + KEPT])
+def backward(n, u, jumps, *refs):
     if u == 1:
-        up_ref, grads_ref, d_product_s, d_edges_s, sums_s, d_pre_s = refs[4 + KEPT :]
+        (pair, *parted), refs = refs[: 1 + len(jumps)], refs[1 + len(jumps) :]
+        up_in_ref, refs = refs[-1], (None,) + refs[:-1]
+        own = own_place(pair)
+        for part, jump in zip(parted, jumps):
+            for side in range(2):
+                rows = part.shape[1] // n
+                up_in_ref[block(place_of(own, jump, side), rows, n), :] = part[side]
     else:
-        d_pre_s, grads_ref, d_product_s, d_edges_s, sums_s = refs[4 + KEPT :]
-    c, h = w.shape[1], edges_s.shape[2]
+        up_in_ref = refs[0]
+    weights, vectors = refs[1:3]
+    (edges_s, slopes_s, gate_s, hat_s, rstd_s) = (ref.at[u] for ref in refs[3:8])
+    (p_hat_s, p_rstd_s, branch_s, normed_s, mixed_s) = (ref.at[u] for ref in refs[8 : 3 + KEPT])
+    if u == 1:
+        up_ref, grads_ref, d_product_s, d_edges_s, sums_s, d_pre_s = refs[3 + KEPT :]
+    else:
+        d_pre_s, grads_ref, d_product_s, d_edges_s, sums_s = refs[3 + KEPT :]
+    c, h = weights.shape[1], edges_s.shape[2]
     width = 4 * h + c
+    gain = vector_parts(vectors[u : u + 1, :], c, width)[1]
     sums_s[...] = jnp.zeros_like(sums_s)
-
-    def upstream(t, rows):
-        if u == 0:
-            return up_in_ref[block(t, rows, n), :]
-        own = n // up_in_ref.shape[0]
-        per = rows // own
-        return joined(up_in_ref, t * per, per, own * n, 1).astype(F32)
 
     @pl.loop(0, n // STEP_ROWS)
     def _(t):
         here = block(t, STEP_ROWS, n)
         d_branch, d_gate, d_product = unmix(
-            upstream(t, STEP_ROWS),
+            up_in_ref[here, :].astype(F32),
             gate_s[here, :],
             branch_s[here, :],
             p_hat_s[here, :],
             p_rstd_s[here, :],
-            gain[u : u + 1, c:],
-            w_out[u],
+            gain[:, c:],
+            weights[u, :, width:],
         )
         sums_s[:, width:] += dot(mixed_s[here, :], d_branch, ((0,), (0,)))
         d_pre_s[here, 4 * h :] = d_gate
@@ -242,9 +245,9 @@
         d_pre = jnp.concatenate([*grads, d_pre_s[here, 4 * h :]], axis=1)
         normed = normed_s[here, :]
         if u == 1:
-            d_normed = dot(d_pre, w[u], ((1,), (1,))) * gain[u : u + 1, :c]
+            d_normed = dot(d_pre, weights[u, :, :width], ((1,), (1,))) * gain[:, :c]
             pulled = norm_vjp(hat_s[here, :], rstd_s[here, :], d_normed)
-            up_ref[here, :] = upstream(t, STEP_ROWS) + pulled
+            up_ref[here, :] = up_in_ref[here, :].astype(F32) + pulled
         else:
             d_pre_s[here, : 4 * h] = d_pre[:, : 4 * h]
         sums_s[:, :width] += dot(normed, d_pre, ((0,), (0,)))
@@ -252,11 +255,13 @@
     grads_ref[...] = sums_s[...].astype(BF16)
 
 
-def own_rows(state_ref, up_ref, d_pre_ref, w, gain, hat_ref, rstd_ref, out_ref):
+def own_rows(pair_ref, up_ref, d_pre_ref, weights, vectors, hat_ref, rstd_ref, out_ref):
     cells, c = out_ref.shape
-    place = own_place(state_ref, cells)
+    place = own_place(pair_ref)
     own = pl.ds(pl.multiple_of(place * cells, cells), cells)
-    d_normed = dot(d_pre_ref[own, :], w[0], ((1,), (1,))) * gain[0:1, :c]
+    width = d_pre_ref.shape[1]
+    gain = vector_parts(vectors[0:1, :], c, width)[1]
+    d_normed = dot(d_pre_ref[own, :], weights[0, :, :width], ((1,), (1,))) * gain[:, :c]
     pulled = norm_vjp(hat_ref[0, own, :], rstd_ref[0, own, :], d_normed)
     out_ref[...] = (up_ref[own, :] + pulled).astype(BF16)
 
@@ -269,24 +274,43 @@
     return (a.astype(F32) + b.astype(F32)).astype(BF16)
 
 
-def prepare(state_ref, mask_ref, cot_ref, sent_ref, state_s, mask_s, cot_s, sems):
-    parts, _, c = sent_ref.shape
-    cells = state_s.shape[0]
-    copies = [
-        pltpu.make_async_copy(*pair, sems.at[k])
-        for k, pair in enumerate(((mask_ref, mask_s), (state_ref, state_s), (cot_ref, cot_s)))
-    ]
+def prepare(
+    index_ref, mask_ref, state_ref, cot_ref, w, w_out, b, gain, shift, b_out, *refs
+):
+    sent_ref, weights_ref, vectors_ref, mask_s, tail_s, sems = refs
+    cells, c = state_ref.shape
+    below, width = cells + TAIL_ROWS, w.shape[2]
+    copies = [(mask_ref, mask_s), (state_ref, sent_ref.at[:cells]), (cot_ref, sent_ref.at[below:])]
+    copies += [(w, weights_ref.at[:, :, :width]), (w_out, weights_ref.at[:, :, width:])]
+    first = 0
+    for vector in (b, gain, shift, b_out):
+        last = first + vector.shape[1]
+        copies.append((vector, vectors_ref.at[:, first:last]))
+        first = last
+    copies = [pltpu.make_async_copy(*pair, sems.at[k]) for k, pair in enumerate(copies)]
     for copy in copies:
         copy.start()
     copies[0].wait()
     length = jnp.max(jnp.sum(mask_s[...].astype(F32), axis=1, keepdims=True))
-    in_length = lax.broadcasted_iota(jnp.int32, (16, c), 1) < 64
+    in_length = lax.broadcasted_iota(jnp.int32, tail_s.shape, 1) < 64
+    place = index_ref[0].astype(F32)
+    tail_s[...] = jnp.where(in_length, length, place).astype(BF16)
+    copies.append(
+        pltpu.make_async_copy(tail_s, sent_ref.at[cells:below], sems.at[len(copies)])
+    )
+    copies[-1].start()
     for copy in copies[1:]:
         copy.wait()
-    for part in range(parts):
-        sent_ref[part, :cells, :] = state_s[...]
-        sent_ref[part, cells : 2 * cells, :] = cot_s[...]
-        sent_ref[part, 2 * cells :, :] = jnp.where(in_length, length, float(part)).astype(BF16)
+
+
+def hold(weights_in, vectors_in, weights_out, vectors_out):
+    weights_out[...] = weights_in[...]
+    vectors_out[...] = vectors_in[...]
+
+
+def vector_parts(row, c, width):
+    ends = [width, width + 2 * c, width + 4 * c, width + 5 * c]
+    return [row[:, first:last] for first, last in zip([0] + ends, ends)]
 
 
 def add_grads(own_0, other_0, own_both, other_both, proj_ref, out_ref):
@@ -329,59 +353,90 @@
             flops=flops, bytes_accessed=planes * pairs * c * 4, transcendentals=0
         )
 
-    sent = pl.pallas_call(
+    packed = (
+        jax.ShapeDtypeStruct((2, c, width + c), BF16),
+        jax.ShapeDtypeStruct((2, width + 5 * c), F32),
+    )
+    sent, *weights = pl.pallas_call(
         prepare,
-        out_shape=jax.ShapeDtypeStruct((parts, 2 * cells + 16, c), BF16),
-        in_specs=[main] * 3,
-        out_specs=vmem,
+        out_shape=(jax.ShapeDtypeStruct((2 * cells + TAIL_ROWS, c), BF16),) + packed,
+        in_specs=[pl.BlockSpec(memory_space=pltpu.SMEM)] + [main] * 9,
+        out_specs=[main] * 3,
         scratch_shapes=[
-            pltpu.VMEM((cells, c), BF16),
             pltpu.VMEM((rows, n), jnp.int32),
-            pltpu.VMEM((cells, c), BF16),
-            pltpu.SemaphoreType.DMA((3,)),
+            pltpu.VMEM((TAIL_ROWS, c), BF16),
+            pltpu.SemaphoreType.DMA((10,)),
         ],
         compiler_params=pltpu.CompilerParams(vmem_limit_bytes=PREPARE_BYTES),
         name="prepare",
-    )(pair_repr.reshape(cells, c), pair_mask[0], cotangent.reshape(cells, c))
-    state = lax.all_to_all(sent, "dap", split_axis=0, concat_axis=0, tiled=True)
+    )(
+        lax.axis_index("dap").astype(jnp.int32)[None],
+        pair_mask[0],
+        pair_repr.reshape(cells, c),
+        cotangent.reshape(cells, c),
+        proj_weight,
+        out_weight,
+        proj_bias,
+        norm_gain,
+        norm_shift,
+        out_bias,
+    )
+    weights = pl.pallas_call(
+        hold,
+        out_shape=packed,
+        in_specs=[vmem] * 2,
+        out_specs=[vmem] * 2,
+        compiler_params=params,
+        cost_estimate=cost(8),
+        name="hold",
+    )(*weights)
+    beside = exchange(sent, "dap", parts, 1)
+    beside, *weights = lax.optimization_barrier((beside, *weights))
+    split = cells + TAIL_ROWS
+    states = [jnp.stack([sent[:split], beside[:split]])]
+    cots = [jnp.stack([sent[split:], beside[split:]])]
+    half = parts // 2
+    jumps = [0, *range(1, half // 2), *reversed(range(half // 2, half))]
+    for group in (states, cots):
+        group += [exchange(group[0], "dap", parts, 2 * jump) for jump in jumps[1:]]
 
     held = pl.pallas_call(
-        functools.partial(forward, n),
+        functools.partial(forward, n, jumps),
         out_shape=kept,
-        in_specs=[vmem] * 7,
+        in_specs=[vmem] * (half + 2),
         out_specs=(vmem,) * KEPT,
         scratch_shapes=[pltpu.VMEM((pairs, c), BF16)],
         compiler_params=params,
         cost_estimate=cost(64),
         name="forward",
-    )(state, proj_weight, proj_bias, norm_gain, norm_shift, out_weight, out_bias)
+    )(*states, *weights)
 
     work = [pltpu.VMEM((2,) + plane, F32)] * 2
     work += [pltpu.VMEM(grads.shape, F32)]
     d_pre = jax.ShapeDtypeStruct((pairs, width), BF16)
     up_1, grads_1 = pl.pallas_call(
-        functools.partial(backward, n, 1),
+        functools.partial(backward, n, 1, jumps),
         out_shape=(jax.ShapeDtypeStruct((pairs, c), F32), grads),
-        in_specs=[vmem] * (4 + KEPT),
+        in_specs=[vmem] * (3 + half + KEPT),
         out_specs=(vmem, vmem),
-        scratch_shapes=work + [pltpu.VMEM(d_pre.shape, BF16)],
+        scratch_shapes=work + [pltpu.VMEM(d_pre.shape, BF16), pltpu.VMEM((pairs, c), BF16)],
         compiler_params=params,
         cost_estimate=cost(48),
         name="backward_second",
-    )(state, proj_weight, norm_gain, out_weight, *held)
+    )(states[0], *cots, *weights, *held)
     far = groups // 2
     others_1 = exchange(grads_1, "dp", groups, far)
 
     d_pre_0, grads_0 = pl.pallas_call(
-        functools.partial(backward, n, 0),
+        functools.partial(backward, n, 0, jumps),
         out_shape=(d_pre, grads),
-        in_specs=[vmem] * (4 + KEPT),
+        in_specs=[vmem] * (3 + KEPT),
         out_specs=(vmem, vmem),
         scratch_shapes=work,
         compiler_params=params,
         cost_estimate=cost(48),
         name="backward_first",
-    )(up_1, proj_weight, norm_gain, out_weight, *held)
+    )(up_1, *weights, *held)
 
     pair_grad = pl.pallas_call(
         own_rows,
@@ -391,7 +446,7 @@
         compiler_params=params,
         cost_estimate=cost(8),
         name="own_rows",
-    )(state, up_1, d_pre_0, proj_weight, norm_gain, held[3], held[4])
+    )(states[0], up_1, d_pre_0, *weights, held[3], held[4])
 
     both = jnp.stack([grads_0, add_narrow(grads_1, others_1)])
     others = jnp.zeros_like(both)
@@ -614,7 +669,7 @@
         n, c = args[0].shape[2:]
         rows = n // parts
         fits = 20 * n * n * c * 4 <= CROP_BUDGET
-        paired = groups > 1 and groups & (groups - 1) == 0
+        paired = all(size > 1 and size & (size - 1) == 0 for size in (groups, parts))
         even = args[7].shape[1] == c == 128 and STEP_ROWS % rows == 0 and n % STEP_ROWS == 0
         body = functools.partial(crop_shards, groups, parts) if fits and even and paired else shards
         return spread_over(body)(*args)

time: 55.6 us -> 61.4 us (1.10)
  the two profiles are of different devices: /device:TPU:0 before, /device:TPU:16 now
where the time goes in v11:
time: 61.4 us; the launch traced here: 61.1 us
  Pallas kernels  33 us (54%)
  starting transfers between devices  15.5 us (25%)
  waiting for transfers between devices  8.47 us (14%)
  local copies, waits for them, and re-layouts  3.27 us (5%)
  between operations  0.75 us (1%)
    ppermute x10, starting transfers between devices, exchange(): return lax.ppermute(value, axis, [(d, d ^ step) for d in range(size)])  15.5 us
    pallas_call x1, Pallas kernels, crop_shards(): pl.pallas_call(prepare, out_shape=(jax.ShapeDtypeStruct((2 * cells + TAIL...  15.4 us
    ppermute x10, waiting for transfers between devices, exchange(): return lax.ppermute(value, axis, [(d, d ^ step) for d in range(size)])  8.47 us
    pallas_call x1, Pallas kernels, crop_shards(): pl.pallas_call(functools.partial(forward, n, jumps), out_shape=kept, in_s...  6.65 us
    pallas_call x1, Pallas kernels, crop_shards(): pl.pallas_call(functools.partial(backward, n, 1, jumps), out_shape=(jax.S...  4.58 us
    pallas_call x1, Pallas kernels, crop_shards(): pl.pallas_call(functools.partial(backward, n, 0, jumps), out_shape=(d_pre...  4.34 us
    unnamed x4, local copies, waits for them, and re-layouts  1.7 us
  transfers between devices with their start and end apart: 10, of which 4 were waited for; matrix products, arithmetic and copies ran while one was open for 3% of the time, Pallas kernels for 20%

profile of v11, /device:TPU:16, one launch (start us, length us, event | category | flops | bytes accessed | tf_op | source)
XLA Modules:
  0.0 61.1 jit_solution(3608407935599158319)
XLA Ops:
  0.6 15.4 %prepare.1 = (bf16[272,128]{1,0:T(8,128)(2,1)}, bf16[2,128,768]{2,1,0:T(8,128)(2,1)}, f32[2,1280]{1,0:T(2,128)}) custom-call(s32[1]{0:T(128)} %bitcast.index_ref, s32[4,32]{1,0:T(4,128)} %bitcast.25, bf16[128,128]{1,0:T(8,128)(2,1)} %bitcast.23, bf16[128,128]{1,0:T(8,128)(2,1)} %bitcast.24, bf16[2,128,640]{2,1,0:T(8,128)(2,1)} %w.1, ...), custom_call_target="tpu_custom_call" | custom-call | tf_op jit(solution)/shard_map/prepare/pallas_call | solution.py:360
  16.0 1.6 %collective-permute-start = (bf16[272,128]{1,0:T(8,128)(2,1)}, bf16[272,128]{1,0:T(8,128)(2,1)S(1)}, u32[]{:S(2)}, u32[]{:S(2)}) collective-permute-start(bf16[272,128]{1,0:T(8,128)(2,1)} %get-tuple-element.27), channel_id=1, source_target_pairs={{0,1},{1,0},{2,3},{3,2},{4,5},{5,4},{6,7},{7,6},{8,9},{9,8},{10,11... | collective-permute-start | bytes 208904 | tf_op jit(solution)/shard_map/ppermute | solution.py:270
  17.6 0.8 %slice_bitcast_fusion.2 = bf16[1,144,128]{2,1,0:T(8,128)(2,1)S(1)} fusion(bf16[272,128]{1,0:T(8,128)(2,1)} %get-tuple-element.27), kind=kLoop, calls=%fused_computation.9 | loop fusion | bytes 73728 | tf_op jit(solution)/shard_map/stack | solution.py:396
  18.4 0.8 %slice_bitcast_fusion.4 = bf16[1,128,128]{2,1,0:T(8,128)(2,1)S(1)} fusion(bf16[272,128]{1,0:T(8,128)(2,1)} %get-tuple-element.27), kind=kLoop, calls=%fused_computation.11 | loop fusion | bytes 65536 | tf_op jit(solution)/shard_map/stack | solution.py:397
  19.2 0.0 copy-start
  19.2 1.0 %copy-done = bf16[2,128,768]{2,1,0:T(8,128)(2,1)S(1)} copy-done((bf16[2,128,768]{2,1,0:T(8,128)(2,1)S(1)}, bf16[2,128,768]{2,1,0:T(8,128)(2,1)}, u32[]{:S(2)}) %copy-start) | copy-done | bytes 393240
  20.2 0.0 copy-start.1
  20.2 0.7 %copy-done.1 = f32[2,1280]{1,0:T(2,128)S(1)} copy-done((f32[2,1280]{1,0:T(2,128)S(1)}, f32[2,1280]{1,0:T(2,128)}, u32[]{:S(2)}) %copy-start.1) | copy-done | bytes 10264
  20.9 0.0 collective-permute-done
  21.0 0.4 collective-permute-start.6
  21.4 2.7 %collective-permute-start.5 = (bf16[2,144,128]{2,1,0:T(8,128)(2,1)S(1)}, bf16[2,144,128]{2,1,0:T(8,128)(2,1)S(1)}, u32[]{:S(2)}, u32[]{:S(2)}) collective-permute-start(bf16[2,144,128]{2,1,0:T(8,128)(2,1)S(1)} %pad_maximum_fusion.1.refs_0_.pair_ref), channel_id=1, source_target_pairs={{0,6},{1,7},{2,4},{3,5},{4,2},{5,3},{6,0},{7,1},{8,14},{9,15},{10,... | collective-permute-start | bytes 221192 | tf_op jit(solution)/shard_map/ppermute | solution.py:270
  24.1 1.3 %collective-permute-start.4 = (bf16[2,144,128]{2,1,0:T(8,128)(2,1)S(1)}, bf16[2,144,128]{2,1,0:T(8,128)(2,1)S(1)}, u32[]{:S(2)}, u32[]{:S(2)}) collective-permute-start(bf16[2,144,128]{2,1,0:T(8,128)(2,1)S(1)} %pad_maximum_fusion.1.refs_0_.pair_ref), channel_id=1, source_target_pairs={{0,2},{1,3},{2,0},{3,1},{4,6},{5,7},{6,4},{7,5},{8,10},{9,11},{10,... | collective-permute-start | bytes 221192 | tf_op jit(solution)/shard_map/ppermute | solution.py:270
  25.4 0.2 collective-permute-start.3
  25.6 2.0 %collective-permute-start.2 = (bf16[2,128,128]{2,1,0:T(8,128)(2,1)S(1)}, bf16[2,128,128]{2,1,0:T(8,128)(2,1)S(1)}, u32[]{:S(2)}, u32[]{:S(2)}) collective-permute-start(bf16[2,128,128]{2,1,0:T(8,128)(2,1)S(1)} %pad_maximum_fusion.2.refs_1_), channel_id=1, source_target_pairs={{0,6},{1,7},{2,4},{3,5},{4,2},{5,3},{6,0},{7,1},{8,14},{9,15},{10,... | collective-permute-start | bytes 196616 | tf_op jit(solution)/shard_map/ppermute | solution.py:270
  27.6 0.0 collective-permute-done.6.refs_3_
  27.6 4.1 %collective-permute-start.1 = (bf16[2,128,128]{2,1,0:T(8,128)(2,1)S(1)}, bf16[2,128,128]{2,1,0:T(8,128)(2,1)S(1)}, u32[]{:S(2)}, u32[]{:S(2)}) collective-permute-start(bf16[2,128,128]{2,1,0:T(8,128)(2,1)S(1)} %pad_maximum_fusion.2.refs_1_), channel_id=1, source_target_pairs={{0,2},{1,3},{2,0},{3,1},{4,6},{5,7},{6,4},{7,5},{8,10},{9,11},{10,... | collective-permute-start | bytes 196616 | tf_op jit(solution)/shard_map/ppermute | solution.py:270
  31.7 1.8 %collective-permute-done.5.refs_2_ = bf16[2,144,128]{2,1,0:T(8,128)(2,1)S(1)} collective-permute-done((bf16[2,144,128]{2,1,0:T(8,128)(2,1)S(1)}, bf16[2,144,128]{2,1,0:T(8,128)(2,1)S(1)}, u32[]{:S(2)}, u32[]{:S(2)}) %collective-permute-start.5) | collective-permute-done | bytes 73760 | tf_op jit(solution)/shard_map/ppermute | solution.py:270
  33.5 0.0 collective-permute-done.4.refs_1_
  33.5 6.7 %forward.1 = (f32[2,4,1032,128]{3,2,1,0:T(8,128)S(1)}, f32[2,2,1032,128]{3,2,1,0:T(8,128)S(1)}, f32[2,1032,128]{2,1,0:T(8,128)S(1)}, f32[2,1032,128]{2,1,0:T(8,1...) custom-call(bf16[2,144,128]{2,1,0:T(8,128)(2,1)S(1)} %pad_maximum_fu, ...), custom_call_target="tpu_custom_call" | custom-call | flops 335544320 | bytes 33554432 | tf_op jit(solution)/shard_map/forward/pallas_call | solution.py:403
  40.2 0.0 collective-permute-done.3.refs_4_
  40.2 0.0 collective-permute-done.2.refs_3_
  40.2 0.0 collective-permute-done.1.refs_2_
  40.2 4.6 %backward_second.1 = (f32[1024,128]{1,0:T(8,128)S(1)}, bf16[128,768]{1,0:T(8,128)(2,1)S(1)}) custom-call(bf16[2,144,128]{2,1,0:T(8,128)(2,1)S(1)} %pad_maximum_fusion.1.refs_0_.pair_ref, bf16[2,128,128]{2,1,0:T(8,128)(2,1)S(1)} %pad_maximum_fusion.2.refs_1_, bf16[2,128,128]{2,1,0:T(8,128)(2,1)S(1)} %collective-permute-done.1.refs_2_, ...), custom_call_target="tpu_custom_call" | custom-call | flops 335544320 | bytes 25165824 | tf_op jit(solution)/shard_map/backward_second/pallas_call | solution.py:417
  44.8 1.6 %collective-permute-start.7 = (bf16[128,768]{1,0:T(8,128)(2,1)S(1)}, bf16[128,768]{1,0:T(8,128)(2,1)S(1)}, u32[]{:S(2)}, u32[]{:S(2)}) collective-permute-start(bf16[128,768]{1,0:T(8,128)(2,1)S(1)} %get-tuple-element.48), channel_id=1, source_target_pairs={{0,16},{8,24},{16,0},{24,8},{1,17},{9,25},{17,1},{25,9},{2,18},{10... | collective-permute-start | bytes 589832 | tf_op jit(solution)/shard_map/ppermute | solution.py:270
  46.4 4.3 %backward_first.1 = (bf16[1024,640]{1,0:T(8,128)(2,1)S(1)}, bf16[128,768]{1,0:T(8,128)(2,1)S(1)}) custom-call(f32[1024,128]{1,0:T(8,128)S(1)} %get-tuple-element.45.refs_0_.up_ref, bf16[2,128,768]{2,1,0:T(8,128)(2,1)S(1)} %get-tuple-element.33.refs_4_.refs_5_.refs_1_.weights, f32[2,1280]{1,0:T(2,128)S(1)} %get-tuple-element.34.refs_5_.refs_6_.refs_2_.vectors, ...), custom_call_target="tpu_custom_call" | custom-call | flops 335544320 | bytes 25165824 | tf_op jit(solution)/shard_map/backward_first/pallas_call | solution.py:430
  50.7 0.5 collective-permute-done.7
  51.3 0.1 collective-permute-start.8
  51.4 1.7 %collective-permute-done.8.other_both = bf16[2,128,768]{2,1,0:T(8,128)(2,1)S(1)} collective-permute-done((bf16[2,128,768]{2,1,0:T(8,128)(2,1)S(1)}, bf16[2,128,768]{2,1,0:T(8,128)(2,1)S(1)}, u32[]{:S(2)}, u32[]{:S(2)}) %collective-permute-start.8) | collective-permute-done | bytes 393248 | tf_op jit(solution)/shard_map/ppermute | solution.py:270
  53.1 1.5 %collective-permute-start.9 = (bf16[128,768]{1,0:T(8,128)(2,1)S(1)}, bf16[128,768]{1,0:T(8,128)(2,1)S(1)}, u32[]{:S(2)}, u32[]{:S(2)}) collective-permute-start(bf16[128,768]{1,0:T(8,128)(2,1)S(1)} %fusion.own_0), channel_id=1, source_target_pairs={{0,16},{8,24},{16,0},{24,8},{1,17},{9,25},{17,1},{25,9},{2,18},{10... | collective-permute-start | bytes 589832 | tf_op jit(solution)/shard_map/ppermute | solution.py:270
  54.7 1.0 %own_rows.1 = bf16[128,128]{1,0:T(8,128)(2,1)} custom-call(bf16[2,144,128]{2,1,0:T(8,128)(2,1)S(1)} %pad_maximum_fusion.1.refs_0_.pair_ref, f32[1024,128]{1,0:T(8,128)S(1)} %get-tuple-element.45.refs_0_.up_ref, bf16[1024,640]{1,0:T(8,128)(2,1)S(1)} %get-tuple-element.46.d_pre_ref, bf16[2,128,768]{2,1,0:T(8,128)(2,1)S(1)} %get-tuple-element.33.refs_4_.refs_5_.refs_1_.weights, ...), custom_call_target="tpu_custom_call" | custom-call | flops 335544320 | bytes 4194304 | tf_op jit(solution)/shard_map/own_rows/pallas_call | solution.py:441
  55.7 4.4 %collective-permute-done.9.other_0 = bf16[128,768]{1,0:T(8,128)(2,1)S(1)} collective-permute-done((bf16[128,768]{1,0:T(8,128)(2,1)S(1)}, bf16[128,768]{1,0:T(8,128)(2,1)S(1)}, u32[]{:S(2)}, u32[]{:S(2)}) %collective-permute-start.9) | collective-permute-done | bytes 196640 | tf_op jit(solution)/shard_map/ppermute | solution.py:270
  60.1 0.9 %add_grads.1 = (f32[2,128,640]{2,1,0:T(8,128)}, f32[2,128,128]{2,1,0:T(8,128)}) custom-call(bf16[128,768]{1,0:T(8,128)(2,1)S(1)} %fusion.own_0, bf16[128,768]{1,0:T(8,128)(2,1)S(1)} %collective-permute-done.9.other_0, bf16[2,128,768]{2,1,0:T(8,128)(2,1)S(1)} %pad_maximum_fusion.own_both, bf16[2,128,768]{2,1,0:T(8,128)(2,1)S(1)} %collective-permute-done.8.other_both), custom_call_target="tpu_custom_call" | custom-call | tf_op jit(solution)/shard_map/add_grads/pallas_call | solution.py:461
  (8 shorter events, 0.2 us)
Async XLA Ops:
  16.0 4.9 %collective-permute-start = (bf16[272,128]{1,0:T(8,128)(2,1)}, bf16[272,128]{1,0:T(8,128)(2,1)S(1)}, u32[]{:S(2)}, u32[]{:S(2)}) collective-permute-start(bf16[272,128]{1,0:T(8,128)(2,1)} %get-tuple-element.27), channel_id=1, source_target_pairs={{0,1},{1,0},{2,3},{3,2},{4,5},{5,4},{6,7},{7,6},{8,9},{9,8},{10,11... | collective-permute-start | bytes 208904 | tf_op jit(solution)/shard_map/ppermute | solution.py:270
  19.2 1.0 %copy-start = (bf16[2,128,768]{2,1,0:T(8,128)(2,1)S(1)}, bf16[2,128,768]{2,1,0:T(8,128)(2,1)}, u32[]{:S(2)}) copy-start(bf16[2,128,768]{2,1,0:T(8,128)(2,1)} %get-tuple-element.28.weights_in) | copy-start | bytes 1179652
  20.2 0.7 %copy-start.1 = (f32[2,1280]{1,0:T(2,128)S(1)}, f32[2,1280]{1,0:T(2,128)}, u32[]{:S(2)}) copy-start(f32[2,1280]{1,0:T(2,128)} %get-tuple-element.29.vectors_in) | copy-start | bytes 30724
  21.0 6.7 %collective-permute-start.6 = (bf16[2,144,128]{2,1,0:T(8,128)(2,1)S(1)}, bf16[2,144,128]{2,1,0:T(8,128)(2,1)S(1)}, u32[]{:S(2)}, u32[]{:S(2)}) collective-permute-start(bf16[2,144,128]{2,1,0:T(8,128)(2,1)S(1)} %pad_maximum_fusion.1.refs_0_.pair_ref), channel_id=1, source_target_pairs={{0,4},{1,5},{2,6},{3,7},{4,0},{5,1},{6,2},{7,3},{8,12},{9,13},{10,... | collective-permute-start | bytes 221192 | tf_op jit(solution)/shard_map/ppermute | solution.py:270
  21.4 12.1 %collective-permute-start.5 = (bf16[2,144,128]{2,1,0:T(8,128)(2,1)S(1)}, bf16[2,144,128]{2,1,0:T(8,128)(2,1)S(1)}, u32[]{:S(2)}, u32[]{:S(2)}) collective-permute-start(bf16[2,144,128]{2,1,0:T(8,128)(2,1)S(1)} %pad_maximum_fusion.1.refs_0_.pair_ref), channel_id=1, source_target_pairs={{0,6},{1,7},{2,4},{3,5},{4,2},{5,3},{6,0},{7,1},{8,14},{9,15},{10,... | collective-permute-start | bytes 221192 | tf_op jit(solution)/shard_map/ppermute | solution.py:270
  24.1 9.4 %collective-permute-start.4 = (bf16[2,144,128]{2,1,0:T(8,128)(2,1)S(1)}, bf16[2,144,128]{2,1,0:T(8,128)(2,1)S(1)}, u32[]{:S(2)}, u32[]{:S(2)}) collective-permute-start(bf16[2,144,128]{2,1,0:T(8,128)(2,1)S(1)} %pad_maximum_fusion.1.refs_0_.pair_ref), channel_id=1, source_target_pairs={{0,2},{1,3},{2,0},{3,1},{4,6},{5,7},{6,4},{7,5},{8,10},{9,11},{10,... | collective-permute-start | bytes 221192 | tf_op jit(solution)/shard_map/ppermute | solution.py:270
  25.4 14.7 %collective-permute-start.3 = (bf16[2,128,128]{2,1,0:T(8,128)(2,1)S(1)}, bf16[2,128,128]{2,1,0:T(8,128)(2,1)S(1)}, u32[]{:S(2)}, u32[]{:S(2)}) collective-permute-start(bf16[2,128,128]{2,1,0:T(8,128)(2,1)S(1)} %pad_maximum_fusion.2.refs_1_), channel_id=1, source_target_pairs={{0,4},{1,5},{2,6},{3,7},{4,0},{5,1},{6,2},{7,3},{8,12},{9,13},{10,... | collective-permute-start | bytes 196616 | tf_op jit(solution)/shard_map/ppermute | solution.py:270
  25.6 14.6 %collective-permute-start.2 = (bf16[2,128,128]{2,1,0:T(8,128)(2,1)S(1)}, bf16[2,128,128]{2,1,0:T(8,128)(2,1)S(1)}, u32[]{:S(2)}, u32[]{:S(2)}) collective-permute-start(bf16[2,128,128]{2,1,0:T(8,128)(2,1)S(1)} %pad_maximum_fusion.2.refs_1_), channel_id=1, source_target_pairs={{0,6},{1,7},{2,4},{3,5},{4,2},{5,3},{6,0},{7,1},{8,14},{9,15},{10,... | collective-permute-start | bytes 196616 | tf_op jit(solution)/shard_map/ppermute | solution.py:270
  27.6 12.6 %collective-permute-start.1 = (bf16[2,128,128]{2,1,0:T(8,128)(2,1)S(1)}, bf16[2,128,128]{2,1,0:T(8,128)(2,1)S(1)}, u32[]{:S(2)}, u32[]{:S(2)}) collective-permute-start(bf16[2,128,128]{2,1,0:T(8,128)(2,1)S(1)} %pad_maximum_fusion.2.refs_1_), channel_id=1, source_target_pairs={{0,2},{1,3},{2,0},{3,1},{4,6},{5,7},{6,4},{7,5},{8,10},{9,11},{10,... | collective-permute-start | bytes 196616 | tf_op jit(solution)/shard_map/ppermute | solution.py:270
  44.8 6.4 %collective-permute-start.7 = (bf16[128,768]{1,0:T(8,128)(2,1)S(1)}, bf16[128,768]{1,0:T(8,128)(2,1)S(1)}, u32[]{:S(2)}, u32[]{:S(2)}) collective-permute-start(bf16[128,768]{1,0:T(8,128)(2,1)S(1)} %get-tuple-element.48), channel_id=1, source_target_pairs={{0,16},{8,24},{16,0},{24,8},{1,17},{9,25},{17,1},{25,9},{2,18},{10... | collective-permute-start | bytes 589832 | tf_op jit(solution)/shard_map/ppermute | solution.py:270
  51.3 1.8 %collective-permute-start.8 = (bf16[2,128,768]{2,1,0:T(8,128)(2,1)S(1)}, bf16[2,128,768]{2,1,0:T(8,128)(2,1)S(1)}, u32[]{:S(2)}, u32[]{:S(2)}) collective-permute-start(bf16[2,128,768]{2,1,0:T(8,128)(2,1)S(1)} %pad_maximum_fusion.own_both), channel_id=1, source_target_pairs={{0,8},{8,0},{16,24},{24,16},{1,9},{9,1},{17,25},{25,17},{2,10},{10... | collective-permute-start | bytes 1179656 | tf_op jit(solution)/shard_map/ppermute | solution.py:270
  53.1 7.0 %collective-permute-start.9 = (bf16[128,768]{1,0:T(8,128)(2,1)S(1)}, bf16[128,768]{1,0:T(8,128)(2,1)S(1)}, u32[]{:S(2)}, u32[]{:S(2)}) collective-permute-start(bf16[128,768]{1,0:T(8,128)(2,1)S(1)} %fusion.own_0), channel_id=1, source_target_pairs={{0,16},{8,24},{16,0},{24,8},{1,17},{9,25},{17,1},{25,9},{2,18},{10... | collective-permute-start | bytes 589832 | tf_op jit(solution)/shard_map/ppermute | solution.py:270

commit v12 on v11

--- a/solution.py
+++ b/solution.py
@@ -277,7 +277,7 @@
 def prepare(
     index_ref, mask_ref, state_ref, cot_ref, w, w_out, b, gain, shift, b_out, *refs
 ):
-    sent_ref, weights_ref, vectors_ref, mask_s, tail_s, sems = refs
+    sent_ref, weights_ref, vectors_ref, mask_s, sems = refs
     cells, c = state_ref.shape
     below, width = cells + TAIL_ROWS, w.shape[2]
     copies = [(mask_ref, mask_s), (state_ref, sent_ref.at[:cells]), (cot_ref, sent_ref.at[below:])]
@@ -292,15 +292,18 @@
         copy.start()
     copies[0].wait()
     length = jnp.max(jnp.sum(mask_s[...].astype(F32), axis=1, keepdims=True))
-    in_length = lax.broadcasted_iota(jnp.int32, tail_s.shape, 1) < 64
+    in_length = lax.broadcasted_iota(jnp.int32, (TAIL_ROWS, c), 1) < 64
     place = index_ref[0].astype(F32)
-    tail_s[...] = jnp.where(in_length, length, place).astype(BF16)
-    copies.append(
-        pltpu.make_async_copy(tail_s, sent_ref.at[cells:below], sems.at[len(copies)])
-    )
-    copies[-1].start()
+    sent_ref[cells:below, :] = jnp.where(in_length, length, place).astype(BF16)
     for copy in copies[1:]:
         copy.wait()
+
+
+def pair_up(near_ref, far_ref, state_ref, cot_ref):
+    split = state_ref.shape[1]
+    for side, ref in enumerate((near_ref, far_ref)):
+        state_ref[side] = ref[:split, :]
+        cot_ref[side] = ref[split:, :]
 
 
 def hold(weights_in, vectors_in, weights_out, vectors_out):
@@ -361,12 +364,8 @@
         prepare,
         out_shape=(jax.ShapeDtypeStruct((2 * cells + TAIL_ROWS, c), BF16),) + packed,
         in_specs=[pl.BlockSpec(memory_space=pltpu.SMEM)] + [main] * 9,
-        out_specs=[main] * 3,
-        scratch_shapes=[
-            pltpu.VMEM((rows, n), jnp.int32),
-            pltpu.VMEM((TAIL_ROWS, c), BF16),
-            pltpu.SemaphoreType.DMA((10,)),
-        ],
+        out_specs=[vmem] * 3,
+        scratch_shapes=[pltpu.VMEM((rows, n), jnp.int32), pltpu.SemaphoreType.DMA((9,))],
         compiler_params=pltpu.CompilerParams(vmem_limit_bytes=PREPARE_BYTES),
         name="prepare",
     )(
@@ -392,9 +391,18 @@
     )(*weights)
     beside = exchange(sent, "dap", parts, 1)
     beside, *weights = lax.optimization_barrier((beside, *weights))
-    split = cells + TAIL_ROWS
-    states = [jnp.stack([sent[:split], beside[:split]])]
-    cots = [jnp.stack([sent[split:], beside[split:]])]
+    state, cot = pl.pallas_call(
+        pair_up,
+        out_shape=(
+            jax.ShapeDtypeStruct((2, cells + TAIL_ROWS, c), BF16),
+            jax.ShapeDtypeStruct((2, cells, c), BF16),
+        ),
+        in_specs=[vmem] * 2,
+        out_specs=[vmem] * 2,
+        compiler_params=params,
+        name="pair_up",
+    )(sent, beside)
+    states, cots = [state], [cot]
     half = parts // 2
     jumps = [0, *range(1, half // 2), *reversed(range(half // 2, half))]
     for group in (states, cots):

time: 61.4 us -> 46.7 us (0.76)
  the two profiles are of different devices: /device:TPU:16 before, /device:TPU:0 now
where the time goes in v12:
time: 46.7 us; the launch traced here: 46.2 us
  Pallas kernels  19.5 us (42%)
  starting transfers between devices  15.2 us (33%)
  waiting for transfers between devices  8.92 us (19%)
  local copies, waits for them, and re-layouts  1.7 us (4%)
  between operations  0.73 us (2%)
    ppermute x10, starting transfers between devices, exchange(): return lax.ppermute(value, axis, [(d, d ^ step) for d in range(size)])  15.2 us
    ppermute x10, waiting for transfers between devices, exchange(): return lax.ppermute(value, axis, [(d, d ^ step) for d in range(size)])  8.92 us
    pallas_call x1, Pallas kernels, crop_shards(): pl.pallas_call(functools.partial(forward, n, jumps), out_shape=kept, in_s...  6.65 us
    pallas_call x1, Pallas kernels, crop_shards(): pl.pallas_call(functools.partial(backward, n, 1, jumps), out_shape=(jax.S...  4.58 us
    pallas_call x1, Pallas kernels, crop_shards(): pl.pallas_call(functools.partial(backward, n, 0, jumps), out_shape=(d_pre...  4.34 us
    pallas_call x1, Pallas kernels, crop_shards(): pl.pallas_call(prepare, out_shape=(jax.ShapeDtypeStruct((2 * cells + TAIL...  1.88 us
    unnamed x6, local copies, waits for them, and re-layouts  1.7 us
    pallas_call x1, Pallas kernels, crop_shards(): pl.pallas_call(own_rows, out_shape=jax.ShapeDtypeStruct((cells, c), BF16)...  1.01 us
  transfers between devices with their start and end apart: 10, of which 5 were waited for; matrix products, arithmetic and copies ran while one was open for 0% of the time, Pallas kernels for 26%

profile of v12, /device:TPU:0, one launch (start us, length us, event | category | flops | bytes accessed | tf_op | source)
XLA Modules:
  0.0 46.2 jit_solution(16586478779840090640)
XLA Ops:
  0.6 1.9 %prepare.1 = (bf16[272,128]{1,0:T(8,128)(2,1)}, bf16[2,128,768]{2,1,0:T(8,128)(2,1)}, f32[2,1280]{1,0:T(2,128)}) custom-call(s32[1]{0:T(128)} %bitcast.index_ref, s32[4,32]{1,0:T(4,128)} %bitcast.17, bf16[128,128]{1,0:T(8,128)(2,1)} %bitcast.15, bf16[128,128]{1,0:T(8,128)(2,1)} %bitcast.16, bf16[2,128,640]{2,1,0:T(8,128)(2,1)} %w.1, ...), custom_call_target="tpu_custom_call" | custom-call | tf_op jit(solution)/shard_map/prepare/pallas_call | solution.py:363
  2.5 0.0 copy-start
  2.5 3.0 %collective-permute-start = (bf16[272,128]{1,0:T(8,128)(2,1)}, bf16[272,128]{1,0:T(8,128)(2,1)S(1)}, u32[]{:S(2)}, u32[]{:S(2)}) collective-permute-start(bf16[272,128]{1,0:T(8,128)(2,1)} %get-tuple-element.29.near_ref), channel_id=1, source_target_pairs={{0,1},{1,0},{2,3},{3,2},{4,5},{5,4},{6,7},{7,6},{8,9},{9,8},{10,11... | collective-permute-start | bytes 208904 | tf_op jit(solution)/shard_map/ppermute | solution.py:270
  5.6 0.0 copy-start.1
  5.6 1.0 %copy-done.1 = bf16[2,128,768]{2,1,0:T(8,128)(2,1)S(1)} copy-done((bf16[2,128,768]{2,1,0:T(8,128)(2,1)S(1)}, bf16[2,128,768]{2,1,0:T(8,128)(2,1)}, u32[]{:S(2)}) %copy-start.1) | copy-done | bytes 393240
  6.6 0.0 copy-start.2
  6.6 0.7 %copy-done.2 = f32[2,1280]{1,0:T(2,128)S(1)} copy-done((f32[2,1280]{1,0:T(2,128)S(1)}, f32[2,1280]{1,0:T(2,128)}, u32[]{:S(2)}) %copy-start.2) | copy-done | bytes 10264
  7.3 0.8 %collective-permute-done.far_ref = bf16[272,128]{1,0:T(8,128)(2,1)S(1)} collective-permute-done((bf16[272,128]{1,0:T(8,128)(2,1)}, bf16[272,128]{1,0:T(8,128)(2,1)S(1)}, u32[]{:S(2)}, u32[]{:S(2)}) %collective-permute-start) | collective-permute-done | bytes 69664 | tf_op jit(solution)/shard_map/ppermute | solution.py:270
  8.1 0.0 copy-done
  8.1 3.2 %collective-permute-start.6 = (bf16[2,144,128]{2,1,0:T(8,128)(2,1)S(1)}, bf16[2,144,128]{2,1,0:T(8,128)(2,1)S(1)}, u32[]{:S(2)}, u32[]{:S(2)}) collective-permute-start(bf16[2,144,128]{2,1,0:T(8,128)(2,1)S(1)} %get-tuple-element.35.refs_0_.pair_ref), channel_id=1, source_target_pairs={{0,4},{1,5},{2,6},{3,7},{4,0},{5,1},{6,2},{7,3},{8,12},{9,13},{10,... | collective-permute-start | bytes 221192 | tf_op jit(solution)/shard_map/ppermute | solution.py:270
  11.2 1.3 %collective-permute-start.5 = (bf16[2,144,128]{2,1,0:T(8,128)(2,1)S(1)}, bf16[2,144,128]{2,1,0:T(8,128)(2,1)S(1)}, u32[]{:S(2)}, u32[]{:S(2)}) collective-permute-start(bf16[2,144,128]{2,1,0:T(8,128)(2,1)S(1)} %get-tuple-element.35.refs_0_.pair_ref), channel_id=1, source_target_pairs={{0,6},{1,7},{2,4},{3,5},{4,2},{5,3},{6,0},{7,1},{8,14},{9,15},{10,... | collective-permute-start | bytes 221192 | tf_op jit(solution)/shard_map/ppermute | solution.py:270
  12.6 0.2 collective-permute-start.4
  12.8 2.8 %collective-permute-start.3 = (bf16[2,128,128]{2,1,0:T(8,128)(2,1)S(1)}, bf16[2,128,128]{2,1,0:T(8,128)(2,1)S(1)}, u32[]{:S(2)}, u32[]{:S(2)}) collective-permute-start(bf16[2,128,128]{2,1,0:T(8,128)(2,1)S(1)} %get-tuple-element.36.refs_1_), channel_id=1, source_target_pairs={{0,4},{1,5},{2,6},{3,7},{4,0},{5,1},{6,2},{7,3},{8,12},{9,13},{10,... | collective-permute-start | bytes 196616 | tf_op jit(solution)/shard_map/ppermute | solution.py:270
  15.6 1.3 %collective-permute-start.2 = (bf16[2,128,128]{2,1,0:T(8,128)(2,1)S(1)}, bf16[2,128,128]{2,1,0:T(8,128)(2,1)S(1)}, u32[]{:S(2)}, u32[]{:S(2)}) collective-permute-start(bf16[2,128,128]{2,1,0:T(8,128)(2,1)S(1)} %get-tuple-element.36.refs_1_), channel_id=1, source_target_pairs={{0,6},{1,7},{2,4},{3,5},{4,2},{5,3},{6,0},{7,1},{8,14},{9,15},{10,... | collective-permute-start | bytes 196616 | tf_op jit(solution)/shard_map/ppermute | solution.py:270
  17.0 0.0 collective-permute-done.6.refs_3_
  17.0 1.5 %collective-permute-start.1 = (bf16[2,128,128]{2,1,0:T(8,128)(2,1)S(1)}, bf16[2,128,128]{2,1,0:T(8,128)(2,1)S(1)}, u32[]{:S(2)}, u32[]{:S(2)}) collective-permute-start(bf16[2,128,128]{2,1,0:T(8,128)(2,1)S(1)} %get-tuple-element.36.refs_1_), channel_id=1, source_target_pairs={{0,2},{1,3},{2,0},{3,1},{4,6},{5,7},{6,4},{7,5},{8,10},{9,11},{10,... | collective-permute-start | bytes 196616 | tf_op jit(solution)/shard_map/ppermute | solution.py:270
  18.5 0.0 collective-permute-done.5.refs_2_
  18.5 0.7 %collective-permute-done.4.refs_1_ = bf16[2,144,128]{2,1,0:T(8,128)(2,1)S(1)} collective-permute-done((bf16[2,144,128]{2,1,0:T(8,128)(2,1)S(1)}, bf16[2,144,128]{2,1,0:T(8,128)(2,1)S(1)}, u32[]{:S(2)}, u32[]{:S(2)}) %collective-permute-start.4) | collective-permute-done | bytes 73760 | tf_op jit(solution)/shard_map/ppermute | solution.py:270
  19.2 6.7 %forward.1 = (f32[2,4,1032,128]{3,2,1,0:T(8,128)S(1)}, f32[2,2,1032,128]{3,2,1,0:T(8,128)S(1)}, f32[2,1032,128]{2,1,0:T(8,128)S(1)}, f32[2,1032,128]{2,1,0:T(8,1...) custom-call(bf16[2,144,128]{2,1,0:T(8,128)(2,1)S(1)} %get-tuple-elem, ...), custom_call_target="tpu_custom_call" | custom-call | flops 335544320 | bytes 33554432 | tf_op jit(solution)/shard_map/forward/pallas_call | solution.py:411
  25.9 0.0 collective-permute-done.3.refs_4_
  25.9 0.0 collective-permute-done.2.refs_3_
  25.9 0.0 collective-permute-done.1.refs_2_
  25.9 4.6 %backward_second.1 = (f32[1024,128]{1,0:T(8,128)S(1)}, bf16[128,768]{1,0:T(8,128)(2,1)S(1)}) custom-call(bf16[2,144,128]{2,1,0:T(8,128)(2,1)S(1)} %get-tuple-element.35.refs_0_.pair_ref, bf16[2,128,128]{2,1,0:T(8,128)(2,1)S(1)} %get-tuple-element.36.refs_1_, bf16[2,128,128]{2,1,0:T(8,128)(2,1)S(1)} %collective-permute-done.1.refs_2_, ...), custom_call_target="tpu_custom_call" | custom-call | flops 335544320 | bytes 25165824 | tf_op jit(solution)/shard_map/backward_second/pallas_call | solution.py:425
  30.5 0.8 %collective-permute-start.7 = (bf16[128,768]{1,0:T(8,128)(2,1)S(1)}, bf16[128,768]{1,0:T(8,128)(2,1)S(1)}, u32[]{:S(2)}, u32[]{:S(2)}) collective-permute-start(bf16[128,768]{1,0:T(8,128)(2,1)S(1)} %get-tuple-element.52), channel_id=1, source_target_pairs={{0,16},{8,24},{16,0},{24,8},{1,17},{9,25},{17,1},{25,9},{2,18},{10... | collective-permute-start | bytes 589832 | tf_op jit(solution)/shard_map/ppermute | solution.py:270
  31.4 4.3 %backward_first.1 = (bf16[1024,640]{1,0:T(8,128)(2,1)S(1)}, bf16[128,768]{1,0:T(8,128)(2,1)S(1)}) custom-call(f32[1024,128]{1,0:T(8,128)S(1)} %get-tuple-element.49.refs_0_.up_ref, bf16[2,128,768]{2,1,0:T(8,128)(2,1)S(1)} %get-tuple-element.37.refs_4_.refs_5_.refs_1_.weights, f32[2,1280]{1,0:T(2,128)S(1)} %get-tuple-element.38.refs_5_.refs_6_.refs_2_.vectors, ...), custom_call_target="tpu_custom_call" | custom-call | flops 335544320 | bytes 25165824 | tf_op jit(solution)/shard_map/backward_first/pallas_call | solution.py:438
  35.7 0.6 %collective-permute-done.7 = bf16[128,768]{1,0:T(8,128)(2,1)S(1)} collective-permute-done((bf16[128,768]{1,0:T(8,128)(2,1)S(1)}, bf16[128,768]{1,0:T(8,128)(2,1)S(1)}, u32[]{:S(2)}, u32[]{:S(2)}) %collective-permute-start.7) | collective-permute-done | bytes 196640 | tf_op jit(solution)/shard_map/ppermute | solution.py:270
  36.2 0.1 fusion.1
  36.4 0.1 collective-permute-start.8
  36.4 1.7 %collective-permute-done.8.other_both = bf16[2,128,768]{2,1,0:T(8,128)(2,1)S(1)} collective-permute-done((bf16[2,128,768]{2,1,0:T(8,128)(2,1)S(1)}, bf16[2,128,768]{2,1,0:T(8,128)(2,1)S(1)}, u32[]{:S(2)}, u32[]{:S(2)}) %collective-permute-start.8) | collective-permute-done | bytes 393248 | tf_op jit(solution)/shard_map/ppermute | solution.py:270
  38.2 0.8 %collective-permute-start.9 = (bf16[128,768]{1,0:T(8,128)(2,1)S(1)}, bf16[128,768]{1,0:T(8,128)(2,1)S(1)}, u32[]{:S(2)}, u32[]{:S(2)}) collective-permute-start(bf16[128,768]{1,0:T(8,128)(2,1)S(1)} %fusion.own_0), channel_id=1, source_target_pairs={{0,16},{8,24},{16,0},{24,8},{1,17},{9,25},{17,1},{25,9},{2,18},{10... | collective-permute-start | bytes 589832 | tf_op jit(solution)/shard_map/ppermute | solution.py:270
  39.0 1.0 %own_rows.1 = bf16[128,128]{1,0:T(8,128)(2,1)} custom-call(bf16[2,144,128]{2,1,0:T(8,128)(2,1)S(1)} %get-tuple-element.35.refs_0_.pair_ref, f32[1024,128]{1,0:T(8,128)S(1)} %get-tuple-element.49.refs_0_.up_ref, bf16[1024,640]{1,0:T(8,128)(2,1)S(1)} %get-tuple-element.50.d_pre_ref, bf16[2,128,768]{2,1,0:T(8,128)(2,1)S(1)} %get-tuple-element.37.refs_4_.refs_5_.refs_1_.weights, ...), custom_call_target="tpu_custom_call" | custom-call | flops 335544320 | bytes 4194304 | tf_op jit(solution)/shard_map/own_rows/pallas_call | solution.py:449
  40.1 5.2 %collective-permute-done.9.other_0 = bf16[128,768]{1,0:T(8,128)(2,1)S(1)} collective-permute-done((bf16[128,768]{1,0:T(8,128)(2,1)S(1)}, bf16[128,768]{1,0:T(8,128)(2,1)S(1)}, u32[]{:S(2)}, u32[]{:S(2)}) %collective-permute-start.9) | collective-permute-done | bytes 196640 | tf_op jit(solution)/shard_map/ppermute | solution.py:270
  45.2 0.9 %add_grads.1 = (f32[2,128,640]{2,1,0:T(8,128)}, f32[2,128,128]{2,1,0:T(8,128)}) custom-call(bf16[128,768]{1,0:T(8,128)(2,1)S(1)} %fusion.own_0, bf16[128,768]{1,0:T(8,128)(2,1)S(1)} %collective-permute-done.9.other_0, bf16[2,128,768]{2,1,0:T(8,128)(2,1)S(1)} %pad_maximum_fusion.own_both, bf16[2,128,768]{2,1,0:T(8,128)(2,1)S(1)} %collective-permute-done.8.other_both), custom_call_target="tpu_custom_call" | custom-call | tf_op jit(solution)/shard_map/add_grads/pallas_call | solution.py:469
  (4 shorter events, 0.1 us)
Async XLA Ops:
  2.5 5.5 %copy-start = (bf16[272,128]{1,0:T(8,128)(2,1)S(1)}, bf16[272,128]{1,0:T(8,128)(2,1)}, u32[]{:S(2)}) copy-start(bf16[272,128]{1,0:T(8,128)(2,1)} %get-tuple-element.29.near_ref) | copy-start | bytes 208900
  2.5 5.5 %collective-permute-start = (bf16[272,128]{1,0:T(8,128)(2,1)}, bf16[272,128]{1,0:T(8,128)(2,1)S(1)}, u32[]{:S(2)}, u32[]{:S(2)}) collective-permute-start(bf16[272,128]{1,0:T(8,128)(2,1)} %get-tuple-element.29.near_ref), channel_id=1, source_target_pairs={{0,1},{1,0},{2,3},{3,2},{4,5},{5,4},{6,7},{7,6},{8,9},{9,8},{10,11... | collective-permute-start | bytes 208904 | tf_op jit(solution)/shard_map/ppermute | solution.py:270
  5.6 1.0 %copy-start.1 = (bf16[2,128,768]{2,1,0:T(8,128)(2,1)S(1)}, bf16[2,128,768]{2,1,0:T(8,128)(2,1)}, u32[]{:S(2)}) copy-start(bf16[2,128,768]{2,1,0:T(8,128)(2,1)} %get-tuple-element.30.weights_in) | copy-start | bytes 1179652
  6.6 0.7 %copy-start.2 = (f32[2,1280]{1,0:T(2,128)S(1)}, f32[2,1280]{1,0:T(2,128)}, u32[]{:S(2)}) copy-start(f32[2,1280]{1,0:T(2,128)} %get-tuple-element.31.vectors_in) | copy-start | bytes 30724
  8.1 8.9 %collective-permute-start.6 = (bf16[2,144,128]{2,1,0:T(8,128)(2,1)S(1)}, bf16[2,144,128]{2,1,0:T(8,128)(2,1)S(1)}, u32[]{:S(2)}, u32[]{:S(2)}) collective-permute-start(bf16[2,144,128]{2,1,0:T(8,128)(2,1)S(1)} %get-tuple-element.35.refs_0_.pair_ref), channel_id=1, source_target_pairs={{0,4},{1,5},{2,6},{3,7},{4,0},{5,1},{6,2},{7,3},{8,12},{9,13},{10,... | collective-permute-start | bytes 221192 | tf_op jit(solution)/shard_map/ppermute | solution.py:270
  11.2 7.3 %collective-permute-start.5 = (bf16[2,144,128]{2,1,0:T(8,128)(2,1)S(1)}, bf16[2,144,128]{2,1,0:T(8,128)(2,1)S(1)}, u32[]{:S(2)}, u32[]{:S(2)}) collective-permute-start(bf16[2,144,128]{2,1,0:T(8,128)(2,1)S(1)} %get-tuple-element.35.refs_0_.pair_ref), channel_id=1, source_target_pairs={{0,6},{1,7},{2,4},{3,5},{4,2},{5,3},{6,0},{7,1},{8,14},{9,15},{10,... | collective-permute-start | bytes 221192 | tf_op jit(solution)/shard_map/ppermute | solution.py:270
  12.6 6.6 %collective-permute-start.4 = (bf16[2,144,128]{2,1,0:T(8,128)(2,1)S(1)}, bf16[2,144,128]{2,1,0:T(8,128)(2,1)S(1)}, u32[]{:S(2)}, u32[]{:S(2)}) collective-permute-start(bf16[2,144,128]{2,1,0:T(8,128)(2,1)S(1)} %get-tuple-element.35.refs_0_.pair_ref), channel_id=1, source_target_pairs={{0,2},{1,3},{2,0},{3,1},{4,6},{5,7},{6,4},{7,5},{8,10},{9,11},{10,... | collective-permute-start | bytes 221192 | tf_op jit(solution)/shard_map/ppermute | solution.py:270
  12.8 13.1 %collective-permute-start.3 = (bf16[2,128,128]{2,1,0:T(8,128)(2,1)S(1)}, bf16[2,128,128]{2,1,0:T(8,128)(2,1)S(1)}, u32[]{:S(2)}, u32[]{:S(2)}) collective-permute-start(bf16[2,128,128]{2,1,0:T(8,128)(2,1)S(1)} %get-tuple-element.36.refs_1_), channel_id=1, source_target_pairs={{0,4},{1,5},{2,6},{3,7},{4,0},{5,1},{6,2},{7,3},{8,12},{9,13},{10,... | collective-permute-start | bytes 196616 | tf_op jit(solution)/shard_map/ppermute | solution.py:270
  15.6 10.3 %collective-permute-start.2 = (bf16[2,128,128]{2,1,0:T(8,128)(2,1)S(1)}, bf16[2,128,128]{2,1,0:T(8,128)(2,1)S(1)}, u32[]{:S(2)}, u32[]{:S(2)}) collective-permute-start(bf16[2,128,128]{2,1,0:T(8,128)(2,1)S(1)} %get-tuple-element.36.refs_1_), channel_id=1, source_target_pairs={{0,6},{1,7},{2,4},{3,5},{4,2},{5,3},{6,0},{7,1},{8,14},{9,15},{10,... | collective-permute-start | bytes 196616 | tf_op jit(solution)/shard_map/ppermute | solution.py:270
  17.0 8.9 %collective-permute-start.1 = (bf16[2,128,128]{2,1,0:T(8,128)(2,1)S(1)}, bf16[2,128,128]{2,1,0:T(8,128)(2,1)S(1)}, u32[]{:S(2)}, u32[]{:S(2)}) collective-permute-start(bf16[2,128,128]{2,1,0:T(8,128)(2,1)S(1)} %get-tuple-element.36.refs_1_), channel_id=1, source_target_pairs={{0,2},{1,3},{2,0},{3,1},{4,6},{5,7},{6,4},{7,5},{8,10},{9,11},{10,... | collective-permute-start | bytes 196616 | tf_op jit(solution)/shard_map/ppermute | solution.py:270
  30.5 5.7 %collective-permute-start.7 = (bf16[128,768]{1,0:T(8,128)(2,1)S(1)}, bf16[128,768]{1,0:T(8,128)(2,1)S(1)}, u32[]{:S(2)}, u32[]{:S(2)}) collective-permute-start(bf16[128,768]{1,0:T(8,128)(2,1)S(1)} %get-tuple-element.52), channel_id=1, source_target_pairs={{0,16},{8,24},{16,0},{24,8},{1,17},{9,25},{17,1},{25,9},{2,18},{10... | collective-permute-start | bytes 589832 | tf_op jit(solution)/shard_map/ppermute | solution.py:270
  36.4 1.8 %collective-permute-start.8 = (bf16[2,128,768]{2,1,0:T(8,128)(2,1)S(1)}, bf16[2,128,768]{2,1,0:T(8,128)(2,1)S(1)}, u32[]{:S(2)}, u32[]{:S(2)}) collective-permute-start(bf16[2,128,768]{2,1,0:T(8,128)(2,1)S(1)} %pad_maximum_fusion.own_both), channel_id=1, source_target_pairs={{0,8},{8,0},{16,24},{24,16},{1,9},{9,1},{17,25},{25,17},{2,10},{10... | collective-permute-start | bytes 1179656 | tf_op jit(solution)/shard_map/ppermute | solution.py:270
  38.2 7.0 %collective-permute-start.9 = (bf16[128,768]{1,0:T(8,128)(2,1)S(1)}, bf16[128,768]{1,0:T(8,128)(2,1)S(1)}, u32[]{:S(2)}, u32[]{:S(2)}) collective-permute-start(bf16[128,768]{1,0:T(8,128)(2,1)S(1)} %fusion.own_0), channel_id=1, source_target_pairs={{0,16},{8,24},{16,0},{24,8},{1,17},{9,25},{17,1},{25,9},{2,18},{10... | collective-permute-start | bytes 589832 | tf_op jit(solution)/shard_map/ppermute | solution.py:270

commit v13 on v12

--- a/solution.py
+++ b/solution.py
@@ -91,13 +91,9 @@
     return jnp.stack(totals).reshape(BLOCK_ROWS * n, lanes)
 
 
-def edge_grads(d_left, d_right, s_left, s_right, left, right):
-    return (
-        (d_left * s_left).astype(BF16),
-        (d_left * left * (1.0 - s_left)).astype(BF16),
-        (d_right * s_right).astype(BF16),
-        (d_right * right * (1.0 - s_right)).astype(BF16),
-    )
+def edge_grads(d_edge, slope, edge):
+    grads = (d_edge * slope).astype(BF16), (d_edge * edge * (1.0 - slope)).astype(BF16)
+    return jnp.concatenate(grads, axis=1)
 
 
 def tail_values(block, lanes_from, lanes_to):
@@ -180,94 +176,155 @@
             next_s[here, :] = (x + gate_s[u, here, :] * branch).astype(BF16)
 
 
-def backward(n, u, jumps, *refs):
-    if u == 1:
-        (pair, *parted), refs = refs[: 1 + len(jumps)], refs[1 + len(jumps) :]
-        up_in_ref, refs = refs[-1], (None,) + refs[:-1]
-        own = own_place(pair)
-        for part, jump in zip(parted, jumps):
-            for side in range(2):
-                rows = part.shape[1] // n
-                up_in_ref[block(place_of(own, jump, side), rows, n), :] = part[side]
-    else:
-        up_in_ref = refs[0]
-    weights, vectors = refs[1:3]
-    (edges_s, slopes_s, gate_s, hat_s, rstd_s) = (ref.at[u] for ref in refs[3:8])
-    (p_hat_s, p_rstd_s, branch_s, normed_s, mixed_s) = (ref.at[u] for ref in refs[8 : 3 + KEPT])
-    if u == 1:
-        up_ref, grads_ref, d_product_s, d_edges_s, sums_s, d_pre_s = refs[3 + KEPT :]
-    else:
-        d_pre_s, grads_ref, d_product_s, d_edges_s, sums_s = refs[3 + KEPT :]
+def kept_parts(refs, u):
+    return [ref.at[u] for ref in refs[:KEPT]]
+
+
+def store_swapped(ref, rows, n, first, values):
+    for r in range(rows):
+        ref[pl.ds(first + r, n, stride=n), :] = values[r * n : (r + 1) * n]
+
+
+def backward_second(n, jumps, pair, *refs):
+    parted, refs = refs[: len(jumps)], refs[len(jumps) :]
+    weights, vectors = refs[:2]
+    (edges_s, slopes_s, gate_s, hat_s, rstd_s, *kept) = kept_parts(refs[2:], 1)
+    (p_hat_s, p_rstd_s, branch_s, normed_s, mixed_s) = kept
+    up_ref, grads_ref, d_product_s, d_edges_s, d_pre_s, cot_s = refs[2 + KEPT :]
     c, h = weights.shape[1], edges_s.shape[2]
     width = 4 * h + c
-    gain = vector_parts(vectors[u : u + 1, :], c, width)[1]
-    sums_s[...] = jnp.zeros_like(sums_s)
+    gain = vector_parts(vectors[1:2, :], c, width)[1]
+    own = own_place(pair)
+    for part, jump in zip(parted, jumps):
+        for side in range(2):
+            cot_s[block(place_of(own, jump, side), part.shape[1] // n, n), :] = part[side]
 
     @pl.loop(0, n // STEP_ROWS)
     def _(t):
         here = block(t, STEP_ROWS, n)
         d_branch, d_gate, d_product = unmix(
-            up_in_ref[here, :].astype(F32),
+            cot_s[here, :].astype(F32),
             gate_s[here, :],
             branch_s[here, :],
             p_hat_s[here, :],
             p_rstd_s[here, :],
             gain[:, c:],
-            weights[u, :, width:],
-        )
-        sums_s[:, width:] += dot(mixed_s[here, :], d_branch, ((0,), (0,)))
+            weights[1, :, width:],
+        )
+        d_out = dot(mixed_s[here, :], d_branch, ((0,), (0,)))
         d_pre_s[here, 4 * h :] = d_gate
-        d_product_s[u, here, :] = d_product
-        for r in range(STEP_ROWS):
-            swapped = pl.ds(t * STEP_ROWS + r, n, stride=n)
-            d_product_s[1 - u, swapped, :] = d_product[r * n : (r + 1) * n]
+        d_product_s[1, here, :] = d_product
+        store_swapped(d_product_s.at[0], STEP_ROWS, n, t * STEP_ROWS, d_product)
+        grads_ref[:, width:] = d_out.astype(BF16)
 
     blocks = n // BLOCK_ROWS
 
     @pl.loop(0, 2 * blocks)
     def _(step):
         side, t = step // blocks, step % blocks
-        edges, d_product = edges_s.at[1 - side], d_product_s.at[side]
-        x, y = (edges, d_product) if u == 1 else (d_product, edges)
-        d_edges_s[side, block(t, BLOCK_ROWS, n), :] = contract(n, t * BLOCK_ROWS, x, y)
+        d_edges_s[side, block(t, BLOCK_ROWS, n), :] = contract(
+            n, t * BLOCK_ROWS, edges_s.at[1 - side], d_product_s.at[side]
+        )
 
     @pl.loop(0, n // STEP_ROWS)
     def _(t):
         here = block(t, STEP_ROWS, n)
-        grads = edge_grads(
-            d_edges_s[0, here, :],
-            d_edges_s[1, here, :],
-            slopes_s[0, here, :],
-            slopes_s[1, here, :],
-            edges_s[0, here, :],
-            edges_s[1, here, :],
-        )
+        grads = [
+            edge_grads(d_edges_s[side, here, :], slopes_s[side, here, :], edges_s[side, here, :])
+            for side in range(2)
+        ]
         d_pre = jnp.concatenate([*grads, d_pre_s[here, 4 * h :]], axis=1)
         normed = normed_s[here, :]
-        if u == 1:
-            d_normed = dot(d_pre, weights[u, :, :width], ((1,), (1,))) * gain[:, :c]
-            pulled = norm_vjp(hat_s[here, :], rstd_s[here, :], d_normed)
-            up_ref[here, :] = up_in_ref[here, :].astype(F32) + pulled
-        else:
-            d_pre_s[here, : 4 * h] = d_pre[:, : 4 * h]
-        sums_s[:, :width] += dot(normed, d_pre, ((0,), (0,)))
-
-    grads_ref[...] = sums_s[...].astype(BF16)
-
-
-def own_rows(pair_ref, up_ref, d_pre_ref, weights, vectors, hat_ref, rstd_ref, out_ref):
+        d_normed = dot(d_pre, weights[1, :, :width], ((1,), (1,))) * gain[:, :c]
+        pulled = norm_vjp(hat_s[here, :], rstd_s[here, :], d_normed)
+        up_ref[here, :] = cot_s[here, :].astype(F32) + pulled
+        grads_ref[:, :width] = dot(normed, d_pre, ((0,), (0,))).astype(BF16)
+
+
+def backward_left(n, up_in_ref, weights, vectors, *refs):
+    (edges_s, slopes_s, gate_s, _, _, *kept) = kept_parts(refs, 0)
+    (p_hat_s, p_rstd_s, branch_s, normed_s, mixed_s) = kept
+    d_pre_ref, d_product_t_ref, grads_ref, d_product_s, d_edge_s = refs[KEPT:]
+    c, h = weights.shape[1], edges_s.shape[2]
+    width = 4 * h + c
+    gain = vector_parts(vectors[0:1, :], c, width)[1]
+
+    @pl.loop(0, n // STEP_ROWS)
+    def _(t):
+        here = block(t, STEP_ROWS, n)
+        d_branch, d_gate, d_product = unmix(
+            up_in_ref[here, :],
+            gate_s[here, :],
+            branch_s[here, :],
+            p_hat_s[here, :],
+            p_rstd_s[here, :],
+            gain[:, c:],
+            weights[0, :, width:],
+        )
+        d_out = dot(mixed_s[here, :], d_branch, ((0,), (0,)))
+        d_pre_ref[here, 2 * h :] = d_gate
+        d_product_s[here, :] = d_product
+        store_swapped(d_product_t_ref, STEP_ROWS, n, t * STEP_ROWS, d_product)
+        grads_ref[:, 2 * h + c :] = d_out.astype(BF16)
+
+    one_side(n, 0, d_product_s, edges_s, slopes_s, d_edge_s, d_pre_ref)
+    d_pre = dot(normed_s[...], d_pre_ref[...], ((0,), (0,)))
+    grads_ref[:, : 2 * h + c] = d_pre.astype(BF16)
+
+
+def backward_right(n, d_product_t_ref, *refs):
+    (edges_s, slopes_s, *kept) = kept_parts(refs, 0)
+    normed_s = kept[-2]
+    d_pre_ref, grads_ref, d_edge_s = refs[KEPT:]
+    one_side(n, 1, d_product_t_ref, edges_s, slopes_s, d_edge_s, d_pre_ref)
+    grads_ref[...] = dot(normed_s[...], d_pre_ref[...], ((0,), (0,))).astype(BF16)
+
+
+def one_side(n, side, x, edges_s, slopes_s, d_edge_s, d_pre_ref):
+    h = edges_s.shape[2]
+
+    @pl.loop(0, n // BLOCK_ROWS)
+    def _(t):
+        d_edge_s[block(t, BLOCK_ROWS, n), :] = contract(
+            n, t * BLOCK_ROWS, x, edges_s.at[1 - side]
+        )
+
+    @pl.loop(0, n // STEP_ROWS)
+    def _(t):
+        here = block(t, STEP_ROWS, n)
+        d_pre_ref[here, : 2 * h] = edge_grads(
+            d_edge_s[here, :], slopes_s[side, here, :], edges_s[side, here, :]
+        )
+
+
+def own_rows(
+    pair_ref, up_ref, d_left_ref, d_right_ref, weights, vectors, hat_ref, rstd_ref, out_ref
+):
     cells, c = out_ref.shape
+    half = d_right_ref.shape[1]
     place = own_place(pair_ref)
     own = pl.ds(pl.multiple_of(place * cells, cells), cells)
-    width = d_pre_ref.shape[1]
+    width = d_left_ref.shape[1] + half
     gain = vector_parts(vectors[0:1, :], c, width)[1]
-    d_normed = dot(d_pre_ref[own, :], weights[0, :, :width], ((1,), (1,))) * gain[:, :c]
+    d_left, d_right = d_left_ref[own, :], d_right_ref[own, :]
+    d_pre = jnp.concatenate([d_left[:, :half], d_right, d_left[:, half:]], axis=1)
+    d_normed = dot(d_pre, weights[0, :, :width], ((1,), (1,))) * gain[:, :c]
     pulled = norm_vjp(hat_ref[0, own, :], rstd_ref[0, own, :], d_normed)
     out_ref[...] = (up_ref[own, :] + pulled).astype(BF16)
 
 
 def exchange(value, axis, size, step):
     return lax.ppermute(value, axis, [(d, d ^ step) for d in range(size)])
+
+
+def near_rounds(value, groups):
+    other = exchange(value, "dp", groups, 1)
+    step = 2
+    while step < groups // 2:
+        value = add_narrow(value, other)
+        other = exchange(value, "dp", groups, step)
+        step *= 2
+    return value, other
 
 
 def add_narrow(a, b):
@@ -316,12 +373,18 @@
     return [row[:, first:last] for first, last in zip([0] + ends, ends)]
 
 
-def add_grads(own_0, other_0, own_both, other_both, proj_ref, out_ref):
+def add_grads(left, left_far, rest, rest_near, right, right_far, proj_ref, out_ref):
     width = proj_ref.shape[2]
-    for u, (own, other) in enumerate(((own_0, other_0), (own_both.at[1], other_both.at[1]))):
-        total = own[...].astype(F32) + other[...].astype(F32)
-        proj_ref[u] = total[:, :width]
-        out_ref[u] = total[:, width:]
+    c = out_ref.shape[2]
+    half = (width - c) // 2
+    total = left[...].astype(F32) + left_far[...].astype(F32)
+    proj_ref[0, :, :half] = total[:, :half]
+    proj_ref[0, :, 2 * half :] = total[:, half : half + c]
+    out_ref[0] = total[:, half + c :]
+    proj_ref[0, :, half : 2 * half] = right[...].astype(F32) + right_far[...].astype(F32)
+    total = rest[:, : width + c].astype(F32) + rest_near[:, : width + c].astype(F32)
+    proj_ref[1] = total[:, :width]
+    out_ref[1] = total[:, width:]
 
 
 def crop_shards(
@@ -419,15 +482,18 @@
         name="forward",
     )(*states, *weights)
 
-    work = [pltpu.VMEM((2,) + plane, F32)] * 2
-    work += [pltpu.VMEM(grads.shape, F32)]
-    d_pre = jax.ShapeDtypeStruct((pairs, width), BF16)
+    double, single = pltpu.VMEM((2,) + plane, F32), pltpu.VMEM(plane, F32)
     up_1, grads_1 = pl.pallas_call(
-        functools.partial(backward, n, 1, jumps),
+        functools.partial(backward_second, n, jumps),
         out_shape=(jax.ShapeDtypeStruct((pairs, c), F32), grads),
         in_specs=[vmem] * (3 + half + KEPT),
         out_specs=(vmem, vmem),
-        scratch_shapes=work + [pltpu.VMEM(d_pre.shape, BF16), pltpu.VMEM((pairs, c), BF16)],
+        scratch_shapes=[
+            double,
+            double,
+            pltpu.VMEM((pairs, width), BF16),
+            pltpu.VMEM((pairs, c), BF16),
+        ],
         compiler_params=params,
         cost_estimate=cost(48),
         name="backward_second",
@@ -435,36 +501,52 @@
     far = groups // 2
     others_1 = exchange(grads_1, "dp", groups, far)
 
-    d_pre_0, grads_0 = pl.pallas_call(
-        functools.partial(backward, n, 0, jumps),
-        out_shape=(d_pre, grads),
+    d_left, d_product_t, grads_left = pl.pallas_call(
+        functools.partial(backward_left, n),
+        out_shape=(
+            jax.ShapeDtypeStruct((pairs, 2 * h + c), BF16),
+            jax.ShapeDtypeStruct(plane, F32),
+            jax.ShapeDtypeStruct((c, 2 * h + 2 * c), BF16),
+        ),
         in_specs=[vmem] * (3 + KEPT),
-        out_specs=(vmem, vmem),
-        scratch_shapes=work,
+        out_specs=[vmem] * 3,
+        scratch_shapes=[single, single],
         compiler_params=params,
-        cost_estimate=cost(48),
-        name="backward_first",
+        cost_estimate=cost(24),
+        name="backward_left",
     )(up_1, *weights, *held)
-
+    grads_left = near_rounds(grads_left, groups)
+
+    d_right, grads_right = pl.pallas_call(
+        functools.partial(backward_right, n),
+        out_shape=(
+            jax.ShapeDtypeStruct((pairs, 2 * h), BF16),
+            jax.ShapeDtypeStruct((c, 2 * h), BF16),
+        ),
+        in_specs=[vmem] * (1 + KEPT),
+        out_specs=[vmem] * 2,
+        scratch_shapes=[single],
+        compiler_params=params,
+        cost_estimate=cost(24),
+        name="backward_right",
+    )(d_product_t, *held)
     pair_grad = pl.pallas_call(
         own_rows,
         out_shape=jax.ShapeDtypeStruct((cells, c), BF16),
-        in_specs=[vmem] * 7,
+        in_specs=[vmem] * 8,
         out_specs=vmem,
         compiler_params=params,
         cost_estimate=cost(8),
         name="own_rows",
-    )(states[0], up_1, d_pre_0, *weights, held[3], held[4])
-
-    both = jnp.stack([grads_0, add_narrow(grads_1, others_1)])
-    others = jnp.zeros_like(both)
-    step = 1
-    while step < far:
-        both = add_narrow(both, others) if step > 1 else both
-        others = exchange(both, "dp", groups, step)
-        step *= 2
-    grads_0 = add_narrow(both[0], others[0])
-    others_0 = exchange(grads_0, "dp", groups, far)
+    )(states[0], up_1, d_left, d_right, *weights, held[3], held[4])
+
+    left = add_narrow(*grads_left)
+    left_far = exchange(left, "dp", groups, far)
+    rest, rest_near = near_rounds(
+        jnp.concatenate([add_narrow(grads_1, others_1), grads_right], axis=1), groups
+    )
+    right = add_narrow(rest[:, width + c :], rest_near[:, width + c :])
+    right_far = exchange(right, "dp", groups, far)
 
     proj_total, out_total = pl.pallas_call(
         add_grads,
@@ -472,11 +554,11 @@
             jax.ShapeDtypeStruct((2, c, width), F32),
             jax.ShapeDtypeStruct((2, h, c), F32),
         ),
-        in_specs=[vmem] * 4,
+        in_specs=[vmem] * 6,
         out_specs=(vmem, vmem),
         compiler_params=params,
         name="add_grads",
-    )(grads_0, others_0, both, others)
+    )(left, left_far, rest, rest_near, right, right_far)
     return pair_grad.reshape(pair_repr.shape), proj_total, out_total
 
 
@@ -677,8 +759,8 @@
         n, c = args[0].shape[2:]
         rows = n // parts
         fits = 20 * n * n * c * 4 <= CROP_BUDGET
-        paired = all(size > 1 and size & (size - 1) == 0 for size in (groups, parts))
-        even = args[7].shape[1] == c == 128 and STEP_ROWS % rows == 0 and n % STEP_ROWS == 0
+        paired = all(size >= 4 and size & (size - 1) == 0 for size in (groups, parts))
+        even = args[7].shape[1] == c == 128 and STEP_ROWS % rows == 0 and n == STEP_ROWS
         body = functools.partial(crop_shards, groups, parts) if fits and even and paired else shards
         return spread_over(body)(*args)
 

time: 46.7 us -> 45.5 us (0.974)
  waiting for transfers between devices: 8.92 us -> 6.03 us
  starting transfers between devices: 15.2 us -> 16.7 us
    ppermute x10 -> x12, waiting for transfers between devices: 8.92 us -> 6.03 us  [exchange(): return lax.ppermute(value, axis, [(d, d ^ step) for d in range(size)])]
    ppermute x10 -> x12, starting transfers between devices: 15.2 us -> 16.7 us  [exchange(): return lax.ppermute(value, axis, [(d, d ^ step) for d in range(size)])]
    pallas_call x2 -> x3, Pallas kernels: 8.93 us -> 9.05 us  [the longest x1 4.73 us: crop_shards(): pl.pallas_call(functools.partial(backward_second, n, jumps), out_shape=(j...]
  transfers between devices with their start and end apart: 10 -> 12, of which waited for: 5 -> 6; matrix products, arithmetic and copies ran while one was open for 0% -> 0% of each run, Pallas kernels for 26% -> 27%
where the time goes in v13:
time: 45.5 us; the launch traced here: 44.9 us
  Pallas kernels  19.5 us (43%)
  starting transfers between devices  16.7 us (37%)
  waiting for transfers between devices  6.03 us (13%)
  local copies, waits for them, and re-layouts  1.7 us (4%)
  between operations  0.75 us (2%)
    ppermute x12, starting transfers between devices, exchange(): return lax.ppermute(value, axis, [(d, d ^ step) for d in range(size)])  16.7 us
    pallas_call x1, Pallas kernels, crop_shards(): pl.pallas_call(functools.partial(forward, n, jumps), out_shape=kept, in_s...  6.62 us
    ppermute x12, waiting for transfers between devices, exchange(): return lax.ppermute(value, axis, [(d, d ^ step) for d in range(size)])  6.03 us
    pallas_call x1, Pallas kernels, crop_shards(): pl.pallas_call(functools.partial(backward_second, n, jumps), out_shape=(j...  4.73 us
    pallas_call x1, Pallas kernels, crop_shards(): pl.pallas_call(functools.partial(backward_left, n), out_shape=(jax.ShapeD...  2.59 us
    pallas_call x1, Pallas kernels, crop_shards(): pl.pallas_call(prepare, out_shape=(jax.ShapeDtypeStruct((2 * cells + TAIL...  1.88 us
    pallas_call x1, Pallas kernels, crop_shards(): pl.pallas_call(functools.partial(backward_right, n), out_shape=(jax.Shape...  1.73 us
    unnamed x6, local copies, waits for them, and re-layouts  1.7 us
  transfers between devices with their start and end apart: 12, of which 6 were waited for; matrix products, arithmetic and copies ran while one was open for 0% of the time, Pallas kernels for 27%

profile of v13, /device:TPU:0, one launch (start us, length us, event | category | flops | bytes accessed | tf_op | source)
XLA Modules:
  0.0 44.9 jit_solution(12621217341501371135)
XLA Ops:
  0.6 1.9 %prepare.1 = (bf16[272,128]{1,0:T(8,128)(2,1)}, bf16[2,128,768]{2,1,0:T(8,128)(2,1)}, f32[2,1280]{1,0:T(2,128)}) custom-call(s32[1]{0:T(128)} %bitcast.index_ref, s32[4,32]{1,0:T(4,128)} %bitcast.8, bf16[128,128]{1,0:T(8,128)(2,1)} %bitcast.6, bf16[128,128]{1,0:T(8,128)(2,1)} %bitcast.7, bf16[2,128,640]{2,1,0:T(8,128)(2,1)} %w.1, ...), custom_call_target="tpu_custom_call" | custom-call | tf_op jit(solution)/shard_map/prepare/pallas_call | solution.py:426
  2.5 0.0 copy-start
  2.5 3.0 %collective-permute-start = (bf16[272,128]{1,0:T(8,128)(2,1)}, bf16[272,128]{1,0:T(8,128)(2,1)S(1)}, u32[]{:S(2)}, u32[]{:S(2)}) collective-permute-start(bf16[272,128]{1,0:T(8,128)(2,1)} %get-tuple-element.32.near_ref), channel_id=1, source_target_pairs={{0,1},{1,0},{2,3},{3,2},{4,5},{5,4},{6,7},{7,6},{8,9},{9,8},{10,11... | collective-permute-start | bytes 208904 | tf_op jit(solution)/shard_map/ppermute | solution.py:317
  5.6 0.0 copy-start.1
  5.6 1.0 %copy-done.1 = bf16[2,128,768]{2,1,0:T(8,128)(2,1)S(1)} copy-done((bf16[2,128,768]{2,1,0:T(8,128)(2,1)S(1)}, bf16[2,128,768]{2,1,0:T(8,128)(2,1)}, u32[]{:S(2)}) %copy-start.1) | copy-done | bytes 393240
  6.6 0.0 copy-start.2
  6.6 0.7 %copy-done.2 = f32[2,1280]{1,0:T(2,128)S(1)} copy-done((f32[2,1280]{1,0:T(2,128)S(1)}, f32[2,1280]{1,0:T(2,128)}, u32[]{:S(2)}) %copy-start.2) | copy-done | bytes 10264
  7.3 0.8 %collective-permute-done.far_ref = bf16[272,128]{1,0:T(8,128)(2,1)S(1)} collective-permute-done((bf16[272,128]{1,0:T(8,128)(2,1)}, bf16[272,128]{1,0:T(8,128)(2,1)S(1)}, u32[]{:S(2)}, u32[]{:S(2)}) %collective-permute-start) | collective-permute-done | bytes 69664 | tf_op jit(solution)/shard_map/ppermute | solution.py:317
  8.1 0.0 copy-done
  8.1 3.2 %collective-permute-start.6 = (bf16[2,144,128]{2,1,0:T(8,128)(2,1)S(1)}, bf16[2,144,128]{2,1,0:T(8,128)(2,1)S(1)}, u32[]{:S(2)}, u32[]{:S(2)}) collective-permute-start(bf16[2,144,128]{2,1,0:T(8,128)(2,1)S(1)} %get-tuple-element.38.refs_0_.pair.pair_ref), channel_id=1, source_target_pairs={{0,4},{1,5},{2,6},{3,7},{4,0},{5,1},{6,2},{7,3},{8,12},{9,13},{10,... | collective-permute-start | bytes 221192 | tf_op jit(solution)/shard_map/ppermute | solution.py:317
  11.2 1.3 %collective-permute-start.5 = (bf16[2,144,128]{2,1,0:T(8,128)(2,1)S(1)}, bf16[2,144,128]{2,1,0:T(8,128)(2,1)S(1)}, u32[]{:S(2)}, u32[]{:S(2)}) collective-permute-start(bf16[2,144,128]{2,1,0:T(8,128)(2,1)S(1)} %get-tuple-element.38.refs_0_.pair.pair_ref), channel_id=1, source_target_pairs={{0,6},{1,7},{2,4},{3,5},{4,2},{5,3},{6,0},{7,1},{8,14},{9,15},{10,... | collective-permute-start | bytes 221192 | tf_op jit(solution)/shard_map/ppermute | solution.py:317
  12.6 0.2 collective-permute-start.4
  12.8 2.8 %collective-permute-start.3 = (bf16[2,128,128]{2,1,0:T(8,128)(2,1)S(1)}, bf16[2,128,128]{2,1,0:T(8,128)(2,1)S(1)}, u32[]{:S(2)}, u32[]{:S(2)}) collective-permute-start(bf16[2,128,128]{2,1,0:T(8,128)(2,1)S(1)} %get-tuple-element.39.refs_0_), channel_id=1, source_target_pairs={{0,4},{1,5},{2,6},{3,7},{4,0},{5,1},{6,2},{7,3},{8,12},{9,13},{10,... | collective-permute-start | bytes 196616 | tf_op jit(solution)/shard_map/ppermute | solution.py:317
  15.6 1.3 %collective-permute-start.2 = (bf16[2,128,128]{2,1,0:T(8,128)(2,1)S(1)}, bf16[2,128,128]{2,1,0:T(8,128)(2,1)S(1)}, u32[]{:S(2)}, u32[]{:S(2)}) collective-permute-start(bf16[2,128,128]{2,1,0:T(8,128)(2,1)S(1)} %get-tuple-element.39.refs_0_), channel_id=1, source_target_pairs={{0,6},{1,7},{2,4},{3,5},{4,2},{5,3},{6,0},{7,1},{8,14},{9,15},{10,... | collective-permute-start | bytes 196616 | tf_op jit(solution)/shard_map/ppermute | solution.py:317
  17.0 0.0 collective-permute-done.6.refs_3_
  17.0 1.5 %collective-permute-start.1 = (bf16[2,128,128]{2,1,0:T(8,128)(2,1)S(1)}, bf16[2,128,128]{2,1,0:T(8,128)(2,1)S(1)}, u32[]{:S(2)}, u32[]{:S(2)}) collective-permute-start(bf16[2,128,128]{2,1,0:T(8,128)(2,1)S(1)} %get-tuple-element.39.refs_0_), channel_id=1, source_target_pairs={{0,2},{1,3},{2,0},{3,1},{4,6},{5,7},{6,4},{7,5},{8,10},{9,11},{10,... | collective-permute-start | bytes 196616 | tf_op jit(solution)/shard_map/ppermute | solution.py:317
  18.5 0.0 collective-permute-done.5.refs_2_
  18.5 0.7 %collective-permute-done.4.refs_1_ = bf16[2,144,128]{2,1,0:T(8,128)(2,1)S(1)} collective-permute-done((bf16[2,144,128]{2,1,0:T(8,128)(2,1)S(1)}, bf16[2,144,128]{2,1,0:T(8,128)(2,1)S(1)}, u32[]{:S(2)}, u32[]{:S(2)}) %collective-permute-start.4) | collective-permute-done | bytes 73760 | tf_op jit(solution)/shard_map/ppermute | solution.py:317
  19.2 6.6 %forward.1 = (f32[2,4,1032,128]{3,2,1,0:T(8,128)S(1)}, f32[2,2,1032,128]{3,2,1,0:T(8,128)S(1)}, f32[2,1032,128]{2,1,0:T(8,128)S(1)}, f32[2,1032,128]{2,1,0:T(8,1...) custom-call(bf16[2,144,128]{2,1,0:T(8,128)(2,1)S(1)} %get-tuple-elem, ...), custom_call_target="tpu_custom_call" | custom-call | flops 335544320 | bytes 33554432 | tf_op jit(solution)/shard_map/forward/pallas_call | solution.py:474
  25.9 0.0 collective-permute-done.3.refs_3_
  25.9 0.0 collective-permute-done.2.refs_2_
  25.9 0.0 collective-permute-done.1.refs_1_
  25.9 4.7 %backward_second.1 = (f32[1024,128]{1,0:T(8,128)S(1)}, bf16[128,768]{1,0:T(8,128)(2,1)S(1)}) custom-call(bf16[2,144,128]{2,1,0:T(8,128)(2,1)S(1)} %get-tuple-element.38.refs_0_.pair.pair_ref, bf16[2,128,128]{2,1,0:T(8,128)(2,1)S(1)} %get-tuple-element.39.refs_0_, bf16[2,128,128]{2,1,0:T(8,128)(2,1)S(1)} %collective-permute-done.1.refs_1_, ...), custom_call_target="tpu_custom_call" | custom-call | flops 335544320 | bytes 25165824 | tf_op jit(solution)/shard_map/backward_second/pallas_call | solution.py:486
  30.6 0.8 %collective-permute-start.9 = (bf16[128,768]{1,0:T(8,128)(2,1)S(1)}, bf16[128,768]{1,0:T(8,128)(2,1)S(1)}, u32[]{:S(2)}, u32[]{:S(2)}) collective-permute-start(bf16[128,768]{1,0:T(8,128)(2,1)S(1)} %get-tuple-element.57), channel_id=1, source_target_pairs={{0,16},{8,24},{16,0},{24,8},{1,17},{9,25},{17,1},{25,9},{2,18},{10... | collective-permute-start | bytes 589832 | tf_op jit(solution)/shard_map/ppermute | solution.py:317
  31.5 2.6 %backward_left.1 = (bf16[1024,384]{1,0:T(8,128)(2,1)S(1)}, f32[1032,128]{1,0:T(8,128)S(1)}, bf16[128,512]{1,0:T(8,128)(2,1)S(1)}) custom-call(f32[1024,128]{1,0:T(8,128)S(1)} %get-tuple-element.52.up_in_ref.up_ref, bf16[2,128,768]{2,1,0:T(8,128)(2,1)S(1)} %get-tuple-element.40.refs_4_.weights, f32[2,1280]{1,0:T(2,128)S(1)} %get-tuple-element.41.refs_5_.vectors, ...), custom_call_target="tpu_custom_call" | custom-call | flops 335544320 | bytes 12582912 | tf_op jit(solution)/shard_map/backward_left/pallas_call | solution.py:504
  34.1 0.1 collective-permute-start.7
  34.1 1.7 %backward_right.1 = (bf16[1024,256]{1,0:T(8,128)(2,1)S(1)}, bf16[128,256]{1,0:T(8,128)(2,1)S(1)}) custom-call(f32[1032,128]{1,0:T(8,128)S(1)} %get-tuple-element.54.d_product_t_ref, f32[2,4,1032,128]{3,2,1,0:T(8,128)S(1)} %get-tuple-element.42.refs_6_.refs_0_, f32[2,2,1032,128]{3,2,1,0:T(8,128)S(1)} %get-tuple-element.43.refs_7_.refs_1_, ...), custom_call_target="tpu_custom_call" | custom-call | flops 335544320 | bytes 12582912 | tf_op jit(solution)/shard_map/backward_right/pallas_call | solution.py:520
  35.9 0.5 %collective-permute-done.9 = bf16[128,768]{1,0:T(8,128)(2,1)S(1)} collective-permute-done((bf16[128,768]{1,0:T(8,128)(2,1)S(1)}, bf16[128,768]{1,0:T(8,128)(2,1)S(1)}, u32[]{:S(2)}, u32[]{:S(2)}) %collective-permute-start.9) | collective-permute-done | bytes 196640 | tf_op jit(solution)/shard_map/ppermute | solution.py:317
  36.4 0.1 collective-permute-start.10
  36.5 0.0 collective-permute-done.7
  36.6 1.3 %collective-permute-start.8 = (bf16[128,512]{1,0:T(8,128)(2,1)S(1)}, bf16[128,512]{1,0:T(8,128)(2,1)S(1)}, u32[]{:S(2)}, u32[]{:S(2)}) collective-permute-start(bf16[128,512]{1,0:T(8,128)(2,1)S(1)} %add_convert_fusion.1.left), channel_id=1, source_target_pairs={{0,16},{8,24},{16,0},{24,8},{1,17},{9,25},{17,1},{25,9},{2,18},{10... | collective-permute-start | bytes 393224 | tf_op jit(solution)/shard_map/ppermute | solution.py:317
  37.9 0.2 collective-permute-done.10.rest_near
  38.1 1.0 %collective-permute-start.11 = (bf16[128,256]{1,0:T(8,128)(2,1)S(1)}, bf16[128,256]{1,0:T(8,128)(2,1)S(1)}, u32[]{:S(2)}, u32[]{:S(2)}) collective-permute-start(bf16[128,256]{1,0:T(8,128)(2,1)S(1)} %add_convert_fusion.2.right), channel_id=1, source_target_pairs={{0,16},{8,24},{16,0},{24,8},{1,17},{9,25},{17,1},{25,9},{2,18},{10... | collective-permute-start | bytes 196616 | tf_op jit(solution)/shard_map/ppermute | solution.py:317
  39.0 1.0 %own_rows.1 = bf16[128,128]{1,0:T(8,128)(2,1)} custom-call(bf16[2,144,128]{2,1,0:T(8,128)(2,1)S(1)} %get-tuple-element.38.refs_0_.pair.pair_ref, f32[1024,128]{1,0:T(8,128)S(1)} %get-tuple-element.52.up_in_ref.up_ref, bf16[1024,384]{1,0:T(8,128)(2,1)S(1)} %get-tuple-element.53.d_left_ref, bf16[1024,256]{1,0:T(8,128)(2,1)S(1)} %get-tuple-element.55.d_right_ref, ...), custom_call_target="tpu_custom_call" | custom-call | flops 335544320 | bytes 4194304 | tf_op jit(solution)/shard_map/own_rows/pallas_call | solution.py:533
  40.1 2.9 %collective-permute-done.8.left_far = bf16[128,512]{1,0:T(8,128)(2,1)S(1)} collective-permute-done((bf16[128,512]{1,0:T(8,128)(2,1)S(1)}, bf16[128,512]{1,0:T(8,128)(2,1)S(1)}, u32[]{:S(2)}, u32[]{:S(2)}) %collective-permute-start.8) | collective-permute-done | bytes 131104 | tf_op jit(solution)/shard_map/ppermute | solution.py:317
  42.9 1.0 %collective-permute-done.11.right_far = bf16[128,256]{1,0:T(8,128)(2,1)S(1)} collective-permute-done((bf16[128,256]{1,0:T(8,128)(2,1)S(1)}, bf16[128,256]{1,0:T(8,128)(2,1)S(1)}, u32[]{:S(2)}, u32[]{:S(2)}) %collective-permute-start.11) | collective-permute-done | bytes 65568 | tf_op jit(solution)/shard_map/ppermute | solution.py:317
  43.9 0.9 %add_grads.1 = (f32[2,128,640]{2,1,0:T(8,128)}, f32[2,128,128]{2,1,0:T(8,128)}) custom-call(bf16[128,512]{1,0:T(8,128)(2,1)S(1)} %add_convert_fusion.1.left, bf16[128,512]{1,0:T(8,128)(2,1)S(1)} %collective-permute-done.8.left_far, bf16[128,1024]{1,0:T(8,128)(2,1)S(1)} %pad_maximum_fusion.rest, bf16[128,1024]{1,0:T(8,128)(2,1)S(1)} %collective-permute-done.10.rest_near, ...), custom_call_target="tpu_custom_call" | custom-call | tf_op jit(solution)/shard_map/add_grads/pallas_call | solution.py:551
  (6 shorter events, 0.2 us)
Async XLA Ops:
  2.5 5.5 %copy-start = (bf16[272,128]{1,0:T(8,128)(2,1)S(1)}, bf16[272,128]{1,0:T(8,128)(2,1)}, u32[]{:S(2)}) copy-start(bf16[272,128]{1,0:T(8,128)(2,1)} %get-tuple-element.32.near_ref) | copy-start | bytes 208900
  2.5 5.5 %collective-permute-start = (bf16[272,128]{1,0:T(8,128)(2,1)}, bf16[272,128]{1,0:T(8,128)(2,1)S(1)}, u32[]{:S(2)}, u32[]{:S(2)}) collective-permute-start(bf16[272,128]{1,0:T(8,128)(2,1)} %get-tuple-element.32.near_ref), channel_id=1, source_target_pairs={{0,1},{1,0},{2,3},{3,2},{4,5},{5,4},{6,7},{7,6},{8,9},{9,8},{10,11... | collective-permute-start | bytes 208904 | tf_op jit(solution)/shard_map/ppermute | solution.py:317
  5.6 1.0 %copy-start.1 = (bf16[2,128,768]{2,1,0:T(8,128)(2,1)S(1)}, bf16[2,128,768]{2,1,0:T(8,128)(2,1)}, u32[]{:S(2)}) copy-start(bf16[2,128,768]{2,1,0:T(8,128)(2,1)} %get-tuple-element.33.weights_in) | copy-start | bytes 1179652
  6.6 0.7 %copy-start.2 = (f32[2,1280]{1,0:T(2,128)S(1)}, f32[2,1280]{1,0:T(2,128)}, u32[]{:S(2)}) copy-start(f32[2,1280]{1,0:T(2,128)} %get-tuple-element.34.vectors_in) | copy-start | bytes 30724
  8.1 8.9 %collective-permute-start.6 = (bf16[2,144,128]{2,1,0:T(8,128)(2,1)S(1)}, bf16[2,144,128]{2,1,0:T(8,128)(2,1)S(1)}, u32[]{:S(2)}, u32[]{:S(2)}) collective-permute-start(bf16[2,144,128]{2,1,0:T(8,128)(2,1)S(1)} %get-tuple-element.38.refs_0_.pair.pair_ref), channel_id=1, source_target_pairs={{0,4},{1,5},{2,6},{3,7},{4,0},{5,1},{6,2},{7,3},{8,12},{9,13},{10,... | collective-permute-start | bytes 221192 | tf_op jit(solution)/shard_map/ppermute | solution.py:317
  11.2 7.3 %collective-permute-start.5 = (bf16[2,144,128]{2,1,0:T(8,128)(2,1)S(1)}, bf16[2,144,128]{2,1,0:T(8,128)(2,1)S(1)}, u32[]{:S(2)}, u32[]{:S(2)}) collective-permute-start(bf16[2,144,128]{2,1,0:T(8,128)(2,1)S(1)} %get-tuple-element.38.refs_0_.pair.pair_ref), channel_id=1, source_target_pairs={{0,6},{1,7},{2,4},{3,5},{4,2},{5,3},{6,0},{7,1},{8,14},{9,15},{10,... | collective-permute-start | bytes 221192 | tf_op jit(solution)/shard_map/ppermute | solution.py:317
  12.6 6.6 %collective-permute-start.4 = (bf16[2,144,128]{2,1,0:T(8,128)(2,1)S(1)}, bf16[2,144,128]{2,1,0:T(8,128)(2,1)S(1)}, u32[]{:S(2)}, u32[]{:S(2)}) collective-permute-start(bf16[2,144,128]{2,1,0:T(8,128)(2,1)S(1)} %get-tuple-element.38.refs_0_.pair.pair_ref), channel_id=1, source_target_pairs={{0,2},{1,3},{2,0},{3,1},{4,6},{5,7},{6,4},{7,5},{8,10},{9,11},{10,... | collective-permute-start | bytes 221192 | tf_op jit(solution)/shard_map/ppermute | solution.py:317
  12.8 13.0 %collective-permute-start.3 = (bf16[2,128,128]{2,1,0:T(8,128)(2,1)S(1)}, bf16[2,128,128]{2,1,0:T(8,128)(2,1)S(1)}, u32[]{:S(2)}, u32[]{:S(2)}) collective-permute-start(bf16[2,128,128]{2,1,0:T(8,128)(2,1)S(1)} %get-tuple-element.39.refs_0_), channel_id=1, source_target_pairs={{0,4},{1,5},{2,6},{3,7},{4,0},{5,1},{6,2},{7,3},{8,12},{9,13},{10,... | collective-permute-start | bytes 196616 | tf_op jit(solution)/shard_map/ppermute | solution.py:317
  15.6 10.2 %collective-permute-start.2 = (bf16[2,128,128]{2,1,0:T(8,128)(2,1)S(1)}, bf16[2,128,128]{2,1,0:T(8,128)(2,1)S(1)}, u32[]{:S(2)}, u32[]{:S(2)}) collective-permute-start(bf16[2,128,128]{2,1,0:T(8,128)(2,1)S(1)} %get-tuple-element.39.refs_0_), channel_id=1, source_target_pairs={{0,6},{1,7},{2,4},{3,5},{4,2},{5,3},{6,0},{7,1},{8,14},{9,15},{10,... | collective-permute-start | bytes 196616 | tf_op jit(solution)/shard_map/ppermute | solution.py:317
  17.0 8.9 %collective-permute-start.1 = (bf16[2,128,128]{2,1,0:T(8,128)(2,1)S(1)}, bf16[2,128,128]{2,1,0:T(8,128)(2,1)S(1)}, u32[]{:S(2)}, u32[]{:S(2)}) collective-permute-start(bf16[2,128,128]{2,1,0:T(8,128)(2,1)S(1)} %get-tuple-element.39.refs_0_), channel_id=1, source_target_pairs={{0,2},{1,3},{2,0},{3,1},{4,6},{5,7},{6,4},{7,5},{8,10},{9,11},{10,... | collective-permute-start | bytes 196616 | tf_op jit(solution)/shard_map/ppermute | solution.py:317
  30.6 5.7 %collective-permute-start.9 = (bf16[128,768]{1,0:T(8,128)(2,1)S(1)}, bf16[128,768]{1,0:T(8,128)(2,1)S(1)}, u32[]{:S(2)}, u32[]{:S(2)}) collective-permute-start(bf16[128,768]{1,0:T(8,128)(2,1)S(1)} %get-tuple-element.57), channel_id=1, source_target_pairs={{0,16},{8,24},{16,0},{24,8},{1,17},{9,25},{17,1},{25,9},{2,18},{10... | collective-permute-start | bytes 589832 | tf_op jit(solution)/shard_map/ppermute | solution.py:317
  34.1 2.5 %collective-permute-start.7 = (bf16[128,512]{1,0:T(8,128)(2,1)S(1)}, bf16[128,512]{1,0:T(8,128)(2,1)S(1)}, u32[]{:S(2)}, u32[]{:S(2)}) collective-permute-start(bf16[128,512]{1,0:T(8,128)(2,1)S(1)} %get-tuple-element.56), channel_id=1, source_target_pairs={{0,8},{8,0},{16,24},{24,16},{1,9},{9,1},{17,25},{25,17},{2,10},{10... | collective-permute-start | bytes 393224 | tf_op jit(solution)/shard_map/ppermute | solution.py:317
  36.4 1.6 %collective-permute-start.10 = (bf16[128,1024]{1,0:T(8,128)(2,1)S(1)}, bf16[128,1024]{1,0:T(8,128)(2,1)S(1)}, u32[]{:S(2)}, u32[]{:S(2)}) collective-permute-start(bf16[128,1024]{1,0:T(8,128)(2,1)S(1)} %pad_maximum_fusion.rest), channel_id=1, source_target_pairs={{0,8},{8,0},{16,24},{24,16},{1,9},{9,1},{17,25},{25,17},{2,10},{10... | collective-permute-start | bytes 786440 | tf_op jit(solution)/shard_map/ppermute | solution.py:317
  36.6 6.4 %collective-permute-start.8 = (bf16[128,512]{1,0:T(8,128)(2,1)S(1)}, bf16[128,512]{1,0:T(8,128)(2,1)S(1)}, u32[]{:S(2)}, u32[]{:S(2)}) collective-permute-start(bf16[128,512]{1,0:T(8,128)(2,1)S(1)} %add_convert_fusion.1.left), channel_id=1, source_target_pairs={{0,16},{8,24},{16,0},{24,8},{1,17},{9,25},{17,1},{25,9},{2,18},{10... | collective-permute-start | bytes 393224 | tf_op jit(solution)/shard_map/ppermute | solution.py:317
  38.1 5.9 %collective-permute-start.11 = (bf16[128,256]{1,0:T(8,128)(2,1)S(1)}, bf16[128,256]{1,0:T(8,128)(2,1)S(1)}, u32[]{:S(2)}, u32[]{:S(2)}) collective-permute-start(bf16[128,256]{1,0:T(8,128)(2,1)S(1)} %add_convert_fusion.2.right), channel_id=1, source_target_pairs={{0,16},{8,24},{16,0},{24,8},{1,17},{9,25},{17,1},{25,9},{2,18},{10... | collective-permute-start | bytes 196616 | tf_op jit(solution)/shard_map/ppermute | solution.py:317

commit v14 on v13

--- a/solution.py
+++ b/solution.py
@@ -373,18 +373,18 @@
     return [row[:, first:last] for first, last in zip([0] + ends, ends)]
 
 
-def add_grads(left, left_far, rest, rest_near, right, right_far, proj_ref, out_ref):
+def add_grads(rest, rest_near, left, left_near, right, right_far, proj_ref, out_ref):
     width = proj_ref.shape[2]
     c = out_ref.shape[2]
     half = (width - c) // 2
-    total = left[...].astype(F32) + left_far[...].astype(F32)
+    total = rest[:, : width + c].astype(F32) + rest_near[:, : width + c].astype(F32)
+    proj_ref[1] = total[:, :width]
+    out_ref[1] = total[:, width:]
+    total = left[...].astype(F32) + left_near[...].astype(F32)
     proj_ref[0, :, :half] = total[:, :half]
     proj_ref[0, :, 2 * half :] = total[:, half : half + c]
     out_ref[0] = total[:, half + c :]
     proj_ref[0, :, half : 2 * half] = right[...].astype(F32) + right_far[...].astype(F32)
-    total = rest[:, : width + c].astype(F32) + rest_near[:, : width + c].astype(F32)
-    proj_ref[1] = total[:, :width]
-    out_ref[1] = total[:, width:]
 
 
 def crop_shards(
@@ -515,7 +515,7 @@
         cost_estimate=cost(24),
         name="backward_left",
     )(up_1, *weights, *held)
-    grads_left = near_rounds(grads_left, groups)
+    others_left = exchange(grads_left, "dp", groups, far)
 
     d_right, grads_right = pl.pallas_call(
         functools.partial(backward_right, n),
@@ -540,13 +540,13 @@
         name="own_rows",
     )(states[0], up_1, d_left, d_right, *weights, held[3], held[4])
 
-    left = add_narrow(*grads_left)
-    left_far = exchange(left, "dp", groups, far)
     rest, rest_near = near_rounds(
         jnp.concatenate([add_narrow(grads_1, others_1), grads_right], axis=1), groups
     )
     right = add_narrow(rest[:, width + c :], rest_near[:, width + c :])
     right_far = exchange(right, "dp", groups, far)
+    _, others_left = lax.optimization_barrier((right, others_left))
+    ends_left = near_rounds(add_narrow(grads_left, others_left), groups)
 
     proj_total, out_total = pl.pallas_call(
         add_grads,
@@ -558,7 +558,7 @@
         out_specs=(vmem, vmem),
         compiler_params=params,
         name="add_grads",
-    )(left, left_far, rest, rest_near, right, right_far)
+    )(rest, rest_near, *ends_left, right, right_far)
     return pair_grad.reshape(pair_repr.shape), proj_total, out_total
 
 

time: 45.5 us -> 48.6 us (1.068)
  waiting for transfers between devices: 6.03 us -> 9.79 us
  starting transfers between devices: 16.7 us -> 16.1 us
    ppermute x12, waiting for transfers between devices: 6.03 us -> 9.79 us  [exchange(): return lax.ppermute(value, axis, [(d, d ^ step) for d in range(size)])]
    ppermute x12, starting transfers between devices: 16.7 us -> 16.1 us  [exchange(): return lax.ppermute(value, axis, [(d, d ^ step) for d in range(size)])]
  transfers between devices with their start and end apart: 12 -> 12, of which waited for: 6 -> 6; matrix products, arithmetic and copies ran while one was open for 0% -> 0% of each run, Pallas kernels for 27% -> 25%
where the time goes in v14:
time: 48.6 us; the launch traced here: 48 us
  Pallas kernels  19.5 us (40%)
  starting transfers between devices  16.1 us (33%)
  waiting for transfers between devices  9.79 us (20%)
  local copies, waits for them, and re-layouts  1.7 us (3%)
  between operations  0.75 us (2%)
    ppermute x12, starting transfers between devices, exchange(): return lax.ppermute(value, axis, [(d, d ^ step) for d in range(size)])  16.1 us
    ppermute x12, waiting for transfers between devices, exchange(): return lax.ppermute(value, axis, [(d, d ^ step) for d in range(size)])  9.79 us
    pallas_call x1, Pallas kernels, crop_shards(): pl.pallas_call(functools.partial(forward, n, jumps), out_shape=kept, in_s...  6.62 us
    pallas_call x1, Pallas kernels, crop_shards(): pl.pallas_call(functools.partial(backward_second, n, jumps), out_shape=(j...  4.73 us
    pallas_call x1, Pallas kernels, crop_shards(): pl.pallas_call(functools.partial(backward_left, n), out_shape=(jax.ShapeD...  2.59 us
    pallas_call x1, Pallas kernels, crop_shards(): pl.pallas_call(prepare, out_shape=(jax.ShapeDtypeStruct((2 * cells + TAIL...  1.88 us
    pallas_call x1, Pallas kernels, crop_shards(): pl.pallas_call(functools.partial(backward_right, n), out_shape=(jax.Shape...  1.73 us
    unnamed x6, local copies, waits for them, and re-layouts  1.7 us
  transfers between devices with their start and end apart: 12, of which 6 were waited for; matrix products, arithmetic and copies ran while one was open for 0% of the time, Pallas kernels for 25%

profile of v14, /device:TPU:0, one launch (start us, length us, event | category | flops | bytes accessed | tf_op | source)
XLA Modules:
  0.0 48.0 jit_solution(16225568671636848627)
XLA Ops:
  0.6 1.9 %prepare.1 = (bf16[272,128]{1,0:T(8,128)(2,1)}, bf16[2,128,768]{2,1,0:T(8,128)(2,1)}, f32[2,1280]{1,0:T(2,128)}) custom-call(s32[1]{0:T(128)} %bitcast.index_ref, s32[4,32]{1,0:T(4,128)} %bitcast.8, bf16[128,128]{1,0:T(8,128)(2,1)} %bitcast.6, bf16[128,128]{1,0:T(8,128)(2,1)} %bitcast.7, bf16[2,128,640]{2,1,0:T(8,128)(2,1)} %w.1, ...), custom_call_target="tpu_custom_call" | custom-call | tf_op jit(solution)/shard_map/prepare/pallas_call | solution.py:426
  2.5 0.0 copy-start
  2.5 3.0 %collective-permute-start = (bf16[272,128]{1,0:T(8,128)(2,1)}, bf16[272,128]{1,0:T(8,128)(2,1)S(1)}, u32[]{:S(2)}, u32[]{:S(2)}) collective-permute-start(bf16[272,128]{1,0:T(8,128)(2,1)} %get-tuple-element.33.near_ref), channel_id=1, source_target_pairs={{0,1},{1,0},{2,3},{3,2},{4,5},{5,4},{6,7},{7,6},{8,9},{9,8},{10,11... | collective-permute-start | bytes 208904 | tf_op jit(solution)/shard_map/ppermute | solution.py:317
  5.6 0.0 copy-start.1
  5.6 1.0 %copy-done.1 = bf16[2,128,768]{2,1,0:T(8,128)(2,1)S(1)} copy-done((bf16[2,128,768]{2,1,0:T(8,128)(2,1)S(1)}, bf16[2,128,768]{2,1,0:T(8,128)(2,1)}, u32[]{:S(2)}) %copy-start.1) | copy-done | bytes 393240
  6.6 0.0 copy-start.2
  6.6 0.7 %copy-done.2 = f32[2,1280]{1,0:T(2,128)S(1)} copy-done((f32[2,1280]{1,0:T(2,128)S(1)}, f32[2,1280]{1,0:T(2,128)}, u32[]{:S(2)}) %copy-start.2) | copy-done | bytes 10264
  7.3 0.8 %collective-permute-done.far_ref = bf16[272,128]{1,0:T(8,128)(2,1)S(1)} collective-permute-done((bf16[272,128]{1,0:T(8,128)(2,1)}, bf16[272,128]{1,0:T(8,128)(2,1)S(1)}, u32[]{:S(2)}, u32[]{:S(2)}) %collective-permute-start) | collective-permute-done | bytes 69664 | tf_op jit(solution)/shard_map/ppermute | solution.py:317
  8.1 0.0 copy-done
  8.1 3.2 %collective-permute-start.6 = (bf16[2,144,128]{2,1,0:T(8,128)(2,1)S(1)}, bf16[2,144,128]{2,1,0:T(8,128)(2,1)S(1)}, u32[]{:S(2)}, u32[]{:S(2)}) collective-permute-start(bf16[2,144,128]{2,1,0:T(8,128)(2,1)S(1)} %get-tuple-element.39.refs_0_.pair.pair_ref), channel_id=1, source_target_pairs={{0,4},{1,5},{2,6},{3,7},{4,0},{5,1},{6,2},{7,3},{8,12},{9,13},{10,... | collective-permute-start | bytes 221192 | tf_op jit(solution)/shard_map/ppermute | solution.py:317
  11.2 1.3 %collective-permute-start.5 = (bf16[2,144,128]{2,1,0:T(8,128)(2,1)S(1)}, bf16[2,144,128]{2,1,0:T(8,128)(2,1)S(1)}, u32[]{:S(2)}, u32[]{:S(2)}) collective-permute-start(bf16[2,144,128]{2,1,0:T(8,128)(2,1)S(1)} %get-tuple-element.39.refs_0_.pair.pair_ref), channel_id=1, source_target_pairs={{0,6},{1,7},{2,4},{3,5},{4,2},{5,3},{6,0},{7,1},{8,14},{9,15},{10,... | collective-permute-start | bytes 221192 | tf_op jit(solution)/shard_map/ppermute | solution.py:317
  12.6 0.2 collective-permute-start.4
  12.8 2.8 %collective-permute-start.3 = (bf16[2,128,128]{2,1,0:T(8,128)(2,1)S(1)}, bf16[2,128,128]{2,1,0:T(8,128)(2,1)S(1)}, u32[]{:S(2)}, u32[]{:S(2)}) collective-permute-start(bf16[2,128,128]{2,1,0:T(8,128)(2,1)S(1)} %get-tuple-element.40.refs_0_), channel_id=1, source_target_pairs={{0,4},{1,5},{2,6},{3,7},{4,0},{5,1},{6,2},{7,3},{8,12},{9,13},{10,... | collective-permute-start | bytes 196616 | tf_op jit(solution)/shard_map/ppermute | solution.py:317
  15.6 1.3 %collective-permute-start.2 = (bf16[2,128,128]{2,1,0:T(8,128)(2,1)S(1)}, bf16[2,128,128]{2,1,0:T(8,128)(2,1)S(1)}, u32[]{:S(2)}, u32[]{:S(2)}) collective-permute-start(bf16[2,128,128]{2,1,0:T(8,128)(2,1)S(1)} %get-tuple-element.40.refs_0_), channel_id=1, source_target_pairs={{0,6},{1,7},{2,4},{3,5},{4,2},{5,3},{6,0},{7,1},{8,14},{9,15},{10,... | collective-permute-start | bytes 196616 | tf_op jit(solution)/shard_map/ppermute | solution.py:317
  17.0 0.0 collective-permute-done.6.refs_3_
  17.0 1.5 %collective-permute-start.1 = (bf16[2,128,128]{2,1,0:T(8,128)(2,1)S(1)}, bf16[2,128,128]{2,1,0:T(8,128)(2,1)S(1)}, u32[]{:S(2)}, u32[]{:S(2)}) collective-permute-start(bf16[2,128,128]{2,1,0:T(8,128)(2,1)S(1)} %get-tuple-element.40.refs_0_), channel_id=1, source_target_pairs={{0,2},{1,3},{2,0},{3,1},{4,6},{5,7},{6,4},{7,5},{8,10},{9,11},{10,... | collective-permute-start | bytes 196616 | tf_op jit(solution)/shard_map/ppermute | solution.py:317
  18.5 0.0 collective-permute-done.5.refs_2_
  18.5 0.7 %collective-permute-done.4.refs_1_ = bf16[2,144,128]{2,1,0:T(8,128)(2,1)S(1)} collective-permute-done((bf16[2,144,128]{2,1,0:T(8,128)(2,1)S(1)}, bf16[2,144,128]{2,1,0:T(8,128)(2,1)S(1)}, u32[]{:S(2)}, u32[]{:S(2)}) %collective-permute-start.4) | collective-permute-done | bytes 73760 | tf_op jit(solution)/shard_map/ppermute | solution.py:317
  19.2 6.6 %forward.1 = (f32[2,4,1032,128]{3,2,1,0:T(8,128)S(1)}, f32[2,2,1032,128]{3,2,1,0:T(8,128)S(1)}, f32[2,1032,128]{2,1,0:T(8,128)S(1)}, f32[2,1032,128]{2,1,0:T(8,1...) custom-call(bf16[2,144,128]{2,1,0:T(8,128)(2,1)S(1)} %get-tuple-elem, ...), custom_call_target="tpu_custom_call" | custom-call | flops 335544320 | bytes 33554432 | tf_op jit(solution)/shard_map/forward/pallas_call | solution.py:474
  25.9 0.0 collective-permute-done.3.refs_3_
  25.9 0.0 collective-permute-done.2.refs_2_
  25.9 0.0 collective-permute-done.1.refs_1_
  25.9 4.7 %backward_second.1 = (f32[1024,128]{1,0:T(8,128)S(1)}, bf16[128,768]{1,0:T(8,128)(2,1)S(1)}) custom-call(bf16[2,144,128]{2,1,0:T(8,128)(2,1)S(1)} %get-tuple-element.39.refs_0_.pair.pair_ref, bf16[2,128,128]{2,1,0:T(8,128)(2,1)S(1)} %get-tuple-element.40.refs_0_, bf16[2,128,128]{2,1,0:T(8,128)(2,1)S(1)} %collective-permute-done.1.refs_1_, ...), custom_call_target="tpu_custom_call" | custom-call | flops 335544320 | bytes 25165824 | tf_op jit(solution)/shard_map/backward_second/pallas_call | solution.py:486
  30.6 0.8 %collective-permute-start.7 = (bf16[128,768]{1,0:T(8,128)(2,1)S(1)}, bf16[128,768]{1,0:T(8,128)(2,1)S(1)}, u32[]{:S(2)}, u32[]{:S(2)}) collective-permute-start(bf16[128,768]{1,0:T(8,128)(2,1)S(1)} %get-tuple-element.57), channel_id=1, source_target_pairs={{0,16},{8,24},{16,0},{24,8},{1,17},{9,25},{17,1},{25,9},{2,18},{10... | collective-permute-start | bytes 589832 | tf_op jit(solution)/shard_map/ppermute | solution.py:317
  31.5 2.6 %backward_left.1 = (bf16[1024,384]{1,0:T(8,128)(2,1)S(1)}, f32[1032,128]{1,0:T(8,128)S(1)}, bf16[128,512]{1,0:T(8,128)(2,1)S(1)}) custom-call(f32[1024,128]{1,0:T(8,128)S(1)} %get-tuple-element.53.up_in_ref.up_ref, bf16[2,128,768]{2,1,0:T(8,128)(2,1)S(1)} %get-tuple-element.41.refs_4_.weights, f32[2,1280]{1,0:T(2,128)S(1)} %get-tuple-element.42.refs_5_.vectors, ...), custom_call_target="tpu_custom_call" | custom-call | flops 335544320 | bytes 12582912 | tf_op jit(solution)/shard_map/backward_left/pallas_call | solution.py:504
  34.1 1.7 %backward_right.1 = (bf16[1024,256]{1,0:T(8,128)(2,1)S(1)}, bf16[128,256]{1,0:T(8,128)(2,1)S(1)}) custom-call(f32[1032,128]{1,0:T(8,128)S(1)} %get-tuple-element.55.d_product_t_ref, f32[2,4,1032,128]{3,2,1,0:T(8,128)S(1)} %get-tuple-element.43.refs_6_.refs_0_, f32[2,2,1032,128]{3,2,1,0:T(8,128)S(1)} %get-tuple-element.44.refs_7_.refs_1_, ...), custom_call_target="tpu_custom_call" | custom-call | flops 335544320 | bytes 12582912 | tf_op jit(solution)/shard_map/backward_right/pallas_call | solution.py:520
  35.8 0.6 %collective-permute-done.7 = bf16[128,768]{1,0:T(8,128)(2,1)S(1)} collective-permute-done((bf16[128,768]{1,0:T(8,128)(2,1)S(1)}, bf16[128,768]{1,0:T(8,128)(2,1)S(1)}, u32[]{:S(2)}, u32[]{:S(2)}) %collective-permute-start.7) | collective-permute-done | bytes 196640 | tf_op jit(solution)/shard_map/ppermute | solution.py:317
  36.4 0.1 add_convert_fusion
  36.5 0.1 collective-permute-start.8
  36.5 0.8 %collective-permute-start.9 = (bf16[128,512]{1,0:T(8,128)(2,1)S(1)}, bf16[128,512]{1,0:T(8,128)(2,1)S(1)}, u32[]{:S(2)}, u32[]{:S(2)}) collective-permute-start(bf16[128,512]{1,0:T(8,128)(2,1)S(1)} %get-tuple-element.59), channel_id=1, source_target_pairs={{0,16},{8,24},{16,0},{24,8},{1,17},{9,25},{17,1},{25,9},{2,18},{10... | collective-permute-start | bytes 393224 | tf_op jit(solution)/shard_map/ppermute | solution.py:317
  37.4 0.7 %collective-permute-done.8.rest_near = bf16[128,1024]{1,0:T(8,128)(2,1)S(1)} collective-permute-done((bf16[128,1024]{1,0:T(8,128)(2,1)S(1)}, bf16[128,1024]{1,0:T(8,128)(2,1)S(1)}, u32[]{:S(2)}, u32[]{:S(2)}) %collective-permute-start.8) | collective-permute-done | bytes 262176 | tf_op jit(solution)/shard_map/ppermute | solution.py:317
  38.1 4.4 %collective-permute-done.9 = bf16[128,512]{1,0:T(8,128)(2,1)S(1)} collective-permute-done((bf16[128,512]{1,0:T(8,128)(2,1)S(1)}, bf16[128,512]{1,0:T(8,128)(2,1)S(1)}, u32[]{:S(2)}, u32[]{:S(2)}) %collective-permute-start.9) | collective-permute-done | bytes 131104 | tf_op jit(solution)/shard_map/ppermute | solution.py:317
  42.5 0.1 collective-permute-start.10
  42.6 0.8 %collective-permute-start.11 = (bf16[128,256]{1,0:T(8,128)(2,1)S(1)}, bf16[128,256]{1,0:T(8,128)(2,1)S(1)}, u32[]{:S(2)}, u32[]{:S(2)}) collective-permute-start(bf16[128,256]{1,0:T(8,128)(2,1)S(1)} %add_convert_fusion.2.right), channel_id=1, source_target_pairs={{0,16},{8,24},{16,0},{24,8},{1,17},{9,25},{17,1},{25,9},{2,18},{10... | collective-permute-start | bytes 196616 | tf_op jit(solution)/shard_map/ppermute | solution.py:317
  43.4 1.0 %own_rows.1 = bf16[128,128]{1,0:T(8,128)(2,1)} custom-call(bf16[2,144,128]{2,1,0:T(8,128)(2,1)S(1)} %get-tuple-element.39.refs_0_.pair.pair_ref, f32[1024,128]{1,0:T(8,128)S(1)} %get-tuple-element.53.up_in_ref.up_ref, bf16[1024,384]{1,0:T(8,128)(2,1)S(1)} %get-tuple-element.54.d_left_ref, bf16[1024,256]{1,0:T(8,128)(2,1)S(1)} %get-tuple-element.56.d_right_ref, ...), custom_call_target="tpu_custom_call" | custom-call | flops 335544320 | bytes 4194304 | tf_op jit(solution)/shard_map/own_rows/pallas_call | solution.py:533
  44.4 2.7 %collective-permute-done.11.right_far = bf16[128,256]{1,0:T(8,128)(2,1)S(1)} collective-permute-done((bf16[128,256]{1,0:T(8,128)(2,1)S(1)}, bf16[128,256]{1,0:T(8,128)(2,1)S(1)}, u32[]{:S(2)}, u32[]{:S(2)}) %collective-permute-start.11) | collective-permute-done | bytes 65568 | tf_op jit(solution)/shard_map/ppermute | solution.py:317
  47.1 0.0 collective-permute-done.10.left_near
  47.1 0.9 %add_grads.1 = (f32[2,128,640]{2,1,0:T(8,128)}, f32[2,128,128]{2,1,0:T(8,128)}) custom-call(bf16[128,1024]{1,0:T(8,128)(2,1)S(1)} %pad_maximum_fusion.rest, bf16[128,1024]{1,0:T(8,128)(2,1)S(1)} %collective-permute-done.8.rest_near, bf16[128,512]{1,0:T(8,128)(2,1)S(1)} %add_convert_fusion.1.left, bf16[128,512]{1,0:T(8,128)(2,1)S(1)} %collective-permute-done.10.left_near, ...), custom_call_target="tpu_custom_call" | custom-call | tf_op jit(solution)/shard_map/add_grads/pallas_call | solution.py:551
  (5 shorter events, 0.1 us)
Async XLA Ops:
  2.5 5.5 %copy-start = (bf16[272,128]{1,0:T(8,128)(2,1)S(1)}, bf16[272,128]{1,0:T(8,128)(2,1)}, u32[]{:S(2)}) copy-start(bf16[272,128]{1,0:T(8,128)(2,1)} %get-tuple-element.33.near_ref) | copy-start | bytes 208900
  2.5 5.5 %collective-permute-start = (bf16[272,128]{1,0:T(8,128)(2,1)}, bf16[272,128]{1,0:T(8,128)(2,1)S(1)}, u32[]{:S(2)}, u32[]{:S(2)}) collective-permute-start(bf16[272,128]{1,0:T(8,128)(2,1)} %get-tuple-element.33.near_ref), channel_id=1, source_target_pairs={{0,1},{1,0},{2,3},{3,2},{4,5},{5,4},{6,7},{7,6},{8,9},{9,8},{10,11... | collective-permute-start | bytes 208904 | tf_op jit(solution)/shard_map/ppermute | solution.py:317
  5.6 1.0 %copy-start.1 = (bf16[2,128,768]{2,1,0:T(8,128)(2,1)S(1)}, bf16[2,128,768]{2,1,0:T(8,128)(2,1)}, u32[]{:S(2)}) copy-start(bf16[2,128,768]{2,1,0:T(8,128)(2,1)} %get-tuple-element.34.weights_in) | copy-start | bytes 1179652
  6.6 0.7 %copy-start.2 = (f32[2,1280]{1,0:T(2,128)S(1)}, f32[2,1280]{1,0:T(2,128)}, u32[]{:S(2)}) copy-start(f32[2,1280]{1,0:T(2,128)} %get-tuple-element.35.vectors_in) | copy-start | bytes 30724
  8.1 8.9 %collective-permute-start.6 = (bf16[2,144,128]{2,1,0:T(8,128)(2,1)S(1)}, bf16[2,144,128]{2,1,0:T(8,128)(2,1)S(1)}, u32[]{:S(2)}, u32[]{:S(2)}) collective-permute-start(bf16[2,144,128]{2,1,0:T(8,128)(2,1)S(1)} %get-tuple-element.39.refs_0_.pair.pair_ref), channel_id=1, source_target_pairs={{0,4},{1,5},{2,6},{3,7},{4,0},{5,1},{6,2},{7,3},{8,12},{9,13},{10,... | collective-permute-start | bytes 221192 | tf_op jit(solution)/shard_map/ppermute | solution.py:317
  11.2 7.3 %collective-permute-start.5 = (bf16[2,144,128]{2,1,0:T(8,128)(2,1)S(1)}, bf16[2,144,128]{2,1,0:T(8,128)(2,1)S(1)}, u32[]{:S(2)}, u32[]{:S(2)}) collective-permute-start(bf16[2,144,128]{2,1,0:T(8,128)(2,1)S(1)} %get-tuple-element.39.refs_0_.pair.pair_ref), channel_id=1, source_target_pairs={{0,6},{1,7},{2,4},{3,5},{4,2},{5,3},{6,0},{7,1},{8,14},{9,15},{10,... | collective-permute-start | bytes 221192 | tf_op jit(solution)/shard_map/ppermute | solution.py:317
  12.6 6.6 %collective-permute-start.4 = (bf16[2,144,128]{2,1,0:T(8,128)(2,1)S(1)}, bf16[2,144,128]{2,1,0:T(8,128)(2,1)S(1)}, u32[]{:S(2)}, u32[]{:S(2)}) collective-permute-start(bf16[2,144,128]{2,1,0:T(8,128)(2,1)S(1)} %get-tuple-element.39.refs_0_.pair.pair_ref), channel_id=1, source_target_pairs={{0,2},{1,3},{2,0},{3,1},{4,6},{5,7},{6,4},{7,5},{8,10},{9,11},{10,... | collective-permute-start | bytes 221192 | tf_op jit(solution)/shard_map/ppermute | solution.py:317
  12.8 13.0 %collective-permute-start.3 = (bf16[2,128,128]{2,1,0:T(8,128)(2,1)S(1)}, bf16[2,128,128]{2,1,0:T(8,128)(2,1)S(1)}, u32[]{:S(2)}, u32[]{:S(2)}) collective-permute-start(bf16[2,128,128]{2,1,0:T(8,128)(2,1)S(1)} %get-tuple-element.40.refs_0_), channel_id=1, source_target_pairs={{0,4},{1,5},{2,6},{3,7},{4,0},{5,1},{6,2},{7,3},{8,12},{9,13},{10,... | collective-permute-start | bytes 196616 | tf_op jit(solution)/shard_map/ppermute | solution.py:317
  15.6 10.2 %collective-permute-start.2 = (bf16[2,128,128]{2,1,0:T(8,128)(2,1)S(1)}, bf16[2,128,128]{2,1,0:T(8,128)(2,1)S(1)}, u32[]{:S(2)}, u32[]{:S(2)}) collective-permute-start(bf16[2,128,128]{2,1,0:T(8,128)(2,1)S(1)} %get-tuple-element.40.refs_0_), channel_id=1, source_target_pairs={{0,6},{1,7},{2,4},{3,5},{4,2},{5,3},{6,0},{7,1},{8,14},{9,15},{10,... | collective-permute-start | bytes 196616 | tf_op jit(solution)/shard_map/ppermute | solution.py:317
  17.0 8.9 %collective-permute-start.1 = (bf16[2,128,128]{2,1,0:T(8,128)(2,1)S(1)}, bf16[2,128,128]{2,1,0:T(8,128)(2,1)S(1)}, u32[]{:S(2)}, u32[]{:S(2)}) collective-permute-start(bf16[2,128,128]{2,1,0:T(8,128)(2,1)S(1)} %get-tuple-element.40.refs_0_), channel_id=1, source_target_pairs={{0,2},{1,3},{2,0},{3,1},{4,6},{5,7},{6,4},{7,5},{8,10},{9,11},{10,... | collective-permute-start | bytes 196616 | tf_op jit(solution)/shard_map/ppermute | solution.py:317
  30.6 5.7 %collective-permute-start.7 = (bf16[128,768]{1,0:T(8,128)(2,1)S(1)}, bf16[128,768]{1,0:T(8,128)(2,1)S(1)}, u32[]{:S(2)}, u32[]{:S(2)}) collective-permute-start(bf16[128,768]{1,0:T(8,128)(2,1)S(1)} %get-tuple-element.57), channel_id=1, source_target_pairs={{0,16},{8,24},{16,0},{24,8},{1,17},{9,25},{17,1},{25,9},{2,18},{10... | collective-permute-start | bytes 589832 | tf_op jit(solution)/shard_map/ppermute | solution.py:317
  36.5 1.6 %collective-permute-start.8 = (bf16[128,1024]{1,0:T(8,128)(2,1)S(1)}, bf16[128,1024]{1,0:T(8,128)(2,1)S(1)}, u32[]{:S(2)}, u32[]{:S(2)}) collective-permute-start(bf16[128,1024]{1,0:T(8,128)(2,1)S(1)} %pad_maximum_fusion.rest), channel_id=1, source_target_pairs={{0,8},{8,0},{16,24},{24,16},{1,9},{9,1},{17,25},{25,17},{2,10},{10... | collective-permute-start | bytes 786440 | tf_op jit(solution)/shard_map/ppermute | solution.py:317
  36.5 5.9 %collective-permute-start.9 = (bf16[128,512]{1,0:T(8,128)(2,1)S(1)}, bf16[128,512]{1,0:T(8,128)(2,1)S(1)}, u32[]{:S(2)}, u32[]{:S(2)}) collective-permute-start(bf16[128,512]{1,0:T(8,128)(2,1)S(1)} %get-tuple-element.59), channel_id=1, source_target_pairs={{0,16},{8,24},{16,0},{24,8},{1,17},{9,25},{17,1},{25,9},{2,18},{10... | collective-permute-start | bytes 393224 | tf_op jit(solution)/shard_map/ppermute | solution.py:317
  42.5 4.6 %collective-permute-start.10 = (bf16[128,512]{1,0:T(8,128)(2,1)S(1)}, bf16[128,512]{1,0:T(8,128)(2,1)S(1)}, u32[]{:S(2)}, u32[]{:S(2)}) collective-permute-start(bf16[128,512]{1,0:T(8,128)(2,1)S(1)} %add_convert_fusion.1.left), channel_id=1, source_target_pairs={{0,8},{8,0},{16,24},{24,16},{1,9},{9,1},{17,25},{25,17},{2,10},{10... | collective-permute-start | bytes 393224 | tf_op jit(solution)/shard_map/ppermute | solution.py:317
  42.6 4.5 %collective-permute-start.11 = (bf16[128,256]{1,0:T(8,128)(2,1)S(1)}, bf16[128,256]{1,0:T(8,128)(2,1)S(1)}, u32[]{:S(2)}, u32[]{:S(2)}) collective-permute-start(bf16[128,256]{1,0:T(8,128)(2,1)S(1)} %add_convert_fusion.2.right), channel_id=1, source_target_pairs={{0,16},{8,24},{16,0},{24,8},{1,17},{9,25},{17,1},{25,9},{2,18},{10... | collective-permute-start | bytes 196616 | tf_op jit(solution)/shard_map/ppermute | solution.py:317

commit v15 on v14

--- a/solution.py
+++ b/solution.py
@@ -545,7 +545,6 @@
     )
     right = add_narrow(rest[:, width + c :], rest_near[:, width + c :])
     right_far = exchange(right, "dp", groups, far)
-    _, others_left = lax.optimization_barrier((right, others_left))
     ends_left = near_rounds(add_narrow(grads_left, others_left), groups)
 
     proj_total, out_total = pl.pallas_call(

time: 48.6 us -> 45.8 us (0.942)
  the two profiles are of different devices: /device:TPU:0 before, /device:TPU:20 now
where the time goes in v15:
time: 45.8 us; the launch traced here: 45.6 us
  Pallas kernels  19.5 us (43%)
  starting transfers between devices  14.3 us (31%)
  waiting for transfers between devices  9.11 us (20%)
  local copies, waits for them, and re-layouts  1.7 us (4%)
  between operations  0.76 us (2%)
    ppermute x12, starting transfers between devices, exchange(): return lax.ppermute(value, axis, [(d, d ^ step) for d in range(size)])  14.3 us
    ppermute x12, waiting for transfers between devices, exchange(): return lax.ppermute(value, axis, [(d, d ^ step) for d in range(size)])  9.11 us
    pallas_call x1, Pallas kernels, crop_shards(): pl.pallas_call(functools.partial(forward, n, jumps), out_shape=kept, in_s...  6.62 us
    pallas_call x1, Pallas kernels, crop_shards(): pl.pallas_call(functools.partial(backward_second, n, jumps), out_shape=(j...  4.73 us
    pallas_call x1, Pallas kernels, crop_shards(): pl.pallas_call(functools.partial(backward_left, n), out_shape=(jax.ShapeD...  2.59 us
    pallas_call x1, Pallas kernels, crop_shards(): pl.pallas_call(prepare, out_shape=(jax.ShapeDtypeStruct((2 * cells + TAIL...  1.88 us
    pallas_call x1, Pallas kernels, crop_shards(): pl.pallas_call(functools.partial(backward_right, n), out_shape=(jax.Shape...  1.72 us
    unnamed x6, local copies, waits for them, and re-layouts  1.7 us
  transfers between devices with their start and end apart: 12, of which 5 were waited for; matrix products, arithmetic and copies ran while one was open for 0% of the time, Pallas kernels for 26%

profile of v15, /device:TPU:20, one launch (start us, length us, event | category | flops | bytes accessed | tf_op | source)
XLA Modules:
  0.0 45.6 jit_solution(147888669185898605)
XLA Ops:
  0.6 1.9 %prepare.1 = (bf16[272,128]{1,0:T(8,128)(2,1)}, bf16[2,128,768]{2,1,0:T(8,128)(2,1)}, f32[2,1280]{1,0:T(2,128)}) custom-call(s32[1]{0:T(128)} %bitcast.index_ref, s32[4,32]{1,0:T(4,128)} %bitcast.8, bf16[128,128]{1,0:T(8,128)(2,1)} %bitcast.6, bf16[128,128]{1,0:T(8,128)(2,1)} %bitcast.7, bf16[2,128,640]{2,1,0:T(8,128)(2,1)} %w.1, ...), custom_call_target="tpu_custom_call" | custom-call | tf_op jit(solution)/shard_map/prepare/pallas_call | solution.py:426
  2.5 0.0 copy-start
  2.5 0.6 %collective-permute-start = (bf16[272,128]{1,0:T(8,128)(2,1)}, bf16[272,128]{1,0:T(8,128)(2,1)S(1)}, u32[]{:S(2)}, u32[]{:S(2)}) collective-permute-start(bf16[272,128]{1,0:T(8,128)(2,1)} %get-tuple-element.32.near_ref), channel_id=1, source_target_pairs={{0,1},{1,0},{2,3},{3,2},{4,5},{5,4},{6,7},{7,6},{8,9},{9,8},{10,11... | collective-permute-start | bytes 208904 | tf_op jit(solution)/shard_map/ppermute | solution.py:317
  3.1 0.0 copy-start.1
  3.1 1.0 %copy-done.1 = bf16[2,128,768]{2,1,0:T(8,128)(2,1)S(1)} copy-done((bf16[2,128,768]{2,1,0:T(8,128)(2,1)S(1)}, bf16[2,128,768]{2,1,0:T(8,128)(2,1)}, u32[]{:S(2)}) %copy-start.1) | copy-done | bytes 393240
  4.1 0.0 copy-start.2
  4.1 0.7 %copy-done.2 = f32[2,1280]{1,0:T(2,128)S(1)} copy-done((f32[2,1280]{1,0:T(2,128)S(1)}, f32[2,1280]{1,0:T(2,128)}, u32[]{:S(2)}) %copy-start.2) | copy-done | bytes 10264
  4.8 2.3 %collective-permute-done.far_ref = bf16[272,128]{1,0:T(8,128)(2,1)S(1)} collective-permute-done((bf16[272,128]{1,0:T(8,128)(2,1)}, bf16[272,128]{1,0:T(8,128)(2,1)S(1)}, u32[]{:S(2)}, u32[]{:S(2)}) %collective-permute-start) | collective-permute-done | bytes 69664 | tf_op jit(solution)/shard_map/ppermute | solution.py:317
  7.1 0.0 copy-done
  7.1 0.4 collective-permute-start.6
  7.5 2.7 %collective-permute-start.5 = (bf16[2,144,128]{2,1,0:T(8,128)(2,1)S(1)}, bf16[2,144,128]{2,1,0:T(8,128)(2,1)S(1)}, u32[]{:S(2)}, u32[]{:S(2)}) collective-permute-start(bf16[2,144,128]{2,1,0:T(8,128)(2,1)S(1)} %get-tuple-element.38.refs_0_.pair.pair_ref), channel_id=1, source_target_pairs={{0,6},{1,7},{2,4},{3,5},{4,2},{5,3},{6,0},{7,1},{8,14},{9,15},{10,... | collective-permute-start | bytes 221192 | tf_op jit(solution)/shard_map/ppermute | solution.py:317
  10.2 1.3 %collective-permute-start.4 = (bf16[2,144,128]{2,1,0:T(8,128)(2,1)S(1)}, bf16[2,144,128]{2,1,0:T(8,128)(2,1)S(1)}, u32[]{:S(2)}, u32[]{:S(2)}) collective-permute-start(bf16[2,144,128]{2,1,0:T(8,128)(2,1)S(1)} %get-tuple-element.38.refs_0_.pair.pair_ref), channel_id=1, source_target_pairs={{0,2},{1,3},{2,0},{3,1},{4,6},{5,7},{6,4},{7,5},{8,10},{9,11},{10,... | collective-permute-start | bytes 221192 | tf_op jit(solution)/shard_map/ppermute | solution.py:317
  11.6 0.1 collective-permute-start.3
  11.7 2.0 %collective-permute-start.2 = (bf16[2,128,128]{2,1,0:T(8,128)(2,1)S(1)}, bf16[2,128,128]{2,1,0:T(8,128)(2,1)S(1)}, u32[]{:S(2)}, u32[]{:S(2)}) collective-permute-start(bf16[2,128,128]{2,1,0:T(8,128)(2,1)S(1)} %get-tuple-element.39.refs_0_), channel_id=1, source_target_pairs={{0,6},{1,7},{2,4},{3,5},{4,2},{5,3},{6,0},{7,1},{8,14},{9,15},{10,... | collective-permute-start | bytes 196616 | tf_op jit(solution)/shard_map/ppermute | solution.py:317
  13.7 0.0 collective-permute-done.6.refs_3_
  13.7 4.3 %collective-permute-start.1 = (bf16[2,128,128]{2,1,0:T(8,128)(2,1)S(1)}, bf16[2,128,128]{2,1,0:T(8,128)(2,1)S(1)}, u32[]{:S(2)}, u32[]{:S(2)}) collective-permute-start(bf16[2,128,128]{2,1,0:T(8,128)(2,1)S(1)} %get-tuple-element.39.refs_0_), channel_id=1, source_target_pairs={{0,2},{1,3},{2,0},{3,1},{4,6},{5,7},{6,4},{7,5},{8,10},{9,11},{10,... | collective-permute-start | bytes 196616 | tf_op jit(solution)/shard_map/ppermute | solution.py:317
  18.0 1.3 %collective-permute-done.5.refs_2_ = bf16[2,144,128]{2,1,0:T(8,128)(2,1)S(1)} collective-permute-done((bf16[2,144,128]{2,1,0:T(8,128)(2,1)S(1)}, bf16[2,144,128]{2,1,0:T(8,128)(2,1)S(1)}, u32[]{:S(2)}, u32[]{:S(2)}) %collective-permute-start.5) | collective-permute-done | bytes 73760 | tf_op jit(solution)/shard_map/ppermute | solution.py:317
  19.3 0.0 collective-permute-done.4.refs_1_
  19.4 6.6 %forward.1 = (f32[2,4,1032,128]{3,2,1,0:T(8,128)S(1)}, f32[2,2,1032,128]{3,2,1,0:T(8,128)S(1)}, f32[2,1032,128]{2,1,0:T(8,128)S(1)}, f32[2,1032,128]{2,1,0:T(8,1...) custom-call(bf16[2,144,128]{2,1,0:T(8,128)(2,1)S(1)} %get-tuple-elem, ...), custom_call_target="tpu_custom_call" | custom-call | flops 335544320 | bytes 33554432 | tf_op jit(solution)/shard_map/forward/pallas_call | solution.py:474
  26.0 0.0 collective-permute-done.3.refs_3_
  26.0 0.0 collective-permute-done.2.refs_2_
  26.0 0.0 collective-permute-done.1.refs_1_
  26.0 4.7 %backward_second.1 = (f32[1024,128]{1,0:T(8,128)S(1)}, bf16[128,768]{1,0:T(8,128)(2,1)S(1)}) custom-call(bf16[2,144,128]{2,1,0:T(8,128)(2,1)S(1)} %get-tuple-element.38.refs_0_.pair.pair_ref, bf16[2,128,128]{2,1,0:T(8,128)(2,1)S(1)} %get-tuple-element.39.refs_0_, bf16[2,128,128]{2,1,0:T(8,128)(2,1)S(1)} %collective-permute-done.1.refs_1_, ...), custom_call_target="tpu_custom_call" | custom-call | flops 335544320 | bytes 25165824 | tf_op jit(solution)/shard_map/backward_second/pallas_call | solution.py:486
  30.7 1.6 %collective-permute-start.7 = (bf16[128,768]{1,0:T(8,128)(2,1)S(1)}, bf16[128,768]{1,0:T(8,128)(2,1)S(1)}, u32[]{:S(2)}, u32[]{:S(2)}) collective-permute-start(bf16[128,768]{1,0:T(8,128)(2,1)S(1)} %get-tuple-element.56), channel_id=1, source_target_pairs={{0,16},{8,24},{16,0},{24,8},{1,17},{9,25},{17,1},{25,9},{2,18},{10... | collective-permute-start | bytes 589832 | tf_op jit(solution)/shard_map/ppermute | solution.py:317
  32.3 2.6 %backward_left.1 = (bf16[1024,384]{1,0:T(8,128)(2,1)S(1)}, f32[1032,128]{1,0:T(8,128)S(1)}, bf16[128,512]{1,0:T(8,128)(2,1)S(1)}) custom-call(f32[1024,128]{1,0:T(8,128)S(1)} %get-tuple-element.52.up_in_ref.up_ref, bf16[2,128,768]{2,1,0:T(8,128)(2,1)S(1)} %get-tuple-element.40.refs_4_.weights, f32[2,1280]{1,0:T(2,128)S(1)} %get-tuple-element.41.refs_5_.vectors, ...), custom_call_target="tpu_custom_call" | custom-call | flops 335544320 | bytes 12582912 | tf_op jit(solution)/shard_map/backward_left/pallas_call | solution.py:504
  34.9 0.6 %collective-permute-start.9 = (bf16[128,512]{1,0:T(8,128)(2,1)S(1)}, bf16[128,512]{1,0:T(8,128)(2,1)S(1)}, u32[]{:S(2)}, u32[]{:S(2)}) collective-permute-start(bf16[128,512]{1,0:T(8,128)(2,1)S(1)} %get-tuple-element.58), channel_id=1, source_target_pairs={{0,16},{8,24},{16,0},{24,8},{1,17},{9,25},{17,1},{25,9},{2,18},{10... | collective-permute-start | bytes 393224 | tf_op jit(solution)/shard_map/ppermute | solution.py:317
  35.5 1.7 %backward_right.1 = (bf16[1024,256]{1,0:T(8,128)(2,1)S(1)}, bf16[128,256]{1,0:T(8,128)(2,1)S(1)}) custom-call(f32[1032,128]{1,0:T(8,128)S(1)} %get-tuple-element.54.d_product_t_ref, f32[2,4,1032,128]{3,2,1,0:T(8,128)S(1)} %get-tuple-element.42.refs_6_.refs_0_, f32[2,2,1032,128]{3,2,1,0:T(8,128)S(1)} %get-tuple-element.43.refs_7_.refs_1_, ...), custom_call_target="tpu_custom_call" | custom-call | flops 335544320 | bytes 12582912 | tf_op jit(solution)/shard_map/backward_right/pallas_call | solution.py:520
  37.2 0.7 %collective-permute-done.7 = bf16[128,768]{1,0:T(8,128)(2,1)S(1)} collective-permute-done((bf16[128,768]{1,0:T(8,128)(2,1)S(1)}, bf16[128,768]{1,0:T(8,128)(2,1)S(1)}, u32[]{:S(2)}, u32[]{:S(2)}) %collective-permute-start.7) | collective-permute-done | bytes 196640 | tf_op jit(solution)/shard_map/ppermute | solution.py:317
  37.9 0.1 add_convert_fusion
  38.0 0.1 collective-permute-start.8
  38.1 1.9 %collective-permute-done.9 = bf16[128,512]{1,0:T(8,128)(2,1)S(1)} collective-permute-done((bf16[128,512]{1,0:T(8,128)(2,1)S(1)}, bf16[128,512]{1,0:T(8,128)(2,1)S(1)}, u32[]{:S(2)}, u32[]{:S(2)}) %collective-permute-start.9) | collective-permute-done | bytes 131104 | tf_op jit(solution)/shard_map/ppermute | solution.py:317
  40.0 0.1 collective-permute-start.10
  40.1 0.0 collective-permute-done.8.rest_near
  40.1 0.6 %collective-permute-start.11 = (bf16[128,256]{1,0:T(8,128)(2,1)S(1)}, bf16[128,256]{1,0:T(8,128)(2,1)S(1)}, u32[]{:S(2)}, u32[]{:S(2)}) collective-permute-start(bf16[128,256]{1,0:T(8,128)(2,1)S(1)} %add_convert_fusion.2.right), channel_id=1, source_target_pairs={{0,16},{8,24},{16,0},{24,8},{1,17},{9,25},{17,1},{25,9},{2,18},{10... | collective-permute-start | bytes 196616 | tf_op jit(solution)/shard_map/ppermute | solution.py:317
  40.7 1.0 %own_rows.1 = bf16[128,128]{1,0:T(8,128)(2,1)} custom-call(bf16[2,144,128]{2,1,0:T(8,128)(2,1)S(1)} %get-tuple-element.38.refs_0_.pair.pair_ref, f32[1024,128]{1,0:T(8,128)S(1)} %get-tuple-element.52.up_in_ref.up_ref, bf16[1024,384]{1,0:T(8,128)(2,1)S(1)} %get-tuple-element.53.d_left_ref, bf16[1024,256]{1,0:T(8,128)(2,1)S(1)} %get-tuple-element.55.d_right_ref, ...), custom_call_target="tpu_custom_call" | custom-call | flops 335544320 | bytes 4194304 | tf_op jit(solution)/shard_map/own_rows/pallas_call | solution.py:533
  41.7 0.0 collective-permute-done.10.left_near
  41.7 2.9 %collective-permute-done.11.right_far = bf16[128,256]{1,0:T(8,128)(2,1)S(1)} collective-permute-done((bf16[128,256]{1,0:T(8,128)(2,1)S(1)}, bf16[128,256]{1,0:T(8,128)(2,1)S(1)}, u32[]{:S(2)}, u32[]{:S(2)}) %collective-permute-start.11) | collective-permute-done | bytes 65568 | tf_op jit(solution)/shard_map/ppermute | solution.py:317
  44.6 0.9 %add_grads.1 = (f32[2,128,640]{2,1,0:T(8,128)}, f32[2,128,128]{2,1,0:T(8,128)}) custom-call(bf16[128,1024]{1,0:T(8,128)(2,1)S(1)} %pad_maximum_fusion.rest, bf16[128,1024]{1,0:T(8,128)(2,1)S(1)} %collective-permute-done.8.rest_near, bf16[128,512]{1,0:T(8,128)(2,1)S(1)} %add_convert_fusion.1.left, bf16[128,512]{1,0:T(8,128)(2,1)S(1)} %collective-permute-done.10.left_near, ...), custom_call_target="tpu_custom_call" | custom-call | tf_op jit(solution)/shard_map/add_grads/pallas_call | solution.py:550
  (5 shorter events, 0.1 us)
Async XLA Ops:
  2.5 4.6 %copy-start = (bf16[272,128]{1,0:T(8,128)(2,1)S(1)}, bf16[272,128]{1,0:T(8,128)(2,1)}, u32[]{:S(2)}) copy-start(bf16[272,128]{1,0:T(8,128)(2,1)} %get-tuple-element.32.near_ref) | copy-start | bytes 208900
  2.5 4.6 %collective-permute-start = (bf16[272,128]{1,0:T(8,128)(2,1)}, bf16[272,128]{1,0:T(8,128)(2,1)S(1)}, u32[]{:S(2)}, u32[]{:S(2)}) collective-permute-start(bf16[272,128]{1,0:T(8,128)(2,1)} %get-tuple-element.32.near_ref), channel_id=1, source_target_pairs={{0,1},{1,0},{2,3},{3,2},{4,5},{5,4},{6,7},{7,6},{8,9},{9,8},{10,11... | collective-permute-start | bytes 208904 | tf_op jit(solution)/shard_map/ppermute | solution.py:317
  3.1 1.0 %copy-start.1 = (bf16[2,128,768]{2,1,0:T(8,128)(2,1)S(1)}, bf16[2,128,768]{2,1,0:T(8,128)(2,1)}, u32[]{:S(2)}) copy-start(bf16[2,128,768]{2,1,0:T(8,128)(2,1)} %get-tuple-element.33.weights_in) | copy-start | bytes 1179652
  4.1 0.7 %copy-start.2 = (f32[2,1280]{1,0:T(2,128)S(1)}, f32[2,1280]{1,0:T(2,128)}, u32[]{:S(2)}) copy-start(f32[2,1280]{1,0:T(2,128)} %get-tuple-element.34.vectors_in) | copy-start | bytes 30724
  7.1 6.6 %collective-permute-start.6 = (bf16[2,144,128]{2,1,0:T(8,128)(2,1)S(1)}, bf16[2,144,128]{2,1,0:T(8,128)(2,1)S(1)}, u32[]{:S(2)}, u32[]{:S(2)}) collective-permute-start(bf16[2,144,128]{2,1,0:T(8,128)(2,1)S(1)} %get-tuple-element.38.refs_0_.pair.pair_ref), channel_id=1, source_target_pairs={{0,4},{1,5},{2,6},{3,7},{4,0},{5,1},{6,2},{7,3},{8,12},{9,13},{10,... | collective-permute-start | bytes 221192 | tf_op jit(solution)/shard_map/ppermute | solution.py:317
  7.5 11.8 %collective-permute-start.5 = (bf16[2,144,128]{2,1,0:T(8,128)(2,1)S(1)}, bf16[2,144,128]{2,1,0:T(8,128)(2,1)S(1)}, u32[]{:S(2)}, u32[]{:S(2)}) collective-permute-start(bf16[2,144,128]{2,1,0:T(8,128)(2,1)S(1)} %get-tuple-element.38.refs_0_.pair.pair_ref), channel_id=1, source_target_pairs={{0,6},{1,7},{2,4},{3,5},{4,2},{5,3},{6,0},{7,1},{8,14},{9,15},{10,... | collective-permute-start | bytes 221192 | tf_op jit(solution)/shard_map/ppermute | solution.py:317
  10.2 9.1 %collective-permute-start.4 = (bf16[2,144,128]{2,1,0:T(8,128)(2,1)S(1)}, bf16[2,144,128]{2,1,0:T(8,128)(2,1)S(1)}, u32[]{:S(2)}, u32[]{:S(2)}) collective-permute-start(bf16[2,144,128]{2,1,0:T(8,128)(2,1)S(1)} %get-tuple-element.38.refs_0_.pair.pair_ref), channel_id=1, source_target_pairs={{0,2},{1,3},{2,0},{3,1},{4,6},{5,7},{6,4},{7,5},{8,10},{9,11},{10,... | collective-permute-start | bytes 221192 | tf_op jit(solution)/shard_map/ppermute | solution.py:317
  11.6 14.4 %collective-permute-start.3 = (bf16[2,128,128]{2,1,0:T(8,128)(2,1)S(1)}, bf16[2,128,128]{2,1,0:T(8,128)(2,1)S(1)}, u32[]{:S(2)}, u32[]{:S(2)}) collective-permute-start(bf16[2,128,128]{2,1,0:T(8,128)(2,1)S(1)} %get-tuple-element.39.refs_0_), channel_id=1, source_target_pairs={{0,4},{1,5},{2,6},{3,7},{4,0},{5,1},{6,2},{7,3},{8,12},{9,13},{10,... | collective-permute-start | bytes 196616 | tf_op jit(solution)/shard_map/ppermute | solution.py:317
  11.7 14.3 %collective-permute-start.2 = (bf16[2,128,128]{2,1,0:T(8,128)(2,1)S(1)}, bf16[2,128,128]{2,1,0:T(8,128)(2,1)S(1)}, u32[]{:S(2)}, u32[]{:S(2)}) collective-permute-start(bf16[2,128,128]{2,1,0:T(8,128)(2,1)S(1)} %get-tuple-element.39.refs_0_), channel_id=1, source_target_pairs={{0,6},{1,7},{2,4},{3,5},{4,2},{5,3},{6,0},{7,1},{8,14},{9,15},{10,... | collective-permute-start | bytes 196616 | tf_op jit(solution)/shard_map/ppermute | solution.py:317
  13.7 12.3 %collective-permute-start.1 = (bf16[2,128,128]{2,1,0:T(8,128)(2,1)S(1)}, bf16[2,128,128]{2,1,0:T(8,128)(2,1)S(1)}, u32[]{:S(2)}, u32[]{:S(2)}) collective-permute-start(bf16[2,128,128]{2,1,0:T(8,128)(2,1)S(1)} %get-tuple-element.39.refs_0_), channel_id=1, source_target_pairs={{0,2},{1,3},{2,0},{3,1},{4,6},{5,7},{6,4},{7,5},{8,10},{9,11},{10,... | collective-permute-start | bytes 196616 | tf_op jit(solution)/shard_map/ppermute | solution.py:317
  30.7 7.1 %collective-permute-start.7 = (bf16[128,768]{1,0:T(8,128)(2,1)S(1)}, bf16[128,768]{1,0:T(8,128)(2,1)S(1)}, u32[]{:S(2)}, u32[]{:S(2)}) collective-permute-start(bf16[128,768]{1,0:T(8,128)(2,1)S(1)} %get-tuple-element.56), channel_id=1, source_target_pairs={{0,16},{8,24},{16,0},{24,8},{1,17},{9,25},{17,1},{25,9},{2,18},{10... | collective-permute-start | bytes 589832 | tf_op jit(solution)/shard_map/ppermute | solution.py:317
  34.9 5.0 %collective-permute-start.9 = (bf16[128,512]{1,0:T(8,128)(2,1)S(1)}, bf16[128,512]{1,0:T(8,128)(2,1)S(1)}, u32[]{:S(2)}, u32[]{:S(2)}) collective-permute-start(bf16[128,512]{1,0:T(8,128)(2,1)S(1)} %get-tuple-element.58), channel_id=1, source_target_pairs={{0,16},{8,24},{16,0},{24,8},{1,17},{9,25},{17,1},{25,9},{2,18},{10... | collective-permute-start | bytes 393224 | tf_op jit(solution)/shard_map/ppermute | solution.py:317
  38.0 2.1 %collective-permute-start.8 = (bf16[128,1024]{1,0:T(8,128)(2,1)S(1)}, bf16[128,1024]{1,0:T(8,128)(2,1)S(1)}, u32[]{:S(2)}, u32[]{:S(2)}) collective-permute-start(bf16[128,1024]{1,0:T(8,128)(2,1)S(1)} %pad_maximum_fusion.rest), channel_id=1, source_target_pairs={{0,8},{8,0},{16,24},{24,16},{1,9},{9,1},{17,25},{25,17},{2,10},{10... | collective-permute-start | bytes 786440 | tf_op jit(solution)/shard_map/ppermute | solution.py:317
  40.0 1.7 %collective-permute-start.10 = (bf16[128,512]{1,0:T(8,128)(2,1)S(1)}, bf16[128,512]{1,0:T(8,128)(2,1)S(1)}, u32[]{:S(2)}, u32[]{:S(2)}) collective-permute-start(bf16[128,512]{1,0:T(8,128)(2,1)S(1)} %add_convert_fusion.1.left), channel_id=1, source_target_pairs={{0,8},{8,0},{16,24},{24,16},{1,9},{9,1},{17,25},{25,17},{2,10},{10... | collective-permute-start | bytes 393224 | tf_op jit(solution)/shard_map/ppermute | solution.py:317
  40.1 4.5 %collective-permute-start.11 = (bf16[128,256]{1,0:T(8,128)(2,1)S(1)}, bf16[128,256]{1,0:T(8,128)(2,1)S(1)}, u32[]{:S(2)}, u32[]{:S(2)}) collective-permute-start(bf16[128,256]{1,0:T(8,128)(2,1)S(1)} %add_convert_fusion.2.right), channel_id=1, source_target_pairs={{0,16},{8,24},{16,0},{24,8},{1,17},{9,25},{17,1},{25,9},{2,18},{10... | collective-permute-start | bytes 196616 | tf_op jit(solution)/shard_map/ppermute | solution.py:317

commit v16 on v15

--- a/solution.py
+++ b/solution.py
@@ -124,7 +124,7 @@
     width = weights.shape[2] - c
     rows = n // (2 * len(jumps))
     cells = rows * n
-    tails = jnp.stack([pair[:, cells:, :] for pair in pairs])
+    tails = jnp.stack([pair[:, cells:, :] for pair in pairs if pair.shape[1] > cells])
     length = tail_values(tails, 0, 64)
     own = own_place(pairs[0])
     for pair, jump in zip(pairs, jumps):
@@ -188,9 +188,9 @@
 def backward_second(n, jumps, pair, *refs):
     parted, refs = refs[: len(jumps)], refs[len(jumps) :]
     weights, vectors = refs[:2]
-    (edges_s, slopes_s, gate_s, hat_s, rstd_s, *kept) = kept_parts(refs[2:], 1)
+    (edges_s, slopes_s, gate_s, _, _, *kept) = kept_parts(refs[2:], 1)
     (p_hat_s, p_rstd_s, branch_s, normed_s, mixed_s) = kept
-    up_ref, grads_ref, d_product_s, d_edges_s, d_pre_s, cot_s = refs[2 + KEPT :]
+    d_pre_s, cot_s, grads_ref, d_product_s, d_edges_s = refs[2 + KEPT :]
     c, h = weights.shape[1], edges_s.shape[2]
     width = 4 * h + c
     gain = vector_parts(vectors[1:2, :], c, width)[1]
@@ -234,26 +234,28 @@
             for side in range(2)
         ]
         d_pre = jnp.concatenate([*grads, d_pre_s[here, 4 * h :]], axis=1)
-        normed = normed_s[here, :]
-        d_normed = dot(d_pre, weights[1, :, :width], ((1,), (1,))) * gain[:, :c]
-        pulled = norm_vjp(hat_s[here, :], rstd_s[here, :], d_normed)
-        up_ref[here, :] = cot_s[here, :].astype(F32) + pulled
-        grads_ref[:, :width] = dot(normed, d_pre, ((0,), (0,))).astype(BF16)
-
-
-def backward_left(n, up_in_ref, weights, vectors, *refs):
+        d_pre_s[here, : 4 * h] = d_pre[:, : 4 * h]
+        grads_ref[:, :width] = dot(normed_s[here, :], d_pre, ((0,), (0,))).astype(BF16)
+
+
+def backward_left(n, d_pre_1_ref, cot_ref, weights, vectors, *refs):
+    hat_1_s, rstd_1_s = kept_parts(refs, 1)[3:5]
     (edges_s, slopes_s, gate_s, _, _, *kept) = kept_parts(refs, 0)
     (p_hat_s, p_rstd_s, branch_s, normed_s, mixed_s) = kept
-    d_pre_ref, d_product_t_ref, grads_ref, d_product_s, d_edge_s = refs[KEPT:]
+    up_ref, d_pre_ref, d_product_t_ref, grads_ref, d_product_s, d_edge_s = refs[KEPT:]
     c, h = weights.shape[1], edges_s.shape[2]
     width = 4 * h + c
-    gain = vector_parts(vectors[0:1, :], c, width)[1]
+    gain, gain_1 = (vector_parts(vectors[u : u + 1, :], c, width)[1] for u in range(2))
 
     @pl.loop(0, n // STEP_ROWS)
     def _(t):
         here = block(t, STEP_ROWS, n)
+        d_normed = dot(d_pre_1_ref[here, :], weights[1, :, :width], ((1,), (1,)))
+        pulled = norm_vjp(hat_1_s[here, :], rstd_1_s[here, :], d_normed * gain_1[:, :c])
+        up = cot_ref[here, :].astype(F32) + pulled
+        up_ref[here, :] = up
         d_branch, d_gate, d_product = unmix(
-            up_in_ref[here, :],
+            up,
             gate_s[here, :],
             branch_s[here, :],
             p_hat_s[here, :],
@@ -356,10 +358,11 @@
         copy.wait()
 
 
-def pair_up(near_ref, far_ref, state_ref, cot_ref):
-    split = state_ref.shape[1]
+def pair_up(near_ref, far_ref, state_ref, rows_ref, cot_ref):
+    split, cells = state_ref.shape[1], rows_ref.shape[1]
     for side, ref in enumerate((near_ref, far_ref)):
         state_ref[side] = ref[:split, :]
+        rows_ref[side] = ref[:cells, :]
         cot_ref[side] = ref[split:, :]
 
 
@@ -454,22 +457,25 @@
     )(*weights)
     beside = exchange(sent, "dap", parts, 1)
     beside, *weights = lax.optimization_barrier((beside, *weights))
-    state, cot = pl.pallas_call(
+    state, state_rows, cot = pl.pallas_call(
         pair_up,
         out_shape=(
             jax.ShapeDtypeStruct((2, cells + TAIL_ROWS, c), BF16),
             jax.ShapeDtypeStruct((2, cells, c), BF16),
+            jax.ShapeDtypeStruct((2, cells, c), BF16),
         ),
         in_specs=[vmem] * 2,
-        out_specs=[vmem] * 2,
+        out_specs=[vmem] * 3,
         compiler_params=params,
         name="pair_up",
     )(sent, beside)
     states, cots = [state], [cot]
     half = parts // 2
     jumps = [0, *range(1, half // 2), *reversed(range(half // 2, half))]
-    for group in (states, cots):
-        group += [exchange(group[0], "dap", parts, 2 * jump) for jump in jumps[1:]]
+    for jump in jumps[1:]:
+        with_tail = jump == half // 2
+        states.append(exchange(state if with_tail else state_rows, "dap", parts, 2 * jump))
+    cots += [exchange(cot, "dap", parts, 2 * jump) for jump in jumps[1:]]
 
     held = pl.pallas_call(
         functools.partial(forward, n, jumps),
@@ -483,17 +489,16 @@
     )(*states, *weights)
 
     double, single = pltpu.VMEM((2,) + plane, F32), pltpu.VMEM(plane, F32)
-    up_1, grads_1 = pl.pallas_call(
+    d_pre_1, cot, grads_1 = pl.pallas_call(
         functools.partial(backward_second, n, jumps),
-        out_shape=(jax.ShapeDtypeStruct((pairs, c), F32), grads),
+        out_shape=(
+            jax.ShapeDtypeStruct((pairs, width), BF16),
+            jax.ShapeDtypeStruct((pairs, c), BF16),
+            grads,
+        ),
         in_specs=[vmem] * (3 + half + KEPT),
-        out_specs=(vmem, vmem),
-        scratch_shapes=[
-            double,
-            double,
-            pltpu.VMEM((pairs, width), BF16),
-            pltpu.VMEM((pairs, c), BF16),
-        ],
+        out_specs=[vmem] * 3,
+        scratch_shapes=[double, double],
         compiler_params=params,
         cost_estimate=cost(48),
         name="backward_second",
@@ -501,20 +506,21 @@
     far = groups // 2
     others_1 = exchange(grads_1, "dp", groups, far)
 
-    d_left, d_product_t, grads_left = pl.pallas_call(
+    up_1, d_left, d_product_t, grads_left = pl.pallas_call(
         functools.partial(backward_left, n),
         out_shape=(
+            jax.ShapeDtypeStruct((pairs, c), F32),
             jax.ShapeDtypeStruct((pairs, 2 * h + c), BF16),
             jax.ShapeDtypeStruct(plane, F32),
             jax.ShapeDtypeStruct((c, 2 * h + 2 * c), BF16),
         ),
-        in_specs=[vmem] * (3 + KEPT),
-        out_specs=[vmem] * 3,
+        in_specs=[vmem] * (4 + KEPT),
+        out_specs=[vmem] * 4,
         scratch_shapes=[single, single],
         compiler_params=params,
         cost_estimate=cost(24),
         name="backward_left",
-    )(up_1, *weights, *held)
+    )(d_pre_1, cot, *weights, *held)
     others_left = exchange(grads_left, "dp", groups, far)
 
     d_right, grads_right = pl.pallas_call(

time: 45.8 us -> 48.3 us (1.055)
  the two profiles are of different devices: /device:TPU:20 before, /device:TPU:0 now
where the time goes in v16:
time: 48.3 us; the launch traced here: 48 us
  Pallas kernels  20 us (41%)
  starting transfers between devices  15 us (31%)
  waiting for transfers between devices  10.4 us (22%)
  local copies, waits for them, and re-layouts  1.7 us (4%)
  between operations  0.78 us (2%)
    ppermute x12, starting transfers between devices, exchange(): return lax.ppermute(value, axis, [(d, d ^ step) for d in range(size)])  15 us
    ppermute x12, waiting for transfers between devices, exchange(): return lax.ppermute(value, axis, [(d, d ^ step) for d in range(size)])  10.4 us
    pallas_call x1, Pallas kernels, crop_shards(): pl.pallas_call(functools.partial(forward, n, jumps), out_shape=kept, in_s...  6.62 us
    pallas_call x1, Pallas kernels, crop_shards(): pl.pallas_call(functools.partial(backward_second, n, jumps), out_shape=(j...  4.42 us
    pallas_call x1, Pallas kernels, crop_shards(): pl.pallas_call(functools.partial(backward_left, n), out_shape=(jax.ShapeD...  3.28 us
    pallas_call x1, Pallas kernels, crop_shards(): pl.pallas_call(prepare, out_shape=(jax.ShapeDtypeStruct((2 * cells + TAIL...  1.88 us
    pallas_call x1, Pallas kernels, crop_shards(): pl.pallas_call(functools.partial(backward_right, n), out_shape=(jax.Shape...  1.73 us
    unnamed x6, local copies, waits for them, and re-layouts  1.7 us
  transfers between devices with their start and end apart: 12, of which 5 were waited for; matrix products, arithmetic and copies ran while one was open for 0% of the time, Pallas kernels for 26%

profile of v16, /device:TPU:0, one launch (start us, length us, event | category | flops | bytes accessed | tf_op | source)
XLA Modules:
  0.0 48.0 jit_solution(16645776044160235787)
XLA Ops:
  0.6 1.9 %prepare.1 = (bf16[272,128]{1,0:T(8,128)(2,1)}, bf16[2,128,768]{2,1,0:T(8,128)(2,1)}, f32[2,1280]{1,0:T(2,128)}) custom-call(s32[1]{0:T(128)} %bitcast.index_ref, s32[4,32]{1,0:T(4,128)} %bitcast.8, bf16[128,128]{1,0:T(8,128)(2,1)} %bitcast.6, bf16[128,128]{1,0:T(8,128)(2,1)} %bitcast.7, bf16[2,128,640]{2,1,0:T(8,128)(2,1)} %w.1, ...), custom_call_target="tpu_custom_call" | custom-call | tf_op jit(solution)/shard_map/prepare/pallas_call | solution.py:429
  2.5 0.0 copy-start
  2.5 3.0 %collective-permute-start = (bf16[272,128]{1,0:T(8,128)(2,1)}, bf16[272,128]{1,0:T(8,128)(2,1)S(1)}, u32[]{:S(2)}, u32[]{:S(2)}) collective-permute-start(bf16[272,128]{1,0:T(8,128)(2,1)} %get-tuple-element.35.near_ref), channel_id=1, source_target_pairs={{0,1},{1,0},{2,3},{3,2},{4,5},{5,4},{6,7},{7,6},{8,9},{9,8},{10,11... | collective-permute-start | bytes 208904 | tf_op jit(solution)/shard_map/ppermute | solution.py:319
  5.6 0.0 copy-start.1
  5.6 1.0 %copy-done.1 = bf16[2,128,768]{2,1,0:T(8,128)(2,1)S(1)} copy-done((bf16[2,128,768]{2,1,0:T(8,128)(2,1)S(1)}, bf16[2,128,768]{2,1,0:T(8,128)(2,1)}, u32[]{:S(2)}) %copy-start.1) | copy-done | bytes 393240
  6.6 0.0 copy-start.2
  6.6 0.7 %copy-done.2 = f32[2,1280]{1,0:T(2,128)S(1)} copy-done((f32[2,1280]{1,0:T(2,128)S(1)}, f32[2,1280]{1,0:T(2,128)}, u32[]{:S(2)}) %copy-start.2) | copy-done | bytes 10264
  7.3 0.8 %collective-permute-done.far_ref = bf16[272,128]{1,0:T(8,128)(2,1)S(1)} collective-permute-done((bf16[272,128]{1,0:T(8,128)(2,1)}, bf16[272,128]{1,0:T(8,128)(2,1)S(1)}, u32[]{:S(2)}, u32[]{:S(2)}) %collective-permute-start) | collective-permute-done | bytes 69664 | tf_op jit(solution)/shard_map/ppermute | solution.py:319
  8.1 0.0 copy-done
  8.1 4.2 %collective-permute-start.5 = (bf16[2,128,128]{2,1,0:T(8,128)(2,1)S(1)}, bf16[2,128,128]{2,1,0:T(8,128)(2,1)S(1)}, u32[]{:S(2)}, u32[]{:S(2)}) collective-permute-start(bf16[2,128,128]{2,1,0:T(8,128)(2,1)S(1)} %get-tuple-element.45), channel_id=1, source_target_pairs={{0,6},{1,7},{2,4},{3,5},{4,2},{5,3},{6,0},{7,1},{8,14},{9,15},{10,... | collective-permute-start | bytes 196616 | tf_op jit(solution)/shard_map/ppermute | solution.py:319
  12.3 0.0 collective-permute-start.6
  12.3 0.6 %collective-permute-start.4 = (bf16[2,128,128]{2,1,0:T(8,128)(2,1)S(1)}, bf16[2,128,128]{2,1,0:T(8,128)(2,1)S(1)}, u32[]{:S(2)}, u32[]{:S(2)}) collective-permute-start(bf16[2,128,128]{2,1,0:T(8,128)(2,1)S(1)} %get-tuple-element.45), channel_id=1, source_target_pairs={{0,2},{1,3},{2,0},{3,1},{4,6},{5,7},{6,4},{7,5},{8,10},{9,11},{10,... | collective-permute-start | bytes 196616 | tf_op jit(solution)/shard_map/ppermute | solution.py:319
  12.9 2.3 %collective-permute-start.3 = (bf16[2,128,128]{2,1,0:T(8,128)(2,1)S(1)}, bf16[2,128,128]{2,1,0:T(8,128)(2,1)S(1)}, u32[]{:S(2)}, u32[]{:S(2)}) collective-permute-start(bf16[2,128,128]{2,1,0:T(8,128)(2,1)S(1)} %get-tuple-element.42.refs_0_), channel_id=1, source_target_pairs={{0,4},{1,5},{2,6},{3,7},{4,0},{5,1},{6,2},{7,3},{8,12},{9,13},{10,... | collective-permute-start | bytes 196616 | tf_op jit(solution)/shard_map/ppermute | solution.py:319
  15.2 1.5 %collective-permute-start.2 = (bf16[2,128,128]{2,1,0:T(8,128)(2,1)S(1)}, bf16[2,128,128]{2,1,0:T(8,128)(2,1)S(1)}, u32[]{:S(2)}, u32[]{:S(2)}) collective-permute-start(bf16[2,128,128]{2,1,0:T(8,128)(2,1)S(1)} %get-tuple-element.42.refs_0_), channel_id=1, source_target_pairs={{0,6},{1,7},{2,4},{3,5},{4,2},{5,3},{6,0},{7,1},{8,14},{9,15},{10,... | collective-permute-start | bytes 196616 | tf_op jit(solution)/shard_map/ppermute | solution.py:319
  16.7 0.0 collective-permute-done.5.refs_2_
  16.7 0.6 %collective-permute-start.1 = (bf16[2,128,128]{2,1,0:T(8,128)(2,1)S(1)}, bf16[2,128,128]{2,1,0:T(8,128)(2,1)S(1)}, u32[]{:S(2)}, u32[]{:S(2)}) collective-permute-start(bf16[2,128,128]{2,1,0:T(8,128)(2,1)S(1)} %get-tuple-element.42.refs_0_), channel_id=1, source_target_pairs={{0,2},{1,3},{2,0},{3,1},{4,6},{5,7},{6,4},{7,5},{8,10},{9,11},{10,... | collective-permute-start | bytes 196616 | tf_op jit(solution)/shard_map/ppermute | solution.py:319
  17.2 0.5 collective-permute-done.4.refs_1_
  17.7 3.7 %collective-permute-done.6.refs_3_ = bf16[2,144,128]{2,1,0:T(8,128)(2,1)S(1)} collective-permute-done((bf16[2,144,128]{2,1,0:T(8,128)(2,1)S(1)}, bf16[2,144,128]{2,1,0:T(8,128)(2,1)S(1)}, u32[]{:S(2)}, u32[]{:S(2)}) %collective-permute-start.6) | collective-permute-done | bytes 73760 | tf_op jit(solution)/shard_map/ppermute | solution.py:319
  21.4 6.6 %forward.1 = (f32[2,4,1032,128]{3,2,1,0:T(8,128)S(1)}, f32[2,2,1032,128]{3,2,1,0:T(8,128)S(1)}, f32[2,1032,128]{2,1,0:T(8,128)S(1)}, f32[2,1032,128]{2,1,0:T(8,1...) custom-call(bf16[2,144,128]{2,1,0:T(8,128)(2,1)S(1)} %get-tuple-elem, ...), custom_call_target="tpu_custom_call" | custom-call | flops 335544320 | bytes 33554432 | tf_op jit(solution)/shard_map/forward/pallas_call | solution.py:480
  28.0 0.0 collective-permute-done.3.refs_3_
  28.0 0.0 collective-permute-done.2.refs_2_
  28.0 0.0 collective-permute-done.1.refs_1_
  28.0 4.4 %backward_second.1 = (bf16[1024,640]{1,0:T(8,128)(2,1)S(1)}, bf16[1024,128]{1,0:T(8,128)(2,1)S(1)}, bf16[128,768]{1,0:T(8,128)(2,1)S(1)}) custom-call(bf16[2,144,128]{2,1,0:T(8,128)(2,1)S(1)} %get-tuple-element.41.refs_0_.pair.pair_ref, bf16[2,128,128]{2,1,0:T(8,128)(2,1)S(1)} %get-tuple-element.42.refs_0_, ...), custom_call_target="tpu_custom_call" | custom-call | flops 335544320 | bytes 25165824 | tf_op jit(solution)/shard_map/backward_second/pallas_call | solution.py:492
  32.5 1.6 %collective-permute-start.7 = (bf16[128,768]{1,0:T(8,128)(2,1)S(1)}, bf16[128,768]{1,0:T(8,128)(2,1)S(1)}, u32[]{:S(2)}, u32[]{:S(2)}) collective-permute-start(bf16[128,768]{1,0:T(8,128)(2,1)S(1)} %get-tuple-element.62), channel_id=1, source_target_pairs={{0,16},{8,24},{16,0},{24,8},{1,17},{9,25},{17,1},{25,9},{2,18},{10... | collective-permute-start | bytes 589832 | tf_op jit(solution)/shard_map/ppermute | solution.py:319
  34.0 3.3 %backward_left.1 = (f32[1024,128]{1,0:T(8,128)S(1)}, bf16[1024,384]{1,0:T(8,128)(2,1)S(1)}, f32[1032,128]{1,0:T(8,128)S(1)}, bf16[128,512]{1,0:T(8,128)(2,1)S(1)}) custom-call(bf16[1024,640]{1,0:T(8,128)(2,1)S(1)} %get-tuple-element.56.d_pre_1_ref, bf16[1024,128]{1,0:T(8,128)(2,1)S(1)} %get-tuple-element.57.cot_ref, ...), custom_call_target="tpu_custom_call" | custom-call | flops 335544320 | bytes 12582912 | tf_op jit(solution)/shard_map/backward_left/pallas_call | solution.py:509
  37.3 0.6 %collective-permute-start.9 = (bf16[128,512]{1,0:T(8,128)(2,1)S(1)}, bf16[128,512]{1,0:T(8,128)(2,1)S(1)}, u32[]{:S(2)}, u32[]{:S(2)}) collective-permute-start(bf16[128,512]{1,0:T(8,128)(2,1)S(1)} %get-tuple-element.64), channel_id=1, source_target_pairs={{0,16},{8,24},{16,0},{24,8},{1,17},{9,25},{17,1},{25,9},{2,18},{10... | collective-permute-start | bytes 393224 | tf_op jit(solution)/shard_map/ppermute | solution.py:319
  37.9 1.7 %backward_right.1 = (bf16[1024,256]{1,0:T(8,128)(2,1)S(1)}, bf16[128,256]{1,0:T(8,128)(2,1)S(1)}) custom-call(f32[1032,128]{1,0:T(8,128)S(1)} %get-tuple-element.60.d_product_t_ref, f32[2,4,1032,128]{3,2,1,0:T(8,128)S(1)} %get-tuple-element.46.refs_6_.refs_0_, f32[2,2,1032,128]{3,2,1,0:T(8,128)S(1)} %get-tuple-element.47.refs_7_.refs_1_, ...), custom_call_target="tpu_custom_call" | custom-call | flops 335544320 | bytes 12582912 | tf_op jit(solution)/shard_map/backward_right/pallas_call | solution.py:526
  39.6 0.0 collective-permute-done.7
  39.7 0.1 add_convert_fusion
  39.7 0.1 collective-permute-start.8
  39.8 2.5 %collective-permute-done.9 = bf16[128,512]{1,0:T(8,128)(2,1)S(1)} collective-permute-done((bf16[128,512]{1,0:T(8,128)(2,1)S(1)}, bf16[128,512]{1,0:T(8,128)(2,1)S(1)}, u32[]{:S(2)}, u32[]{:S(2)}) %collective-permute-start.9) | collective-permute-done | bytes 131104 | tf_op jit(solution)/shard_map/ppermute | solution.py:319
  42.4 0.1 collective-permute-start.10
  42.5 0.0 collective-permute-done.8.rest_near
  42.5 0.6 %collective-permute-start.11 = (bf16[128,256]{1,0:T(8,128)(2,1)S(1)}, bf16[128,256]{1,0:T(8,128)(2,1)S(1)}, u32[]{:S(2)}, u32[]{:S(2)}) collective-permute-start(bf16[128,256]{1,0:T(8,128)(2,1)S(1)} %add_convert_fusion.2.right), channel_id=1, source_target_pairs={{0,16},{8,24},{16,0},{24,8},{1,17},{9,25},{17,1},{25,9},{2,18},{10... | collective-permute-start | bytes 196616 | tf_op jit(solution)/shard_map/ppermute | solution.py:319
  43.1 1.0 %own_rows.1 = bf16[128,128]{1,0:T(8,128)(2,1)} custom-call(bf16[2,144,128]{2,1,0:T(8,128)(2,1)S(1)} %get-tuple-element.41.refs_0_.pair.pair_ref, f32[1024,128]{1,0:T(8,128)S(1)} %get-tuple-element.58.up_ref, bf16[1024,384]{1,0:T(8,128)(2,1)S(1)} %get-tuple-element.59.d_left_ref, bf16[1024,256]{1,0:T(8,128)(2,1)S(1)} %get-tuple-element.61.d_right_ref, ...), custom_call_target="tpu_custom_call" | custom-call | flops 335544320 | bytes 4194304 | tf_op jit(solution)/shard_map/own_rows/pallas_call | solution.py:539
  44.1 0.0 collective-permute-done.10.left_near
  44.1 2.9 %collective-permute-done.11.right_far = bf16[128,256]{1,0:T(8,128)(2,1)S(1)} collective-permute-done((bf16[128,256]{1,0:T(8,128)(2,1)S(1)}, bf16[128,256]{1,0:T(8,128)(2,1)S(1)}, u32[]{:S(2)}, u32[]{:S(2)}) %collective-permute-start.11) | collective-permute-done | bytes 65568 | tf_op jit(solution)/shard_map/ppermute | solution.py:319
  47.1 1.0 %add_grads.1 = (f32[2,128,640]{2,1,0:T(8,128)}, f32[2,128,128]{2,1,0:T(8,128)}) custom-call(bf16[128,1024]{1,0:T(8,128)(2,1)S(1)} %pad_maximum_fusion.rest, bf16[128,1024]{1,0:T(8,128)(2,1)S(1)} %collective-permute-done.8.rest_near, bf16[128,512]{1,0:T(8,128)(2,1)S(1)} %add_convert_fusion.1.left, bf16[128,512]{1,0:T(8,128)(2,1)S(1)} %collective-permute-done.10.left_near, ...), custom_call_target="tpu_custom_call" | custom-call | tf_op jit(solution)/shard_map/add_grads/pallas_call | solution.py:556
  (5 shorter events, 0.1 us)
Async XLA Ops:
  2.5 5.5 %copy-start = (bf16[272,128]{1,0:T(8,128)(2,1)S(1)}, bf16[272,128]{1,0:T(8,128)(2,1)}, u32[]{:S(2)}) copy-start(bf16[272,128]{1,0:T(8,128)(2,1)} %get-tuple-element.35.near_ref) | copy-start | bytes 208900
  2.5 5.5 %collective-permute-start = (bf16[272,128]{1,0:T(8,128)(2,1)}, bf16[272,128]{1,0:T(8,128)(2,1)S(1)}, u32[]{:S(2)}, u32[]{:S(2)}) collective-permute-start(bf16[272,128]{1,0:T(8,128)(2,1)} %get-tuple-element.35.near_ref), channel_id=1, source_target_pairs={{0,1},{1,0},{2,3},{3,2},{4,5},{5,4},{6,7},{7,6},{8,9},{9,8},{10,11... | collective-permute-start | bytes 208904 | tf_op jit(solution)/shard_map/ppermute | solution.py:319
  5.6 1.0 %copy-start.1 = (bf16[2,128,768]{2,1,0:T(8,128)(2,1)S(1)}, bf16[2,128,768]{2,1,0:T(8,128)(2,1)}, u32[]{:S(2)}) copy-start(bf16[2,128,768]{2,1,0:T(8,128)(2,1)} %get-tuple-element.36.weights_in) | copy-start | bytes 1179652
  6.6 0.7 %copy-start.2 = (f32[2,1280]{1,0:T(2,128)S(1)}, f32[2,1280]{1,0:T(2,128)}, u32[]{:S(2)}) copy-start(f32[2,1280]{1,0:T(2,128)} %get-tuple-element.37.vectors_in) | copy-start | bytes 30724
  8.1 8.6 %collective-permute-start.5 = (bf16[2,128,128]{2,1,0:T(8,128)(2,1)S(1)}, bf16[2,128,128]{2,1,0:T(8,128)(2,1)S(1)}, u32[]{:S(2)}, u32[]{:S(2)}) collective-permute-start(bf16[2,128,128]{2,1,0:T(8,128)(2,1)S(1)} %get-tuple-element.45), channel_id=1, source_target_pairs={{0,6},{1,7},{2,4},{3,5},{4,2},{5,3},{6,0},{7,1},{8,14},{9,15},{10,... | collective-permute-start | bytes 196616 | tf_op jit(solution)/shard_map/ppermute | solution.py:319
  12.3 9.1 %collective-permute-start.6 = (bf16[2,144,128]{2,1,0:T(8,128)(2,1)S(1)}, bf16[2,144,128]{2,1,0:T(8,128)(2,1)S(1)}, u32[]{:S(2)}, u32[]{:S(2)}) collective-permute-start(bf16[2,144,128]{2,1,0:T(8,128)(2,1)S(1)} %get-tuple-element.41.refs_0_.pair.pair_ref), channel_id=1, source_target_pairs={{0,4},{1,5},{2,6},{3,7},{4,0},{5,1},{6,2},{7,3},{8,12},{9,13},{10,... | collective-permute-start | bytes 221192 | tf_op jit(solution)/shard_map/ppermute | solution.py:319
  12.3 5.4 %collective-permute-start.4 = (bf16[2,128,128]{2,1,0:T(8,128)(2,1)S(1)}, bf16[2,128,128]{2,1,0:T(8,128)(2,1)S(1)}, u32[]{:S(2)}, u32[]{:S(2)}) collective-permute-start(bf16[2,128,128]{2,1,0:T(8,128)(2,1)S(1)} %get-tuple-element.45), channel_id=1, source_target_pairs={{0,2},{1,3},{2,0},{3,1},{4,6},{5,7},{6,4},{7,5},{8,10},{9,11},{10,... | collective-permute-start | bytes 196616 | tf_op jit(solution)/shard_map/ppermute | solution.py:319
  12.9 15.1 %collective-permute-start.3 = (bf16[2,128,128]{2,1,0:T(8,128)(2,1)S(1)}, bf16[2,128,128]{2,1,0:T(8,128)(2,1)S(1)}, u32[]{:S(2)}, u32[]{:S(2)}) collective-permute-start(bf16[2,128,128]{2,1,0:T(8,128)(2,1)S(1)} %get-tuple-element.42.refs_0_), channel_id=1, source_target_pairs={{0,4},{1,5},{2,6},{3,7},{4,0},{5,1},{6,2},{7,3},{8,12},{9,13},{10,... | collective-permute-start | bytes 196616 | tf_op jit(solution)/shard_map/ppermute | solution.py:319
  15.2 12.8 %collective-permute-start.2 = (bf16[2,128,128]{2,1,0:T(8,128)(2,1)S(1)}, bf16[2,128,128]{2,1,0:T(8,128)(2,1)S(1)}, u32[]{:S(2)}, u32[]{:S(2)}) collective-permute-start(bf16[2,128,128]{2,1,0:T(8,128)(2,1)S(1)} %get-tuple-element.42.refs_0_), channel_id=1, source_target_pairs={{0,6},{1,7},{2,4},{3,5},{4,2},{5,3},{6,0},{7,1},{8,14},{9,15},{10,... | collective-permute-start | bytes 196616 | tf_op jit(solution)/shard_map/ppermute | solution.py:319
  16.7 11.4 %collective-permute-start.1 = (bf16[2,128,128]{2,1,0:T(8,128)(2,1)S(1)}, bf16[2,128,128]{2,1,0:T(8,128)(2,1)S(1)}, u32[]{:S(2)}, u32[]{:S(2)}) collective-permute-start(bf16[2,128,128]{2,1,0:T(8,128)(2,1)S(1)} %get-tuple-element.42.refs_0_), channel_id=1, source_target_pairs={{0,2},{1,3},{2,0},{3,1},{4,6},{5,7},{6,4},{7,5},{8,10},{9,11},{10,... | collective-permute-start | bytes 196616 | tf_op jit(solution)/shard_map/ppermute | solution.py:319
  32.5 7.2 %collective-permute-start.7 = (bf16[128,768]{1,0:T(8,128)(2,1)S(1)}, bf16[128,768]{1,0:T(8,128)(2,1)S(1)}, u32[]{:S(2)}, u32[]{:S(2)}) collective-permute-start(bf16[128,768]{1,0:T(8,128)(2,1)S(1)} %get-tuple-element.62), channel_id=1, source_target_pairs={{0,16},{8,24},{16,0},{24,8},{1,17},{9,25},{17,1},{25,9},{2,18},{10... | collective-permute-start | bytes 589832 | tf_op jit(solution)/shard_map/ppermute | solution.py:319
  37.3 5.0 %collective-permute-start.9 = (bf16[128,512]{1,0:T(8,128)(2,1)S(1)}, bf16[128,512]{1,0:T(8,128)(2,1)S(1)}, u32[]{:S(2)}, u32[]{:S(2)}) collective-permute-start(bf16[128,512]{1,0:T(8,128)(2,1)S(1)} %get-tuple-element.64), channel_id=1, source_target_pairs={{0,16},{8,24},{16,0},{24,8},{1,17},{9,25},{17,1},{25,9},{2,18},{10... | collective-permute-start | bytes 393224 | tf_op jit(solution)/shard_map/ppermute | solution.py:319
  39.7 2.7 %collective-permute-start.8 = (bf16[128,1024]{1,0:T(8,128)(2,1)S(1)}, bf16[128,1024]{1,0:T(8,128)(2,1)S(1)}, u32[]{:S(2)}, u32[]{:S(2)}) collective-permute-start(bf16[128,1024]{1,0:T(8,128)(2,1)S(1)} %pad_maximum_fusion.rest), channel_id=1, source_target_pairs={{0,8},{8,0},{16,24},{24,16},{1,9},{9,1},{17,25},{25,17},{2,10},{10... | collective-permute-start | bytes 786440 | tf_op jit(solution)/shard_map/ppermute | solution.py:319
  42.4 1.7 %collective-permute-start.10 = (bf16[128,512]{1,0:T(8,128)(2,1)S(1)}, bf16[128,512]{1,0:T(8,128)(2,1)S(1)}, u32[]{:S(2)}, u32[]{:S(2)}) collective-permute-start(bf16[128,512]{1,0:T(8,128)(2,1)S(1)} %add_convert_fusion.1.left), channel_id=1, source_target_pairs={{0,8},{8,0},{16,24},{24,16},{1,9},{9,1},{17,25},{25,17},{2,10},{10... | collective-permute-start | bytes 393224 | tf_op jit(solution)/shard_map/ppermute | solution.py:319
  42.5 4.5 %collective-permute-start.11 = (bf16[128,256]{1,0:T(8,128)(2,1)S(1)}, bf16[128,256]{1,0:T(8,128)(2,1)S(1)}, u32[]{:S(2)}, u32[]{:S(2)}) collective-permute-start(bf16[128,256]{1,0:T(8,128)(2,1)S(1)} %add_convert_fusion.2.right), channel_id=1, source_target_pairs={{0,16},{8,24},{16,0},{24,8},{1,17},{9,25},{17,1},{25,9},{2,18},{10... | collective-permute-start | bytes 196616 | tf_op jit(solution)/shard_map/ppermute | solution.py:319

commit v17 on v16

--- a/solution.py
+++ b/solution.py
@@ -124,7 +124,7 @@
     width = weights.shape[2] - c
     rows = n // (2 * len(jumps))
     cells = rows * n
-    tails = jnp.stack([pair[:, cells:, :] for pair in pairs if pair.shape[1] > cells])
+    tails = jnp.stack([pair[:, cells:, :] for pair in pairs])
     length = tail_values(tails, 0, 64)
     own = own_place(pairs[0])
     for pair, jump in zip(pairs, jumps):
@@ -358,11 +358,10 @@
         copy.wait()
 
 
-def pair_up(near_ref, far_ref, state_ref, rows_ref, cot_ref):
-    split, cells = state_ref.shape[1], rows_ref.shape[1]
+def pair_up(near_ref, far_ref, state_ref, cot_ref):
+    split = state_ref.shape[1]
     for side, ref in enumerate((near_ref, far_ref)):
         state_ref[side] = ref[:split, :]
-        rows_ref[side] = ref[:cells, :]
         cot_ref[side] = ref[split:, :]
 
 
@@ -457,25 +456,23 @@
     )(*weights)
     beside = exchange(sent, "dap", parts, 1)
     beside, *weights = lax.optimization_barrier((beside, *weights))
-    state, state_rows, cot = pl.pallas_call(
+    state, cot = pl.pallas_call(
         pair_up,
         out_shape=(
             jax.ShapeDtypeStruct((2, cells + TAIL_ROWS, c), BF16),
             jax.ShapeDtypeStruct((2, cells, c), BF16),
-            jax.ShapeDtypeStruct((2, cells, c), BF16),
         ),
         in_specs=[vmem] * 2,
-        out_specs=[vmem] * 3,
+        out_specs=[vmem] * 2,
         compiler_params=params,
         name="pair_up",
     )(sent, beside)
     states, cots = [state], [cot]
     half = parts // 2
     jumps = [0, *range(1, half // 2), *reversed(range(half // 2, half))]
-    for jump in jumps[1:]:
-        with_tail = jump == half // 2
-        states.append(exchange(state if with_tail else state_rows, "dap", parts, 2 * jump))
-    cots += [exchange(cot, "dap", parts, 2 * jump) for jump in jumps[1:]]
+    states += [exchange(state, "dap", parts, 2 * jump) for jump in jumps[1:]]
+    cot_jumps = [0, *reversed(range(1, half))]
+    cots += [exchange(cot, "dap", parts, 2 * jump) for jump in cot_jumps[1:]]
 
     held = pl.pallas_call(
         functools.partial(forward, n, jumps),
@@ -490,7 +487,7 @@
 
     double, single = pltpu.VMEM((2,) + plane, F32), pltpu.VMEM(plane, F32)
     d_pre_1, cot, grads_1 = pl.pallas_call(
-        functools.partial(backward_second, n, jumps),
+        functools.partial(backward_second, n, cot_jumps),
         out_shape=(
             jax.ShapeDtypeStruct((pairs, width), BF16),
             jax.ShapeDtypeStruct((pairs, c), BF16),

time: 48.3 us -> 47.5 us (0.983)
  waiting for transfers between devices: 10.4 us -> 6.24 us
  starting transfers between devices: 15 us -> 18.5 us
    ppermute x12, waiting for transfers between devices: 10.4 us -> 6.24 us  [exchange(): return lax.ppermute(value, axis, [(d, d ^ step) for d in range(size)])]
    ppermute x12, starting transfers between devices: 15 us -> 18.5 us  [exchange(): return lax.ppermute(value, axis, [(d, d ^ step) for d in range(size)])]
  transfers between devices with their start and end apart: 12 -> 12, of which waited for: 5 -> 3; matrix products, arithmetic and copies ran while one was open for 0% -> 0% of each run, Pallas kernels for 26% -> 27%
where the time goes in v17:
time: 47.5 us; the launch traced here: 47.3 us
  Pallas kernels  20 us (42%)
  starting transfers between devices  18.5 us (39%)
  waiting for transfers between devices  6.24 us (13%)
  local copies, waits for them, and re-layouts  1.7 us (4%)
  between operations  0.77 us (2%)
    ppermute x12, starting transfers between devices, exchange(): return lax.ppermute(value, axis, [(d, d ^ step) for d in range(size)])  18.5 us
    pallas_call x1, Pallas kernels, crop_shards(): pl.pallas_call(functools.partial(forward, n, jumps), out_shape=kept, in_s...  6.63 us
    ppermute x12, waiting for transfers between devices, exchange(): return lax.ppermute(value, axis, [(d, d ^ step) for d in range(size)])  6.24 us
    pallas_call x1, Pallas kernels, crop_shards(): pl.pallas_call(functools.partial(backward_second, n, cot_jumps), out_shap...  4.43 us
    pallas_call x1, Pallas kernels, crop_shards(): pl.pallas_call(functools.partial(backward_left, n), out_shape=(jax.ShapeD...  3.29 us
    pallas_call x1, Pallas kernels, crop_shards(): pl.pallas_call(prepare, out_shape=(jax.ShapeDtypeStruct((2 * cells + TAIL...  1.88 us
    pallas_call x1, Pallas kernels, crop_shards(): pl.pallas_call(functools.partial(backward_right, n), out_shape=(jax.Shape...  1.73 us
    unnamed x6, local copies, waits for them, and re-layouts  1.7 us
  transfers between devices with their start and end apart: 12, of which 3 were waited for; matrix products, arithmetic and copies ran while one was open for 0% of the time, Pallas kernels for 27%

profile of v17, /device:TPU:0, one launch (start us, length us, event | category | flops | bytes accessed | tf_op | source)
XLA Modules:
  0.0 47.3 jit_solution(2519629904838078283)
XLA Ops:
  0.6 1.9 %prepare.1 = (bf16[272,128]{1,0:T(8,128)(2,1)}, bf16[2,128,768]{2,1,0:T(8,128)(2,1)}, f32[2,1280]{1,0:T(2,128)}) custom-call(s32[1]{0:T(128)} %bitcast.index_ref, s32[4,32]{1,0:T(4,128)} %bitcast.8, bf16[128,128]{1,0:T(8,128)(2,1)} %bitcast.6, bf16[128,128]{1,0:T(8,128)(2,1)} %bitcast.7, bf16[2,128,640]{2,1,0:T(8,128)(2,1)} %w.1, ...), custom_call_target="tpu_custom_call" | custom-call | tf_op jit(solution)/shard_map/prepare/pallas_call | solution.py:428
  2.5 0.0 copy-start
  2.5 3.0 %collective-permute-start = (bf16[272,128]{1,0:T(8,128)(2,1)}, bf16[272,128]{1,0:T(8,128)(2,1)S(1)}, u32[]{:S(2)}, u32[]{:S(2)}) collective-permute-start(bf16[272,128]{1,0:T(8,128)(2,1)} %get-tuple-element.34.near_ref), channel_id=1, source_target_pairs={{0,1},{1,0},{2,3},{3,2},{4,5},{5,4},{6,7},{7,6},{8,9},{9,8},{10,11... | collective-permute-start | bytes 208904 | tf_op jit(solution)/shard_map/ppermute | solution.py:319
  5.6 0.0 copy-start.1
  5.6 1.0 %copy-done.1 = bf16[2,128,768]{2,1,0:T(8,128)(2,1)S(1)} copy-done((bf16[2,128,768]{2,1,0:T(8,128)(2,1)S(1)}, bf16[2,128,768]{2,1,0:T(8,128)(2,1)}, u32[]{:S(2)}) %copy-start.1) | copy-done | bytes 393240
  6.6 0.0 copy-start.2
  6.6 0.7 %copy-done.2 = f32[2,1280]{1,0:T(2,128)S(1)} copy-done((f32[2,1280]{1,0:T(2,128)S(1)}, f32[2,1280]{1,0:T(2,128)}, u32[]{:S(2)}) %copy-start.2) | copy-done | bytes 10264
  7.3 0.8 %collective-permute-done.far_ref = bf16[272,128]{1,0:T(8,128)(2,1)S(1)} collective-permute-done((bf16[272,128]{1,0:T(8,128)(2,1)}, bf16[272,128]{1,0:T(8,128)(2,1)S(1)}, u32[]{:S(2)}, u32[]{:S(2)}) %collective-permute-start) | collective-permute-done | bytes 69664 | tf_op jit(solution)/shard_map/ppermute | solution.py:319
  8.1 0.0 copy-done
  8.1 3.2 %collective-permute-start.6 = (bf16[2,144,128]{2,1,0:T(8,128)(2,1)S(1)}, bf16[2,144,128]{2,1,0:T(8,128)(2,1)S(1)}, u32[]{:S(2)}, u32[]{:S(2)}) collective-permute-start(bf16[2,144,128]{2,1,0:T(8,128)(2,1)S(1)} %get-tuple-element.40.refs_0_.pair.pair_ref), channel_id=1, source_target_pairs={{0,4},{1,5},{2,6},{3,7},{4,0},{5,1},{6,2},{7,3},{8,12},{9,13},{10,... | collective-permute-start | bytes 221192 | tf_op jit(solution)/shard_map/ppermute | solution.py:319
  11.2 1.3 %collective-permute-start.5 = (bf16[2,144,128]{2,1,0:T(8,128)(2,1)S(1)}, bf16[2,144,128]{2,1,0:T(8,128)(2,1)S(1)}, u32[]{:S(2)}, u32[]{:S(2)}) collective-permute-start(bf16[2,144,128]{2,1,0:T(8,128)(2,1)S(1)} %get-tuple-element.40.refs_0_.pair.pair_ref), channel_id=1, source_target_pairs={{0,6},{1,7},{2,4},{3,5},{4,2},{5,3},{6,0},{7,1},{8,14},{9,15},{10,... | collective-permute-start | bytes 221192 | tf_op jit(solution)/shard_map/ppermute | solution.py:319
  12.6 0.2 collective-permute-start.4
  12.8 1.8 %collective-permute-start.3 = (bf16[2,128,128]{2,1,0:T(8,128)(2,1)S(1)}, bf16[2,128,128]{2,1,0:T(8,128)(2,1)S(1)}, u32[]{:S(2)}, u32[]{:S(2)}) collective-permute-start(bf16[2,128,128]{2,1,0:T(8,128)(2,1)S(1)} %get-tuple-element.41.refs_0_), channel_id=1, source_target_pairs={{0,2},{1,3},{2,0},{3,1},{4,6},{5,7},{6,4},{7,5},{8,10},{9,11},{10,... | collective-permute-start | bytes 196616 | tf_op jit(solution)/shard_map/ppermute | solution.py:319
  14.6 1.7 %collective-permute-start.2 = (bf16[2,128,128]{2,1,0:T(8,128)(2,1)S(1)}, bf16[2,128,128]{2,1,0:T(8,128)(2,1)S(1)}, u32[]{:S(2)}, u32[]{:S(2)}) collective-permute-start(bf16[2,128,128]{2,1,0:T(8,128)(2,1)S(1)} %get-tuple-element.41.refs_0_), channel_id=1, source_target_pairs={{0,4},{1,5},{2,6},{3,7},{4,0},{5,1},{6,2},{7,3},{8,12},{9,13},{10,... | collective-permute-start | bytes 196616 | tf_op jit(solution)/shard_map/ppermute | solution.py:319
  16.3 0.0 collective-permute-done.6.refs_3_
  16.3 4.3 %collective-permute-start.1 = (bf16[2,128,128]{2,1,0:T(8,128)(2,1)S(1)}, bf16[2,128,128]{2,1,0:T(8,128)(2,1)S(1)}, u32[]{:S(2)}, u32[]{:S(2)}) collective-permute-start(bf16[2,128,128]{2,1,0:T(8,128)(2,1)S(1)} %get-tuple-element.41.refs_0_), channel_id=1, source_target_pairs={{0,6},{1,7},{2,4},{3,5},{4,2},{5,3},{6,0},{7,1},{8,14},{9,15},{10,... | collective-permute-start | bytes 196616 | tf_op jit(solution)/shard_map/ppermute | solution.py:319
  20.6 0.0 collective-permute-done.5.refs_2_
  20.6 0.0 collective-permute-done.4.refs_1_
  20.6 6.6 %forward.1 = (f32[2,4,1032,128]{3,2,1,0:T(8,128)S(1)}, f32[2,2,1032,128]{3,2,1,0:T(8,128)S(1)}, f32[2,1032,128]{2,1,0:T(8,128)S(1)}, f32[2,1032,128]{2,1,0:T(8,1...) custom-call(bf16[2,144,128]{2,1,0:T(8,128)(2,1)S(1)} %get-tuple-elem, ...), custom_call_target="tpu_custom_call" | custom-call | flops 335544320 | bytes 33554432 | tf_op jit(solution)/shard_map/forward/pallas_call | solution.py:477
  27.2 0.0 collective-permute-done.3.refs_3_
  27.3 0.0 collective-permute-done.2.refs_2_
  27.3 0.0 collective-permute-done.1.refs_1_
  27.3 4.4 %backward_second.1 = (bf16[1024,640]{1,0:T(8,128)(2,1)S(1)}, bf16[1024,128]{1,0:T(8,128)(2,1)S(1)}, bf16[128,768]{1,0:T(8,128)(2,1)S(1)}) custom-call(bf16[2,144,128]{2,1,0:T(8,128)(2,1)S(1)} %get-tuple-element.40.refs_0_.pair.pair_ref, bf16[2,128,128]{2,1,0:T(8,128)(2,1)S(1)} %get-tuple-element.41.refs_0_, ...), custom_call_target="tpu_custom_call" | custom-call | flops 335544320 | bytes 25165824 | tf_op jit(solution)/shard_map/backward_second/pallas_call | solution.py:489
  31.7 1.6 %collective-permute-start.7 = (bf16[128,768]{1,0:T(8,128)(2,1)S(1)}, bf16[128,768]{1,0:T(8,128)(2,1)S(1)}, u32[]{:S(2)}, u32[]{:S(2)}) collective-permute-start(bf16[128,768]{1,0:T(8,128)(2,1)S(1)} %get-tuple-element.60), channel_id=1, source_target_pairs={{0,16},{8,24},{16,0},{24,8},{1,17},{9,25},{17,1},{25,9},{2,18},{10... | collective-permute-start | bytes 589832 | tf_op jit(solution)/shard_map/ppermute | solution.py:319
  33.3 3.3 %backward_left.1 = (f32[1024,128]{1,0:T(8,128)S(1)}, bf16[1024,384]{1,0:T(8,128)(2,1)S(1)}, f32[1032,128]{1,0:T(8,128)S(1)}, bf16[128,512]{1,0:T(8,128)(2,1)S(1)}) custom-call(bf16[1024,640]{1,0:T(8,128)(2,1)S(1)} %get-tuple-element.54.d_pre_1_ref, bf16[1024,128]{1,0:T(8,128)(2,1)S(1)} %get-tuple-element.55.cot_ref, ...), custom_call_target="tpu_custom_call" | custom-call | flops 335544320 | bytes 12582912 | tf_op jit(solution)/shard_map/backward_left/pallas_call | solution.py:506
  36.6 0.6 %collective-permute-start.9 = (bf16[128,512]{1,0:T(8,128)(2,1)S(1)}, bf16[128,512]{1,0:T(8,128)(2,1)S(1)}, u32[]{:S(2)}, u32[]{:S(2)}) collective-permute-start(bf16[128,512]{1,0:T(8,128)(2,1)S(1)} %get-tuple-element.62), channel_id=1, source_target_pairs={{0,16},{8,24},{16,0},{24,8},{1,17},{9,25},{17,1},{25,9},{2,18},{10... | collective-permute-start | bytes 393224 | tf_op jit(solution)/shard_map/ppermute | solution.py:319
  37.2 1.7 %backward_right.1 = (bf16[1024,256]{1,0:T(8,128)(2,1)S(1)}, bf16[128,256]{1,0:T(8,128)(2,1)S(1)}) custom-call(f32[1032,128]{1,0:T(8,128)S(1)} %get-tuple-element.58.d_product_t_ref, f32[2,4,1032,128]{3,2,1,0:T(8,128)S(1)} %get-tuple-element.44.refs_6_.refs_0_, f32[2,2,1032,128]{3,2,1,0:T(8,128)S(1)} %get-tuple-element.45.refs_7_.refs_1_, ...), custom_call_target="tpu_custom_call" | custom-call | flops 335544320 | bytes 12582912 | tf_op jit(solution)/shard_map/backward_right/pallas_call | solution.py:523
  38.9 0.0 collective-permute-done.7
  38.9 0.1 add_convert_fusion
  39.0 0.1 collective-permute-start.8
  39.1 2.5 %collective-permute-done.9 = bf16[128,512]{1,0:T(8,128)(2,1)S(1)} collective-permute-done((bf16[128,512]{1,0:T(8,128)(2,1)S(1)}, bf16[128,512]{1,0:T(8,128)(2,1)S(1)}, u32[]{:S(2)}, u32[]{:S(2)}) %collective-permute-start.9) | collective-permute-done | bytes 131104 | tf_op jit(solution)/shard_map/ppermute | solution.py:319
  41.6 0.1 collective-permute-start.10
  41.7 0.0 collective-permute-done.8.rest_near
  41.8 0.6 %collective-permute-start.11 = (bf16[128,256]{1,0:T(8,128)(2,1)S(1)}, bf16[128,256]{1,0:T(8,128)(2,1)S(1)}, u32[]{:S(2)}, u32[]{:S(2)}) collective-permute-start(bf16[128,256]{1,0:T(8,128)(2,1)S(1)} %add_convert_fusion.2.right), channel_id=1, source_target_pairs={{0,16},{8,24},{16,0},{24,8},{1,17},{9,25},{17,1},{25,9},{2,18},{10... | collective-permute-start | bytes 196616 | tf_op jit(solution)/shard_map/ppermute | solution.py:319
  42.4 1.0 %own_rows.1 = bf16[128,128]{1,0:T(8,128)(2,1)} custom-call(bf16[2,144,128]{2,1,0:T(8,128)(2,1)S(1)} %get-tuple-element.40.refs_0_.pair.pair_ref, f32[1024,128]{1,0:T(8,128)S(1)} %get-tuple-element.56.up_ref, bf16[1024,384]{1,0:T(8,128)(2,1)S(1)} %get-tuple-element.57.d_left_ref, bf16[1024,256]{1,0:T(8,128)(2,1)S(1)} %get-tuple-element.59.d_right_ref, ...), custom_call_target="tpu_custom_call" | custom-call | flops 335544320 | bytes 4194304 | tf_op jit(solution)/shard_map/own_rows/pallas_call | solution.py:536
  43.4 0.0 collective-permute-done.10.left_near
  43.4 2.9 %collective-permute-done.11.right_far = bf16[128,256]{1,0:T(8,128)(2,1)S(1)} collective-permute-done((bf16[128,256]{1,0:T(8,128)(2,1)S(1)}, bf16[128,256]{1,0:T(8,128)(2,1)S(1)}, u32[]{:S(2)}, u32[]{:S(2)}) %collective-permute-start.11) | collective-permute-done | bytes 65568 | tf_op jit(solution)/shard_map/ppermute | solution.py:319
  46.3 1.0 %add_grads.1 = (f32[2,128,640]{2,1,0:T(8,128)}, f32[2,128,128]{2,1,0:T(8,128)}) custom-call(bf16[128,1024]{1,0:T(8,128)(2,1)S(1)} %pad_maximum_fusion.rest, bf16[128,1024]{1,0:T(8,128)(2,1)S(1)} %collective-permute-done.8.rest_near, bf16[128,512]{1,0:T(8,128)(2,1)S(1)} %add_convert_fusion.1.left, bf16[128,512]{1,0:T(8,128)(2,1)S(1)} %collective-permute-done.10.left_near, ...), custom_call_target="tpu_custom_call" | custom-call | tf_op jit(solution)/shard_map/add_grads/pallas_call | solution.py:553
  (5 shorter events, 0.1 us)
Async XLA Ops:
  2.5 5.5 %copy-start = (bf16[272,128]{1,0:T(8,128)(2,1)S(1)}, bf16[272,128]{1,0:T(8,128)(2,1)}, u32[]{:S(2)}) copy-start(bf16[272,128]{1,0:T(8,128)(2,1)} %get-tuple-element.34.near_ref) | copy-start | bytes 208900
  2.5 5.5 %collective-permute-start = (bf16[272,128]{1,0:T(8,128)(2,1)}, bf16[272,128]{1,0:T(8,128)(2,1)S(1)}, u32[]{:S(2)}, u32[]{:S(2)}) collective-permute-start(bf16[272,128]{1,0:T(8,128)(2,1)} %get-tuple-element.34.near_ref), channel_id=1, source_target_pairs={{0,1},{1,0},{2,3},{3,2},{4,5},{5,4},{6,7},{7,6},{8,9},{9,8},{10,11... | collective-permute-start | bytes 208904 | tf_op jit(solution)/shard_map/ppermute | solution.py:319
  5.6 1.0 %copy-start.1 = (bf16[2,128,768]{2,1,0:T(8,128)(2,1)S(1)}, bf16[2,128,768]{2,1,0:T(8,128)(2,1)}, u32[]{:S(2)}) copy-start(bf16[2,128,768]{2,1,0:T(8,128)(2,1)} %get-tuple-element.35.weights_in) | copy-start | bytes 1179652
  6.6 0.7 %copy-start.2 = (f32[2,1280]{1,0:T(2,128)S(1)}, f32[2,1280]{1,0:T(2,128)}, u32[]{:S(2)}) copy-start(f32[2,1280]{1,0:T(2,128)} %get-tuple-element.36.vectors_in) | copy-start | bytes 30724
  8.1 8.2 %collective-permute-start.6 = (bf16[2,144,128]{2,1,0:T(8,128)(2,1)S(1)}, bf16[2,144,128]{2,1,0:T(8,128)(2,1)S(1)}, u32[]{:S(2)}, u32[]{:S(2)}) collective-permute-start(bf16[2,144,128]{2,1,0:T(8,128)(2,1)S(1)} %get-tuple-element.40.refs_0_.pair.pair_ref), channel_id=1, source_target_pairs={{0,4},{1,5},{2,6},{3,7},{4,0},{5,1},{6,2},{7,3},{8,12},{9,13},{10,... | collective-permute-start | bytes 221192 | tf_op jit(solution)/shard_map/ppermute | solution.py:319
  11.2 9.4 %collective-permute-start.5 = (bf16[2,144,128]{2,1,0:T(8,128)(2,1)S(1)}, bf16[2,144,128]{2,1,0:T(8,128)(2,1)S(1)}, u32[]{:S(2)}, u32[]{:S(2)}) collective-permute-start(bf16[2,144,128]{2,1,0:T(8,128)(2,1)S(1)} %get-tuple-element.40.refs_0_.pair.pair_ref), channel_id=1, source_target_pairs={{0,6},{1,7},{2,4},{3,5},{4,2},{5,3},{6,0},{7,1},{8,14},{9,15},{10,... | collective-permute-start | bytes 221192 | tf_op jit(solution)/shard_map/ppermute | solution.py:319
  12.6 8.0 %collective-permute-start.4 = (bf16[2,144,128]{2,1,0:T(8,128)(2,1)S(1)}, bf16[2,144,128]{2,1,0:T(8,128)(2,1)S(1)}, u32[]{:S(2)}, u32[]{:S(2)}) collective-permute-start(bf16[2,144,128]{2,1,0:T(8,128)(2,1)S(1)} %get-tuple-element.40.refs_0_.pair.pair_ref), channel_id=1, source_target_pairs={{0,2},{1,3},{2,0},{3,1},{4,6},{5,7},{6,4},{7,5},{8,10},{9,11},{10,... | collective-permute-start | bytes 221192 | tf_op jit(solution)/shard_map/ppermute | solution.py:319
  12.8 14.4 %collective-permute-start.3 = (bf16[2,128,128]{2,1,0:T(8,128)(2,1)S(1)}, bf16[2,128,128]{2,1,0:T(8,128)(2,1)S(1)}, u32[]{:S(2)}, u32[]{:S(2)}) collective-permute-start(bf16[2,128,128]{2,1,0:T(8,128)(2,1)S(1)} %get-tuple-element.41.refs_0_), channel_id=1, source_target_pairs={{0,2},{1,3},{2,0},{3,1},{4,6},{5,7},{6,4},{7,5},{8,10},{9,11},{10,... | collective-permute-start | bytes 196616 | tf_op jit(solution)/shard_map/ppermute | solution.py:319
  14.6 12.6 %collective-permute-start.2 = (bf16[2,128,128]{2,1,0:T(8,128)(2,1)S(1)}, bf16[2,128,128]{2,1,0:T(8,128)(2,1)S(1)}, u32[]{:S(2)}, u32[]{:S(2)}) collective-permute-start(bf16[2,128,128]{2,1,0:T(8,128)(2,1)S(1)} %get-tuple-element.41.refs_0_), channel_id=1, source_target_pairs={{0,4},{1,5},{2,6},{3,7},{4,0},{5,1},{6,2},{7,3},{8,12},{9,13},{10,... | collective-permute-start | bytes 196616 | tf_op jit(solution)/shard_map/ppermute | solution.py:319
  16.3 11.0 %collective-permute-start.1 = (bf16[2,128,128]{2,1,0:T(8,128)(2,1)S(1)}, bf16[2,128,128]{2,1,0:T(8,128)(2,1)S(1)}, u32[]{:S(2)}, u32[]{:S(2)}) collective-permute-start(bf16[2,128,128]{2,1,0:T(8,128)(2,1)S(1)} %get-tuple-element.41.refs_0_), channel_id=1, source_target_pairs={{0,6},{1,7},{2,4},{3,5},{4,2},{5,3},{6,0},{7,1},{8,14},{9,15},{10,... | collective-permute-start | bytes 196616 | tf_op jit(solution)/shard_map/ppermute | solution.py:319
  31.7 7.2 %collective-permute-start.7 = (bf16[128,768]{1,0:T(8,128)(2,1)S(1)}, bf16[128,768]{1,0:T(8,128)(2,1)S(1)}, u32[]{:S(2)}, u32[]{:S(2)}) collective-permute-start(bf16[128,768]{1,0:T(8,128)(2,1)S(1)} %get-tuple-element.60), channel_id=1, source_target_pairs={{0,16},{8,24},{16,0},{24,8},{1,17},{9,25},{17,1},{25,9},{2,18},{10... | collective-permute-start | bytes 589832 | tf_op jit(solution)/shard_map/ppermute | solution.py:319
  36.6 5.0 %collective-permute-start.9 = (bf16[128,512]{1,0:T(8,128)(2,1)S(1)}, bf16[128,512]{1,0:T(8,128)(2,1)S(1)}, u32[]{:S(2)}, u32[]{:S(2)}) collective-permute-start(bf16[128,512]{1,0:T(8,128)(2,1)S(1)} %get-tuple-element.62), channel_id=1, source_target_pairs={{0,16},{8,24},{16,0},{24,8},{1,17},{9,25},{17,1},{25,9},{2,18},{10... | collective-permute-start | bytes 393224 | tf_op jit(solution)/shard_map/ppermute | solution.py:319
  39.0 2.7 %collective-permute-start.8 = (bf16[128,1024]{1,0:T(8,128)(2,1)S(1)}, bf16[128,1024]{1,0:T(8,128)(2,1)S(1)}, u32[]{:S(2)}, u32[]{:S(2)}) collective-permute-start(bf16[128,1024]{1,0:T(8,128)(2,1)S(1)} %pad_maximum_fusion.rest), channel_id=1, source_target_pairs={{0,8},{8,0},{16,24},{24,16},{1,9},{9,1},{17,25},{25,17},{2,10},{10... | collective-permute-start | bytes 786440 | tf_op jit(solution)/shard_map/ppermute | solution.py:319
  41.6 1.7 %collective-permute-start.10 = (bf16[128,512]{1,0:T(8,128)(2,1)S(1)}, bf16[128,512]{1,0:T(8,128)(2,1)S(1)}, u32[]{:S(2)}, u32[]{:S(2)}) collective-permute-start(bf16[128,512]{1,0:T(8,128)(2,1)S(1)} %add_convert_fusion.1.left), channel_id=1, source_target_pairs={{0,8},{8,0},{16,24},{24,16},{1,9},{9,1},{17,25},{25,17},{2,10},{10... | collective-permute-start | bytes 393224 | tf_op jit(solution)/shard_map/ppermute | solution.py:319
  41.8 4.5 %collective-permute-start.11 = (bf16[128,256]{1,0:T(8,128)(2,1)S(1)}, bf16[128,256]{1,0:T(8,128)(2,1)S(1)}, u32[]{:S(2)}, u32[]{:S(2)}) collective-permute-start(bf16[128,256]{1,0:T(8,128)(2,1)S(1)} %add_convert_fusion.2.right), channel_id=1, source_target_pairs={{0,16},{8,24},{16,0},{24,8},{1,17},{9,25},{17,1},{25,9},{2,18},{10... | collective-permute-start | bytes 196616 | tf_op jit(solution)/shard_map/ppermute | solution.py:319

commit v18 on v15

--- a/solution.py
+++ b/solution.py
@@ -373,14 +373,14 @@
     return [row[:, first:last] for first, last in zip([0] + ends, ends)]
 
 
-def add_grads(rest, rest_near, left, left_near, right, right_far, proj_ref, out_ref):
+def add_grads(second, second_far, left, left_far, right, right_far, proj_ref, out_ref):
     width = proj_ref.shape[2]
     c = out_ref.shape[2]
     half = (width - c) // 2
-    total = rest[:, : width + c].astype(F32) + rest_near[:, : width + c].astype(F32)
+    total = second[...].astype(F32) + second_far[...].astype(F32)
     proj_ref[1] = total[:, :width]
     out_ref[1] = total[:, width:]
-    total = left[...].astype(F32) + left_near[...].astype(F32)
+    total = left[...].astype(F32) + left_far[...].astype(F32)
     proj_ref[0, :, :half] = total[:, :half]
     proj_ref[0, :, 2 * half :] = total[:, half : half + c]
     out_ref[0] = total[:, half + c :]
@@ -499,7 +499,7 @@
         name="backward_second",
     )(states[0], *cots, *weights, *held)
     far = groups // 2
-    others_1 = exchange(grads_1, "dp", groups, far)
+    near_1 = near_rounds(grads_1, groups)
 
     d_left, d_product_t, grads_left = pl.pallas_call(
         functools.partial(backward_left, n),
@@ -515,7 +515,10 @@
         cost_estimate=cost(24),
         name="backward_left",
     )(up_1, *weights, *held)
-    others_left = exchange(grads_left, "dp", groups, far)
+    near_left = near_rounds(grads_left, groups)
+    second = add_narrow(*near_1)
+    second, d_product_t = lax.optimization_barrier((second, d_product_t))
+    second_far = exchange(second, "dp", groups, far)
 
     d_right, grads_right = pl.pallas_call(
         functools.partial(backward_right, n),
@@ -540,12 +543,11 @@
         name="own_rows",
     )(states[0], up_1, d_left, d_right, *weights, held[3], held[4])
 
-    rest, rest_near = near_rounds(
-        jnp.concatenate([add_narrow(grads_1, others_1), grads_right], axis=1), groups
-    )
-    right = add_narrow(rest[:, width + c :], rest_near[:, width + c :])
+    left = add_narrow(*near_left)
+    left_far = exchange(left, "dp", groups, far)
+    grads_right, second_far = lax.optimization_barrier((grads_right, second_far))
+    right = add_narrow(*near_rounds(grads_right, groups))
     right_far = exchange(right, "dp", groups, far)
-    ends_left = near_rounds(add_narrow(grads_left, others_left), groups)
 
     proj_total, out_total = pl.pallas_call(
         add_grads,
@@ -557,7 +559,7 @@
         out_specs=(vmem, vmem),
         compiler_params=params,
         name="add_grads",
-    )(rest, rest_near, *ends_left, right, right_far)
+    )(second, second_far, left, left_far, right, right_far)
     return pair_grad.reshape(pair_repr.shape), proj_total, out_total
 
 

time: 45.8 us -> 49.5 us (1.081)
  the two profiles are of different devices: /device:TPU:20 before, /device:TPU:0 now
where the time goes in v18:
time: 49.5 us; the launch traced here: 49.1 us
  Pallas kernels  19.5 us (39%)
  starting transfers between devices  16.4 us (33%)
  waiting for transfers between devices  10.6 us (21%)
  local copies, waits for them, and re-layouts  1.7 us (3%)
  between operations  0.75 us (2%)
    ppermute x13, starting transfers between devices, exchange(): return lax.ppermute(value, axis, [(d, d ^ step) for d in range(size)])  16.4 us
    ppermute x13, waiting for transfers between devices, exchange(): return lax.ppermute(value, axis, [(d, d ^ step) for d in range(size)])  10.6 us
    pallas_call x1, Pallas kernels, crop_shards(): pl.pallas_call(functools.partial(forward, n, jumps), out_shape=kept, in_s...  6.62 us
    pallas_call x1, Pallas kernels, crop_shards(): pl.pallas_call(functools.partial(backward_second, n, jumps), out_shape=(j...  4.73 us
    pallas_call x1, Pallas kernels, crop_shards(): pl.pallas_call(functools.partial(backward_left, n), out_shape=(jax.ShapeD...  2.6 us
    pallas_call x1, Pallas kernels, crop_shards(): pl.pallas_call(prepare, out_shape=(jax.ShapeDtypeStruct((2 * cells + TAIL...  1.88 us
    pallas_call x1, Pallas kernels, crop_shards(): pl.pallas_call(functools.partial(backward_right, n), out_shape=(jax.Shape...  1.72 us
    unnamed x6, local copies, waits for them, and re-layouts  1.7 us
  transfers between devices with their start and end apart: 13, of which 6 were waited for; matrix products, arithmetic and copies ran while one was open for 0% of the time, Pallas kernels for 24%

profile of v18, /device:TPU:0, one launch (start us, length us, event | category | flops | bytes accessed | tf_op | source)
XLA Modules:
  0.0 49.1 jit_solution(11783784334896398521)
XLA Ops:
  0.6 1.9 %prepare.1 = (bf16[272,128]{1,0:T(8,128)(2,1)}, bf16[2,128,768]{2,1,0:T(8,128)(2,1)}, f32[2,1280]{1,0:T(2,128)}) custom-call(s32[1]{0:T(128)} %bitcast.index_ref, s32[4,32]{1,0:T(4,128)} %bitcast.8, bf16[128,128]{1,0:T(8,128)(2,1)} %bitcast.6, bf16[128,128]{1,0:T(8,128)(2,1)} %bitcast.7, bf16[2,128,640]{2,1,0:T(8,128)(2,1)} %w.1, ...), custom_call_target="tpu_custom_call" | custom-call | tf_op jit(solution)/shard_map/prepare/pallas_call | solution.py:426
  2.5 0.0 copy-start
  2.5 3.0 %collective-permute-start = (bf16[272,128]{1,0:T(8,128)(2,1)}, bf16[272,128]{1,0:T(8,128)(2,1)S(1)}, u32[]{:S(2)}, u32[]{:S(2)}) collective-permute-start(bf16[272,128]{1,0:T(8,128)(2,1)} %get-tuple-element.36.near_ref), channel_id=1, source_target_pairs={{0,1},{1,0},{2,3},{3,2},{4,5},{5,4},{6,7},{7,6},{8,9},{9,8},{10,11... | collective-permute-start | bytes 208904 | tf_op jit(solution)/shard_map/ppermute | solution.py:317
  5.6 0.0 copy-start.1
  5.6 1.0 %copy-done.1 = bf16[2,128,768]{2,1,0:T(8,128)(2,1)S(1)} copy-done((bf16[2,128,768]{2,1,0:T(8,128)(2,1)S(1)}, bf16[2,128,768]{2,1,0:T(8,128)(2,1)}, u32[]{:S(2)}) %copy-start.1) | copy-done | bytes 393240
  6.6 0.0 copy-start.2
  6.6 0.7 %copy-done.2 = f32[2,1280]{1,0:T(2,128)S(1)} copy-done((f32[2,1280]{1,0:T(2,128)S(1)}, f32[2,1280]{1,0:T(2,128)}, u32[]{:S(2)}) %copy-start.2) | copy-done | bytes 10264
  7.3 0.8 %collective-permute-done.far_ref = bf16[272,128]{1,0:T(8,128)(2,1)S(1)} collective-permute-done((bf16[272,128]{1,0:T(8,128)(2,1)}, bf16[272,128]{1,0:T(8,128)(2,1)S(1)}, u32[]{:S(2)}, u32[]{:S(2)}) %collective-permute-start) | collective-permute-done | bytes 69664 | tf_op jit(solution)/shard_map/ppermute | solution.py:317
  8.1 0.0 copy-done
  8.1 3.2 %collective-permute-start.6 = (bf16[2,144,128]{2,1,0:T(8,128)(2,1)S(1)}, bf16[2,144,128]{2,1,0:T(8,128)(2,1)S(1)}, u32[]{:S(2)}, u32[]{:S(2)}) collective-permute-start(bf16[2,144,128]{2,1,0:T(8,128)(2,1)S(1)} %get-tuple-element.42.refs_0_.pair.pair_ref), channel_id=1, source_target_pairs={{0,4},{1,5},{2,6},{3,7},{4,0},{5,1},{6,2},{7,3},{8,12},{9,13},{10,... | collective-permute-start | bytes 221192 | tf_op jit(solution)/shard_map/ppermute | solution.py:317
  11.2 1.3 %collective-permute-start.5 = (bf16[2,144,128]{2,1,0:T(8,128)(2,1)S(1)}, bf16[2,144,128]{2,1,0:T(8,128)(2,1)S(1)}, u32[]{:S(2)}, u32[]{:S(2)}) collective-permute-start(bf16[2,144,128]{2,1,0:T(8,128)(2,1)S(1)} %get-tuple-element.42.refs_0_.pair.pair_ref), channel_id=1, source_target_pairs={{0,6},{1,7},{2,4},{3,5},{4,2},{5,3},{6,0},{7,1},{8,14},{9,15},{10,... | collective-permute-start | bytes 221192 | tf_op jit(solution)/shard_map/ppermute | solution.py:317
  12.6 0.2 collective-permute-start.4
  12.8 2.8 %collective-permute-start.3 = (bf16[2,128,128]{2,1,0:T(8,128)(2,1)S(1)}, bf16[2,128,128]{2,1,0:T(8,128)(2,1)S(1)}, u32[]{:S(2)}, u32[]{:S(2)}) collective-permute-start(bf16[2,128,128]{2,1,0:T(8,128)(2,1)S(1)} %get-tuple-element.43.refs_0_), channel_id=1, source_target_pairs={{0,4},{1,5},{2,6},{3,7},{4,0},{5,1},{6,2},{7,3},{8,12},{9,13},{10,... | collective-permute-start | bytes 196616 | tf_op jit(solution)/shard_map/ppermute | solution.py:317
  15.6 1.3 %collective-permute-start.2 = (bf16[2,128,128]{2,1,0:T(8,128)(2,1)S(1)}, bf16[2,128,128]{2,1,0:T(8,128)(2,1)S(1)}, u32[]{:S(2)}, u32[]{:S(2)}) collective-permute-start(bf16[2,128,128]{2,1,0:T(8,128)(2,1)S(1)} %get-tuple-element.43.refs_0_), channel_id=1, source_target_pairs={{0,6},{1,7},{2,4},{3,5},{4,2},{5,3},{6,0},{7,1},{8,14},{9,15},{10,... | collective-permute-start | bytes 196616 | tf_op jit(solution)/shard_map/ppermute | solution.py:317
  17.0 0.0 collective-permute-done.6.refs_3_
  17.0 1.5 %collective-permute-start.1 = (bf16[2,128,128]{2,1,0:T(8,128)(2,1)S(1)}, bf16[2,128,128]{2,1,0:T(8,128)(2,1)S(1)}, u32[]{:S(2)}, u32[]{:S(2)}) collective-permute-start(bf16[2,128,128]{2,1,0:T(8,128)(2,1)S(1)} %get-tuple-element.43.refs_0_), channel_id=1, source_target_pairs={{0,2},{1,3},{2,0},{3,1},{4,6},{5,7},{6,4},{7,5},{8,10},{9,11},{10,... | collective-permute-start | bytes 196616 | tf_op jit(solution)/shard_map/ppermute | solution.py:317
  18.5 0.0 collective-permute-done.5.refs_2_
  18.5 0.7 %collective-permute-done.4.refs_1_ = bf16[2,144,128]{2,1,0:T(8,128)(2,1)S(1)} collective-permute-done((bf16[2,144,128]{2,1,0:T(8,128)(2,1)S(1)}, bf16[2,144,128]{2,1,0:T(8,128)(2,1)S(1)}, u32[]{:S(2)}, u32[]{:S(2)}) %collective-permute-start.4) | collective-permute-done | bytes 73760 | tf_op jit(solution)/shard_map/ppermute | solution.py:317
  19.2 6.6 %forward.1 = (f32[2,4,1032,128]{3,2,1,0:T(8,128)S(1)}, f32[2,2,1032,128]{3,2,1,0:T(8,128)S(1)}, f32[2,1032,128]{2,1,0:T(8,128)S(1)}, f32[2,1032,128]{2,1,0:T(8,1...) custom-call(bf16[2,144,128]{2,1,0:T(8,128)(2,1)S(1)} %get-tuple-elem, ...), custom_call_target="tpu_custom_call" | custom-call | flops 335544320 | bytes 33554432 | tf_op jit(solution)/shard_map/forward/pallas_call | solution.py:474
  25.9 0.0 collective-permute-done.3.refs_3_
  25.9 0.0 collective-permute-done.2.refs_2_
  25.9 0.0 collective-permute-done.1.refs_1_
  25.9 4.7 %backward_second.1 = (f32[1024,128]{1,0:T(8,128)S(1)}, bf16[128,768]{1,0:T(8,128)(2,1)S(1)}) custom-call(bf16[2,144,128]{2,1,0:T(8,128)(2,1)S(1)} %get-tuple-element.42.refs_0_.pair.pair_ref, bf16[2,128,128]{2,1,0:T(8,128)(2,1)S(1)} %get-tuple-element.43.refs_0_, bf16[2,128,128]{2,1,0:T(8,128)(2,1)S(1)} %collective-permute-done.1.refs_1_, ...), custom_call_target="tpu_custom_call" | custom-call | flops 335544320 | bytes 25165824 | tf_op jit(solution)/shard_map/backward_second/pallas_call | solution.py:486
  30.6 0.1 collective-permute-start.7
  30.7 2.6 %backward_left.1 = (bf16[1024,384]{1,0:T(8,128)(2,1)S(1)}, f32[1032,128]{1,0:T(8,128)S(1)}, bf16[128,512]{1,0:T(8,128)(2,1)S(1)}) custom-call(f32[1024,128]{1,0:T(8,128)S(1)} %get-tuple-element.56.up_in_ref.up_ref, bf16[2,128,768]{2,1,0:T(8,128)(2,1)S(1)} %get-tuple-element.44.refs_4_.weights, f32[2,1280]{1,0:T(2,128)S(1)} %get-tuple-element.45.refs_5_.vectors, ...), custom_call_target="tpu_custom_call" | custom-call | flops 335544320 | bytes 12582912 | tf_op jit(solution)/shard_map/backward_left/pallas_call | solution.py:504
  33.3 0.0 collective-permute-done.7
  33.3 0.1 add_convert_fusion.second
  33.4 0.8 %collective-permute-start.8 = (bf16[128,768]{1,0:T(8,128)(2,1)S(1)}, bf16[128,768]{1,0:T(8,128)(2,1)S(1)}, u32[]{:S(2)}, u32[]{:S(2)}) collective-permute-start(bf16[128,768]{1,0:T(8,128)(2,1)S(1)} %add_convert_fusion.second), channel_id=1, source_target_pairs={{0,16},{8,24},{16,0},{24,8},{1,17},{9,25},{17,1},{25,9},{2,18},{10... | collective-permute-start | bytes 589832 | tf_op jit(solution)/shard_map/ppermute | solution.py:317
  34.2 0.2 collective-permute-start.9
  34.4 1.7 %backward_right.1 = (bf16[1024,256]{1,0:T(8,128)(2,1)S(1)}, bf16[128,256]{1,0:T(8,128)(2,1)S(1)}) custom-call(f32[1032,128]{1,0:T(8,128)S(1)} %get-tuple-element.60.d_product_t_ref, f32[2,4,1032,128]{3,2,1,0:T(8,128)S(1)} %get-tuple-element.46.refs_6_.refs_0_, f32[2,2,1032,128]{3,2,1,0:T(8,128)S(1)} %get-tuple-element.47.refs_7_.refs_1_, ...), custom_call_target="tpu_custom_call" | custom-call | flops 335544320 | bytes 12582912 | tf_op jit(solution)/shard_map/backward_right/pallas_call | solution.py:523
  36.2 4.6 %collective-permute-done.8.second_far = bf16[128,768]{1,0:T(8,128)(2,1)S(1)} collective-permute-done((bf16[128,768]{1,0:T(8,128)(2,1)S(1)}, bf16[128,768]{1,0:T(8,128)(2,1)S(1)}, u32[]{:S(2)}, u32[]{:S(2)}) %collective-permute-start.8) | collective-permute-done | bytes 196640 | tf_op jit(solution)/shard_map/ppermute | solution.py:317
  40.7 0.0 collective-permute-start.11
  40.7 0.0 collective-permute-done.9
  40.8 0.8 %collective-permute-start.10 = (bf16[128,512]{1,0:T(8,128)(2,1)S(1)}, bf16[128,512]{1,0:T(8,128)(2,1)S(1)}, u32[]{:S(2)}, u32[]{:S(2)}) collective-permute-start(bf16[128,512]{1,0:T(8,128)(2,1)S(1)} %add_convert_fusion.1.left), channel_id=1, source_target_pairs={{0,16},{8,24},{16,0},{24,8},{1,17},{9,25},{17,1},{25,9},{2,18},{10... | collective-permute-start | bytes 393224 | tf_op jit(solution)/shard_map/ppermute | solution.py:317
  41.6 0.4 collective-permute-done.11
  42.0 0.9 %collective-permute-start.12 = (bf16[128,256]{1,0:T(8,128)(2,1)S(1)}, bf16[128,256]{1,0:T(8,128)(2,1)S(1)}, u32[]{:S(2)}, u32[]{:S(2)}) collective-permute-start(bf16[128,256]{1,0:T(8,128)(2,1)S(1)} %add_convert_fusion.2.right), channel_id=1, source_target_pairs={{0,16},{8,24},{16,0},{24,8},{1,17},{9,25},{17,1},{25,9},{2,18},{10... | collective-permute-start | bytes 196616 | tf_op jit(solution)/shard_map/ppermute | solution.py:317
  43.0 1.0 %own_rows.1 = bf16[128,128]{1,0:T(8,128)(2,1)} custom-call(bf16[2,144,128]{2,1,0:T(8,128)(2,1)S(1)} %get-tuple-element.42.refs_0_.pair.pair_ref, f32[1024,128]{1,0:T(8,128)S(1)} %get-tuple-element.56.up_in_ref.up_ref, bf16[1024,384]{1,0:T(8,128)(2,1)S(1)} %get-tuple-element.57.d_left_ref, bf16[1024,256]{1,0:T(8,128)(2,1)S(1)} %get-tuple-element.61.d_right_ref, ...), custom_call_target="tpu_custom_call" | custom-call | flops 335544320 | bytes 4194304 | tf_op jit(solution)/shard_map/own_rows/pallas_call | solution.py:536
  44.0 3.2 %collective-permute-done.10.left_far = bf16[128,512]{1,0:T(8,128)(2,1)S(1)} collective-permute-done((bf16[128,512]{1,0:T(8,128)(2,1)S(1)}, bf16[128,512]{1,0:T(8,128)(2,1)S(1)}, u32[]{:S(2)}, u32[]{:S(2)}) %collective-permute-start.10) | collective-permute-done | bytes 131104 | tf_op jit(solution)/shard_map/ppermute | solution.py:317
  47.1 1.0 %collective-permute-done.12.right_far = bf16[128,256]{1,0:T(8,128)(2,1)S(1)} collective-permute-done((bf16[128,256]{1,0:T(8,128)(2,1)S(1)}, bf16[128,256]{1,0:T(8,128)(2,1)S(1)}, u32[]{:S(2)}, u32[]{:S(2)}) %collective-permute-start.12) | collective-permute-done | bytes 65568 | tf_op jit(solution)/shard_map/ppermute | solution.py:317
  48.2 0.9 %add_grads.1 = (f32[2,128,640]{2,1,0:T(8,128)}, f32[2,128,128]{2,1,0:T(8,128)}) custom-call(bf16[128,768]{1,0:T(8,128)(2,1)S(1)} %add_convert_fusion.second, bf16[128,768]{1,0:T(8,128)(2,1)S(1)} %collective-permute-done.8.second_far, bf16[128,512]{1,0:T(8,128)(2,1)S(1)} %add_convert_fusion.1.left, bf16[128,512]{1,0:T(8,128)(2,1)S(1)} %collective-permute-done.10.left_far, ...), custom_call_target="tpu_custom_call" | custom-call | tf_op jit(solution)/shard_map/add_grads/pallas_call | solution.py:552
  (4 shorter events, 0.1 us)
Async XLA Ops:
  2.5 5.5 %copy-start = (bf16[272,128]{1,0:T(8,128)(2,1)S(1)}, bf16[272,128]{1,0:T(8,128)(2,1)}, u32[]{:S(2)}) copy-start(bf16[272,128]{1,0:T(8,128)(2,1)} %get-tuple-element.36.near_ref) | copy-start | bytes 208900
  2.5 5.5 %collective-permute-start = (bf16[272,128]{1,0:T(8,128)(2,1)}, bf16[272,128]{1,0:T(8,128)(2,1)S(1)}, u32[]{:S(2)}, u32[]{:S(2)}) collective-permute-start(bf16[272,128]{1,0:T(8,128)(2,1)} %get-tuple-element.36.near_ref), channel_id=1, source_target_pairs={{0,1},{1,0},{2,3},{3,2},{4,5},{5,4},{6,7},{7,6},{8,9},{9,8},{10,11... | collective-permute-start | bytes 208904 | tf_op jit(solution)/shard_map/ppermute | solution.py:317
  5.6 1.0 %copy-start.1 = (bf16[2,128,768]{2,1,0:T(8,128)(2,1)S(1)}, bf16[2,128,768]{2,1,0:T(8,128)(2,1)}, u32[]{:S(2)}) copy-start(bf16[2,128,768]{2,1,0:T(8,128)(2,1)} %get-tuple-element.37.weights_in) | copy-start | bytes 1179652
  6.6 0.7 %copy-start.2 = (f32[2,1280]{1,0:T(2,128)S(1)}, f32[2,1280]{1,0:T(2,128)}, u32[]{:S(2)}) copy-start(f32[2,1280]{1,0:T(2,128)} %get-tuple-element.38.vectors_in) | copy-start | bytes 30724
  8.1 8.9 %collective-permute-start.6 = (bf16[2,144,128]{2,1,0:T(8,128)(2,1)S(1)}, bf16[2,144,128]{2,1,0:T(8,128)(2,1)S(1)}, u32[]{:S(2)}, u32[]{:S(2)}) collective-permute-start(bf16[2,144,128]{2,1,0:T(8,128)(2,1)S(1)} %get-tuple-element.42.refs_0_.pair.pair_ref), channel_id=1, source_target_pairs={{0,4},{1,5},{2,6},{3,7},{4,0},{5,1},{6,2},{7,3},{8,12},{9,13},{10,... | collective-permute-start | bytes 221192 | tf_op jit(solution)/shard_map/ppermute | solution.py:317
  11.2 7.3 %collective-permute-start.5 = (bf16[2,144,128]{2,1,0:T(8,128)(2,1)S(1)}, bf16[2,144,128]{2,1,0:T(8,128)(2,1)S(1)}, u32[]{:S(2)}, u32[]{:S(2)}) collective-permute-start(bf16[2,144,128]{2,1,0:T(8,128)(2,1)S(1)} %get-tuple-element.42.refs_0_.pair.pair_ref), channel_id=1, source_target_pairs={{0,6},{1,7},{2,4},{3,5},{4,2},{5,3},{6,0},{7,1},{8,14},{9,15},{10,... | collective-permute-start | bytes 221192 | tf_op jit(solution)/shard_map/ppermute | solution.py:317
  12.6 6.6 %collective-permute-start.4 = (bf16[2,144,128]{2,1,0:T(8,128)(2,1)S(1)}, bf16[2,144,128]{2,1,0:T(8,128)(2,1)S(1)}, u32[]{:S(2)}, u32[]{:S(2)}) collective-permute-start(bf16[2,144,128]{2,1,0:T(8,128)(2,1)S(1)} %get-tuple-element.42.refs_0_.pair.pair_ref), channel_id=1, source_target_pairs={{0,2},{1,3},{2,0},{3,1},{4,6},{5,7},{6,4},{7,5},{8,10},{9,11},{10,... | collective-permute-start | bytes 221192 | tf_op jit(solution)/shard_map/ppermute | solution.py:317
  12.8 13.0 %collective-permute-start.3 = (bf16[2,128,128]{2,1,0:T(8,128)(2,1)S(1)}, bf16[2,128,128]{2,1,0:T(8,128)(2,1)S(1)}, u32[]{:S(2)}, u32[]{:S(2)}) collective-permute-start(bf16[2,128,128]{2,1,0:T(8,128)(2,1)S(1)} %get-tuple-element.43.refs_0_), channel_id=1, source_target_pairs={{0,4},{1,5},{2,6},{3,7},{4,0},{5,1},{6,2},{7,3},{8,12},{9,13},{10,... | collective-permute-start | bytes 196616 | tf_op jit(solution)/shard_map/ppermute | solution.py:317
  15.6 10.2 %collective-permute-start.2 = (bf16[2,128,128]{2,1,0:T(8,128)(2,1)S(1)}, bf16[2,128,128]{2,1,0:T(8,128)(2,1)S(1)}, u32[]{:S(2)}, u32[]{:S(2)}) collective-permute-start(bf16[2,128,128]{2,1,0:T(8,128)(2,1)S(1)} %get-tuple-element.43.refs_0_), channel_id=1, source_target_pairs={{0,6},{1,7},{2,4},{3,5},{4,2},{5,3},{6,0},{7,1},{8,14},{9,15},{10,... | collective-permute-start | bytes 196616 | tf_op jit(solution)/shard_map/ppermute | solution.py:317
  17.0 8.9 %collective-permute-start.1 = (bf16[2,128,128]{2,1,0:T(8,128)(2,1)S(1)}, bf16[2,128,128]{2,1,0:T(8,128)(2,1)S(1)}, u32[]{:S(2)}, u32[]{:S(2)}) collective-permute-start(bf16[2,128,128]{2,1,0:T(8,128)(2,1)S(1)} %get-tuple-element.43.refs_0_), channel_id=1, source_target_pairs={{0,2},{1,3},{2,0},{3,1},{4,6},{5,7},{6,4},{7,5},{8,10},{9,11},{10,... | collective-permute-start | bytes 196616 | tf_op jit(solution)/shard_map/ppermute | solution.py:317
  30.6 2.7 %collective-permute-start.7 = (bf16[128,768]{1,0:T(8,128)(2,1)S(1)}, bf16[128,768]{1,0:T(8,128)(2,1)S(1)}, u32[]{:S(2)}, u32[]{:S(2)}) collective-permute-start(bf16[128,768]{1,0:T(8,128)(2,1)S(1)} %get-tuple-element.58), channel_id=1, source_target_pairs={{0,8},{8,0},{16,24},{24,16},{1,9},{9,1},{17,25},{25,17},{2,10},{10... | collective-permute-start | bytes 589832 | tf_op jit(solution)/shard_map/ppermute | solution.py:317
  33.4 7.4 %collective-permute-start.8 = (bf16[128,768]{1,0:T(8,128)(2,1)S(1)}, bf16[128,768]{1,0:T(8,128)(2,1)S(1)}, u32[]{:S(2)}, u32[]{:S(2)}) collective-permute-start(bf16[128,768]{1,0:T(8,128)(2,1)S(1)} %add_convert_fusion.second), channel_id=1, source_target_pairs={{0,16},{8,24},{16,0},{24,8},{1,17},{9,25},{17,1},{25,9},{2,18},{10... | collective-permute-start | bytes 589832 | tf_op jit(solution)/shard_map/ppermute | solution.py:317
  34.2 6.5 %collective-permute-start.9 = (bf16[128,512]{1,0:T(8,128)(2,1)S(1)}, bf16[128,512]{1,0:T(8,128)(2,1)S(1)}, u32[]{:S(2)}, u32[]{:S(2)}) collective-permute-start(bf16[128,512]{1,0:T(8,128)(2,1)S(1)} %get-tuple-element.65), channel_id=1, source_target_pairs={{0,8},{8,0},{16,24},{24,16},{1,9},{9,1},{17,25},{25,17},{2,10},{10... | collective-permute-start | bytes 393224 | tf_op jit(solution)/shard_map/ppermute | solution.py:317
  40.7 1.3 %collective-permute-start.11 = (bf16[128,256]{1,0:T(8,128)(2,1)S(1)}, bf16[128,256]{1,0:T(8,128)(2,1)S(1)}, u32[]{:S(2)}, u32[]{:S(2)}) collective-permute-start(bf16[128,256]{1,0:T(8,128)(2,1)S(1)} %get-tuple-element.66), channel_id=1, source_target_pairs={{0,8},{8,0},{16,24},{24,16},{1,9},{9,1},{17,25},{25,17},{2,10},{10... | collective-permute-start | bytes 196616 | tf_op jit(solution)/shard_map/ppermute | solution.py:317
  40.8 6.4 %collective-permute-start.10 = (bf16[128,512]{1,0:T(8,128)(2,1)S(1)}, bf16[128,512]{1,0:T(8,128)(2,1)S(1)}, u32[]{:S(2)}, u32[]{:S(2)}) collective-permute-start(bf16[128,512]{1,0:T(8,128)(2,1)S(1)} %add_convert_fusion.1.left), channel_id=1, source_target_pairs={{0,16},{8,24},{16,0},{24,8},{1,17},{9,25},{17,1},{25,9},{2,18},{10... | collective-permute-start | bytes 393224 | tf_op jit(solution)/shard_map/ppermute | solution.py:317
  42.0 6.1 %collective-permute-start.12 = (bf16[128,256]{1,0:T(8,128)(2,1)S(1)}, bf16[128,256]{1,0:T(8,128)(2,1)S(1)}, u32[]{:S(2)}, u32[]{:S(2)}) collective-permute-start(bf16[128,256]{1,0:T(8,128)(2,1)S(1)} %add_convert_fusion.2.right), channel_id=1, source_target_pairs={{0,16},{8,24},{16,0},{24,8},{1,17},{9,25},{17,1},{25,9},{2,18},{10... | collective-permute-start | bytes 196616 | tf_op jit(solution)/shard_map/ppermute | solution.py:317

commit v19 on v15

--- a/solution.py
+++ b/solution.py
@@ -75,14 +75,17 @@
     return d_branch, d_gate, norm_vjp(p_hat, p_rstd, d_mixed)
 
 
-def contract(n, first, x, y):
+def contract(n, first, x, y, swapped=False):
     lanes = y.shape[1]
     tiles = (n // 8, 8, lanes)
+
+    def row(a, e):
+        return e * n + first + a if swapped else (first + a) * n + e
 
     def step(e, totals):
         block = y[pl.ds(pl.multiple_of(e * n, n), n), :].reshape(tiles)
         return tuple(
-            totals[a] + x[pl.ds((first + a) * n + e, 8, stride=0), :][None] * block
+            totals[a] + x[pl.ds(row(a, e), 8, stride=0), :][None] * block
             for a in range(BLOCK_ROWS)
         )
 
@@ -119,7 +122,7 @@
     (weights, vectors), refs = refs[:2], refs[2:]
     (edges_s, slopes_s, gate_s, hat_s, rstd_s) = refs[:5]
     (p_hat_s, p_rstd_s, branch_s, normed_s, mixed_s) = refs[5:KEPT]
-    (next_s,) = refs[KEPT:]
+    next_s, right_t_s = refs[KEPT:]
     c = weights.shape[1]
     width = weights.shape[2] - c
     rows = n // (2 * len(jumps))
@@ -132,10 +135,8 @@
             next_s[block(place_of(own, jump, side), rows, n), :] = pair[side, :cells, :]
     steps = n // STEP_ROWS
 
-    @pl.loop(0, 2)
-    def _(u):
-        row = jnp.where(u == 0, vectors[0:1, :], vectors[1:2, :])
-        bias, gains, shifts, bias_out = vector_parts(row, c, width)
+    for u in range(2):
+        bias, gains, shifts, bias_out = vector_parts(vectors[u : u + 1, :], c, width)
 
         @pl.loop(0, steps)
         def _(t):
@@ -147,10 +148,8 @@
             )
             edges_s[u, 0, here, :] = left
             edges_s[u, 1, here, :] = right
-            for r in range(STEP_ROWS):
-                swapped = pl.ds(first + r, n, stride=n)
-                edges_s[u, 2, swapped, :] = right[r * n : (r + 1) * n]
-                edges_s[u, 3, swapped, :] = left[r * n : (r + 1) * n]
+            if u == 0:
+                store_swapped(right_t_s, STEP_ROWS, n, first, right)
             slopes_s[u, 0, here, :] = s_left
             slopes_s[u, 1, here, :] = s_right
             gate_s[u, here, :] = gate
@@ -161,19 +160,25 @@
         @pl.loop(0, steps)
         def _(t):
             here = block(t, STEP_ROWS, n)
-            x, y = edges_s.at[u, 3 * u], edges_s.at[u, 2 - u]
+            x, y = edges_s.at[u, 0], edges_s.at[1, 1] if u == 1 else right_t_s
             product = [
-                contract(n, t * STEP_ROWS + r, x, y) for r in range(0, STEP_ROWS, BLOCK_ROWS)
+                contract(n, t * STEP_ROWS + r, x, y, u == 1)
+                for r in range(0, STEP_ROWS, BLOCK_ROWS)
             ]
             p_hat, p_rstd, mixed, branch = mix(
-                jnp.concatenate(product).astype(BF16), gains[:, c:], shifts[:, c:], weights[u, :, width:], bias_out
+                jnp.concatenate(product).astype(BF16),
+                gains[:, c:],
+                shifts[:, c:],
+                weights[u, :, width:],
+                bias_out,
             )
             p_hat_s[u, here, :] = p_hat
             p_rstd_s[u, here, :] = p_rstd
             mixed_s[u, here, :] = mixed
             branch_s[u, here, :] = branch
-            x = next_s[here, :].astype(F32)
-            next_s[here, :] = (x + gate_s[u, here, :] * branch).astype(BF16)
+            if u == 0:
+                x = next_s[here, :].astype(F32)
+                next_s[here, :] = (x + gate_s[u, here, :] * branch).astype(BF16)
 
 
 def kept_parts(refs, u):
@@ -244,7 +249,7 @@
 def backward_left(n, up_in_ref, weights, vectors, *refs):
     (edges_s, slopes_s, gate_s, _, _, *kept) = kept_parts(refs, 0)
     (p_hat_s, p_rstd_s, branch_s, normed_s, mixed_s) = kept
-    d_pre_ref, d_product_t_ref, grads_ref, d_product_s, d_edge_s = refs[KEPT:]
+    d_pre_ref, d_product_ref, grads_ref, d_edge_s = refs[KEPT:]
     c, h = weights.shape[1], edges_s.shape[2]
     width = 4 * h + c
     gain = vector_parts(vectors[0:1, :], c, width)[1]
@@ -263,20 +268,19 @@
         )
         d_out = dot(mixed_s[here, :], d_branch, ((0,), (0,)))
         d_pre_ref[here, 2 * h :] = d_gate
-        d_product_s[here, :] = d_product
-        store_swapped(d_product_t_ref, STEP_ROWS, n, t * STEP_ROWS, d_product)
+        d_product_ref[here, :] = d_product
         grads_ref[:, 2 * h + c :] = d_out.astype(BF16)
 
-    one_side(n, 0, d_product_s, edges_s, slopes_s, d_edge_s, d_pre_ref)
+    one_side(n, 0, d_product_ref, edges_s, slopes_s, d_edge_s, d_pre_ref)
     d_pre = dot(normed_s[...], d_pre_ref[...], ((0,), (0,)))
     grads_ref[:, : 2 * h + c] = d_pre.astype(BF16)
 
 
-def backward_right(n, d_product_t_ref, *refs):
+def backward_right(n, d_product_ref, *refs):
     (edges_s, slopes_s, *kept) = kept_parts(refs, 0)
     normed_s = kept[-2]
     d_pre_ref, grads_ref, d_edge_s = refs[KEPT:]
-    one_side(n, 1, d_product_t_ref, edges_s, slopes_s, d_edge_s, d_pre_ref)
+    one_side(n, 1, d_product_ref, edges_s, slopes_s, d_edge_s, d_pre_ref)
     grads_ref[...] = dot(normed_s[...], d_pre_ref[...], ((0,), (0,))).astype(BF16)
 
 
@@ -286,7 +290,7 @@
     @pl.loop(0, n // BLOCK_ROWS)
     def _(t):
         d_edge_s[block(t, BLOCK_ROWS, n), :] = contract(
-            n, t * BLOCK_ROWS, x, edges_s.at[1 - side]
+            n, t * BLOCK_ROWS, x, edges_s.at[1 - side], side == 1
         )
 
     @pl.loop(0, n // STEP_ROWS)
@@ -405,7 +409,7 @@
     width = proj_weight.shape[2]
     cells, pairs = rows * n, n * n
     plane = (pairs + 8, h)
-    kept = [jax.ShapeDtypeStruct((2, 4) + plane, F32), jax.ShapeDtypeStruct((2, 2) + plane, F32)]
+    kept = [jax.ShapeDtypeStruct((2, 2) + plane, F32)] * 2
     kept += [jax.ShapeDtypeStruct((2,) + plane, F32)] * 6
     kept += [jax.ShapeDtypeStruct((2, pairs, h), BF16)] * 2
     grads = jax.ShapeDtypeStruct((c, width + c), BF16)
@@ -476,7 +480,7 @@
         out_shape=kept,
         in_specs=[vmem] * (half + 2),
         out_specs=(vmem,) * KEPT,
-        scratch_shapes=[pltpu.VMEM((pairs, c), BF16)],
+        scratch_shapes=[pltpu.VMEM((pairs, c), BF16), pltpu.VMEM(plane, F32)],
         compiler_params=params,
         cost_estimate=cost(64),
         name="forward",
@@ -501,7 +505,7 @@
     far = groups // 2
     others_1 = exchange(grads_1, "dp", groups, far)
 
-    d_left, d_product_t, grads_left = pl.pallas_call(
+    d_left, d_product, grads_left = pl.pallas_call(
         functools.partial(backward_left, n),
         out_shape=(
             jax.ShapeDtypeStruct((pairs, 2 * h + c), BF16),
@@ -510,7 +514,7 @@
         ),
         in_specs=[vmem] * (3 + KEPT),
         out_specs=[vmem] * 3,
-        scratch_shapes=[single, single],
+        scratch_shapes=[single],
         compiler_params=params,
         cost_estimate=cost(24),
         name="backward_left",
@@ -529,7 +533,7 @@
         compiler_params=params,
         cost_estimate=cost(24),
         name="backward_right",
-    )(d_product_t, *held)
+    )(d_product, *held)
     pair_grad = pl.pallas_call(
         own_rows,
         out_shape=jax.ShapeDtypeStruct((cells, c), BF16),

time: 45.8 us -> 44.6 us (0.974)
  the two profiles are of different devices: /device:TPU:20 before, /device:TPU:16 now
where the time goes in v19:
time: 44.6 us; the launch traced here: 44.3 us
  Pallas kernels  18.3 us (41%)
  starting transfers between devices  15.4 us (35%)
  waiting for transfers between devices  8.04 us (18%)
  local copies, waits for them, and re-layouts  1.7 us (4%)
  between operations  0.76 us (2%)
    ppermute x12, starting transfers between devices, exchange(): return lax.ppermute(value, axis, [(d, d ^ step) for d in range(size)])  15.4 us
    ppermute x12, waiting for transfers between devices, exchange(): return lax.ppermute(value, axis, [(d, d ^ step) for d in range(size)])  8.04 us
    pallas_call x1, Pallas kernels, crop_shards(): pl.pallas_call(functools.partial(forward, n, jumps), out_shape=kept, in_s...  5.7 us
    pallas_call x1, Pallas kernels, crop_shards(): pl.pallas_call(functools.partial(backward_second, n, jumps), out_shape=(j...  4.68 us
    pallas_call x1, Pallas kernels, crop_shards(): pl.pallas_call(functools.partial(backward_left, n), out_shape=(jax.ShapeD...  2.31 us
    pallas_call x1, Pallas kernels, crop_shards(): pl.pallas_call(prepare, out_shape=(jax.ShapeDtypeStruct((2 * cells + TAIL...  1.88 us
    pallas_call x1, Pallas kernels, crop_shards(): pl.pallas_call(functools.partial(backward_right, n), out_shape=(jax.Shape...  1.77 us
    unnamed x6, local copies, waits for them, and re-layouts  1.7 us
  transfers between devices with their start and end apart: 12, of which 5 were waited for; matrix products, arithmetic and copies ran while one was open for 0% of the time, Pallas kernels for 24%

profile of v19, /device:TPU:16, one launch (start us, length us, event | category | flops | bytes accessed | tf_op | source)
XLA Modules:
  0.0 44.3 jit_solution(896714636741163287)
XLA Ops:
  0.6 1.9 %prepare.1 = (bf16[272,128]{1,0:T(8,128)(2,1)}, bf16[2,128,768]{2,1,0:T(8,128)(2,1)}, f32[2,1280]{1,0:T(2,128)}) custom-call(s32[1]{0:T(128)} %bitcast.index_ref, s32[4,32]{1,0:T(4,128)} %bitcast.8, bf16[128,128]{1,0:T(8,128)(2,1)} %bitcast.6, bf16[128,128]{1,0:T(8,128)(2,1)} %bitcast.7, bf16[2,128,640]{2,1,0:T(8,128)(2,1)} %w.1, ...), custom_call_target="tpu_custom_call" | custom-call | tf_op jit(solution)/shard_map/prepare/pallas_call | solution.py:430
  2.5 0.0 copy-start
  2.5 1.6 %collective-permute-start = (bf16[272,128]{1,0:T(8,128)(2,1)}, bf16[272,128]{1,0:T(8,128)(2,1)S(1)}, u32[]{:S(2)}, u32[]{:S(2)}) collective-permute-start(bf16[272,128]{1,0:T(8,128)(2,1)} %get-tuple-element.32.near_ref), channel_id=1, source_target_pairs={{0,1},{1,0},{2,3},{3,2},{4,5},{5,4},{6,7},{7,6},{8,9},{9,8},{10,11... | collective-permute-start | bytes 208904 | tf_op jit(solution)/shard_map/ppermute | solution.py:321
  4.1 0.0 copy-start.1
  4.1 1.0 %copy-done.1 = bf16[2,128,768]{2,1,0:T(8,128)(2,1)S(1)} copy-done((bf16[2,128,768]{2,1,0:T(8,128)(2,1)S(1)}, bf16[2,128,768]{2,1,0:T(8,128)(2,1)}, u32[]{:S(2)}) %copy-start.1) | copy-done | bytes 393240
  5.1 0.0 copy-start.2
  5.1 0.7 %copy-done.2 = f32[2,1280]{1,0:T(2,128)S(1)} copy-done((f32[2,1280]{1,0:T(2,128)S(1)}, f32[2,1280]{1,0:T(2,128)}, u32[]{:S(2)}) %copy-start.2) | copy-done | bytes 10264
  5.8 1.3 %collective-permute-done.far_ref = bf16[272,128]{1,0:T(8,128)(2,1)S(1)} collective-permute-done((bf16[272,128]{1,0:T(8,128)(2,1)}, bf16[272,128]{1,0:T(8,128)(2,1)S(1)}, u32[]{:S(2)}, u32[]{:S(2)}) %collective-permute-start) | collective-permute-done | bytes 69664 | tf_op jit(solution)/shard_map/ppermute | solution.py:321
  7.1 0.0 copy-done
  7.1 0.1 collective-permute-start.6
  7.2 3.0 %collective-permute-start.5 = (bf16[2,144,128]{2,1,0:T(8,128)(2,1)S(1)}, bf16[2,144,128]{2,1,0:T(8,128)(2,1)S(1)}, u32[]{:S(2)}, u32[]{:S(2)}) collective-permute-start(bf16[2,144,128]{2,1,0:T(8,128)(2,1)S(1)} %get-tuple-element.38.refs_0_.pair.pair_ref), channel_id=1, source_target_pairs={{0,6},{1,7},{2,4},{3,5},{4,2},{5,3},{6,0},{7,1},{8,14},{9,15},{10,... | collective-permute-start | bytes 221192 | tf_op jit(solution)/shard_map/ppermute | solution.py:321
  10.2 1.3 %collective-permute-start.4 = (bf16[2,144,128]{2,1,0:T(8,128)(2,1)S(1)}, bf16[2,144,128]{2,1,0:T(8,128)(2,1)S(1)}, u32[]{:S(2)}, u32[]{:S(2)}) collective-permute-start(bf16[2,144,128]{2,1,0:T(8,128)(2,1)S(1)} %get-tuple-element.38.refs_0_.pair.pair_ref), channel_id=1, source_target_pairs={{0,2},{1,3},{2,0},{3,1},{4,6},{5,7},{6,4},{7,5},{8,10},{9,11},{10,... | collective-permute-start | bytes 221192 | tf_op jit(solution)/shard_map/ppermute | solution.py:321
  11.6 0.1 collective-permute-start.3
  11.7 2.0 %collective-permute-start.2 = (bf16[2,128,128]{2,1,0:T(8,128)(2,1)S(1)}, bf16[2,128,128]{2,1,0:T(8,128)(2,1)S(1)}, u32[]{:S(2)}, u32[]{:S(2)}) collective-permute-start(bf16[2,128,128]{2,1,0:T(8,128)(2,1)S(1)} %get-tuple-element.39.refs_0_), channel_id=1, source_target_pairs={{0,6},{1,7},{2,4},{3,5},{4,2},{5,3},{6,0},{7,1},{8,14},{9,15},{10,... | collective-permute-start | bytes 196616 | tf_op jit(solution)/shard_map/ppermute | solution.py:321
  13.7 0.0 collective-permute-done.6.refs_3_
  13.7 4.3 %collective-permute-start.1 = (bf16[2,128,128]{2,1,0:T(8,128)(2,1)S(1)}, bf16[2,128,128]{2,1,0:T(8,128)(2,1)S(1)}, u32[]{:S(2)}, u32[]{:S(2)}) collective-permute-start(bf16[2,128,128]{2,1,0:T(8,128)(2,1)S(1)} %get-tuple-element.39.refs_0_), channel_id=1, source_target_pairs={{0,2},{1,3},{2,0},{3,1},{4,6},{5,7},{6,4},{7,5},{8,10},{9,11},{10,... | collective-permute-start | bytes 196616 | tf_op jit(solution)/shard_map/ppermute | solution.py:321
  18.0 1.3 %collective-permute-done.5.refs_2_ = bf16[2,144,128]{2,1,0:T(8,128)(2,1)S(1)} collective-permute-done((bf16[2,144,128]{2,1,0:T(8,128)(2,1)S(1)}, bf16[2,144,128]{2,1,0:T(8,128)(2,1)S(1)}, u32[]{:S(2)}, u32[]{:S(2)}) %collective-permute-start.5) | collective-permute-done | bytes 73760 | tf_op jit(solution)/shard_map/ppermute | solution.py:321
  19.3 0.0 collective-permute-done.4.refs_1_
  19.4 5.7 %forward.1 = (f32[2,2,1032,128]{3,2,1,0:T(8,128)S(1)}, f32[2,2,1032,128]{3,2,1,0:T(8,128)S(1)}, f32[2,1032,128]{2,1,0:T(8,128)S(1)}, f32[2,1032,128]{2,1,0:T(8,1...) custom-call(bf16[2,144,128]{2,1,0:T(8,128)(2,1)S(1)} %get-tuple-elem, ...), custom_call_target="tpu_custom_call" | custom-call | flops 335544320 | bytes 33554432 | tf_op jit(solution)/shard_map/forward/pallas_call | solution.py:478
  25.0 0.0 collective-permute-done.3.refs_3_
  25.1 0.0 collective-permute-done.2.refs_2_
  25.1 0.0 collective-permute-done.1.refs_1_
  25.1 4.7 %backward_second.1 = (f32[1024,128]{1,0:T(8,128)S(1)}, bf16[128,768]{1,0:T(8,128)(2,1)S(1)}) custom-call(bf16[2,144,128]{2,1,0:T(8,128)(2,1)S(1)} %get-tuple-element.38.refs_0_.pair.pair_ref, bf16[2,128,128]{2,1,0:T(8,128)(2,1)S(1)} %get-tuple-element.39.refs_0_, bf16[2,128,128]{2,1,0:T(8,128)(2,1)S(1)} %collective-permute-done.1.refs_1_, ...), custom_call_target="tpu_custom_call" | custom-call | flops 335544320 | bytes 25165824 | tf_op jit(solution)/shard_map/backward_second/pallas_call | solution.py:490
  29.8 1.6 %collective-permute-start.7 = (bf16[128,768]{1,0:T(8,128)(2,1)S(1)}, bf16[128,768]{1,0:T(8,128)(2,1)S(1)}, u32[]{:S(2)}, u32[]{:S(2)}) collective-permute-start(bf16[128,768]{1,0:T(8,128)(2,1)S(1)} %get-tuple-element.56), channel_id=1, source_target_pairs={{0,16},{8,24},{16,0},{24,8},{1,17},{9,25},{17,1},{25,9},{2,18},{10... | collective-permute-start | bytes 589832 | tf_op jit(solution)/shard_map/ppermute | solution.py:321
  31.3 2.3 %backward_left.1 = (bf16[1024,384]{1,0:T(8,128)(2,1)S(1)}, f32[1032,128]{1,0:T(8,128)S(1)}, bf16[128,512]{1,0:T(8,128)(2,1)S(1)}) custom-call(f32[1024,128]{1,0:T(8,128)S(1)} %get-tuple-element.52.up_in_ref.up_ref, bf16[2,128,768]{2,1,0:T(8,128)(2,1)S(1)} %get-tuple-element.40.refs_4_.weights, f32[2,1280]{1,0:T(2,128)S(1)} %get-tuple-element.41.refs_5_.vectors, ...), custom_call_target="tpu_custom_call" | custom-call | flops 335544320 | bytes 12582912 | tf_op jit(solution)/shard_map/backward_left/pallas_call | solution.py:508
  33.6 0.6 %collective-permute-start.9 = (bf16[128,512]{1,0:T(8,128)(2,1)S(1)}, bf16[128,512]{1,0:T(8,128)(2,1)S(1)}, u32[]{:S(2)}, u32[]{:S(2)}) collective-permute-start(bf16[128,512]{1,0:T(8,128)(2,1)S(1)} %get-tuple-element.58), channel_id=1, source_target_pairs={{0,16},{8,24},{16,0},{24,8},{1,17},{9,25},{17,1},{25,9},{2,18},{10... | collective-permute-start | bytes 393224 | tf_op jit(solution)/shard_map/ppermute | solution.py:321
  34.2 1.8 %backward_right.1 = (bf16[1024,256]{1,0:T(8,128)(2,1)S(1)}, bf16[128,256]{1,0:T(8,128)(2,1)S(1)}) custom-call(f32[1032,128]{1,0:T(8,128)S(1)} %get-tuple-element.54.d_product_ref, f32[2,2,1032,128]{3,2,1,0:T(8,128)S(1)} %get-tuple-element.42.refs_6_.refs_0_, f32[2,2,1032,128]{3,2,1,0:T(8,128)S(1)} %get-tuple-element.43.refs_7_.refs_1_, ...), custom_call_target="tpu_custom_call" | custom-call | flops 335544320 | bytes 12582912 | tf_op jit(solution)/shard_map/backward_right/pallas_call | solution.py:524
  36.0 0.6 %collective-permute-done.7 = bf16[128,768]{1,0:T(8,128)(2,1)S(1)} collective-permute-done((bf16[128,768]{1,0:T(8,128)(2,1)S(1)}, bf16[128,768]{1,0:T(8,128)(2,1)S(1)}, u32[]{:S(2)}, u32[]{:S(2)}) %collective-permute-start.7) | collective-permute-done | bytes 196640 | tf_op jit(solution)/shard_map/ppermute | solution.py:321
  36.7 0.1 collective-permute-start.8
  36.8 1.9 %collective-permute-done.9 = bf16[128,512]{1,0:T(8,128)(2,1)S(1)} collective-permute-done((bf16[128,512]{1,0:T(8,128)(2,1)S(1)}, bf16[128,512]{1,0:T(8,128)(2,1)S(1)}, u32[]{:S(2)}, u32[]{:S(2)}) %collective-permute-start.9) | collective-permute-done | bytes 131104 | tf_op jit(solution)/shard_map/ppermute | solution.py:321
  38.7 0.1 collective-permute-start.10
  38.8 0.0 collective-permute-done.8.rest_near
  38.8 0.6 %collective-permute-start.11 = (bf16[128,256]{1,0:T(8,128)(2,1)S(1)}, bf16[128,256]{1,0:T(8,128)(2,1)S(1)}, u32[]{:S(2)}, u32[]{:S(2)}) collective-permute-start(bf16[128,256]{1,0:T(8,128)(2,1)S(1)} %add_convert_fusion.2.right), channel_id=1, source_target_pairs={{0,16},{8,24},{16,0},{24,8},{1,17},{9,25},{17,1},{25,9},{2,18},{10... | collective-permute-start | bytes 196616 | tf_op jit(solution)/shard_map/ppermute | solution.py:321
  39.4 1.0 %own_rows.1 = bf16[128,128]{1,0:T(8,128)(2,1)} custom-call(bf16[2,144,128]{2,1,0:T(8,128)(2,1)S(1)} %get-tuple-element.38.refs_0_.pair.pair_ref, f32[1024,128]{1,0:T(8,128)S(1)} %get-tuple-element.52.up_in_ref.up_ref, bf16[1024,384]{1,0:T(8,128)(2,1)S(1)} %get-tuple-element.53.d_left_ref, bf16[1024,256]{1,0:T(8,128)(2,1)S(1)} %get-tuple-element.55.d_right_ref, ...), custom_call_target="tpu_custom_call" | custom-call | flops 335544320 | bytes 4194304 | tf_op jit(solution)/shard_map/own_rows/pallas_call | solution.py:537
  40.4 0.0 collective-permute-done.10.left_near
  40.4 2.9 %collective-permute-done.11.right_far = bf16[128,256]{1,0:T(8,128)(2,1)S(1)} collective-permute-done((bf16[128,256]{1,0:T(8,128)(2,1)S(1)}, bf16[128,256]{1,0:T(8,128)(2,1)S(1)}, u32[]{:S(2)}, u32[]{:S(2)}) %collective-permute-start.11) | collective-permute-done | bytes 65568 | tf_op jit(solution)/shard_map/ppermute | solution.py:321
  43.4 0.9 %add_grads.1 = (f32[2,128,640]{2,1,0:T(8,128)}, f32[2,128,128]{2,1,0:T(8,128)}) custom-call(bf16[128,1024]{1,0:T(8,128)(2,1)S(1)} %pad_maximum_fusion.rest, bf16[128,1024]{1,0:T(8,128)(2,1)S(1)} %collective-permute-done.8.rest_near, bf16[128,512]{1,0:T(8,128)(2,1)S(1)} %add_convert_fusion.1.left, bf16[128,512]{1,0:T(8,128)(2,1)S(1)} %collective-permute-done.10.left_near, ...), custom_call_target="tpu_custom_call" | custom-call | tf_op jit(solution)/shard_map/add_grads/pallas_call | solution.py:554
  (6 shorter events, 0.2 us)
Async XLA Ops:
  2.5 4.6 %copy-start = (bf16[272,128]{1,0:T(8,128)(2,1)S(1)}, bf16[272,128]{1,0:T(8,128)(2,1)}, u32[]{:S(2)}) copy-start(bf16[272,128]{1,0:T(8,128)(2,1)} %get-tuple-element.32.near_ref) | copy-start | bytes 208900
  2.5 4.6 %collective-permute-start = (bf16[272,128]{1,0:T(8,128)(2,1)}, bf16[272,128]{1,0:T(8,128)(2,1)S(1)}, u32[]{:S(2)}, u32[]{:S(2)}) collective-permute-start(bf16[272,128]{1,0:T(8,128)(2,1)} %get-tuple-element.32.near_ref), channel_id=1, source_target_pairs={{0,1},{1,0},{2,3},{3,2},{4,5},{5,4},{6,7},{7,6},{8,9},{9,8},{10,11... | collective-permute-start | bytes 208904 | tf_op jit(solution)/shard_map/ppermute | solution.py:321
  4.1 1.0 %copy-start.1 = (bf16[2,128,768]{2,1,0:T(8,128)(2,1)S(1)}, bf16[2,128,768]{2,1,0:T(8,128)(2,1)}, u32[]{:S(2)}) copy-start(bf16[2,128,768]{2,1,0:T(8,128)(2,1)} %get-tuple-element.33.weights_in) | copy-start | bytes 1179652
  5.1 0.7 %copy-start.2 = (f32[2,1280]{1,0:T(2,128)S(1)}, f32[2,1280]{1,0:T(2,128)}, u32[]{:S(2)}) copy-start(f32[2,1280]{1,0:T(2,128)} %get-tuple-element.34.vectors_in) | copy-start | bytes 30724
  7.1 6.6 %collective-permute-start.6 = (bf16[2,144,128]{2,1,0:T(8,128)(2,1)S(1)}, bf16[2,144,128]{2,1,0:T(8,128)(2,1)S(1)}, u32[]{:S(2)}, u32[]{:S(2)}) collective-permute-start(bf16[2,144,128]{2,1,0:T(8,128)(2,1)S(1)} %get-tuple-element.38.refs_0_.pair.pair_ref), channel_id=1, source_target_pairs={{0,4},{1,5},{2,6},{3,7},{4,0},{5,1},{6,2},{7,3},{8,12},{9,13},{10,... | collective-permute-start | bytes 221192 | tf_op jit(solution)/shard_map/ppermute | solution.py:321
  7.2 12.1 %collective-permute-start.5 = (bf16[2,144,128]{2,1,0:T(8,128)(2,1)S(1)}, bf16[2,144,128]{2,1,0:T(8,128)(2,1)S(1)}, u32[]{:S(2)}, u32[]{:S(2)}) collective-permute-start(bf16[2,144,128]{2,1,0:T(8,128)(2,1)S(1)} %get-tuple-element.38.refs_0_.pair.pair_ref), channel_id=1, source_target_pairs={{0,6},{1,7},{2,4},{3,5},{4,2},{5,3},{6,0},{7,1},{8,14},{9,15},{10,... | collective-permute-start | bytes 221192 | tf_op jit(solution)/shard_map/ppermute | solution.py:321
  10.2 9.1 %collective-permute-start.4 = (bf16[2,144,128]{2,1,0:T(8,128)(2,1)S(1)}, bf16[2,144,128]{2,1,0:T(8,128)(2,1)S(1)}, u32[]{:S(2)}, u32[]{:S(2)}) collective-permute-start(bf16[2,144,128]{2,1,0:T(8,128)(2,1)S(1)} %get-tuple-element.38.refs_0_.pair.pair_ref), channel_id=1, source_target_pairs={{0,2},{1,3},{2,0},{3,1},{4,6},{5,7},{6,4},{7,5},{8,10},{9,11},{10,... | collective-permute-start | bytes 221192 | tf_op jit(solution)/shard_map/ppermute | solution.py:321
  11.6 13.5 %collective-permute-start.3 = (bf16[2,128,128]{2,1,0:T(8,128)(2,1)S(1)}, bf16[2,128,128]{2,1,0:T(8,128)(2,1)S(1)}, u32[]{:S(2)}, u32[]{:S(2)}) collective-permute-start(bf16[2,128,128]{2,1,0:T(8,128)(2,1)S(1)} %get-tuple-element.39.refs_0_), channel_id=1, source_target_pairs={{0,4},{1,5},{2,6},{3,7},{4,0},{5,1},{6,2},{7,3},{8,12},{9,13},{10,... | collective-permute-start | bytes 196616 | tf_op jit(solution)/shard_map/ppermute | solution.py:321
  11.7 13.3 %collective-permute-start.2 = (bf16[2,128,128]{2,1,0:T(8,128)(2,1)S(1)}, bf16[2,128,128]{2,1,0:T(8,128)(2,1)S(1)}, u32[]{:S(2)}, u32[]{:S(2)}) collective-permute-start(bf16[2,128,128]{2,1,0:T(8,128)(2,1)S(1)} %get-tuple-element.39.refs_0_), channel_id=1, source_target_pairs={{0,6},{1,7},{2,4},{3,5},{4,2},{5,3},{6,0},{7,1},{8,14},{9,15},{10,... | collective-permute-start | bytes 196616 | tf_op jit(solution)/shard_map/ppermute | solution.py:321
  13.7 11.3 %collective-permute-start.1 = (bf16[2,128,128]{2,1,0:T(8,128)(2,1)S(1)}, bf16[2,128,128]{2,1,0:T(8,128)(2,1)S(1)}, u32[]{:S(2)}, u32[]{:S(2)}) collective-permute-start(bf16[2,128,128]{2,1,0:T(8,128)(2,1)S(1)} %get-tuple-element.39.refs_0_), channel_id=1, source_target_pairs={{0,2},{1,3},{2,0},{3,1},{4,6},{5,7},{6,4},{7,5},{8,10},{9,11},{10,... | collective-permute-start | bytes 196616 | tf_op jit(solution)/shard_map/ppermute | solution.py:321
  29.8 6.9 %collective-permute-start.7 = (bf16[128,768]{1,0:T(8,128)(2,1)S(1)}, bf16[128,768]{1,0:T(8,128)(2,1)S(1)}, u32[]{:S(2)}, u32[]{:S(2)}) collective-permute-start(bf16[128,768]{1,0:T(8,128)(2,1)S(1)} %get-tuple-element.56), channel_id=1, source_target_pairs={{0,16},{8,24},{16,0},{24,8},{1,17},{9,25},{17,1},{25,9},{2,18},{10... | collective-permute-start | bytes 589832 | tf_op jit(solution)/shard_map/ppermute | solution.py:321
  33.6 5.0 %collective-permute-start.9 = (bf16[128,512]{1,0:T(8,128)(2,1)S(1)}, bf16[128,512]{1,0:T(8,128)(2,1)S(1)}, u32[]{:S(2)}, u32[]{:S(2)}) collective-permute-start(bf16[128,512]{1,0:T(8,128)(2,1)S(1)} %get-tuple-element.58), channel_id=1, source_target_pairs={{0,16},{8,24},{16,0},{24,8},{1,17},{9,25},{17,1},{25,9},{2,18},{10... | collective-permute-start | bytes 393224 | tf_op jit(solution)/shard_map/ppermute | solution.py:321
  36.7 2.1 %collective-permute-start.8 = (bf16[128,1024]{1,0:T(8,128)(2,1)S(1)}, bf16[128,1024]{1,0:T(8,128)(2,1)S(1)}, u32[]{:S(2)}, u32[]{:S(2)}) collective-permute-start(bf16[128,1024]{1,0:T(8,128)(2,1)S(1)} %pad_maximum_fusion.rest), channel_id=1, source_target_pairs={{0,8},{8,0},{16,24},{24,16},{1,9},{9,1},{17,25},{25,17},{2,10},{10... | collective-permute-start | bytes 786440 | tf_op jit(solution)/shard_map/ppermute | solution.py:321
  38.7 1.7 %collective-permute-start.10 = (bf16[128,512]{1,0:T(8,128)(2,1)S(1)}, bf16[128,512]{1,0:T(8,128)(2,1)S(1)}, u32[]{:S(2)}, u32[]{:S(2)}) collective-permute-start(bf16[128,512]{1,0:T(8,128)(2,1)S(1)} %add_convert_fusion.1.left), channel_id=1, source_target_pairs={{0,8},{8,0},{16,24},{24,16},{1,9},{9,1},{17,25},{25,17},{2,10},{10... | collective-permute-start | bytes 393224 | tf_op jit(solution)/shard_map/ppermute | solution.py:321
  38.8 4.5 %collective-permute-start.11 = (bf16[128,256]{1,0:T(8,128)(2,1)S(1)}, bf16[128,256]{1,0:T(8,128)(2,1)S(1)}, u32[]{:S(2)}, u32[]{:S(2)}) collective-permute-start(bf16[128,256]{1,0:T(8,128)(2,1)S(1)} %add_convert_fusion.2.right), channel_id=1, source_target_pairs={{0,16},{8,24},{16,0},{24,8},{1,17},{9,25},{17,1},{25,9},{2,18},{10... | collective-permute-start | bytes 196616 | tf_op jit(solution)/shard_map/ppermute | solution.py:321

commit v20 on v19

--- a/solution.py
+++ b/solution.py
@@ -153,8 +153,9 @@
             slopes_s[u, 0, here, :] = s_left
             slopes_s[u, 1, here, :] = s_right
             gate_s[u, here, :] = gate
-            hat_s[u, here, :] = x_hat
-            rstd_s[u, here, :] = rstd
+            if u == 1:
+                hat_s[here, :] = x_hat
+                rstd_s[here, :] = rstd
             normed_s[u, here, :] = normed
 
         @pl.loop(0, steps)
@@ -182,7 +183,7 @@
 
 
 def kept_parts(refs, u):
-    return [ref.at[u] for ref in refs[:KEPT]]
+    return [ref if ref.shape[0] != 2 else ref.at[u] for ref in refs[:KEPT]]
 
 
 def store_swapped(ref, rows, n, first, values):
@@ -249,7 +250,7 @@
 def backward_left(n, up_in_ref, weights, vectors, *refs):
     (edges_s, slopes_s, gate_s, _, _, *kept) = kept_parts(refs, 0)
     (p_hat_s, p_rstd_s, branch_s, normed_s, mixed_s) = kept
-    d_pre_ref, d_product_ref, grads_ref, d_edge_s = refs[KEPT:]
+    d_pre_ref, d_product_ref, grads_ref = refs[KEPT:]
     c, h = weights.shape[1], edges_s.shape[2]
     width = 4 * h + c
     gain = vector_parts(vectors[0:1, :], c, width)[1]
@@ -271,7 +272,7 @@
         d_product_ref[here, :] = d_product
         grads_ref[:, 2 * h + c :] = d_out.astype(BF16)
 
-    one_side(n, 0, d_product_ref, edges_s, slopes_s, d_edge_s, d_pre_ref)
+    one_side(n, 0, d_product_ref, edges_s, slopes_s, d_pre_ref)
     d_pre = dot(normed_s[...], d_pre_ref[...], ((0,), (0,)))
     grads_ref[:, : 2 * h + c] = d_pre.astype(BF16)
 
@@ -279,30 +280,28 @@
 def backward_right(n, d_product_ref, *refs):
     (edges_s, slopes_s, *kept) = kept_parts(refs, 0)
     normed_s = kept[-2]
-    d_pre_ref, grads_ref, d_edge_s = refs[KEPT:]
-    one_side(n, 1, d_product_ref, edges_s, slopes_s, d_edge_s, d_pre_ref)
+    d_pre_ref, grads_ref = refs[KEPT:]
+    one_side(n, 1, d_product_ref, edges_s, slopes_s, d_pre_ref)
     grads_ref[...] = dot(normed_s[...], d_pre_ref[...], ((0,), (0,))).astype(BF16)
 
 
-def one_side(n, side, x, edges_s, slopes_s, d_edge_s, d_pre_ref):
+def one_side(n, side, x, edges_s, slopes_s, d_pre_ref):
     h = edges_s.shape[2]
-
-    @pl.loop(0, n // BLOCK_ROWS)
-    def _(t):
-        d_edge_s[block(t, BLOCK_ROWS, n), :] = contract(
-            n, t * BLOCK_ROWS, x, edges_s.at[1 - side], side == 1
-        )
 
     @pl.loop(0, n // STEP_ROWS)
     def _(t):
         here = block(t, STEP_ROWS, n)
+        d_edge = [
+            contract(n, t * STEP_ROWS + r, x, edges_s.at[1 - side], side == 1)
+            for r in range(0, STEP_ROWS, BLOCK_ROWS)
+        ]
         d_pre_ref[here, : 2 * h] = edge_grads(
-            d_edge_s[here, :], slopes_s[side, here, :], edges_s[side, here, :]
+            jnp.concatenate(d_edge), slopes_s[side, here, :], edges_s[side, here, :]
         )
 
 
 def own_rows(
-    pair_ref, up_ref, d_left_ref, d_right_ref, weights, vectors, hat_ref, rstd_ref, out_ref
+    pair_ref, up_ref, d_left_ref, d_right_ref, weights, vectors, out_ref
 ):
     cells, c = out_ref.shape
     half = d_right_ref.shape[1]
@@ -313,7 +312,7 @@
     d_left, d_right = d_left_ref[own, :], d_right_ref[own, :]
     d_pre = jnp.concatenate([d_left[:, :half], d_right, d_left[:, half:]], axis=1)
     d_normed = dot(d_pre, weights[0, :, :width], ((1,), (1,))) * gain[:, :c]
-    pulled = norm_vjp(hat_ref[0, own, :], rstd_ref[0, own, :], d_normed)
+    pulled = norm_vjp(*norm_parts(pair_ref[0, :cells, :]), d_normed)
     out_ref[...] = (up_ref[own, :] + pulled).astype(BF16)
 
 
@@ -410,7 +409,8 @@
     cells, pairs = rows * n, n * n
     plane = (pairs + 8, h)
     kept = [jax.ShapeDtypeStruct((2, 2) + plane, F32)] * 2
-    kept += [jax.ShapeDtypeStruct((2,) + plane, F32)] * 6
+    two = jax.ShapeDtypeStruct((2,) + plane, F32)
+    kept += [two] + [jax.ShapeDtypeStruct(plane, F32)] * 2 + [two] * 3
     kept += [jax.ShapeDtypeStruct((2, pairs, h), BF16)] * 2
     grads = jax.ShapeDtypeStruct((c, width + c), BF16)
     vmem = pl.BlockSpec(memory_space=pltpu.VMEM)
@@ -486,7 +486,7 @@
         name="forward",
     )(*states, *weights)
 
-    double, single = pltpu.VMEM((2,) + plane, F32), pltpu.VMEM(plane, F32)
+    double = pltpu.VMEM((2,) + plane, F32)
     up_1, grads_1 = pl.pallas_call(
         functools.partial(backward_second, n, jumps),
         out_shape=(jax.ShapeDtypeStruct((pairs, c), F32), grads),
@@ -514,7 +514,6 @@
         ),
         in_specs=[vmem] * (3 + KEPT),
         out_specs=[vmem] * 3,
-        scratch_shapes=[single],
         compiler_params=params,
         cost_estimate=cost(24),
         name="backward_left",
@@ -529,7 +528,6 @@
         ),
         in_specs=[vmem] * (1 + KEPT),
         out_specs=[vmem] * 2,
-        scratch_shapes=[single],
         compiler_params=params,
         cost_estimate=cost(24),
         name="backward_right",
@@ -537,12 +535,12 @@
     pair_grad = pl.pallas_call(
         own_rows,
         out_shape=jax.ShapeDtypeStruct((cells, c), BF16),
-        in_specs=[vmem] * 8,
+        in_specs=[vmem] * 6,
         out_specs=vmem,
         compiler_params=params,
         cost_estimate=cost(8),
         name="own_rows",
-    )(states[0], up_1, d_left, d_right, *weights, held[3], held[4])
+    )(states[0], up_1, d_left, d_right, *weights)
 
     rest, rest_near = near_rounds(
         jnp.concatenate([add_narrow(grads_1, others_1), grads_right], axis=1), groups

time: 44.6 us -> 45 us (level)
  transfers between devices with their start and end apart: 12 -> 12, of which waited for: 5 -> 5; matrix products, arithmetic and copies ran while one was open for 0% -> 0% of each run, Pallas kernels for 24% -> 25%
where the time goes in v20:
time: 45 us; the launch traced here: 44.7 us
  Pallas kernels  18.7 us (42%)
  starting transfers between devices  15.4 us (34%)
  waiting for transfers between devices  8.09 us (18%)
  local copies, waits for them, and re-layouts  1.7 us (4%)
  between operations  0.76 us (2%)
    ppermute x12, starting transfers between devices, exchange(): return lax.ppermute(value, axis, [(d, d ^ step) for d in range(size)])  15.4 us
    ppermute x12, waiting for transfers between devices, exchange(): return lax.ppermute(value, axis, [(d, d ^ step) for d in range(size)])  8.09 us
    pallas_call x1, Pallas kernels, crop_shards(): pl.pallas_call(functools.partial(forward, n, jumps), out_shape=kept, in_s...  6.04 us
    pallas_call x1, Pallas kernels, crop_shards(): pl.pallas_call(functools.partial(backward_second, n, jumps), out_shape=(j...  4.75 us
    pallas_call x1, Pallas kernels, crop_shards(): pl.pallas_call(functools.partial(backward_left, n), out_shape=(jax.ShapeD...  2.3 us
    pallas_call x1, Pallas kernels, crop_shards(): pl.pallas_call(prepare, out_shape=(jax.ShapeDtypeStruct((2 * cells + TAIL...  1.88 us
    pallas_call x1, Pallas kernels, crop_shards(): pl.pallas_call(functools.partial(backward_right, n), out_shape=(jax.Shape...  1.72 us
    unnamed x6, local copies, waits for them, and re-layouts  1.7 us
  transfers between devices with their start and end apart: 12, of which 5 were waited for; matrix products, arithmetic and copies ran while one was open for 0% of the time, Pallas kernels for 25%

profile of v20, /device:TPU:16, one launch (start us, length us, event | category | flops | bytes accessed | tf_op | source)
XLA Modules:
  0.0 44.7 jit_solution(12557428818961717096)
XLA Ops:
  0.6 1.9 %prepare.1 = (bf16[272,128]{1,0:T(8,128)(2,1)}, bf16[2,128,768]{2,1,0:T(8,128)(2,1)}, f32[2,1280]{1,0:T(2,128)}) custom-call(s32[1]{0:T(128)} %bitcast.index_ref, s32[4,32]{1,0:T(4,128)} %bitcast.8, bf16[128,128]{1,0:T(8,128)(2,1)} %bitcast.6, bf16[128,128]{1,0:T(8,128)(2,1)} %bitcast.7, bf16[2,128,640]{2,1,0:T(8,128)(2,1)} %w.1, ...), custom_call_target="tpu_custom_call" | custom-call | tf_op jit(solution)/shard_map/prepare/pallas_call | solution.py:430
  2.5 0.0 copy-start
  2.5 1.6 %collective-permute-start = (bf16[272,128]{1,0:T(8,128)(2,1)}, bf16[272,128]{1,0:T(8,128)(2,1)S(1)}, u32[]{:S(2)}, u32[]{:S(2)}) collective-permute-start(bf16[272,128]{1,0:T(8,128)(2,1)} %get-tuple-element.32.near_ref), channel_id=1, source_target_pairs={{0,1},{1,0},{2,3},{3,2},{4,5},{5,4},{6,7},{7,6},{8,9},{9,8},{10,11... | collective-permute-start | bytes 208904 | tf_op jit(solution)/shard_map/ppermute | solution.py:320
  4.1 0.0 copy-start.1
  4.1 1.0 %copy-done.1 = bf16[2,128,768]{2,1,0:T(8,128)(2,1)S(1)} copy-done((bf16[2,128,768]{2,1,0:T(8,128)(2,1)S(1)}, bf16[2,128,768]{2,1,0:T(8,128)(2,1)}, u32[]{:S(2)}) %copy-start.1) | copy-done | bytes 393240
  5.1 0.0 copy-start.2
  5.1 0.7 %copy-done.2 = f32[2,1280]{1,0:T(2,128)S(1)} copy-done((f32[2,1280]{1,0:T(2,128)S(1)}, f32[2,1280]{1,0:T(2,128)}, u32[]{:S(2)}) %copy-start.2) | copy-done | bytes 10264
  5.8 1.3 %collective-permute-done.far_ref = bf16[272,128]{1,0:T(8,128)(2,1)S(1)} collective-permute-done((bf16[272,128]{1,0:T(8,128)(2,1)}, bf16[272,128]{1,0:T(8,128)(2,1)S(1)}, u32[]{:S(2)}, u32[]{:S(2)}) %collective-permute-start) | collective-permute-done | bytes 69664 | tf_op jit(solution)/shard_map/ppermute | solution.py:320
  7.1 0.0 copy-done
  7.1 0.1 collective-permute-start.6
  7.2 3.0 %collective-permute-start.5 = (bf16[2,144,128]{2,1,0:T(8,128)(2,1)S(1)}, bf16[2,144,128]{2,1,0:T(8,128)(2,1)S(1)}, u32[]{:S(2)}, u32[]{:S(2)}) collective-permute-start(bf16[2,144,128]{2,1,0:T(8,128)(2,1)S(1)} %get-tuple-element.38.refs_0_.pair.pair_ref), channel_id=1, source_target_pairs={{0,6},{1,7},{2,4},{3,5},{4,2},{5,3},{6,0},{7,1},{8,14},{9,15},{10,... | collective-permute-start | bytes 221192 | tf_op jit(solution)/shard_map/ppermute | solution.py:320
  10.2 1.3 %collective-permute-start.4 = (bf16[2,144,128]{2,1,0:T(8,128)(2,1)S(1)}, bf16[2,144,128]{2,1,0:T(8,128)(2,1)S(1)}, u32[]{:S(2)}, u32[]{:S(2)}) collective-permute-start(bf16[2,144,128]{2,1,0:T(8,128)(2,1)S(1)} %get-tuple-element.38.refs_0_.pair.pair_ref), channel_id=1, source_target_pairs={{0,2},{1,3},{2,0},{3,1},{4,6},{5,7},{6,4},{7,5},{8,10},{9,11},{10,... | collective-permute-start | bytes 221192 | tf_op jit(solution)/shard_map/ppermute | solution.py:320
  11.6 0.1 collective-permute-start.3
  11.7 2.0 %collective-permute-start.2 = (bf16[2,128,128]{2,1,0:T(8,128)(2,1)S(1)}, bf16[2,128,128]{2,1,0:T(8,128)(2,1)S(1)}, u32[]{:S(2)}, u32[]{:S(2)}) collective-permute-start(bf16[2,128,128]{2,1,0:T(8,128)(2,1)S(1)} %get-tuple-element.39.refs_0_), channel_id=1, source_target_pairs={{0,6},{1,7},{2,4},{3,5},{4,2},{5,3},{6,0},{7,1},{8,14},{9,15},{10,... | collective-permute-start | bytes 196616 | tf_op jit(solution)/shard_map/ppermute | solution.py:320
  13.7 0.0 collective-permute-done.6.refs_3_
  13.7 4.3 %collective-permute-start.1 = (bf16[2,128,128]{2,1,0:T(8,128)(2,1)S(1)}, bf16[2,128,128]{2,1,0:T(8,128)(2,1)S(1)}, u32[]{:S(2)}, u32[]{:S(2)}) collective-permute-start(bf16[2,128,128]{2,1,0:T(8,128)(2,1)S(1)} %get-tuple-element.39.refs_0_), channel_id=1, source_target_pairs={{0,2},{1,3},{2,0},{3,1},{4,6},{5,7},{6,4},{7,5},{8,10},{9,11},{10,... | collective-permute-start | bytes 196616 | tf_op jit(solution)/shard_map/ppermute | solution.py:320
  18.0 1.3 %collective-permute-done.5.refs_2_ = bf16[2,144,128]{2,1,0:T(8,128)(2,1)S(1)} collective-permute-done((bf16[2,144,128]{2,1,0:T(8,128)(2,1)S(1)}, bf16[2,144,128]{2,1,0:T(8,128)(2,1)S(1)}, u32[]{:S(2)}, u32[]{:S(2)}) %collective-permute-start.5) | collective-permute-done | bytes 73760 | tf_op jit(solution)/shard_map/ppermute | solution.py:320
  19.3 0.0 collective-permute-done.4.refs_1_
  19.4 6.0 %forward.1 = (f32[2,2,1032,128]{3,2,1,0:T(8,128)S(1)}, f32[2,2,1032,128]{3,2,1,0:T(8,128)S(1)}, f32[2,1032,128]{2,1,0:T(8,128)S(1)}, f32[1032,128]{1,0:T(8,128)S...) custom-call(bf16[2,144,128]{2,1,0:T(8,128)(2,1)S(1)} %get-tuple-elem, ...), custom_call_target="tpu_custom_call" | custom-call | flops 335544320 | bytes 33554432 | tf_op jit(solution)/shard_map/forward/pallas_call | solution.py:478
  25.4 0.0 collective-permute-done.3.refs_3_
  25.4 0.0 collective-permute-done.2.refs_2_
  25.4 0.0 collective-permute-done.1.refs_1_
  25.4 4.7 %backward_second.1 = (f32[1024,128]{1,0:T(8,128)S(1)}, bf16[128,768]{1,0:T(8,128)(2,1)S(1)}) custom-call(bf16[2,144,128]{2,1,0:T(8,128)(2,1)S(1)} %get-tuple-element.38.refs_0_.pair.pair_ref, bf16[2,128,128]{2,1,0:T(8,128)(2,1)S(1)} %get-tuple-element.39.refs_0_, bf16[2,128,128]{2,1,0:T(8,128)(2,1)S(1)} %collective-permute-done.1.refs_1_, ...), custom_call_target="tpu_custom_call" | custom-call | flops 335544320 | bytes 25165824 | tf_op jit(solution)/shard_map/backward_second/pallas_call | solution.py:490
  30.2 1.6 %collective-permute-start.7 = (bf16[128,768]{1,0:T(8,128)(2,1)S(1)}, bf16[128,768]{1,0:T(8,128)(2,1)S(1)}, u32[]{:S(2)}, u32[]{:S(2)}) collective-permute-start(bf16[128,768]{1,0:T(8,128)(2,1)S(1)} %get-tuple-element.56), channel_id=1, source_target_pairs={{0,16},{8,24},{16,0},{24,8},{1,17},{9,25},{17,1},{25,9},{2,18},{10... | collective-permute-start | bytes 589832 | tf_op jit(solution)/shard_map/ppermute | solution.py:320
  31.7 2.3 %backward_left.1 = (bf16[1024,384]{1,0:T(8,128)(2,1)S(1)}, f32[1032,128]{1,0:T(8,128)S(1)}, bf16[128,512]{1,0:T(8,128)(2,1)S(1)}) custom-call(f32[1024,128]{1,0:T(8,128)S(1)} %get-tuple-element.52.up_in_ref.up_ref, bf16[2,128,768]{2,1,0:T(8,128)(2,1)S(1)} %get-tuple-element.40.refs_4_.weights, f32[2,1280]{1,0:T(2,128)S(1)} %get-tuple-element.41.refs_5_.vectors, ...), custom_call_target="tpu_custom_call" | custom-call | flops 335544320 | bytes 12582912 | tf_op jit(solution)/shard_map/backward_left/pallas_call | solution.py:508
  34.0 0.6 %collective-permute-start.9 = (bf16[128,512]{1,0:T(8,128)(2,1)S(1)}, bf16[128,512]{1,0:T(8,128)(2,1)S(1)}, u32[]{:S(2)}, u32[]{:S(2)}) collective-permute-start(bf16[128,512]{1,0:T(8,128)(2,1)S(1)} %get-tuple-element.58), channel_id=1, source_target_pairs={{0,16},{8,24},{16,0},{24,8},{1,17},{9,25},{17,1},{25,9},{2,18},{10... | collective-permute-start | bytes 393224 | tf_op jit(solution)/shard_map/ppermute | solution.py:320
  34.6 1.7 %backward_right.1 = (bf16[1024,256]{1,0:T(8,128)(2,1)S(1)}, bf16[128,256]{1,0:T(8,128)(2,1)S(1)}) custom-call(f32[1032,128]{1,0:T(8,128)S(1)} %get-tuple-element.54.d_product_ref, f32[2,2,1032,128]{3,2,1,0:T(8,128)S(1)} %get-tuple-element.42.refs_6_.refs_0_, f32[2,2,1032,128]{3,2,1,0:T(8,128)S(1)} %get-tuple-element.43.refs_7_.refs_1_, ...), custom_call_target="tpu_custom_call" | custom-call | flops 335544320 | bytes 12582912 | tf_op jit(solution)/shard_map/backward_right/pallas_call | solution.py:523
  36.4 0.7 %collective-permute-done.7 = bf16[128,768]{1,0:T(8,128)(2,1)S(1)} collective-permute-done((bf16[128,768]{1,0:T(8,128)(2,1)S(1)}, bf16[128,768]{1,0:T(8,128)(2,1)S(1)}, u32[]{:S(2)}, u32[]{:S(2)}) %collective-permute-start.7) | collective-permute-done | bytes 196640 | tf_op jit(solution)/shard_map/ppermute | solution.py:320
  37.1 0.1 collective-permute-start.8
  37.2 1.9 %collective-permute-done.9 = bf16[128,512]{1,0:T(8,128)(2,1)S(1)} collective-permute-done((bf16[128,512]{1,0:T(8,128)(2,1)S(1)}, bf16[128,512]{1,0:T(8,128)(2,1)S(1)}, u32[]{:S(2)}, u32[]{:S(2)}) %collective-permute-start.9) | collective-permute-done | bytes 131104 | tf_op jit(solution)/shard_map/ppermute | solution.py:320
  39.1 0.1 collective-permute-start.10
  39.2 0.0 collective-permute-done.8.rest_near
  39.2 0.6 %collective-permute-start.11 = (bf16[128,256]{1,0:T(8,128)(2,1)S(1)}, bf16[128,256]{1,0:T(8,128)(2,1)S(1)}, u32[]{:S(2)}, u32[]{:S(2)}) collective-permute-start(bf16[128,256]{1,0:T(8,128)(2,1)S(1)} %add_convert_fusion.2.right), channel_id=1, source_target_pairs={{0,16},{8,24},{16,0},{24,8},{1,17},{9,25},{17,1},{25,9},{2,18},{10... | collective-permute-start | bytes 196616 | tf_op jit(solution)/shard_map/ppermute | solution.py:320
  39.8 1.0 %own_rows.1 = bf16[128,128]{1,0:T(8,128)(2,1)} custom-call(bf16[2,144,128]{2,1,0:T(8,128)(2,1)S(1)} %get-tuple-element.38.refs_0_.pair.pair_ref, f32[1024,128]{1,0:T(8,128)S(1)} %get-tuple-element.52.up_in_ref.up_ref, bf16[1024,384]{1,0:T(8,128)(2,1)S(1)} %get-tuple-element.53.d_left_ref, bf16[1024,256]{1,0:T(8,128)(2,1)S(1)} %get-tuple-element.55.d_right_ref, ...), custom_call_target="tpu_custom_call" | custom-call | flops 335544320 | bytes 4194304 | tf_op jit(solution)/shard_map/own_rows/pallas_call | solution.py:535
  40.8 0.0 collective-permute-done.10.left_near
  40.8 2.9 %collective-permute-done.11.right_far = bf16[128,256]{1,0:T(8,128)(2,1)S(1)} collective-permute-done((bf16[128,256]{1,0:T(8,128)(2,1)S(1)}, bf16[128,256]{1,0:T(8,128)(2,1)S(1)}, u32[]{:S(2)}, u32[]{:S(2)}) %collective-permute-start.11) | collective-permute-done | bytes 65568 | tf_op jit(solution)/shard_map/ppermute | solution.py:320
  43.8 1.0 %add_grads.1 = (f32[2,128,640]{2,1,0:T(8,128)}, f32[2,128,128]{2,1,0:T(8,128)}) custom-call(bf16[128,1024]{1,0:T(8,128)(2,1)S(1)} %pad_maximum_fusion.rest, bf16[128,1024]{1,0:T(8,128)(2,1)S(1)} %collective-permute-done.8.rest_near, bf16[128,512]{1,0:T(8,128)(2,1)S(1)} %add_convert_fusion.1.left, bf16[128,512]{1,0:T(8,128)(2,1)S(1)} %collective-permute-done.10.left_near, ...), custom_call_target="tpu_custom_call" | custom-call | tf_op jit(solution)/shard_map/add_grads/pallas_call | solution.py:552
  (6 shorter events, 0.2 us)
Async XLA Ops:
  2.5 4.6 %copy-start = (bf16[272,128]{1,0:T(8,128)(2,1)S(1)}, bf16[272,128]{1,0:T(8,128)(2,1)}, u32[]{:S(2)}) copy-start(bf16[272,128]{1,0:T(8,128)(2,1)} %get-tuple-element.32.near_ref) | copy-start | bytes 208900
  2.5 4.6 %collective-permute-start = (bf16[272,128]{1,0:T(8,128)(2,1)}, bf16[272,128]{1,0:T(8,128)(2,1)S(1)}, u32[]{:S(2)}, u32[]{:S(2)}) collective-permute-start(bf16[272,128]{1,0:T(8,128)(2,1)} %get-tuple-element.32.near_ref), channel_id=1, source_target_pairs={{0,1},{1,0},{2,3},{3,2},{4,5},{5,4},{6,7},{7,6},{8,9},{9,8},{10,11... | collective-permute-start | bytes 208904 | tf_op jit(solution)/shard_map/ppermute | solution.py:320
  4.1 1.0 %copy-start.1 = (bf16[2,128,768]{2,1,0:T(8,128)(2,1)S(1)}, bf16[2,128,768]{2,1,0:T(8,128)(2,1)}, u32[]{:S(2)}) copy-start(bf16[2,128,768]{2,1,0:T(8,128)(2,1)} %get-tuple-element.33.weights_in) | copy-start | bytes 1179652
  5.1 0.7 %copy-start.2 = (f32[2,1280]{1,0:T(2,128)S(1)}, f32[2,1280]{1,0:T(2,128)}, u32[]{:S(2)}) copy-start(f32[2,1280]{1,0:T(2,128)} %get-tuple-element.34.vectors_in) | copy-start | bytes 30724
  7.1 6.6 %collective-permute-start.6 = (bf16[2,144,128]{2,1,0:T(8,128)(2,1)S(1)}, bf16[2,144,128]{2,1,0:T(8,128)(2,1)S(1)}, u32[]{:S(2)}, u32[]{:S(2)}) collective-permute-start(bf16[2,144,128]{2,1,0:T(8,128)(2,1)S(1)} %get-tuple-element.38.refs_0_.pair.pair_ref), channel_id=1, source_target_pairs={{0,4},{1,5},{2,6},{3,7},{4,0},{5,1},{6,2},{7,3},{8,12},{9,13},{10,... | collective-permute-start | bytes 221192 | tf_op jit(solution)/shard_map/ppermute | solution.py:320
  7.2 12.1 %collective-permute-start.5 = (bf16[2,144,128]{2,1,0:T(8,128)(2,1)S(1)}, bf16[2,144,128]{2,1,0:T(8,128)(2,1)S(1)}, u32[]{:S(2)}, u32[]{:S(2)}) collective-permute-start(bf16[2,144,128]{2,1,0:T(8,128)(2,1)S(1)} %get-tuple-element.38.refs_0_.pair.pair_ref), channel_id=1, source_target_pairs={{0,6},{1,7},{2,4},{3,5},{4,2},{5,3},{6,0},{7,1},{8,14},{9,15},{10,... | collective-permute-start | bytes 221192 | tf_op jit(solution)/shard_map/ppermute | solution.py:320
  10.2 9.1 %collective-permute-start.4 = (bf16[2,144,128]{2,1,0:T(8,128)(2,1)S(1)}, bf16[2,144,128]{2,1,0:T(8,128)(2,1)S(1)}, u32[]{:S(2)}, u32[]{:S(2)}) collective-permute-start(bf16[2,144,128]{2,1,0:T(8,128)(2,1)S(1)} %get-tuple-element.38.refs_0_.pair.pair_ref), channel_id=1, source_target_pairs={{0,2},{1,3},{2,0},{3,1},{4,6},{5,7},{6,4},{7,5},{8,10},{9,11},{10,... | collective-permute-start | bytes 221192 | tf_op jit(solution)/shard_map/ppermute | solution.py:320
  11.6 13.8 %collective-permute-start.3 = (bf16[2,128,128]{2,1,0:T(8,128)(2,1)S(1)}, bf16[2,128,128]{2,1,0:T(8,128)(2,1)S(1)}, u32[]{:S(2)}, u32[]{:S(2)}) collective-permute-start(bf16[2,128,128]{2,1,0:T(8,128)(2,1)S(1)} %get-tuple-element.39.refs_0_), channel_id=1, source_target_pairs={{0,4},{1,5},{2,6},{3,7},{4,0},{5,1},{6,2},{7,3},{8,12},{9,13},{10,... | collective-permute-start | bytes 196616 | tf_op jit(solution)/shard_map/ppermute | solution.py:320
  11.7 13.7 %collective-permute-start.2 = (bf16[2,128,128]{2,1,0:T(8,128)(2,1)S(1)}, bf16[2,128,128]{2,1,0:T(8,128)(2,1)S(1)}, u32[]{:S(2)}, u32[]{:S(2)}) collective-permute-start(bf16[2,128,128]{2,1,0:T(8,128)(2,1)S(1)} %get-tuple-element.39.refs_0_), channel_id=1, source_target_pairs={{0,6},{1,7},{2,4},{3,5},{4,2},{5,3},{6,0},{7,1},{8,14},{9,15},{10,... | collective-permute-start | bytes 196616 | tf_op jit(solution)/shard_map/ppermute | solution.py:320
  13.7 11.7 %collective-permute-start.1 = (bf16[2,128,128]{2,1,0:T(8,128)(2,1)S(1)}, bf16[2,128,128]{2,1,0:T(8,128)(2,1)S(1)}, u32[]{:S(2)}, u32[]{:S(2)}) collective-permute-start(bf16[2,128,128]{2,1,0:T(8,128)(2,1)S(1)} %get-tuple-element.39.refs_0_), channel_id=1, source_target_pairs={{0,2},{1,3},{2,0},{3,1},{4,6},{5,7},{6,4},{7,5},{8,10},{9,11},{10,... | collective-permute-start | bytes 196616 | tf_op jit(solution)/shard_map/ppermute | solution.py:320
  30.2 6.9 %collective-permute-start.7 = (bf16[128,768]{1,0:T(8,128)(2,1)S(1)}, bf16[128,768]{1,0:T(8,128)(2,1)S(1)}, u32[]{:S(2)}, u32[]{:S(2)}) collective-permute-start(bf16[128,768]{1,0:T(8,128)(2,1)S(1)} %get-tuple-element.56), channel_id=1, source_target_pairs={{0,16},{8,24},{16,0},{24,8},{1,17},{9,25},{17,1},{25,9},{2,18},{10... | collective-permute-start | bytes 589832 | tf_op jit(solution)/shard_map/ppermute | solution.py:320
  34.0 5.0 %collective-permute-start.9 = (bf16[128,512]{1,0:T(8,128)(2,1)S(1)}, bf16[128,512]{1,0:T(8,128)(2,1)S(1)}, u32[]{:S(2)}, u32[]{:S(2)}) collective-permute-start(bf16[128,512]{1,0:T(8,128)(2,1)S(1)} %get-tuple-element.58), channel_id=1, source_target_pairs={{0,16},{8,24},{16,0},{24,8},{1,17},{9,25},{17,1},{25,9},{2,18},{10... | collective-permute-start | bytes 393224 | tf_op jit(solution)/shard_map/ppermute | solution.py:320
  37.1 2.1 %collective-permute-start.8 = (bf16[128,1024]{1,0:T(8,128)(2,1)S(1)}, bf16[128,1024]{1,0:T(8,128)(2,1)S(1)}, u32[]{:S(2)}, u32[]{:S(2)}) collective-permute-start(bf16[128,1024]{1,0:T(8,128)(2,1)S(1)} %pad_maximum_fusion.rest), channel_id=1, source_target_pairs={{0,8},{8,0},{16,24},{24,16},{1,9},{9,1},{17,25},{25,17},{2,10},{10... | collective-permute-start | bytes 786440 | tf_op jit(solution)/shard_map/ppermute | solution.py:320
  39.1 1.7 %collective-permute-start.10 = (bf16[128,512]{1,0:T(8,128)(2,1)S(1)}, bf16[128,512]{1,0:T(8,128)(2,1)S(1)}, u32[]{:S(2)}, u32[]{:S(2)}) collective-permute-start(bf16[128,512]{1,0:T(8,128)(2,1)S(1)} %add_convert_fusion.1.left), channel_id=1, source_target_pairs={{0,8},{8,0},{16,24},{24,16},{1,9},{9,1},{17,25},{25,17},{2,10},{10... | collective-permute-start | bytes 393224 | tf_op jit(solution)/shard_map/ppermute | solution.py:320
  39.2 4.5 %collective-permute-start.11 = (bf16[128,256]{1,0:T(8,128)(2,1)S(1)}, bf16[128,256]{1,0:T(8,128)(2,1)S(1)}, u32[]{:S(2)}, u32[]{:S(2)}) collective-permute-start(bf16[128,256]{1,0:T(8,128)(2,1)S(1)} %add_convert_fusion.2.right), channel_id=1, source_target_pairs={{0,16},{8,24},{16,0},{24,8},{1,17},{9,25},{17,1},{25,9},{2,18},{10... | collective-permute-start | bytes 196616 | tf_op jit(solution)/shard_map/ppermute | solution.py:320

commit v21 on v19

--- a/solution.py
+++ b/solution.py
@@ -75,7 +75,7 @@
     return d_branch, d_gate, norm_vjp(p_hat, p_rstd, d_mixed)
 
 
-def contract(n, first, x, y, swapped=False):
+def contract(n, first, x, y, swapped=False, pitch=0):
     lanes = y.shape[1]
     tiles = (n // 8, 8, lanes)
 
@@ -83,7 +83,7 @@
         return e * n + first + a if swapped else (first + a) * n + e
 
     def step(e, totals):
-        block = y[pl.ds(pl.multiple_of(e * n, n), n), :].reshape(tiles)
+        block = y[pl.ds(pl.multiple_of(e * (pitch or n), 8), n), :].reshape(tiles)
         return tuple(
             totals[a] + x[pl.ds(row(a, e), 8, stride=0), :][None] * block
             for a in range(BLOCK_ROWS)
@@ -162,7 +162,7 @@
             here = block(t, STEP_ROWS, n)
             x, y = edges_s.at[u, 0], edges_s.at[1, 1] if u == 1 else right_t_s
             product = [
-                contract(n, t * STEP_ROWS + r, x, y, u == 1)
+                contract(n, t * STEP_ROWS + r, x, y, u == 1, (1 - u) * (n + 8))
                 for r in range(0, STEP_ROWS, BLOCK_ROWS)
             ]
             p_hat, p_rstd, mixed, branch = mix(
@@ -187,7 +187,7 @@
 
 def store_swapped(ref, rows, n, first, values):
     for r in range(rows):
-        ref[pl.ds(first + r, n, stride=n), :] = values[r * n : (r + 1) * n]
+        ref[pl.ds(first + r, n, stride=n + 8), :] = values[r * n : (r + 1) * n]
 
 
 def backward_second(n, jumps, pair, *refs):
@@ -218,7 +218,9 @@
         )
         d_out = dot(mixed_s[here, :], d_branch, ((0,), (0,)))
         d_pre_s[here, 4 * h :] = d_gate
-        d_product_s[1, here, :] = d_product
+        for r in range(STEP_ROWS):
+            row = pl.ds(pl.multiple_of((t * STEP_ROWS + r) * (n + 8), 8), n)
+            d_product_s[1, row, :] = d_product[r * n : (r + 1) * n]
         store_swapped(d_product_s.at[0], STEP_ROWS, n, t * STEP_ROWS, d_product)
         grads_ref[:, width:] = d_out.astype(BF16)
 
@@ -228,7 +230,7 @@
     def _(step):
         side, t = step // blocks, step % blocks
         d_edges_s[side, block(t, BLOCK_ROWS, n), :] = contract(
-            n, t * BLOCK_ROWS, edges_s.at[1 - side], d_product_s.at[side]
+            n, t * BLOCK_ROWS, edges_s.at[1 - side], d_product_s.at[side], pitch=n + 8
         )
 
     @pl.loop(0, n // STEP_ROWS)
@@ -409,6 +411,7 @@
     width = proj_weight.shape[2]
     cells, pairs = rows * n, n * n
     plane = (pairs + 8, h)
+    wide_plane = (n * (n + 8), h)
     kept = [jax.ShapeDtypeStruct((2, 2) + plane, F32)] * 2
     kept += [jax.ShapeDtypeStruct((2,) + plane, F32)] * 6
     kept += [jax.ShapeDtypeStruct((2, pairs, h), BF16)] * 2
@@ -480,7 +483,7 @@
         out_shape=kept,
         in_specs=[vmem] * (half + 2),
         out_specs=(vmem,) * KEPT,
-        scratch_shapes=[pltpu.VMEM((pairs, c), BF16), pltpu.VMEM(plane, F32)],
+        scratch_shapes=[pltpu.VMEM((pairs, c), BF16), pltpu.VMEM(wide_plane, F32)],
         compiler_params=params,
         cost_estimate=cost(64),
         name="forward",
@@ -493,7 +496,7 @@
         in_specs=[vmem] * (3 + half + KEPT),
         out_specs=(vmem, vmem),
         scratch_shapes=[
-            double,
+            pltpu.VMEM((2,) + wide_plane, F32),
             double,
             pltpu.VMEM((pairs, width), BF16),
             pltpu.VMEM((pairs, c), BF16),

time: 44.6 us -> 43.7 us (0.980)
  Pallas kernels: 18.3 us -> 17.5 us
    pallas_call x1, Pallas kernels: 4.68 us -> 4.1 us  [crop_shards(): pl.pallas_call(functools.partial(backward_second, n, jumps), out_shape=(j...]
where the time goes in v21:
time: 43.7 us; the launch traced here: 43.4 us
  Pallas kernels  17.5 us (40%)
  starting transfers between devices  15.3 us (35%)
  waiting for transfers between devices  8.07 us (18%)
  local copies, waits for them, and re-layouts  1.7 us (4%)
  between operations  0.76 us (2%)
    ppermute x12, starting transfers between devices, exchange(): return lax.ppermute(value, axis, [(d, d ^ step) for d in range(size)])  15.3 us
    ppermute x12, waiting for transfers between devices, exchange(): return lax.ppermute(value, axis, [(d, d ^ step) for d in range(size)])  8.07 us
    pallas_call x1, Pallas kernels, crop_shards(): pl.pallas_call(functools.partial(forward, n, jumps), out_shape=kept, in_s...  5.39 us
    pallas_call x1, Pallas kernels, crop_shards(): pl.pallas_call(functools.partial(backward_second, n, jumps), out_shape=(j...  4.1 us
    pallas_call x1, Pallas kernels, crop_shards(): pl.pallas_call(functools.partial(backward_left, n), out_shape=(jax.ShapeD...  2.32 us
    pallas_call x1, Pallas kernels, crop_shards(): pl.pallas_call(prepare, out_shape=(jax.ShapeDtypeStruct((2 * cells + TAIL...  1.88 us
    pallas_call x1, Pallas kernels, crop_shards(): pl.pallas_call(functools.partial(backward_right, n), out_shape=(jax.Shape...  1.77 us
    unnamed x6, local copies, waits for them, and re-layouts  1.7 us
  transfers between devices with their start and end apart: 12, of which 5 were waited for; matrix products, arithmetic and copies ran while one was open for 0% of the time, Pallas kernels for 24%

profile of v21, /device:TPU:16, one launch (start us, length us, event | category | flops | bytes accessed | tf_op | source)
XLA Modules:
  0.0 43.4 jit_solution(8633544776255857906)
XLA Ops:
  0.6 1.9 %prepare.1 = (bf16[272,128]{1,0:T(8,128)(2,1)}, bf16[2,128,768]{2,1,0:T(8,128)(2,1)}, f32[2,1280]{1,0:T(2,128)}) custom-call(s32[1]{0:T(128)} %bitcast.index_ref, s32[4,32]{1,0:T(4,128)} %bitcast.8, bf16[128,128]{1,0:T(8,128)(2,1)} %bitcast.6, bf16[128,128]{1,0:T(8,128)(2,1)} %bitcast.7, bf16[2,128,640]{2,1,0:T(8,128)(2,1)} %w.1, ...), custom_call_target="tpu_custom_call" | custom-call | tf_op jit(solution)/shard_map/prepare/pallas_call | solution.py:433
  2.5 0.0 copy-start
  2.5 1.6 %collective-permute-start = (bf16[272,128]{1,0:T(8,128)(2,1)}, bf16[272,128]{1,0:T(8,128)(2,1)S(1)}, u32[]{:S(2)}, u32[]{:S(2)}) collective-permute-start(bf16[272,128]{1,0:T(8,128)(2,1)} %get-tuple-element.32.near_ref), channel_id=1, source_target_pairs={{0,1},{1,0},{2,3},{3,2},{4,5},{5,4},{6,7},{7,6},{8,9},{9,8},{10,11... | collective-permute-start | bytes 208904 | tf_op jit(solution)/shard_map/ppermute | solution.py:323
  4.1 0.0 copy-start.1
  4.1 1.0 %copy-done.1 = bf16[2,128,768]{2,1,0:T(8,128)(2,1)S(1)} copy-done((bf16[2,128,768]{2,1,0:T(8,128)(2,1)S(1)}, bf16[2,128,768]{2,1,0:T(8,128)(2,1)}, u32[]{:S(2)}) %copy-start.1) | copy-done | bytes 393240
  5.1 0.0 copy-start.2
  5.1 0.7 %copy-done.2 = f32[2,1280]{1,0:T(2,128)S(1)} copy-done((f32[2,1280]{1,0:T(2,128)S(1)}, f32[2,1280]{1,0:T(2,128)}, u32[]{:S(2)}) %copy-start.2) | copy-done | bytes 10264
  5.8 1.3 %collective-permute-done.far_ref = bf16[272,128]{1,0:T(8,128)(2,1)S(1)} collective-permute-done((bf16[272,128]{1,0:T(8,128)(2,1)}, bf16[272,128]{1,0:T(8,128)(2,1)S(1)}, u32[]{:S(2)}, u32[]{:S(2)}) %collective-permute-start) | collective-permute-done | bytes 69664 | tf_op jit(solution)/shard_map/ppermute | solution.py:323
  7.1 0.0 copy-done
  7.1 0.1 collective-permute-start.6
  7.2 3.0 %collective-permute-start.5 = (bf16[2,144,128]{2,1,0:T(8,128)(2,1)S(1)}, bf16[2,144,128]{2,1,0:T(8,128)(2,1)S(1)}, u32[]{:S(2)}, u32[]{:S(2)}) collective-permute-start(bf16[2,144,128]{2,1,0:T(8,128)(2,1)S(1)} %get-tuple-element.38.refs_0_.pair.pair_ref), channel_id=1, source_target_pairs={{0,6},{1,7},{2,4},{3,5},{4,2},{5,3},{6,0},{7,1},{8,14},{9,15},{10,... | collective-permute-start | bytes 221192 | tf_op jit(solution)/shard_map/ppermute | solution.py:323
  10.2 1.3 %collective-permute-start.4 = (bf16[2,144,128]{2,1,0:T(8,128)(2,1)S(1)}, bf16[2,144,128]{2,1,0:T(8,128)(2,1)S(1)}, u32[]{:S(2)}, u32[]{:S(2)}) collective-permute-start(bf16[2,144,128]{2,1,0:T(8,128)(2,1)S(1)} %get-tuple-element.38.refs_0_.pair.pair_ref), channel_id=1, source_target_pairs={{0,2},{1,3},{2,0},{3,1},{4,6},{5,7},{6,4},{7,5},{8,10},{9,11},{10,... | collective-permute-start | bytes 221192 | tf_op jit(solution)/shard_map/ppermute | solution.py:323
  11.6 0.1 collective-permute-start.3
  11.7 2.0 %collective-permute-start.2 = (bf16[2,128,128]{2,1,0:T(8,128)(2,1)S(1)}, bf16[2,128,128]{2,1,0:T(8,128)(2,1)S(1)}, u32[]{:S(2)}, u32[]{:S(2)}) collective-permute-start(bf16[2,128,128]{2,1,0:T(8,128)(2,1)S(1)} %get-tuple-element.39.refs_0_), channel_id=1, source_target_pairs={{0,6},{1,7},{2,4},{3,5},{4,2},{5,3},{6,0},{7,1},{8,14},{9,15},{10,... | collective-permute-start | bytes 196616 | tf_op jit(solution)/shard_map/ppermute | solution.py:323
  13.7 0.0 collective-permute-done.6.refs_3_
  13.7 4.3 %collective-permute-start.1 = (bf16[2,128,128]{2,1,0:T(8,128)(2,1)S(1)}, bf16[2,128,128]{2,1,0:T(8,128)(2,1)S(1)}, u32[]{:S(2)}, u32[]{:S(2)}) collective-permute-start(bf16[2,128,128]{2,1,0:T(8,128)(2,1)S(1)} %get-tuple-element.39.refs_0_), channel_id=1, source_target_pairs={{0,2},{1,3},{2,0},{3,1},{4,6},{5,7},{6,4},{7,5},{8,10},{9,11},{10,... | collective-permute-start | bytes 196616 | tf_op jit(solution)/shard_map/ppermute | solution.py:323
  18.0 1.3 %collective-permute-done.5.refs_2_ = bf16[2,144,128]{2,1,0:T(8,128)(2,1)S(1)} collective-permute-done((bf16[2,144,128]{2,1,0:T(8,128)(2,1)S(1)}, bf16[2,144,128]{2,1,0:T(8,128)(2,1)S(1)}, u32[]{:S(2)}, u32[]{:S(2)}) %collective-permute-start.5) | collective-permute-done | bytes 73760 | tf_op jit(solution)/shard_map/ppermute | solution.py:323
  19.3 0.0 collective-permute-done.4.refs_1_
  19.4 5.4 %forward.1 = (f32[2,2,1032,128]{3,2,1,0:T(8,128)S(1)}, f32[2,2,1032,128]{3,2,1,0:T(8,128)S(1)}, f32[2,1032,128]{2,1,0:T(8,128)S(1)}, f32[2,1032,128]{2,1,0:T(8,1...) custom-call(bf16[2,144,128]{2,1,0:T(8,128)(2,1)S(1)} %get-tuple-elem, ...), custom_call_target="tpu_custom_call" | custom-call | flops 335544320 | bytes 33554432 | tf_op jit(solution)/shard_map/forward/pallas_call | solution.py:481
  24.7 0.0 collective-permute-done.3.refs_3_
  24.7 0.0 collective-permute-done.2.refs_2_
  24.8 0.0 collective-permute-done.1.refs_1_
  24.8 4.1 %backward_second.1 = (f32[1024,128]{1,0:T(8,128)S(1)}, bf16[128,768]{1,0:T(8,128)(2,1)S(1)}) custom-call(bf16[2,144,128]{2,1,0:T(8,128)(2,1)S(1)} %get-tuple-element.38.refs_0_.pair.pair_ref, bf16[2,128,128]{2,1,0:T(8,128)(2,1)S(1)} %get-tuple-element.39.refs_0_, bf16[2,128,128]{2,1,0:T(8,128)(2,1)S(1)} %collective-permute-done.1.refs_1_, ...), custom_call_target="tpu_custom_call" | custom-call | flops 335544320 | bytes 25165824 | tf_op jit(solution)/shard_map/backward_second/pallas_call | solution.py:493
  28.9 1.6 %collective-permute-start.7 = (bf16[128,768]{1,0:T(8,128)(2,1)S(1)}, bf16[128,768]{1,0:T(8,128)(2,1)S(1)}, u32[]{:S(2)}, u32[]{:S(2)}) collective-permute-start(bf16[128,768]{1,0:T(8,128)(2,1)S(1)} %get-tuple-element.56), channel_id=1, source_target_pairs={{0,16},{8,24},{16,0},{24,8},{1,17},{9,25},{17,1},{25,9},{2,18},{10... | collective-permute-start | bytes 589832 | tf_op jit(solution)/shard_map/ppermute | solution.py:323
  30.4 2.3 %backward_left.1 = (bf16[1024,384]{1,0:T(8,128)(2,1)S(1)}, f32[1032,128]{1,0:T(8,128)S(1)}, bf16[128,512]{1,0:T(8,128)(2,1)S(1)}) custom-call(f32[1024,128]{1,0:T(8,128)S(1)} %get-tuple-element.52.up_in_ref.up_ref, bf16[2,128,768]{2,1,0:T(8,128)(2,1)S(1)} %get-tuple-element.40.refs_4_.weights, f32[2,1280]{1,0:T(2,128)S(1)} %get-tuple-element.41.refs_5_.vectors, ...), custom_call_target="tpu_custom_call" | custom-call | flops 335544320 | bytes 12582912 | tf_op jit(solution)/shard_map/backward_left/pallas_call | solution.py:511
  32.8 0.6 %collective-permute-start.9 = (bf16[128,512]{1,0:T(8,128)(2,1)S(1)}, bf16[128,512]{1,0:T(8,128)(2,1)S(1)}, u32[]{:S(2)}, u32[]{:S(2)}) collective-permute-start(bf16[128,512]{1,0:T(8,128)(2,1)S(1)} %get-tuple-element.58), channel_id=1, source_target_pairs={{0,16},{8,24},{16,0},{24,8},{1,17},{9,25},{17,1},{25,9},{2,18},{10... | collective-permute-start | bytes 393224 | tf_op jit(solution)/shard_map/ppermute | solution.py:323
  33.3 1.8 %backward_right.1 = (bf16[1024,256]{1,0:T(8,128)(2,1)S(1)}, bf16[128,256]{1,0:T(8,128)(2,1)S(1)}) custom-call(f32[1032,128]{1,0:T(8,128)S(1)} %get-tuple-element.54.d_product_ref, f32[2,2,1032,128]{3,2,1,0:T(8,128)S(1)} %get-tuple-element.42.refs_6_.refs_0_, f32[2,2,1032,128]{3,2,1,0:T(8,128)S(1)} %get-tuple-element.43.refs_7_.refs_1_, ...), custom_call_target="tpu_custom_call" | custom-call | flops 335544320 | bytes 12582912 | tf_op jit(solution)/shard_map/backward_right/pallas_call | solution.py:527
  35.1 0.6 %collective-permute-done.7 = bf16[128,768]{1,0:T(8,128)(2,1)S(1)} collective-permute-done((bf16[128,768]{1,0:T(8,128)(2,1)S(1)}, bf16[128,768]{1,0:T(8,128)(2,1)S(1)}, u32[]{:S(2)}, u32[]{:S(2)}) %collective-permute-start.7) | collective-permute-done | bytes 196640 | tf_op jit(solution)/shard_map/ppermute | solution.py:323
  35.8 0.1 collective-permute-start.8
  35.9 1.9 %collective-permute-done.9 = bf16[128,512]{1,0:T(8,128)(2,1)S(1)} collective-permute-done((bf16[128,512]{1,0:T(8,128)(2,1)S(1)}, bf16[128,512]{1,0:T(8,128)(2,1)S(1)}, u32[]{:S(2)}, u32[]{:S(2)}) %collective-permute-start.9) | collective-permute-done | bytes 131104 | tf_op jit(solution)/shard_map/ppermute | solution.py:323
  37.8 0.1 collective-permute-start.10
  37.9 0.0 collective-permute-done.8.rest_near
  37.9 0.6 %collective-permute-start.11 = (bf16[128,256]{1,0:T(8,128)(2,1)S(1)}, bf16[128,256]{1,0:T(8,128)(2,1)S(1)}, u32[]{:S(2)}, u32[]{:S(2)}) collective-permute-start(bf16[128,256]{1,0:T(8,128)(2,1)S(1)} %add_convert_fusion.2.right), channel_id=1, source_target_pairs={{0,16},{8,24},{16,0},{24,8},{1,17},{9,25},{17,1},{25,9},{2,18},{10... | collective-permute-start | bytes 196616 | tf_op jit(solution)/shard_map/ppermute | solution.py:323
  38.5 1.0 %own_rows.1 = bf16[128,128]{1,0:T(8,128)(2,1)} custom-call(bf16[2,144,128]{2,1,0:T(8,128)(2,1)S(1)} %get-tuple-element.38.refs_0_.pair.pair_ref, f32[1024,128]{1,0:T(8,128)S(1)} %get-tuple-element.52.up_in_ref.up_ref, bf16[1024,384]{1,0:T(8,128)(2,1)S(1)} %get-tuple-element.53.d_left_ref, bf16[1024,256]{1,0:T(8,128)(2,1)S(1)} %get-tuple-element.55.d_right_ref, ...), custom_call_target="tpu_custom_call" | custom-call | flops 335544320 | bytes 4194304 | tf_op jit(solution)/shard_map/own_rows/pallas_call | solution.py:540
  39.6 0.0 collective-permute-done.10.left_near
  39.6 2.9 %collective-permute-done.11.right_far = bf16[128,256]{1,0:T(8,128)(2,1)S(1)} collective-permute-done((bf16[128,256]{1,0:T(8,128)(2,1)S(1)}, bf16[128,256]{1,0:T(8,128)(2,1)S(1)}, u32[]{:S(2)}, u32[]{:S(2)}) %collective-permute-start.11) | collective-permute-done | bytes 65568 | tf_op jit(solution)/shard_map/ppermute | solution.py:323
  42.5 0.9 %add_grads.1 = (f32[2,128,640]{2,1,0:T(8,128)}, f32[2,128,128]{2,1,0:T(8,128)}) custom-call(bf16[128,1024]{1,0:T(8,128)(2,1)S(1)} %pad_maximum_fusion.rest, bf16[128,1024]{1,0:T(8,128)(2,1)S(1)} %collective-permute-done.8.rest_near, bf16[128,512]{1,0:T(8,128)(2,1)S(1)} %add_convert_fusion.1.left, bf16[128,512]{1,0:T(8,128)(2,1)S(1)} %collective-permute-done.10.left_near, ...), custom_call_target="tpu_custom_call" | custom-call | tf_op jit(solution)/shard_map/add_grads/pallas_call | solution.py:557
  (6 shorter events, 0.2 us)
Async XLA Ops:
  2.5 4.6 %copy-start = (bf16[272,128]{1,0:T(8,128)(2,1)S(1)}, bf16[272,128]{1,0:T(8,128)(2,1)}, u32[]{:S(2)}) copy-start(bf16[272,128]{1,0:T(8,128)(2,1)} %get-tuple-element.32.near_ref) | copy-start | bytes 208900
  2.5 4.6 %collective-permute-start = (bf16[272,128]{1,0:T(8,128)(2,1)}, bf16[272,128]{1,0:T(8,128)(2,1)S(1)}, u32[]{:S(2)}, u32[]{:S(2)}) collective-permute-start(bf16[272,128]{1,0:T(8,128)(2,1)} %get-tuple-element.32.near_ref), channel_id=1, source_target_pairs={{0,1},{1,0},{2,3},{3,2},{4,5},{5,4},{6,7},{7,6},{8,9},{9,8},{10,11... | collective-permute-start | bytes 208904 | tf_op jit(solution)/shard_map/ppermute | solution.py:323
  4.1 1.0 %copy-start.1 = (bf16[2,128,768]{2,1,0:T(8,128)(2,1)S(1)}, bf16[2,128,768]{2,1,0:T(8,128)(2,1)}, u32[]{:S(2)}) copy-start(bf16[2,128,768]{2,1,0:T(8,128)(2,1)} %get-tuple-element.33.weights_in) | copy-start | bytes 1179652
  5.1 0.7 %copy-start.2 = (f32[2,1280]{1,0:T(2,128)S(1)}, f32[2,1280]{1,0:T(2,128)}, u32[]{:S(2)}) copy-start(f32[2,1280]{1,0:T(2,128)} %get-tuple-element.34.vectors_in) | copy-start | bytes 30724
  7.1 6.6 %collective-permute-start.6 = (bf16[2,144,128]{2,1,0:T(8,128)(2,1)S(1)}, bf16[2,144,128]{2,1,0:T(8,128)(2,1)S(1)}, u32[]{:S(2)}, u32[]{:S(2)}) collective-permute-start(bf16[2,144,128]{2,1,0:T(8,128)(2,1)S(1)} %get-tuple-element.38.refs_0_.pair.pair_ref), channel_id=1, source_target_pairs={{0,4},{1,5},{2,6},{3,7},{4,0},{5,1},{6,2},{7,3},{8,12},{9,13},{10,... | collective-permute-start | bytes 221192 | tf_op jit(solution)/shard_map/ppermute | solution.py:323
  7.2 12.1 %collective-permute-start.5 = (bf16[2,144,128]{2,1,0:T(8,128)(2,1)S(1)}, bf16[2,144,128]{2,1,0:T(8,128)(2,1)S(1)}, u32[]{:S(2)}, u32[]{:S(2)}) collective-permute-start(bf16[2,144,128]{2,1,0:T(8,128)(2,1)S(1)} %get-tuple-element.38.refs_0_.pair.pair_ref), channel_id=1, source_target_pairs={{0,6},{1,7},{2,4},{3,5},{4,2},{5,3},{6,0},{7,1},{8,14},{9,15},{10,... | collective-permute-start | bytes 221192 | tf_op jit(solution)/shard_map/ppermute | solution.py:323
  10.2 9.1 %collective-permute-start.4 = (bf16[2,144,128]{2,1,0:T(8,128)(2,1)S(1)}, bf16[2,144,128]{2,1,0:T(8,128)(2,1)S(1)}, u32[]{:S(2)}, u32[]{:S(2)}) collective-permute-start(bf16[2,144,128]{2,1,0:T(8,128)(2,1)S(1)} %get-tuple-element.38.refs_0_.pair.pair_ref), channel_id=1, source_target_pairs={{0,2},{1,3},{2,0},{3,1},{4,6},{5,7},{6,4},{7,5},{8,10},{9,11},{10,... | collective-permute-start | bytes 221192 | tf_op jit(solution)/shard_map/ppermute | solution.py:323
  11.6 13.2 %collective-permute-start.3 = (bf16[2,128,128]{2,1,0:T(8,128)(2,1)S(1)}, bf16[2,128,128]{2,1,0:T(8,128)(2,1)S(1)}, u32[]{:S(2)}, u32[]{:S(2)}) collective-permute-start(bf16[2,128,128]{2,1,0:T(8,128)(2,1)S(1)} %get-tuple-element.39.refs_0_), channel_id=1, source_target_pairs={{0,4},{1,5},{2,6},{3,7},{4,0},{5,1},{6,2},{7,3},{8,12},{9,13},{10,... | collective-permute-start | bytes 196616 | tf_op jit(solution)/shard_map/ppermute | solution.py:323
  11.7 13.0 %collective-permute-start.2 = (bf16[2,128,128]{2,1,0:T(8,128)(2,1)S(1)}, bf16[2,128,128]{2,1,0:T(8,128)(2,1)S(1)}, u32[]{:S(2)}, u32[]{:S(2)}) collective-permute-start(bf16[2,128,128]{2,1,0:T(8,128)(2,1)S(1)} %get-tuple-element.39.refs_0_), channel_id=1, source_target_pairs={{0,6},{1,7},{2,4},{3,5},{4,2},{5,3},{6,0},{7,1},{8,14},{9,15},{10,... | collective-permute-start | bytes 196616 | tf_op jit(solution)/shard_map/ppermute | solution.py:323
  13.7 11.0 %collective-permute-start.1 = (bf16[2,128,128]{2,1,0:T(8,128)(2,1)S(1)}, bf16[2,128,128]{2,1,0:T(8,128)(2,1)S(1)}, u32[]{:S(2)}, u32[]{:S(2)}) collective-permute-start(bf16[2,128,128]{2,1,0:T(8,128)(2,1)S(1)} %get-tuple-element.39.refs_0_), channel_id=1, source_target_pairs={{0,2},{1,3},{2,0},{3,1},{4,6},{5,7},{6,4},{7,5},{8,10},{9,11},{10,... | collective-permute-start | bytes 196616 | tf_op jit(solution)/shard_map/ppermute | solution.py:323
  28.9 6.9 %collective-permute-start.7 = (bf16[128,768]{1,0:T(8,128)(2,1)S(1)}, bf16[128,768]{1,0:T(8,128)(2,1)S(1)}, u32[]{:S(2)}, u32[]{:S(2)}) collective-permute-start(bf16[128,768]{1,0:T(8,128)(2,1)S(1)} %get-tuple-element.56), channel_id=1, source_target_pairs={{0,16},{8,24},{16,0},{24,8},{1,17},{9,25},{17,1},{25,9},{2,18},{10... | collective-permute-start | bytes 589832 | tf_op jit(solution)/shard_map/ppermute | solution.py:323
  32.8 5.0 %collective-permute-start.9 = (bf16[128,512]{1,0:T(8,128)(2,1)S(1)}, bf16[128,512]{1,0:T(8,128)(2,1)S(1)}, u32[]{:S(2)}, u32[]{:S(2)}) collective-permute-start(bf16[128,512]{1,0:T(8,128)(2,1)S(1)} %get-tuple-element.58), channel_id=1, source_target_pairs={{0,16},{8,24},{16,0},{24,8},{1,17},{9,25},{17,1},{25,9},{2,18},{10... | collective-permute-start | bytes 393224 | tf_op jit(solution)/shard_map/ppermute | solution.py:323
  35.8 2.1 %collective-permute-start.8 = (bf16[128,1024]{1,0:T(8,128)(2,1)S(1)}, bf16[128,1024]{1,0:T(8,128)(2,1)S(1)}, u32[]{:S(2)}, u32[]{:S(2)}) collective-permute-start(bf16[128,1024]{1,0:T(8,128)(2,1)S(1)} %pad_maximum_fusion.rest), channel_id=1, source_target_pairs={{0,8},{8,0},{16,24},{24,16},{1,9},{9,1},{17,25},{25,17},{2,10},{10... | collective-permute-start | bytes 786440 | tf_op jit(solution)/shard_map/ppermute | solution.py:323
  37.8 1.7 %collective-permute-start.10 = (bf16[128,512]{1,0:T(8,128)(2,1)S(1)}, bf16[128,512]{1,0:T(8,128)(2,1)S(1)}, u32[]{:S(2)}, u32[]{:S(2)}) collective-permute-start(bf16[128,512]{1,0:T(8,128)(2,1)S(1)} %add_convert_fusion.1.left), channel_id=1, source_target_pairs={{0,8},{8,0},{16,24},{24,16},{1,9},{9,1},{17,25},{25,17},{2,10},{10... | collective-permute-start | bytes 393224 | tf_op jit(solution)/shard_map/ppermute | solution.py:323
  37.9 4.5 %collective-permute-start.11 = (bf16[128,256]{1,0:T(8,128)(2,1)S(1)}, bf16[128,256]{1,0:T(8,128)(2,1)S(1)}, u32[]{:S(2)}, u32[]{:S(2)}) collective-permute-start(bf16[128,256]{1,0:T(8,128)(2,1)S(1)} %add_convert_fusion.2.right), channel_id=1, source_target_pairs={{0,16},{8,24},{16,0},{24,8},{1,17},{9,25},{17,1},{25,9},{2,18},{10... | collective-permute-start | bytes 196616 | tf_op jit(solution)/shard_map/ppermute | solution.py:323

commit v22 on v21

--- a/solution.py
+++ b/solution.py
@@ -41,11 +41,11 @@
 
 
 def pair_mask_block(length, first_row, rows, n, lanes):
-    shape = (rows, n, lanes)
-    i = lax.broadcasted_iota(jnp.int32, shape, 0) + first_row
-    j = lax.broadcasted_iota(jnp.int32, shape, 1)
-    inside = jnp.where((i < length) & (j < length), 1.0, 0.0)
-    return inside.reshape(rows * n, lanes)
+    i = lax.broadcasted_iota(jnp.int32, (rows, 8, lanes), 0) + first_row
+    j = lax.broadcasted_iota(jnp.int32, (n, lanes), 0)
+    row_inside = jnp.where(i < length, 1.0, 0.0)
+    column_inside = jnp.where(j < length, 1.0, 0.0).reshape(1, n // 8, 8, lanes)
+    return (row_inside[:, None] * column_inside).reshape(rows * n, lanes)
 
 
 def project(x, mask, w, b, gain, shift):

time: 43.7 us -> 43.7 us (level)
  the two profiles are of different devices: /device:TPU:16 before, /device:TPU:20 now
where the time goes in v22:
time: 43.7 us; the launch traced here: 43.5 us
  Pallas kernels  17.5 us (40%)
  starting transfers between devices  14.3 us (33%)
  waiting for transfers between devices  9.06 us (21%)
  local copies, waits for them, and re-layouts  1.7 us (4%)
  between operations  0.75 us (2%)
    ppermute x12, starting transfers between devices, exchange(): return lax.ppermute(value, axis, [(d, d ^ step) for d in range(size)])  14.3 us
    ppermute x12, waiting for transfers between devices, exchange(): return lax.ppermute(value, axis, [(d, d ^ step) for d in range(size)])  9.06 us
    pallas_call x1, Pallas kernels, crop_shards(): pl.pallas_call(functools.partial(forward, n, jumps), out_shape=kept, in_s...  5.41 us
    pallas_call x1, Pallas kernels, crop_shards(): pl.pallas_call(functools.partial(backward_second, n, jumps), out_shape=(j...  4.1 us
    pallas_call x1, Pallas kernels, crop_shards(): pl.pallas_call(functools.partial(backward_left, n), out_shape=(jax.ShapeD...  2.32 us
    pallas_call x1, Pallas kernels, crop_shards(): pl.pallas_call(prepare, out_shape=(jax.ShapeDtypeStruct((2 * cells + TAIL...  1.88 us
    pallas_call x1, Pallas kernels, crop_shards(): pl.pallas_call(functools.partial(backward_right, n), out_shape=(jax.Shape...  1.77 us
    unnamed x6, local copies, waits for them, and re-layouts  1.7 us
  transfers between devices with their start and end apart: 12, of which 5 were waited for; matrix products, arithmetic and copies ran while one was open for 0% of the time, Pallas kernels for 24%

profile of v22, /device:TPU:20, one launch (start us, length us, event | category | flops | bytes accessed | tf_op | source)
XLA Modules:
  0.0 43.5 jit_solution(16918696355512638574)
XLA Ops:
  0.6 1.9 %prepare.1 = (bf16[272,128]{1,0:T(8,128)(2,1)}, bf16[2,128,768]{2,1,0:T(8,128)(2,1)}, f32[2,1280]{1,0:T(2,128)}) custom-call(s32[1]{0:T(128)} %bitcast.index_ref, s32[4,32]{1,0:T(4,128)} %bitcast.8, bf16[128,128]{1,0:T(8,128)(2,1)} %bitcast.6, bf16[128,128]{1,0:T(8,128)(2,1)} %bitcast.7, bf16[2,128,640]{2,1,0:T(8,128)(2,1)} %w.1, ...), custom_call_target="tpu_custom_call" | custom-call | tf_op jit(solution)/shard_map/prepare/pallas_call | solution.py:433
  2.5 0.0 copy-start
  2.5 0.6 %collective-permute-start = (bf16[272,128]{1,0:T(8,128)(2,1)}, bf16[272,128]{1,0:T(8,128)(2,1)S(1)}, u32[]{:S(2)}, u32[]{:S(2)}) collective-permute-start(bf16[272,128]{1,0:T(8,128)(2,1)} %get-tuple-element.32.near_ref), channel_id=1, source_target_pairs={{0,1},{1,0},{2,3},{3,2},{4,5},{5,4},{6,7},{7,6},{8,9},{9,8},{10,11... | collective-permute-start | bytes 208904 | tf_op jit(solution)/shard_map/ppermute | solution.py:323
  3.1 0.0 copy-start.1
  3.1 1.0 %copy-done.1 = bf16[2,128,768]{2,1,0:T(8,128)(2,1)S(1)} copy-done((bf16[2,128,768]{2,1,0:T(8,128)(2,1)S(1)}, bf16[2,128,768]{2,1,0:T(8,128)(2,1)}, u32[]{:S(2)}) %copy-start.1) | copy-done | bytes 393240
  4.1 0.0 copy-start.2
  4.1 0.7 %copy-done.2 = f32[2,1280]{1,0:T(2,128)S(1)} copy-done((f32[2,1280]{1,0:T(2,128)S(1)}, f32[2,1280]{1,0:T(2,128)}, u32[]{:S(2)}) %copy-start.2) | copy-done | bytes 10264
  4.8 2.3 %collective-permute-done.far_ref = bf16[272,128]{1,0:T(8,128)(2,1)S(1)} collective-permute-done((bf16[272,128]{1,0:T(8,128)(2,1)}, bf16[272,128]{1,0:T(8,128)(2,1)S(1)}, u32[]{:S(2)}, u32[]{:S(2)}) %collective-permute-start) | collective-permute-done | bytes 69664 | tf_op jit(solution)/shard_map/ppermute | solution.py:323
  7.1 0.0 copy-done
  7.1 0.4 collective-permute-start.6
  7.5 2.7 %collective-permute-start.5 = (bf16[2,144,128]{2,1,0:T(8,128)(2,1)S(1)}, bf16[2,144,128]{2,1,0:T(8,128)(2,1)S(1)}, u32[]{:S(2)}, u32[]{:S(2)}) collective-permute-start(bf16[2,144,128]{2,1,0:T(8,128)(2,1)S(1)} %get-tuple-element.38.refs_0_.pair.pair_ref), channel_id=1, source_target_pairs={{0,6},{1,7},{2,4},{3,5},{4,2},{5,3},{6,0},{7,1},{8,14},{9,15},{10,... | collective-permute-start | bytes 221192 | tf_op jit(solution)/shard_map/ppermute | solution.py:323
  10.2 1.3 %collective-permute-start.4 = (bf16[2,144,128]{2,1,0:T(8,128)(2,1)S(1)}, bf16[2,144,128]{2,1,0:T(8,128)(2,1)S(1)}, u32[]{:S(2)}, u32[]{:S(2)}) collective-permute-start(bf16[2,144,128]{2,1,0:T(8,128)(2,1)S(1)} %get-tuple-element.38.refs_0_.pair.pair_ref), channel_id=1, source_target_pairs={{0,2},{1,3},{2,0},{3,1},{4,6},{5,7},{6,4},{7,5},{8,10},{9,11},{10,... | collective-permute-start | bytes 221192 | tf_op jit(solution)/shard_map/ppermute | solution.py:323
  11.6 0.1 collective-permute-start.3
  11.7 2.0 %collective-permute-start.2 = (bf16[2,128,128]{2,1,0:T(8,128)(2,1)S(1)}, bf16[2,128,128]{2,1,0:T(8,128)(2,1)S(1)}, u32[]{:S(2)}, u32[]{:S(2)}) collective-permute-start(bf16[2,128,128]{2,1,0:T(8,128)(2,1)S(1)} %get-tuple-element.39.refs_0_), channel_id=1, source_target_pairs={{0,6},{1,7},{2,4},{3,5},{4,2},{5,3},{6,0},{7,1},{8,14},{9,15},{10,... | collective-permute-start | bytes 196616 | tf_op jit(solution)/shard_map/ppermute | solution.py:323
  13.7 0.0 collective-permute-done.6.refs_3_
  13.7 4.3 %collective-permute-start.1 = (bf16[2,128,128]{2,1,0:T(8,128)(2,1)S(1)}, bf16[2,128,128]{2,1,0:T(8,128)(2,1)S(1)}, u32[]{:S(2)}, u32[]{:S(2)}) collective-permute-start(bf16[2,128,128]{2,1,0:T(8,128)(2,1)S(1)} %get-tuple-element.39.refs_0_), channel_id=1, source_target_pairs={{0,2},{1,3},{2,0},{3,1},{4,6},{5,7},{6,4},{7,5},{8,10},{9,11},{10,... | collective-permute-start | bytes 196616 | tf_op jit(solution)/shard_map/ppermute | solution.py:323
  18.0 1.3 %collective-permute-done.5.refs_2_ = bf16[2,144,128]{2,1,0:T(8,128)(2,1)S(1)} collective-permute-done((bf16[2,144,128]{2,1,0:T(8,128)(2,1)S(1)}, bf16[2,144,128]{2,1,0:T(8,128)(2,1)S(1)}, u32[]{:S(2)}, u32[]{:S(2)}) %collective-permute-start.5) | collective-permute-done | bytes 73760 | tf_op jit(solution)/shard_map/ppermute | solution.py:323
  19.3 0.0 collective-permute-done.4.refs_1_
  19.4 5.4 %forward.1 = (f32[2,2,1032,128]{3,2,1,0:T(8,128)S(1)}, f32[2,2,1032,128]{3,2,1,0:T(8,128)S(1)}, f32[2,1032,128]{2,1,0:T(8,128)S(1)}, f32[2,1032,128]{2,1,0:T(8,1...) custom-call(bf16[2,144,128]{2,1,0:T(8,128)(2,1)S(1)} %get-tuple-elem, ...), custom_call_target="tpu_custom_call" | custom-call | flops 335544320 | bytes 33554432 | tf_op jit(solution)/shard_map/forward/pallas_call | solution.py:481
  24.8 0.0 collective-permute-done.3.refs_3_
  24.8 0.0 collective-permute-done.2.refs_2_
  24.8 0.0 collective-permute-done.1.refs_1_
  24.8 4.1 %backward_second.1 = (f32[1024,128]{1,0:T(8,128)S(1)}, bf16[128,768]{1,0:T(8,128)(2,1)S(1)}) custom-call(bf16[2,144,128]{2,1,0:T(8,128)(2,1)S(1)} %get-tuple-element.38.refs_0_.pair.pair_ref, bf16[2,128,128]{2,1,0:T(8,128)(2,1)S(1)} %get-tuple-element.39.refs_0_, bf16[2,128,128]{2,1,0:T(8,128)(2,1)S(1)} %collective-permute-done.1.refs_1_, ...), custom_call_target="tpu_custom_call" | custom-call | flops 335544320 | bytes 25165824 | tf_op jit(solution)/shard_map/backward_second/pallas_call | solution.py:493
  28.9 1.6 %collective-permute-start.7 = (bf16[128,768]{1,0:T(8,128)(2,1)S(1)}, bf16[128,768]{1,0:T(8,128)(2,1)S(1)}, u32[]{:S(2)}, u32[]{:S(2)}) collective-permute-start(bf16[128,768]{1,0:T(8,128)(2,1)S(1)} %get-tuple-element.56), channel_id=1, source_target_pairs={{0,16},{8,24},{16,0},{24,8},{1,17},{9,25},{17,1},{25,9},{2,18},{10... | collective-permute-start | bytes 589832 | tf_op jit(solution)/shard_map/ppermute | solution.py:323
  30.5 2.3 %backward_left.1 = (bf16[1024,384]{1,0:T(8,128)(2,1)S(1)}, f32[1032,128]{1,0:T(8,128)S(1)}, bf16[128,512]{1,0:T(8,128)(2,1)S(1)}) custom-call(f32[1024,128]{1,0:T(8,128)S(1)} %get-tuple-element.52.up_in_ref.up_ref, bf16[2,128,768]{2,1,0:T(8,128)(2,1)S(1)} %get-tuple-element.40.refs_4_.weights, f32[2,1280]{1,0:T(2,128)S(1)} %get-tuple-element.41.refs_5_.vectors, ...), custom_call_target="tpu_custom_call" | custom-call | flops 335544320 | bytes 12582912 | tf_op jit(solution)/shard_map/backward_left/pallas_call | solution.py:511
  32.8 0.6 %collective-permute-start.9 = (bf16[128,512]{1,0:T(8,128)(2,1)S(1)}, bf16[128,512]{1,0:T(8,128)(2,1)S(1)}, u32[]{:S(2)}, u32[]{:S(2)}) collective-permute-start(bf16[128,512]{1,0:T(8,128)(2,1)S(1)} %get-tuple-element.58), channel_id=1, source_target_pairs={{0,16},{8,24},{16,0},{24,8},{1,17},{9,25},{17,1},{25,9},{2,18},{10... | collective-permute-start | bytes 393224 | tf_op jit(solution)/shard_map/ppermute | solution.py:323
  33.4 1.8 %backward_right.1 = (bf16[1024,256]{1,0:T(8,128)(2,1)S(1)}, bf16[128,256]{1,0:T(8,128)(2,1)S(1)}) custom-call(f32[1032,128]{1,0:T(8,128)S(1)} %get-tuple-element.54.d_product_ref, f32[2,2,1032,128]{3,2,1,0:T(8,128)S(1)} %get-tuple-element.42.refs_6_.refs_0_, f32[2,2,1032,128]{3,2,1,0:T(8,128)S(1)} %get-tuple-element.43.refs_7_.refs_1_, ...), custom_call_target="tpu_custom_call" | custom-call | flops 335544320 | bytes 12582912 | tf_op jit(solution)/shard_map/backward_right/pallas_call | solution.py:527
  35.2 0.6 %collective-permute-done.7 = bf16[128,768]{1,0:T(8,128)(2,1)S(1)} collective-permute-done((bf16[128,768]{1,0:T(8,128)(2,1)S(1)}, bf16[128,768]{1,0:T(8,128)(2,1)S(1)}, u32[]{:S(2)}, u32[]{:S(2)}) %collective-permute-start.7) | collective-permute-done | bytes 196640 | tf_op jit(solution)/shard_map/ppermute | solution.py:323
  35.9 0.1 collective-permute-start.8
  35.9 1.9 %collective-permute-done.9 = bf16[128,512]{1,0:T(8,128)(2,1)S(1)} collective-permute-done((bf16[128,512]{1,0:T(8,128)(2,1)S(1)}, bf16[128,512]{1,0:T(8,128)(2,1)S(1)}, u32[]{:S(2)}, u32[]{:S(2)}) %collective-permute-start.9) | collective-permute-done | bytes 131104 | tf_op jit(solution)/shard_map/ppermute | solution.py:323
  37.9 0.1 collective-permute-start.10
  37.9 0.0 collective-permute-done.8.rest_near
  38.0 0.6 %collective-permute-start.11 = (bf16[128,256]{1,0:T(8,128)(2,1)S(1)}, bf16[128,256]{1,0:T(8,128)(2,1)S(1)}, u32[]{:S(2)}, u32[]{:S(2)}) collective-permute-start(bf16[128,256]{1,0:T(8,128)(2,1)S(1)} %add_convert_fusion.2.right), channel_id=1, source_target_pairs={{0,16},{8,24},{16,0},{24,8},{1,17},{9,25},{17,1},{25,9},{2,18},{10... | collective-permute-start | bytes 196616 | tf_op jit(solution)/shard_map/ppermute | solution.py:323
  38.6 1.0 %own_rows.1 = bf16[128,128]{1,0:T(8,128)(2,1)} custom-call(bf16[2,144,128]{2,1,0:T(8,128)(2,1)S(1)} %get-tuple-element.38.refs_0_.pair.pair_ref, f32[1024,128]{1,0:T(8,128)S(1)} %get-tuple-element.52.up_in_ref.up_ref, bf16[1024,384]{1,0:T(8,128)(2,1)S(1)} %get-tuple-element.53.d_left_ref, bf16[1024,256]{1,0:T(8,128)(2,1)S(1)} %get-tuple-element.55.d_right_ref, ...), custom_call_target="tpu_custom_call" | custom-call | flops 335544320 | bytes 4194304 | tf_op jit(solution)/shard_map/own_rows/pallas_call | solution.py:540
  39.6 0.0 collective-permute-done.10.left_near
  39.6 2.9 %collective-permute-done.11.right_far = bf16[128,256]{1,0:T(8,128)(2,1)S(1)} collective-permute-done((bf16[128,256]{1,0:T(8,128)(2,1)S(1)}, bf16[128,256]{1,0:T(8,128)(2,1)S(1)}, u32[]{:S(2)}, u32[]{:S(2)}) %collective-permute-start.11) | collective-permute-done | bytes 65568 | tf_op jit(solution)/shard_map/ppermute | solution.py:323
  42.5 0.9 %add_grads.1 = (f32[2,128,640]{2,1,0:T(8,128)}, f32[2,128,128]{2,1,0:T(8,128)}) custom-call(bf16[128,1024]{1,0:T(8,128)(2,1)S(1)} %pad_maximum_fusion.rest, bf16[128,1024]{1,0:T(8,128)(2,1)S(1)} %collective-permute-done.8.rest_near, bf16[128,512]{1,0:T(8,128)(2,1)S(1)} %add_convert_fusion.1.left, bf16[128,512]{1,0:T(8,128)(2,1)S(1)} %collective-permute-done.10.left_near, ...), custom_call_target="tpu_custom_call" | custom-call | tf_op jit(solution)/shard_map/add_grads/pallas_call | solution.py:557
  (6 shorter events, 0.2 us)
Async XLA Ops:
  2.5 4.6 %copy-start = (bf16[272,128]{1,0:T(8,128)(2,1)S(1)}, bf16[272,128]{1,0:T(8,128)(2,1)}, u32[]{:S(2)}) copy-start(bf16[272,128]{1,0:T(8,128)(2,1)} %get-tuple-element.32.near_ref) | copy-start | bytes 208900
  2.5 4.6 %collective-permute-start = (bf16[272,128]{1,0:T(8,128)(2,1)}, bf16[272,128]{1,0:T(8,128)(2,1)S(1)}, u32[]{:S(2)}, u32[]{:S(2)}) collective-permute-start(bf16[272,128]{1,0:T(8,128)(2,1)} %get-tuple-element.32.near_ref), channel_id=1, source_target_pairs={{0,1},{1,0},{2,3},{3,2},{4,5},{5,4},{6,7},{7,6},{8,9},{9,8},{10,11... | collective-permute-start | bytes 208904 | tf_op jit(solution)/shard_map/ppermute | solution.py:323
  3.1 1.0 %copy-start.1 = (bf16[2,128,768]{2,1,0:T(8,128)(2,1)S(1)}, bf16[2,128,768]{2,1,0:T(8,128)(2,1)}, u32[]{:S(2)}) copy-start(bf16[2,128,768]{2,1,0:T(8,128)(2,1)} %get-tuple-element.33.weights_in) | copy-start | bytes 1179652
  4.1 0.7 %copy-start.2 = (f32[2,1280]{1,0:T(2,128)S(1)}, f32[2,1280]{1,0:T(2,128)}, u32[]{:S(2)}) copy-start(f32[2,1280]{1,0:T(2,128)} %get-tuple-element.34.vectors_in) | copy-start | bytes 30724
  7.1 6.6 %collective-permute-start.6 = (bf16[2,144,128]{2,1,0:T(8,128)(2,1)S(1)}, bf16[2,144,128]{2,1,0:T(8,128)(2,1)S(1)}, u32[]{:S(2)}, u32[]{:S(2)}) collective-permute-start(bf16[2,144,128]{2,1,0:T(8,128)(2,1)S(1)} %get-tuple-element.38.refs_0_.pair.pair_ref), channel_id=1, source_target_pairs={{0,4},{1,5},{2,6},{3,7},{4,0},{5,1},{6,2},{7,3},{8,12},{9,13},{10,... | collective-permute-start | bytes 221192 | tf_op jit(solution)/shard_map/ppermute | solution.py:323
  7.5 11.8 %collective-permute-start.5 = (bf16[2,144,128]{2,1,0:T(8,128)(2,1)S(1)}, bf16[2,144,128]{2,1,0:T(8,128)(2,1)S(1)}, u32[]{:S(2)}, u32[]{:S(2)}) collective-permute-start(bf16[2,144,128]{2,1,0:T(8,128)(2,1)S(1)} %get-tuple-element.38.refs_0_.pair.pair_ref), channel_id=1, source_target_pairs={{0,6},{1,7},{2,4},{3,5},{4,2},{5,3},{6,0},{7,1},{8,14},{9,15},{10,... | collective-permute-start | bytes 221192 | tf_op jit(solution)/shard_map/ppermute | solution.py:323
  10.2 9.1 %collective-permute-start.4 = (bf16[2,144,128]{2,1,0:T(8,128)(2,1)S(1)}, bf16[2,144,128]{2,1,0:T(8,128)(2,1)S(1)}, u32[]{:S(2)}, u32[]{:S(2)}) collective-permute-start(bf16[2,144,128]{2,1,0:T(8,128)(2,1)S(1)} %get-tuple-element.38.refs_0_.pair.pair_ref), channel_id=1, source_target_pairs={{0,2},{1,3},{2,0},{3,1},{4,6},{5,7},{6,4},{7,5},{8,10},{9,11},{10,... | collective-permute-start | bytes 221192 | tf_op jit(solution)/shard_map/ppermute | solution.py:323
  11.6 13.2 %collective-permute-start.3 = (bf16[2,128,128]{2,1,0:T(8,128)(2,1)S(1)}, bf16[2,128,128]{2,1,0:T(8,128)(2,1)S(1)}, u32[]{:S(2)}, u32[]{:S(2)}) collective-permute-start(bf16[2,128,128]{2,1,0:T(8,128)(2,1)S(1)} %get-tuple-element.39.refs_0_), channel_id=1, source_target_pairs={{0,4},{1,5},{2,6},{3,7},{4,0},{5,1},{6,2},{7,3},{8,12},{9,13},{10,... | collective-permute-start | bytes 196616 | tf_op jit(solution)/shard_map/ppermute | solution.py:323
  11.7 13.1 %collective-permute-start.2 = (bf16[2,128,128]{2,1,0:T(8,128)(2,1)S(1)}, bf16[2,128,128]{2,1,0:T(8,128)(2,1)S(1)}, u32[]{:S(2)}, u32[]{:S(2)}) collective-permute-start(bf16[2,128,128]{2,1,0:T(8,128)(2,1)S(1)} %get-tuple-element.39.refs_0_), channel_id=1, source_target_pairs={{0,6},{1,7},{2,4},{3,5},{4,2},{5,3},{6,0},{7,1},{8,14},{9,15},{10,... | collective-permute-start | bytes 196616 | tf_op jit(solution)/shard_map/ppermute | solution.py:323
  13.7 11.0 %collective-permute-start.1 = (bf16[2,128,128]{2,1,0:T(8,128)(2,1)S(1)}, bf16[2,128,128]{2,1,0:T(8,128)(2,1)S(1)}, u32[]{:S(2)}, u32[]{:S(2)}) collective-permute-start(bf16[2,128,128]{2,1,0:T(8,128)(2,1)S(1)} %get-tuple-element.39.refs_0_), channel_id=1, source_target_pairs={{0,2},{1,3},{2,0},{3,1},{4,6},{5,7},{6,4},{7,5},{8,10},{9,11},{10,... | collective-permute-start | bytes 196616 | tf_op jit(solution)/shard_map/ppermute | solution.py:323
  28.9 6.9 %collective-permute-start.7 = (bf16[128,768]{1,0:T(8,128)(2,1)S(1)}, bf16[128,768]{1,0:T(8,128)(2,1)S(1)}, u32[]{:S(2)}, u32[]{:S(2)}) collective-permute-start(bf16[128,768]{1,0:T(8,128)(2,1)S(1)} %get-tuple-element.56), channel_id=1, source_target_pairs={{0,16},{8,24},{16,0},{24,8},{1,17},{9,25},{17,1},{25,9},{2,18},{10... | collective-permute-start | bytes 589832 | tf_op jit(solution)/shard_map/ppermute | solution.py:323
  32.8 5.0 %collective-permute-start.9 = (bf16[128,512]{1,0:T(8,128)(2,1)S(1)}, bf16[128,512]{1,0:T(8,128)(2,1)S(1)}, u32[]{:S(2)}, u32[]{:S(2)}) collective-permute-start(bf16[128,512]{1,0:T(8,128)(2,1)S(1)} %get-tuple-element.58), channel_id=1, source_target_pairs={{0,16},{8,24},{16,0},{24,8},{1,17},{9,25},{17,1},{25,9},{2,18},{10... | collective-permute-start | bytes 393224 | tf_op jit(solution)/shard_map/ppermute | solution.py:323
  35.9 2.1 %collective-permute-start.8 = (bf16[128,1024]{1,0:T(8,128)(2,1)S(1)}, bf16[128,1024]{1,0:T(8,128)(2,1)S(1)}, u32[]{:S(2)}, u32[]{:S(2)}) collective-permute-start(bf16[128,1024]{1,0:T(8,128)(2,1)S(1)} %pad_maximum_fusion.rest), channel_id=1, source_target_pairs={{0,8},{8,0},{16,24},{24,16},{1,9},{9,1},{17,25},{25,17},{2,10},{10... | collective-permute-start | bytes 786440 | tf_op jit(solution)/shard_map/ppermute | solution.py:323
  37.9 1.7 %collective-permute-start.10 = (bf16[128,512]{1,0:T(8,128)(2,1)S(1)}, bf16[128,512]{1,0:T(8,128)(2,1)S(1)}, u32[]{:S(2)}, u32[]{:S(2)}) collective-permute-start(bf16[128,512]{1,0:T(8,128)(2,1)S(1)} %add_convert_fusion.1.left), channel_id=1, source_target_pairs={{0,8},{8,0},{16,24},{24,16},{1,9},{9,1},{17,25},{25,17},{2,10},{10... | collective-permute-start | bytes 393224 | tf_op jit(solution)/shard_map/ppermute | solution.py:323
  38.0 4.5 %collective-permute-start.11 = (bf16[128,256]{1,0:T(8,128)(2,1)S(1)}, bf16[128,256]{1,0:T(8,128)(2,1)S(1)}, u32[]{:S(2)}, u32[]{:S(2)}) collective-permute-start(bf16[128,256]{1,0:T(8,128)(2,1)S(1)} %add_convert_fusion.2.right), channel_id=1, source_target_pairs={{0,16},{8,24},{16,0},{24,8},{1,17},{9,25},{17,1},{25,9},{2,18},{10... | collective-permute-start | bytes 196616 | tf_op jit(solution)/shard_map/ppermute | solution.py:323
